TPU v7x, 32 devices: a whole 2x2x4 slice. The times are simulated.
32 devices in a mesh: row: 16 (over z, y, x), col: 2 (over core).
Axes of the slice: x: 2, y: 2, z: 4, core: 2. Of those that a mesh axis runs over, the one named last changes fastest.
Arguments:
- hamiltonian_blocks: bfloat16 [16, 2, 64, 128, 128], P('row', 'col'), may hold values from -0.046875 to 0.046875
- block_rows: int32 [16, 2, 64], P('row', 'col'), may hold values from 0 to 1, as said below
- block_cols: int32 [16, 2, 64], P('row', 'col'), may hold values from 0 to 15
- block_counts: int32 [16, 2], P('row', 'col'), may hold values from 16 to 64, as said below
- initial: float32 [4096, 128], P(('row', 'col')), may hold values from -6 to 6
- center: float32 [1], replicated, may hold values from -0.3 to 0.3
- halfwidth: float32 [1], replicated, may hold values from 1 to 1.5
Outputs:
- filtered: float32 [4096, 128], P(('row', 'col'))
Inputs may be any that keep to these rules, and one draw needn't show every extreme that they name: `block_rows`: padded slots hold arbitrary values. `block_counts`: some tile is full in every draw.
All inputs are finite; a program needn't handle non-finite values.
Results may differ from a plain program's by a relative error of at most 0.0068.
Values may be sent and summed in bfloat16 or wider, within the bound.
No kernel may reach another device: no remote copies, remote signals or barrier semaphores. Data moves between devices by JAX's collectives and lax.ppermute only.
A program may use at most 128 MiB of HBM per device.

v0:
```python
import jax
import jax.numpy as jnp
from jax import lax
from jax.sharding import PartitionSpec as P

SLAB = 1
DEGREE = 3


def body(hamiltonian_blocks, block_rows, block_cols, block_counts, initial, center, halfwidth):
    stacked = hamiltonian_blocks[0, 0]
    slot_rows = block_rows[0, 0]
    slot_cols = block_cols[0, 0]
    live_count = block_counts[0, 0]
    grid_rows = lax.axis_size("row")
    grid_cols = lax.axis_size("col")
    orbitals = stacked.shape[1]
    vectors = initial.shape[1]
    slots = stacked.shape[0]
    row_segments = grid_cols * SLAB
    col_segments = grid_rows * SLAB
    highest = lax.Precision.HIGHEST
    is_live = jnp.arange(slots, dtype=jnp.int32) < live_count
    row_onehot = (
        (slot_rows[None, :] == jnp.arange(row_segments, dtype=jnp.int32)[:, None])
        & is_live[None, :]
    ).astype(jnp.float32)
    col_onehot = (
        (slot_cols[None, :] == jnp.arange(col_segments, dtype=jnp.int32)[:, None])
        & is_live[None, :]
    ).astype(jnp.float32)

    def column_tile(col_index):
        weights = (row_onehot * col_onehot[col_index][None, :]).astype(jnp.bfloat16)
        return jnp.einsum("rs,sab->rab", weights, stacked, preferred_element_type=jnp.float32)

    dense_tile = lax.map(column_tile, jnp.arange(col_segments, dtype=jnp.int32))
    previous = initial
    current = initial
    for degree_step in range(DEGREE):
        panel = current.astype(jnp.bfloat16)
        apply_column_panel = lax.all_gather(panel, "row", axis=0, tiled=True).reshape(
            -1, orbitals, vectors
        )
        apply_row_panel = lax.all_gather(panel, "col", axis=0, tiled=True).reshape(
            -1, orbitals, vectors
        )
        upper_partial = jnp.einsum(
            "crab,cbv->rav", dense_tile, apply_column_panel.astype(jnp.float32), precision=highest
        )
        upper_sum = lax.psum_scatter(
            upper_partial.reshape(-1, vectors), "col", scatter_dimension=0, tiled=True
        )
        lower_partial = jnp.einsum(
            "crab,rav->cbv", dense_tile, apply_row_panel.astype(jnp.float32), precision=highest
        )
        lower_sum = lax.psum_scatter(
            lower_partial.reshape(-1, vectors), "row", scatter_dimension=0, tiled=True
        )
        applied = upper_sum + lower_sum
        shifted = (applied - center[0] * current) / halfwidth[0]
        if degree_step == 0:
            following = shifted
        else:
            following = 2.0 * shifted - previous
        previous = current
        current = following
    return current


def solution(mesh):
    in_specs = (
        P("row", "col", None, None, None),
        P("row", "col", None),
        P("row", "col", None),
        P("row", "col"),
        P(("row", "col"), None),
        P(),
        P(),
    )
    out_specs = P(("row", "col"), None)
    return jax.shard_map(body, mesh=mesh, in_specs=in_specs, out_specs=out_specs, check_vma=False)
```

profile of v0, /device:TPU:0, one launch (start us, length us, event | category | flops | bytes accessed | tf_op | source)
XLA Modules:
  0.0 463.6 jit_solution(8193208447330940956)
XLA Ops:
  7.2 3.0 copy.19
  10.2 53.1 %while.11 = (s32[]{:T(128)}, f32[16,2,128,128]{3,1,2,0:T(2,128)}, s32[16]{0:T(128)S(1)}, bf16[16,64]{1,0:T(8,128)(2,1)S(1)}, bf16[64,128,128]{2,0,1:T(8,128)(2,1...) while((s32[]{:T(128)}, f32[16,2,128,128]{3,1,2,0:T(2,128)}, ...), condition=%wide.region_1.2_spmd.clone, body=%wide.region_0.1_spmd.clone.sunk | while | flops 4194693 | bytes 2229591 | solution.py:37
  10.3 0.6 dynamic_slice.13
  12.5 1.0 fusion.32
  13.6 0.6 dynamic_slice.13
  15.8 1.0 fusion.32
  16.9 0.6 dynamic_slice.13
  19.2 1.0 fusion.32
  20.2 0.6 dynamic_slice.13
  22.5 1.0 fusion.32
  23.5 0.6 dynamic_slice.13
  25.8 1.0 fusion.32
  26.8 0.6 dynamic_slice.13
  29.1 1.0 fusion.32
  30.1 0.6 dynamic_slice.13
  32.4 1.0 fusion.32
  33.5 0.6 dynamic_slice.13
  35.7 1.0 fusion.32
  39.1 1.0 fusion.32
  42.4 1.0 fusion.32
  45.7 1.0 fusion.32
  49.0 1.0 fusion.32
  52.3 1.0 fusion.32
  55.6 1.0 fusion.32
  58.9 1.0 fusion.32
  62.3 1.0 fusion.32
  63.3 1.8 copy.15
  65.2 45.3 %all_gather.18 = bf16[2048,128]{1,0:T(8,128)(2,1)S(1)} all-gather(bf16[128,128]{1,0:T(8,128)(2,1)S(1)} %convert_element_type.26), channel_id=1, replica_groups=mesh['row'=16,'col'=2] {'row'}, dimensions={0}, use_global_device_ids=true | all-gather | bytes 557056 | tf_op jit(solution)/shard_map/all_gather | solution.py:42
  110.5 1.7 convolution_bitcast_fusion.6
  112.3 2.8 copy.12
  115.1 1.9 all_gather.19
  116.9 2.1 convolution_bitcast_fusion.3
  120.4 76.7 %reduce-scatter.9.cloned.1.call-done = f32[128,128]{1,0:T(8,128)} async-done(((f32[2048,128]{1,0:T(8,128)}), f32[128,128]{1,0:T(8,128)}) %reduce-scatter.9.cloned.1.call-update) | async-done | bytes 65552 | tf_op jit(solution)/shard_map/reduce_scatter | solution.py:57
  197.1 0.9 fusion.13
  198.0 38.9 %all_gather.20 = bf16[2048,128]{1,0:T(8,128)(2,1)S(1)} all-gather(bf16[128,128]{1,0:T(8,128)(2,1)S(1)} %get-tuple-element.72), channel_id=1, replica_groups=mesh['row'=16,'col'=2] {'row'}, dimensions={0}, use_global_device_ids=true | all-gather | bytes 557056 | tf_op jit(solution)/shard_map/all_gather | solution.py:42
  236.9 3.3 convolution_bitcast_fusion.5
  240.3 1.9 all_gather.21
  242.1 2.1 convolution_bitcast_fusion.2
  244.3 0.7 reduce-scatter.11.cloned.1.call-done
  245.0 81.2 %reduce-scatter.13.cloned.1.call-done = f32[128,128]{1,0:T(8,128)} async-done(((f32[2048,128]{1,0:T(8,128)}), f32[128,128]{1,0:T(8,128)}) %reduce-scatter.13.cloned.1.call-update) | async-done | bytes 65552 | tf_op jit(solution)/shard_map/reduce_scatter | solution.py:57
  326.2 0.9 fusion.12
  327.1 38.9 %all_gather.22 = bf16[2048,128]{1,0:T(8,128)(2,1)S(1)} all-gather(bf16[128,128]{1,0:T(8,128)(2,1)S(1)} %get-tuple-element.70), channel_id=1, replica_groups=mesh['row'=16,'col'=2] {'row'}, dimensions={0}, use_global_device_ids=true | all-gather | bytes 557056 | tf_op jit(solution)/shard_map/all_gather | solution.py:42
  366.0 3.3 convolution_bitcast_fusion.4
  369.4 1.9 all_gather.23
  371.2 2.0 convolution_bitcast_fusion.1
  373.3 0.8 reduce-scatter.15.cloned.1.call-done
  374.1 81.1 %reduce-scatter.17.cloned.1.call-done = f32[128,128]{1,0:T(8,128)} async-done(((f32[2048,128]{1,0:T(8,128)}), f32[128,128]{1,0:T(8,128)}) %reduce-scatter.17.cloned.1.call-update) | async-done | bytes 65552 | tf_op jit(solution)/shard_map/reduce_scatter | solution.py:57
  455.3 1.5 multiply_subtract_fusion
  (50 shorter events, 5.2 us)
Async XLA Ops:
  6.5 113.8 %reduce-scatter.7.cloned.1.call-start = ((), (), s32[]{:S(2)}) async-start(), calls=%async_computation.6 | async-start | bytes 196608 | tf_op jit(solution)/shard_map/reduce_scatter | solution.py:51
  7.2 3.0 copy-start.3
  7.2 3.0 copy-start.2
  10.2 53.1 %copy-start.1 = (f32[128,128]{1,0:T(8,128)S(1)}, f32[128,128]{1,0:T(8,128)}, u32[]{:S(2)}) copy-start(f32[128,128]{1,0:T(8,128)} %param.13) | copy-start | bytes 196612
  65.2 45.4 %copy-start = (f32[16,2,128,128]{3,2,1,0:T(8,128)}, f32[16,2,128,128]{3,2,1,0:T(8,128)S(1)}, u32[]{:S(2)}) copy-start(f32[16,2,128,128]{3,2,1,0:T(8,128)S(1)} %copy.15) | copy-start | bytes 6291460
  112.2 84.9 %reduce-scatter.9.cloned.1.call-start = ((), (), s32[]{:S(2)}) async-start(), calls=%async_computation.7 | async-start | bytes 1114112 | tf_op jit(solution)/shard_map/reduce_scatter | solution.py:57
  119.0 126.0 %reduce-scatter.11.cloned.1.call-start = ((), (), s32[]{:S(2)}) async-start(), calls=%async_computation.8 | async-start | bytes 196608 | tf_op jit(solution)/shard_map/reduce_scatter | solution.py:51
  240.2 86.0 %reduce-scatter.13.cloned.1.call-start = ((), (), s32[]{:S(2)}) async-start(), calls=%async_computation.9 | async-start | bytes 1114112 | tf_op jit(solution)/shard_map/reduce_scatter | solution.py:57
  244.2 129.9 %reduce-scatter.15.cloned.1.call-start = ((), (), s32[]{:S(2)}) async-start(), calls=%async_computation.10 | async-start | bytes 196608 | tf_op jit(solution)/shard_map/reduce_scatter | solution.py:51
  369.3 85.9 %reduce-scatter.17.cloned.1.call-start = ((), (), s32[]{:S(2)}) async-start(), calls=%async_computation.11 | async-start | bytes 1114112 | tf_op jit(solution)/shard_map/reduce_scatter | solution.py:57
Sparse Core Ops, SparseCore 0:
  112.4 3.3 reduce-scatter.6
  119.1 77.9 reduce-scatter.8
  240.4 4.5 reduce-scatter.10
  247.2 78.9 reduce-scatter.12
  369.5 4.6 reduce-scatter.14
  376.2 78.9 reduce-scatter.16
where the time goes:
time: 465 us; the launch traced here: 464 us
  waiting for transfers between devices  241 us (52%)
  blocking collectives  129 us (28%)
  matrix products  31 us (7%)
  loops' own time  27.1 us (6%)
  local copies, waits for them, and re-layouts  17 us (4%)
  between operations  15.5 us (3%)
    reduce_scatter x3, waiting for transfers between devices, body(): lax.psum_scatter(lower_partial.reshape(-1, vectors), 'row', scatter_dimen...  239 us
    all_gather x3, blocking collectives, body(): lax.all_gather(panel, 'row', axis=0, tiled=True)  123 us
    another operation x1, loops' own time, body(): dense_tile = lax.map(column_tile, jnp.arange(col_segments, dtype=jnp.int32))  27.1 us
    dot_general x16, matrix products, column_tile(): jnp.einsum('rs,sab->rab', weights, stacked, preferred_element_type=jnp.fl...  16.6 us
  transfers between devices with their start and end apart: 6, of which 5 were waited for; matrix products, arithmetic and copies ran while one was open for 2% of the time, Pallas kernels for 0%

commit v1 on v0

v1 whole, which is shorter than its diff:
```python
import functools

import jax
import jax.numpy as jnp
from jax import lax
from jax.experimental import pallas as pl
from jax.experimental.pallas import tpu as pltpu
from jax.sharding import PartitionSpec as P

DEGREE = 3
RADIX = 4
CHUNK = 8


def stage_strides(size):
    found = []
    stride = 1
    while stride < size:
        radix = RADIX if size % (stride * RADIX) == 0 else size // stride
        found.append((stride, radix))
        stride *= radix
    return found[::-1]


def arrival_order(strides):
    order = [0]
    for stride, radix in strides:
        order = [k * stride ^ offset for k in range(radix) for offset in order]
    return order


def swap(x, axis, size, offset):
    return lax.ppermute(x, axis, [(source, source ^ offset) for source in range(size)])


def build_tile(rows, cols, count, stacked, grid_rows, grid_cols):
    slots, orb, _ = stacked.shape
    chunk = CHUNK if slots % CHUNK == 0 else slots
    cells = grid_rows * grid_cols

    def kernel(rows_ref, cols_ref, count_ref, stack_ref, dense_ref, acc_ref):
        step = pl.program_id(0)

        @pl.when(step == 0)
        def _():
            acc_ref[...] = jnp.zeros_like(acc_ref)

        first = step * chunk

        def add(s, carry):
            cell = cols_ref[first + s] * grid_cols + rows_ref[first + s]
            acc_ref[cell] += stack_ref[s].astype(jnp.float32)
            return carry

        lax.fori_loop(0, jnp.clip(count_ref[0] - first, 0, chunk), add, 0)

        @pl.when(step == pl.num_programs(0) - 1)
        def _():
            def put(cell, carry):
                dense_ref[cell] = acc_ref[cell].astype(jnp.bfloat16)
                return carry

            lax.fori_loop(0, cells, put, 0)

    return pl.pallas_call(
        kernel,
        grid_spec=pltpu.PrefetchScalarGridSpec(
            num_scalar_prefetch=3,
            grid=(slots // chunk,),
            in_specs=[pl.BlockSpec((chunk, orb, orb), lambda s, *_: (s, 0, 0))],
            out_specs=pl.BlockSpec((cells, orb, orb), lambda s, *_: (0, 0, 0)),
            scratch_shapes=[pltpu.VMEM((cells, orb, orb), jnp.float32)],
        ),
        out_shape=jax.ShapeDtypeStruct((cells, orb, orb), jnp.bfloat16),
        compiler_params=pltpu.CompilerParams(vmem_limit_bytes=60 * 2**20),
        name="build_tile",
    )(rows, cols, count, stacked)


def merge_tile(sources, targets, dense, received):
    cells, orb, _ = dense.shape
    grid_rows = sources.shape[0]
    grid_cols = targets.shape[0]

    def kernel(sources_ref, targets_ref, dense_ref, received_ref, tile_ref):
        first = sources_ref[pl.program_id(0)] * grid_cols
        for d in range(grid_cols):
            cell = first + targets_ref[d]
            block = dense_ref[cell].astype(jnp.float32) + received_ref[cell].astype(jnp.float32).T
            tile_ref[d * orb : (d + 1) * orb, :] = block.astype(jnp.bfloat16)

    return pl.pallas_call(
        kernel,
        grid_spec=pltpu.PrefetchScalarGridSpec(
            num_scalar_prefetch=2,
            grid=(grid_rows,),
            in_specs=[pl.BlockSpec((cells, orb, orb), lambda k, *_: (0, 0, 0))] * 2,
            out_specs=pl.BlockSpec((grid_cols * orb, orb), lambda k, *_: (0, k)),
        ),
        out_shape=jax.ShapeDtypeStruct((grid_cols * orb, grid_rows * orb), jnp.bfloat16),
        compiler_params=pltpu.CompilerParams(vmem_limit_bytes=60 * 2**20),
        name="merge_tile",
    )(sources, targets, dense, received)


def apply_tile(tile, pieces, grid_cols):
    height, width = tile.shape
    orb = height // grid_cols
    vectors = pieces[0].shape[1]

    def kernel(tile_ref, *refs):
        pieces_refs = refs[: len(pieces)]
        outs = refs[len(pieces) :]
        total = None
        at = 0
        for ref in pieces_refs:
            depth = ref.shape[0]
            part = jnp.dot(
                tile_ref[:, at : at + depth], ref[...], preferred_element_type=jnp.float32
            )
            total = part if total is None else total + part
            at += depth
        for d, out in enumerate(outs):
            out[...] = total[d * orb : (d + 1) * orb]

    return pl.pallas_call(
        kernel,
        out_shape=[jax.ShapeDtypeStruct((orb, vectors), jnp.float32)] * grid_cols,
        compiler_params=pltpu.CompilerParams(vmem_limit_bytes=60 * 2**20),
        name="apply_tile",
    )(tile, *pieces)


def body(hamiltonian_blocks, block_rows, block_cols, block_counts, initial, center, halfwidth):
    grid_rows = lax.axis_size("row")
    grid_cols = lax.axis_size("col")
    strides = stage_strides(grid_rows)

    def gather(panel):
        gathered = panel
        for index, (stride, radix) in enumerate(strides):
            parts = [gathered] + [
                swap(gathered, "row", grid_rows, k * stride) for k in range(1, radix)
            ]
            if index < len(strides) - 1:
                gathered = jnp.concatenate(parts, axis=0)
        return parts

    sources = jnp.array(arrival_order(strides), jnp.int32) ^ lax.axis_index("row")
    targets = jnp.arange(grid_cols, dtype=jnp.int32) ^ lax.axis_index("col")
    dense = build_tile(
        block_rows[0, 0], block_cols[0, 0], block_counts[0], hamiltonian_blocks[0, 0],
        grid_rows, grid_cols,
    )
    received = lax.all_to_all(dense, ("row", "col"), 0, 0)
    tile = merge_tile(sources, targets, dense, received)

    previous = initial
    current = initial
    for degree_step in range(DEGREE):
        pieces = gather(current.astype(jnp.bfloat16))
        own, *others = apply_tile(tile, pieces, grid_cols)
        applied = own
        for d, other in enumerate(others, start=1):
            applied = applied + swap(other, "col", grid_cols, d)
        shifted = (applied - center[0] * current) / halfwidth[0]
        following = shifted if degree_step == 0 else 2.0 * shifted - previous
        previous = current
        current = following
    return current


def solution(mesh):
    in_specs = (
        P("row", "col", None, None, None),
        P("row", "col", None),
        P("row", "col", None),
        P("row", "col"),
        P(("row", "col"), None),
        P(),
        P(),
    )
    out_specs = P(("row", "col"), None)
    return jax.shard_map(body, mesh=mesh, in_specs=in_specs, out_specs=out_specs, check_vma=False)
```

time: 465 us -> 108 us (0.23)
  waiting for transfers between devices: 241 us -> 43.8 us
  blocking collectives: 129 us -> 0 us
  starting transfers between devices: 0.21 us -> 31.5 us
  matrix products: 31 us -> 0 us
  loops' own time: 27.1 us -> 0 us
  Pallas kernels: 0 us -> 21.9 us
  between operations: 15.5 us -> 2.12 us
  local copies, waits for them, and re-layouts: 17 us -> 4.3 us
    reduce_scatter x6 -> x0, waiting for transfers between devices: 241 us -> none  [the longest x3 239 us: body(): lax.psum_scatter(lower_partial.reshape(-1, vectors), 'row', scatter_dimen...]
    all_gather x6 -> x0, blocking collectives: 129 us -> none  [the longest x3 123 us: body(): lax.all_gather(panel, 'row', axis=0, tiled=True)]
    ppermute x0 -> x21, waiting for transfers between devices: none -> 43.8 us  [swap(): lax.ppermute(x, axis, [(source, source ^ offset) for source in range(size)])]
    dot_general x22 -> x0, matrix products: 31 us -> none  [the longest x16 16.6 us: column_tile(): jnp.einsum('rs,sab->rab', weights, stacked, preferred_element_type=jnp.fl...]
    another operation x1 -> x0, loops' own time: 27.1 us -> none  [body(): dense_tile = lax.map(column_tile, jnp.arange(col_segments, dtype=jnp.int32))]
    ppermute x0 -> x21, starting transfers between devices: none -> 24 us  [swap(): lax.ppermute(x, axis, [(source, source ^ offset) for source in range(size)])]
    pallas_call x0 -> x5, Pallas kernels: none -> 21.9 us  [the longest x1 8.27 us: merge_tile(): pl.pallas_call(kernel, grid_spec=pltpu.PrefetchScalarGridSpec(num_scalar_...]
    dynamic_slice x16 -> x0, local copies, waits for them, and re-layouts: 9.21 us -> none  [body(): dense_tile = lax.map(column_tile, jnp.arange(col_segments, dtype=jnp.int32))]
  transfers between devices with their start and end apart: 6 -> 22, of which waited for: 5 -> 14; matrix products, arithmetic and copies ran while one was open for 2% -> 1% of each run, Pallas kernels for 0% -> 8%
where the time goes in v1:
time: 108 us
  waiting for transfers between devices  43.8 us (41%)
  starting transfers between devices  31.5 us (29%)
  Pallas kernels  21.9 us (20%)
  local copies, waits for them, and re-layouts  4.3 us (4%)
  other arithmetic  4.3 us (4%)
  between operations  2.12 us (2%)
    ppermute x21, waiting for transfers between devices, swap(): lax.ppermute(x, axis, [(source, source ^ offset) for source in range(size)])  43.8 us
    ppermute x21, starting transfers between devices, swap(): lax.ppermute(x, axis, [(source, source ^ offset) for source in range(size)])  24 us
    pallas_call x1, Pallas kernels, merge_tile(): pl.pallas_call(kernel, grid_spec=pltpu.PrefetchScalarGridSpec(num_scalar_...  8.27 us
    all_to_all x1, starting transfers between devices, body(): received = lax.all_to_all(dense, ('row', 'col'), 0, 0)  7.48 us
    pallas_call x3, Pallas kernels, apply_tile(): pl.pallas_call(kernel, out_shape=[jax.ShapeDtypeStruct((orb, vectors), jn...  7.34 us
    pallas_call x1, Pallas kernels, build_tile(): pl.pallas_call(kernel, grid_spec=pltpu.PrefetchScalarGridSpec(num_scalar_...  6.24 us
    unnamed x30, local copies, waits for them, and re-layouts  4.3 us
  transfers between devices with their start and end apart: 22, of which 14 were waited for; matrix products, arithmetic and copies ran while one was open for 1% of the time, Pallas kernels for 8%

profile of v1, /device:TPU:0, one launch (start us, length us, event | category | flops | bytes accessed | tf_op | source)
XLA Modules:
  0.0 107.9 jit_solution(9128115582805195008)
XLA Ops:
  0.7 6.2 %build_tile.1.dense_ref = bf16[32,128,128]{2,1,0:T(8,128)(2,1)} custom-call(s32[64]{0:T(128)} %bitcast.14, s32[64]{0:T(128)} %bitcast.15, s32[1]{0:T(128)} %bitcast.6.count_ref, bf16[64,128,128]{2,1,0:T(8,128)(2,1)} %bitcast.13), custom_call_target="tpu_custom_call" | custom-call | tf_op jit(solution)/shard_map/build_tile/pallas_call | solution.py:65
  6.9 7.5 %all-to-all-start = ((bf16[32,128,128]{2,1,0:T(8,128)(2,1)}), bf16[32,128,128]{2,1,0:T(8,128)(2,1)S(1)}, u32[]{:S(2)}, u32[]{:S(2)}) async-start(bf16[32,128,128]{2,1,0:T(8,128)(2,1)} %build_tile.1.dense_ref), calls=%async_computation | async-start | bytes 2097152 | tf_op jit(solution)/shard_map/all_to_all | solution.py:155
  14.4 3.7 %collective-permute-start.2 = (bf16[128,128]{1,0:T(8,128)(2,1)S(1)}, bf16[128,128]{1,0:T(8,128)(2,1)S(1)}, u32[]{:S(2)}, u32[]{:S(2)}) collective-permute-start(bf16[128,128]{1,0:T(8,128)(2,1)S(1)} %convert_element_type.9), channel_id=1, source_target_pairs={{0,24},{2,26},{4,28},{6,30},{8,16},{10,18},{12,20},{14,22},{16,8},... | collective-permute-start | bytes 98312 | tf_op jit(solution)/shard_map/ppermute | solution.py:33
  18.1 0.8 collective-permute-start
  18.9 18.3 %collective-permute-done.2 = bf16[128,128]{1,0:T(8,128)(2,1)S(1)} collective-permute-done((bf16[128,128]{1,0:T(8,128)(2,1)S(1)}, bf16[128,128]{1,0:T(8,128)(2,1)S(1)}, u32[]{:S(2)}, u32[]{:S(2)}) %collective-permute-start.2) | collective-permute-done | bytes 32800 | tf_op jit(solution)/shard_map/ppermute | solution.py:33
  37.2 6.3 %collective-permute-done.1 = bf16[128,128]{1,0:T(8,128)(2,1)S(1)} collective-permute-done((bf16[128,128]{1,0:T(8,128)(2,1)S(1)}, bf16[128,128]{1,0:T(8,128)(2,1)S(1)}, u32[]{:S(2)}, u32[]{:S(2)}) %collective-permute-start.1) | collective-permute-done | bytes 32800 | tf_op jit(solution)/shard_map/ppermute | solution.py:33
  43.5 1.5 %collective-permute-start.3 = (bf16[512,128]{1,0:T(8,128)(2,1)S(1)}, bf16[512,128]{1,0:T(8,128)(2,1)S(1)}, u32[]{:S(2)}, u32[]{:S(2)}) collective-permute-start(bf16[512,128]{1,0:T(8,128)(2,1)S(1)} %pad_maximum_fusion.refs_0_), channel_id=1, source_target_pairs={{0,2},{2,0},{4,6},{6,4},{8,10},{10,8},{12,14},{14,12},{16,18},{18,... | collective-permute-start | bytes 393224 | tf_op jit(solution)/shard_map/ppermute | solution.py:33
  45.0 1.5 %collective-permute-start.4 = (bf16[512,128]{1,0:T(8,128)(2,1)S(1)}, bf16[512,128]{1,0:T(8,128)(2,1)S(1)}, u32[]{:S(2)}, u32[]{:S(2)}) collective-permute-start(bf16[512,128]{1,0:T(8,128)(2,1)S(1)} %pad_maximum_fusion.refs_0_), channel_id=1, source_target_pairs={{0,4},{2,6},{4,0},{6,2},{8,12},{10,14},{12,8},{14,10},{16,20},{18,... | collective-permute-start | bytes 393224 | tf_op jit(solution)/shard_map/ppermute | solution.py:33
  46.5 0.5 collective-permute-start.5
  47.0 0.5 broadcast_xor_fusion.sources_ref
  47.6 0.5 iota_xor_fusion.targets_ref
  48.1 1.0 copy-done
  49.1 8.3 %merge_tile.1.tile_ref = bf16[256,2048]{1,0:T(8,128)(2,1)} custom-call(s32[16]{0:T(128)} %broadcast_xor_fusion.sources_ref, s32[2]{0:T(128)} %iota_xor_fusion.targets_ref, bf16[32,128,128]{2,1,0:T(8,128)(2,1)} %build_tile.1.dense_ref, bf16[32,128,128]{2,1,0:T(8,128)(2,1)} %copy-done), custom_call_target="tpu_custom_call" | custom-call | tf_op jit(solution)/shard_map/merge_tile/pallas_call | solution.py:92
  57.4 0.6 copy-done.5
  58.1 0.6 copy-done.7
  58.7 2.4 %apply_tile.3 = (f32[128,128]{1,0:T(8,128)}, f32[128,128]{1,0:T(8,128)}) custom-call(bf16[256,2048]{1,0:T(8,128)(2,1)} %merge_tile.1.tile_ref, bf16[512,128]{1,0:T(8,128)(2,1)} %copy-done.2, bf16[512,128]{1,0:T(8,128)(2,1)} %copy-done.5, bf16[512,128]{1,0:T(8,128)(2,1)} %copy-done.6, bf16[512,128]{1,0:T(8,128)(2,1)} %copy-done.7), custom_call_target="tpu_custom_call" | custom-call | tf_op jit(solution)/shard_map/apply_tile/pallas_call | solution.py:126
  62.5 0.2 collective-permute-done.6
  62.6 0.9 fusion.1
  63.5 1.4 %collective-permute-start.9 = (bf16[128,128]{1,0:T(8,128)(2,1)S(1)}, bf16[128,128]{1,0:T(8,128)(2,1)S(1)}, u32[]{:S(2)}, u32[]{:S(2)}) collective-permute-start(bf16[128,128]{1,0:T(8,128)(2,1)S(1)} %get-tuple-element.19), channel_id=1, source_target_pairs={{0,24},{2,26},{4,28},{6,30},{8,16},{10,18},{12,20},{14,22},{16,8},... | collective-permute-start | bytes 98312 | tf_op jit(solution)/shard_map/ppermute | solution.py:33
  64.9 0.4 collective-permute-start.8
  65.3 2.7 %collective-permute-start.7 = (bf16[128,128]{1,0:T(8,128)(2,1)S(1)}, bf16[128,128]{1,0:T(8,128)(2,1)S(1)}, u32[]{:S(2)}, u32[]{:S(2)}) collective-permute-start(bf16[128,128]{1,0:T(8,128)(2,1)S(1)} %get-tuple-element.19), channel_id=1, source_target_pairs={{0,8},{2,10},{4,12},{6,14},{8,0},{10,2},{12,4},{14,6},{16,24},{18,... | collective-permute-start | bytes 98312 | tf_op jit(solution)/shard_map/ppermute | solution.py:33
  68.0 1.5 %collective-permute-done.9 = bf16[128,128]{1,0:T(8,128)(2,1)S(1)} collective-permute-done((bf16[128,128]{1,0:T(8,128)(2,1)S(1)}, bf16[128,128]{1,0:T(8,128)(2,1)S(1)}, u32[]{:S(2)}, u32[]{:S(2)}) %collective-permute-start.9) | collective-permute-done | bytes 32800 | tf_op jit(solution)/shard_map/ppermute | solution.py:33
  69.5 1.0 collective-permute-done.8
  70.5 1.5 %collective-permute-start.10 = (bf16[512,128]{1,0:T(8,128)(2,1)S(1)}, bf16[512,128]{1,0:T(8,128)(2,1)S(1)}, u32[]{:S(2)}, u32[]{:S(2)}) collective-permute-start(bf16[512,128]{1,0:T(8,128)(2,1)S(1)} %pad_maximum_fusion.1.refs_0_), channel_id=1, source_target_pairs={{0,2},{2,0},{4,6},{6,4},{8,10},{10,8},{12,14},{14,12},{16,18},{18,... | collective-permute-start | bytes 393224 | tf_op jit(solution)/shard_map/ppermute | solution.py:33
  72.0 1.5 %collective-permute-start.11 = (bf16[512,128]{1,0:T(8,128)(2,1)S(1)}, bf16[512,128]{1,0:T(8,128)(2,1)S(1)}, u32[]{:S(2)}, u32[]{:S(2)}) collective-permute-start(bf16[512,128]{1,0:T(8,128)(2,1)S(1)} %pad_maximum_fusion.1.refs_0_), channel_id=1, source_target_pairs={{0,4},{2,6},{4,0},{6,2},{8,12},{10,14},{12,8},{14,10},{16,20},{18,... | collective-permute-start | bytes 393224 | tf_op jit(solution)/shard_map/ppermute | solution.py:33
  73.5 0.5 collective-permute-start.12
  74.0 2.3 %collective-permute-done.10.refs_1_ = bf16[512,128]{1,0:T(8,128)(2,1)S(1)} collective-permute-done((bf16[512,128]{1,0:T(8,128)(2,1)S(1)}, bf16[512,128]{1,0:T(8,128)(2,1)S(1)}, u32[]{:S(2)}, u32[]{:S(2)}) %collective-permute-start.10) | collective-permute-done | bytes 131104 | tf_op jit(solution)/shard_map/ppermute | solution.py:33
  76.3 3.6 %collective-permute-done.11.refs_2_ = bf16[512,128]{1,0:T(8,128)(2,1)S(1)} collective-permute-done((bf16[512,128]{1,0:T(8,128)(2,1)S(1)}, bf16[512,128]{1,0:T(8,128)(2,1)S(1)}, u32[]{:S(2)}, u32[]{:S(2)}) %collective-permute-start.11) | collective-permute-done | bytes 131104 | tf_op jit(solution)/shard_map/ppermute | solution.py:33
  80.0 0.6 copy-done.11
  80.6 0.7 copy-done.13
  81.3 2.5 %apply_tile.4 = (f32[128,128]{1,0:T(8,128)}, f32[128,128]{1,0:T(8,128)}) custom-call(bf16[256,2048]{1,0:T(8,128)(2,1)} %merge_tile.1.tile_ref, bf16[512,128]{1,0:T(8,128)(2,1)} %copy-done.4, bf16[512,128]{1,0:T(8,128)(2,1)} %copy-done.9, bf16[512,128]{1,0:T(8,128)(2,1)} %copy-done.11, bf16[512,128]{1,0:T(8,128)(2,1)} %copy-done.13), custom_call_target="tpu_custom_call" | custom-call | tf_op jit(solution)/shard_map/apply_tile/pallas_call | solution.py:126
  83.7 1.5 %collective-permute-done.13 = f32[128,128]{1,0:T(8,128)S(1)} collective-permute-done((f32[128,128]{1,0:T(8,128)}, f32[128,128]{1,0:T(8,128)S(1)}, u32[]{:S(2)}, u32[]{:S(2)}) %collective-permute-start.13) | collective-permute-done | bytes 65568 | tf_op jit(solution)/shard_map/ppermute | solution.py:33
  85.2 0.9 fusion
  86.0 1.7 %collective-permute-start.16 = (bf16[128,128]{1,0:T(8,128)(2,1)S(1)}, bf16[128,128]{1,0:T(8,128)(2,1)S(1)}, u32[]{:S(2)}, u32[]{:S(2)}) collective-permute-start(bf16[128,128]{1,0:T(8,128)(2,1)S(1)} %get-tuple-element.17), channel_id=1, source_target_pairs={{0,24},{2,26},{4,28},{6,30},{8,16},{10,18},{12,20},{14,22},{16,8},... | collective-permute-start | bytes 98312 | tf_op jit(solution)/shard_map/ppermute | solution.py:33
  87.7 0.9 collective-permute-start.15
  88.6 1.9 %collective-permute-start.14 = (bf16[128,128]{1,0:T(8,128)(2,1)S(1)}, bf16[128,128]{1,0:T(8,128)(2,1)S(1)}, u32[]{:S(2)}, u32[]{:S(2)}) collective-permute-start(bf16[128,128]{1,0:T(8,128)(2,1)S(1)} %get-tuple-element.17), channel_id=1, source_target_pairs={{0,8},{2,10},{4,12},{6,14},{8,0},{10,2},{12,4},{14,6},{16,24},{18,... | collective-permute-start | bytes 98312 | tf_op jit(solution)/shard_map/ppermute | solution.py:33
  90.5 1.3 %collective-permute-done.16 = bf16[128,128]{1,0:T(8,128)(2,1)S(1)} collective-permute-done((bf16[128,128]{1,0:T(8,128)(2,1)S(1)}, bf16[128,128]{1,0:T(8,128)(2,1)S(1)}, u32[]{:S(2)}, u32[]{:S(2)}) %collective-permute-start.16) | collective-permute-done | bytes 32800 | tf_op jit(solution)/shard_map/ppermute | solution.py:33
  91.8 1.0 collective-permute-done.15
  92.8 0.3 collective-permute-done.14
  93.1 0.2 collective-permute-start.17
  93.3 1.4 %collective-permute-start.18 = (bf16[512,128]{1,0:T(8,128)(2,1)S(1)}, bf16[512,128]{1,0:T(8,128)(2,1)S(1)}, u32[]{:S(2)}, u32[]{:S(2)}) collective-permute-start(bf16[512,128]{1,0:T(8,128)(2,1)S(1)} %pad_maximum_fusion.2.refs_0_), channel_id=1, source_target_pairs={{0,4},{2,6},{4,0},{6,2},{8,12},{10,14},{12,8},{14,10},{16,20},{18,... | collective-permute-start | bytes 393224 | tf_op jit(solution)/shard_map/ppermute | solution.py:33
  94.7 2.0 %collective-permute-start.19 = (bf16[512,128]{1,0:T(8,128)(2,1)S(1)}, bf16[512,128]{1,0:T(8,128)(2,1)S(1)}, u32[]{:S(2)}, u32[]{:S(2)}) collective-permute-start(bf16[512,128]{1,0:T(8,128)(2,1)S(1)} %pad_maximum_fusion.2.refs_0_), channel_id=1, source_target_pairs={{0,6},{2,4},{4,2},{6,0},{8,14},{10,12},{12,10},{14,8},{16,22},{18,... | collective-permute-start | bytes 393224 | tf_op jit(solution)/shard_map/ppermute | solution.py:33
  96.7 2.9 %collective-permute-done.17.refs_1_ = bf16[512,128]{1,0:T(8,128)(2,1)S(1)} collective-permute-done((bf16[512,128]{1,0:T(8,128)(2,1)S(1)}, bf16[512,128]{1,0:T(8,128)(2,1)S(1)}, u32[]{:S(2)}, u32[]{:S(2)}) %collective-permute-start.17) | collective-permute-done | bytes 131104 | tf_op jit(solution)/shard_map/ppermute | solution.py:33
  99.6 2.2 %collective-permute-done.19.refs_3_ = bf16[512,128]{1,0:T(8,128)(2,1)S(1)} collective-permute-done((bf16[512,128]{1,0:T(8,128)(2,1)S(1)}, bf16[512,128]{1,0:T(8,128)(2,1)S(1)}, u32[]{:S(2)}, u32[]{:S(2)}) %collective-permute-start.19) | collective-permute-done | bytes 131104 | tf_op jit(solution)/shard_map/ppermute | solution.py:33
  101.8 0.7 copy-done.12
  102.5 2.4 %apply_tile.5 = (f32[128,128]{1,0:T(8,128)}, f32[128,128]{1,0:T(8,128)}) custom-call(bf16[256,2048]{1,0:T(8,128)(2,1)} %merge_tile.1.tile_ref, bf16[512,128]{1,0:T(8,128)(2,1)} %copy-done.3, bf16[512,128]{1,0:T(8,128)(2,1)} %copy-done.8, bf16[512,128]{1,0:T(8,128)(2,1)} %copy-done.10, bf16[512,128]{1,0:T(8,128)(2,1)} %copy-done.12), custom_call_target="tpu_custom_call" | custom-call | tf_op jit(solution)/shard_map/apply_tile/pallas_call | solution.py:126
  104.9 1.5 %collective-permute-done.20 = f32[128,128]{1,0:T(8,128)S(1)} collective-permute-done((f32[128,128]{1,0:T(8,128)}, f32[128,128]{1,0:T(8,128)S(1)}, u32[]{:S(2)}, u32[]{:S(2)}) %collective-permute-start.20) | collective-permute-done | bytes 65568 | tf_op jit(solution)/shard_map/ppermute | solution.py:33
  106.4 1.5 %multiply_subtract_fusion = f32[128,128]{1,0:T(8,128)} fusion(f32[128,128]{1,0:T(8,128)S(1)} %get-tuple-element.20, f32[128,128]{1,0:T(8,128)S(1)} %get-tuple-element.18, f32[128,128]{1,0:T(8,128)} %get-tuple-element.15, f32[128,128]{1,0:T(8,128)S(1)} %collective-permute-done.20, f32[]{:T(128)} %bitcast.11, f32[]{:T(128)} %bitcast.8), kind=kLoop, calls=%fused_computation.3 | loop fusion | flops 98304 | bytes 327688 | tf_op jit(solution)/shard_map/sub | solution.py:167
  (40 shorter events, 0.2 us)
Async XLA Ops:
  0.7 13.8 %copy-start.1 = (f32[128,128]{1,0:T(8,128)S(1)}, f32[128,128]{1,0:T(8,128)}, u32[]{:S(2)}) copy-start(f32[128,128]{1,0:T(8,128)} %param.12) | copy-start | bytes 196612
  0.7 46.4 %copy-start.14 = (s32[16]{0:T(128)S(1)}, s32[16]{0:T(128)}, u32[]{:S(2)}) copy-start(s32[16]{0:T(128)} %constant.12.clone) | copy-start | bytes 196
  6.9 41.2 %all-to-all-start = ((bf16[32,128,128]{2,1,0:T(8,128)(2,1)}), bf16[32,128,128]{2,1,0:T(8,128)(2,1)S(1)}, u32[]{:S(2)}, u32[]{:S(2)}) async-start(bf16[32,128,128]{2,1,0:T(8,128)(2,1)} %build_tile.1.dense_ref), calls=%async_computation | async-start | bytes 2097152 | tf_op jit(solution)/shard_map/all_to_all | solution.py:155
  14.4 22.7 %collective-permute-start.2 = (bf16[128,128]{1,0:T(8,128)(2,1)S(1)}, bf16[128,128]{1,0:T(8,128)(2,1)S(1)}, u32[]{:S(2)}, u32[]{:S(2)}) collective-permute-start(bf16[128,128]{1,0:T(8,128)(2,1)S(1)} %convert_element_type.9), channel_id=1, source_target_pairs={{0,24},{2,26},{4,28},{6,30},{8,16},{10,18},{12,20},{14,22},{16,8},... | collective-permute-start | bytes 98312 | tf_op jit(solution)/shard_map/ppermute | solution.py:33
  18.1 25.3 %collective-permute-start.1 = (bf16[128,128]{1,0:T(8,128)(2,1)S(1)}, bf16[128,128]{1,0:T(8,128)(2,1)S(1)}, u32[]{:S(2)}, u32[]{:S(2)}) collective-permute-start(bf16[128,128]{1,0:T(8,128)(2,1)S(1)} %convert_element_type.9), channel_id=1, source_target_pairs={{0,16},{2,18},{4,20},{6,22},{8,24},{10,26},{12,28},{14,30},{16,0},... | collective-permute-start | bytes 98312 | tf_op jit(solution)/shard_map/ppermute | solution.py:33
  18.1 25.3 %collective-permute-start = (bf16[128,128]{1,0:T(8,128)(2,1)S(1)}, bf16[128,128]{1,0:T(8,128)(2,1)S(1)}, u32[]{:S(2)}, u32[]{:S(2)}) collective-permute-start(bf16[128,128]{1,0:T(8,128)(2,1)S(1)} %convert_element_type.9), channel_id=1, source_target_pairs={{0,8},{2,10},{4,12},{6,14},{8,0},{10,2},{12,4},{14,6},{16,24},{18,... | collective-permute-start | bytes 98312 | tf_op jit(solution)/shard_map/ppermute | solution.py:33
  43.5 13.9 %copy-start.2 = (bf16[512,128]{1,0:T(8,128)(2,1)}, bf16[512,128]{1,0:T(8,128)(2,1)S(1)}, u32[]{:S(2)}) copy-start(bf16[512,128]{1,0:T(8,128)(2,1)S(1)} %pad_maximum_fusion.refs_0_) | copy-start | bytes 393220
  43.5 13.9 %collective-permute-start.3 = (bf16[512,128]{1,0:T(8,128)(2,1)S(1)}, bf16[512,128]{1,0:T(8,128)(2,1)S(1)}, u32[]{:S(2)}, u32[]{:S(2)}) collective-permute-start(bf16[512,128]{1,0:T(8,128)(2,1)S(1)} %pad_maximum_fusion.refs_0_), channel_id=1, source_target_pairs={{0,2},{2,0},{4,6},{6,4},{8,10},{10,8},{12,14},{14,12},{16,18},{18,... | collective-permute-start | bytes 393224 | tf_op jit(solution)/shard_map/ppermute | solution.py:33
  45.0 12.4 %collective-permute-start.4 = (bf16[512,128]{1,0:T(8,128)(2,1)S(1)}, bf16[512,128]{1,0:T(8,128)(2,1)S(1)}, u32[]{:S(2)}, u32[]{:S(2)}) collective-permute-start(bf16[512,128]{1,0:T(8,128)(2,1)S(1)} %pad_maximum_fusion.refs_0_), channel_id=1, source_target_pairs={{0,4},{2,6},{4,0},{6,2},{8,12},{10,14},{12,8},{14,10},{16,20},{18,... | collective-permute-start | bytes 393224 | tf_op jit(solution)/shard_map/ppermute | solution.py:33
  46.5 10.9 %collective-permute-start.5 = (bf16[512,128]{1,0:T(8,128)(2,1)S(1)}, bf16[512,128]{1,0:T(8,128)(2,1)S(1)}, u32[]{:S(2)}, u32[]{:S(2)}) collective-permute-start(bf16[512,128]{1,0:T(8,128)(2,1)S(1)} %pad_maximum_fusion.refs_0_), channel_id=1, source_target_pairs={{0,6},{2,4},{4,2},{6,0},{8,14},{10,12},{12,10},{14,8},{16,22},{18,... | collective-permute-start | bytes 393224 | tf_op jit(solution)/shard_map/ppermute | solution.py:33
  48.1 1.0 copy-start
  57.4 0.7 copy-start.5
  57.4 0.7 copy-start.6
  58.1 0.6 copy-start.7
  61.2 1.5 %collective-permute-start.6 = (f32[128,128]{1,0:T(8,128)}, f32[128,128]{1,0:T(8,128)S(1)}, u32[]{:S(2)}, u32[]{:S(2)}) collective-permute-start(f32[128,128]{1,0:T(8,128)} %get-tuple-element.12), channel_id=1, source_target_pairs={{0,1},{1,0},{2,3},{3,2},{4,5},{5,4},{6,7},{7,6},{8,9},{9,8},{10,11... | collective-permute-start | bytes 196616 | tf_op jit(solution)/shard_map/ppermute | solution.py:33
  63.5 6.0 %collective-permute-start.9 = (bf16[128,128]{1,0:T(8,128)(2,1)S(1)}, bf16[128,128]{1,0:T(8,128)(2,1)S(1)}, u32[]{:S(2)}, u32[]{:S(2)}) collective-permute-start(bf16[128,128]{1,0:T(8,128)(2,1)S(1)} %get-tuple-element.19), channel_id=1, source_target_pairs={{0,24},{2,26},{4,28},{6,30},{8,16},{10,18},{12,20},{14,22},{16,8},... | collective-permute-start | bytes 98312 | tf_op jit(solution)/shard_map/ppermute | solution.py:33
  64.9 5.6 %collective-permute-start.8 = (bf16[128,128]{1,0:T(8,128)(2,1)S(1)}, bf16[128,128]{1,0:T(8,128)(2,1)S(1)}, u32[]{:S(2)}, u32[]{:S(2)}) collective-permute-start(bf16[128,128]{1,0:T(8,128)(2,1)S(1)} %get-tuple-element.19), channel_id=1, source_target_pairs={{0,16},{2,18},{4,20},{6,22},{8,24},{10,26},{12,28},{14,30},{16,0},... | collective-permute-start | bytes 98312 | tf_op jit(solution)/shard_map/ppermute | solution.py:33
  65.3 5.2 %collective-permute-start.7 = (bf16[128,128]{1,0:T(8,128)(2,1)S(1)}, bf16[128,128]{1,0:T(8,128)(2,1)S(1)}, u32[]{:S(2)}, u32[]{:S(2)}) collective-permute-start(bf16[128,128]{1,0:T(8,128)(2,1)S(1)} %get-tuple-element.19), channel_id=1, source_target_pairs={{0,8},{2,10},{4,12},{6,14},{8,0},{10,2},{12,4},{14,6},{16,24},{18,... | collective-permute-start | bytes 98312 | tf_op jit(solution)/shard_map/ppermute | solution.py:33
  70.5 9.5 %copy-start.4 = (bf16[512,128]{1,0:T(8,128)(2,1)}, bf16[512,128]{1,0:T(8,128)(2,1)S(1)}, u32[]{:S(2)}) copy-start(bf16[512,128]{1,0:T(8,128)(2,1)S(1)} %pad_maximum_fusion.1.refs_0_) | copy-start | bytes 393220
  70.5 5.8 %collective-permute-start.10 = (bf16[512,128]{1,0:T(8,128)(2,1)S(1)}, bf16[512,128]{1,0:T(8,128)(2,1)S(1)}, u32[]{:S(2)}, u32[]{:S(2)}) collective-permute-start(bf16[512,128]{1,0:T(8,128)(2,1)S(1)} %pad_maximum_fusion.1.refs_0_), channel_id=1, source_target_pairs={{0,2},{2,0},{4,6},{6,4},{8,10},{10,8},{12,14},{14,12},{16,18},{18,... | collective-permute-start | bytes 393224 | tf_op jit(solution)/shard_map/ppermute | solution.py:33
  72.0 7.9 %collective-permute-start.11 = (bf16[512,128]{1,0:T(8,128)(2,1)S(1)}, bf16[512,128]{1,0:T(8,128)(2,1)S(1)}, u32[]{:S(2)}, u32[]{:S(2)}) collective-permute-start(bf16[512,128]{1,0:T(8,128)(2,1)S(1)} %pad_maximum_fusion.1.refs_0_), channel_id=1, source_target_pairs={{0,4},{2,6},{4,0},{6,2},{8,12},{10,14},{12,8},{14,10},{16,20},{18,... | collective-permute-start | bytes 393224 | tf_op jit(solution)/shard_map/ppermute | solution.py:33
  73.5 6.4 %collective-permute-start.12 = (bf16[512,128]{1,0:T(8,128)(2,1)S(1)}, bf16[512,128]{1,0:T(8,128)(2,1)S(1)}, u32[]{:S(2)}, u32[]{:S(2)}) collective-permute-start(bf16[512,128]{1,0:T(8,128)(2,1)S(1)} %pad_maximum_fusion.1.refs_0_), channel_id=1, source_target_pairs={{0,6},{2,4},{4,2},{6,0},{8,14},{10,12},{12,10},{14,8},{16,22},{18,... | collective-permute-start | bytes 393224 | tf_op jit(solution)/shard_map/ppermute | solution.py:33
  76.3 3.6 %copy-start.9 = (bf16[512,128]{1,0:T(8,128)(2,1)}, bf16[512,128]{1,0:T(8,128)(2,1)S(1)}, u32[]{:S(2)}) copy-start(bf16[512,128]{1,0:T(8,128)(2,1)S(1)} %collective-permute-done.10.refs_1_) | copy-start | bytes 393220
  79.9 0.6 copy-start.11
  80.6 0.7 copy-start.13
  83.7 1.5 %collective-permute-start.13 = (f32[128,128]{1,0:T(8,128)}, f32[128,128]{1,0:T(8,128)S(1)}, u32[]{:S(2)}, u32[]{:S(2)}) collective-permute-start(f32[128,128]{1,0:T(8,128)} %get-tuple-element.14), channel_id=1, source_target_pairs={{0,1},{1,0},{2,3},{3,2},{4,5},{5,4},{6,7},{7,6},{8,9},{9,8},{10,11... | collective-permute-start | bytes 196616 | tf_op jit(solution)/shard_map/ppermute | solution.py:33
  86.0 5.8 %collective-permute-start.16 = (bf16[128,128]{1,0:T(8,128)(2,1)S(1)}, bf16[128,128]{1,0:T(8,128)(2,1)S(1)}, u32[]{:S(2)}, u32[]{:S(2)}) collective-permute-start(bf16[128,128]{1,0:T(8,128)(2,1)S(1)} %get-tuple-element.17), channel_id=1, source_target_pairs={{0,24},{2,26},{4,28},{6,30},{8,16},{10,18},{12,20},{14,22},{16,8},... | collective-permute-start | bytes 98312 | tf_op jit(solution)/shard_map/ppermute | solution.py:33
  87.7 5.1 %collective-permute-start.15 = (bf16[128,128]{1,0:T(8,128)(2,1)S(1)}, bf16[128,128]{1,0:T(8,128)(2,1)S(1)}, u32[]{:S(2)}, u32[]{:S(2)}) collective-permute-start(bf16[128,128]{1,0:T(8,128)(2,1)S(1)} %get-tuple-element.17), channel_id=1, source_target_pairs={{0,16},{2,18},{4,20},{6,22},{8,24},{10,26},{12,28},{14,30},{16,0},... | collective-permute-start | bytes 98312 | tf_op jit(solution)/shard_map/ppermute | solution.py:33
  88.6 4.5 %collective-permute-start.14 = (bf16[128,128]{1,0:T(8,128)(2,1)S(1)}, bf16[128,128]{1,0:T(8,128)(2,1)S(1)}, u32[]{:S(2)}, u32[]{:S(2)}) collective-permute-start(bf16[128,128]{1,0:T(8,128)(2,1)S(1)} %get-tuple-element.17), channel_id=1, source_target_pairs={{0,8},{2,10},{4,12},{6,14},{8,0},{10,2},{12,4},{14,6},{16,24},{18,... | collective-permute-start | bytes 98312 | tf_op jit(solution)/shard_map/ppermute | solution.py:33
  93.1 8.7 %copy-start.3 = (bf16[512,128]{1,0:T(8,128)(2,1)}, bf16[512,128]{1,0:T(8,128)(2,1)S(1)}, u32[]{:S(2)}) copy-start(bf16[512,128]{1,0:T(8,128)(2,1)S(1)} %pad_maximum_fusion.2.refs_0_) | copy-start | bytes 393220
  93.1 6.5 %collective-permute-start.17 = (bf16[512,128]{1,0:T(8,128)(2,1)S(1)}, bf16[512,128]{1,0:T(8,128)(2,1)S(1)}, u32[]{:S(2)}, u32[]{:S(2)}) collective-permute-start(bf16[512,128]{1,0:T(8,128)(2,1)S(1)} %pad_maximum_fusion.2.refs_0_), channel_id=1, source_target_pairs={{0,2},{2,0},{4,6},{6,4},{8,10},{10,8},{12,14},{14,12},{16,18},{18,... | collective-permute-start | bytes 393224 | tf_op jit(solution)/shard_map/ppermute | solution.py:33
  93.3 6.3 %collective-permute-start.18 = (bf16[512,128]{1,0:T(8,128)(2,1)S(1)}, bf16[512,128]{1,0:T(8,128)(2,1)S(1)}, u32[]{:S(2)}, u32[]{:S(2)}) collective-permute-start(bf16[512,128]{1,0:T(8,128)(2,1)S(1)} %pad_maximum_fusion.2.refs_0_), channel_id=1, source_target_pairs={{0,4},{2,6},{4,0},{6,2},{8,12},{10,14},{12,8},{14,10},{16,20},{18,... | collective-permute-start | bytes 393224 | tf_op jit(solution)/shard_map/ppermute | solution.py:33
  94.7 7.1 %collective-permute-start.19 = (bf16[512,128]{1,0:T(8,128)(2,1)S(1)}, bf16[512,128]{1,0:T(8,128)(2,1)S(1)}, u32[]{:S(2)}, u32[]{:S(2)}) collective-permute-start(bf16[512,128]{1,0:T(8,128)(2,1)S(1)} %pad_maximum_fusion.2.refs_0_), channel_id=1, source_target_pairs={{0,6},{2,4},{4,2},{6,0},{8,14},{10,12},{12,10},{14,8},{16,22},{18,... | collective-permute-start | bytes 393224 | tf_op jit(solution)/shard_map/ppermute | solution.py:33
  99.6 2.2 %copy-start.8 = (bf16[512,128]{1,0:T(8,128)(2,1)}, bf16[512,128]{1,0:T(8,128)(2,1)S(1)}, u32[]{:S(2)}) copy-start(bf16[512,128]{1,0:T(8,128)(2,1)S(1)} %collective-permute-done.17.refs_1_) | copy-start | bytes 393220
  99.6 2.2 %copy-start.10 = (bf16[512,128]{1,0:T(8,128)(2,1)}, bf16[512,128]{1,0:T(8,128)(2,1)S(1)}, u32[]{:S(2)}) copy-start(bf16[512,128]{1,0:T(8,128)(2,1)S(1)} %collective-permute-done.18.refs_2_) | copy-start | bytes 393220
  101.8 0.7 copy-start.12
  104.9 1.5 %collective-permute-start.20 = (f32[128,128]{1,0:T(8,128)}, f32[128,128]{1,0:T(8,128)S(1)}, u32[]{:S(2)}, u32[]{:S(2)}) collective-permute-start(f32[128,128]{1,0:T(8,128)} %get-tuple-element.16), channel_id=1, source_target_pairs={{0,1},{1,0},{2,3},{3,2},{4,5},{5,4},{6,7},{7,6},{8,9},{9,8},{10,11... | collective-permute-start | bytes 196616 | tf_op jit(solution)/shard_map/ppermute | solution.py:33

commit v2 on v1

v2 whole, which is shorter than its diff:
```python
import jax
import jax.numpy as jnp
from jax import lax
from jax.experimental import pallas as pl
from jax.experimental.pallas import tpu as pltpu
from jax.sharding import PartitionSpec as P

DEGREE = 3
RADIX = 4
CHUNK = 8
SPARE = 4 * 2**20

VMEM = pl.BlockSpec(memory_space=pltpu.VMEM)
SMEM = pl.BlockSpec(memory_space=pltpu.SMEM)
HBM = pl.BlockSpec(memory_space=pltpu.HBM)


def stage_strides(size):
    found = []
    stride = 1
    while stride < size:
        radix = RADIX if size % (stride * RADIX) == 0 else size // stride
        found.append((stride, radix))
        stride *= radix
    return found[::-1]


def arrival_order(strides):
    order = [0]
    for stride, radix in strides:
        order = [k * stride ^ offset for k in range(radix) for offset in order]
    return order


def swap(x, axis, size, offset):
    return lax.ppermute(x, axis, [(source, source ^ offset) for source in range(size)])


def build_tile(rows, cols, count, stacked, grid_rows, grid_cols):
    slots, orb, _ = stacked.shape
    chunk = CHUNK if slots % CHUNK == 0 else slots
    chunks = slots // chunk
    cells = grid_rows * grid_cols

    def kernel(rows_ref, cols_ref, count_ref, stack_ref, dense_ref, held_ref, acc_ref, sems):
        copies = [
            pltpu.make_async_copy(
                stack_ref.at[pl.ds(n * chunk, chunk)], held_ref.at[pl.ds(n * chunk, chunk)], sems.at[n]
            )
            for n in range(chunks)
        ]
        for copy in copies:
            copy.start()
        count = count_ref[0]
        acc_ref[...] = jnp.zeros_like(acc_ref)
        for n, copy in enumerate(copies):
            copy.wait()
            for s in range(n * chunk, (n + 1) * chunk):
                cell = jnp.where(s < count, cols_ref[s] * grid_cols + rows_ref[s], cells)
                acc_ref[cell] += held_ref[s].astype(jnp.float32)

        def put(cell, carry):
            dense_ref[cell] = acc_ref[cell].astype(jnp.bfloat16)
            return carry

        lax.fori_loop(0, cells, put, 0, unroll=4 if cells % 4 == 0 else 1)

    need = stacked.size * 2 + (cells + 1) * orb * orb * 4 + cells * orb * orb * 2
    return pl.pallas_call(
        kernel,
        in_specs=[SMEM, SMEM, SMEM, HBM],
        out_specs=VMEM,
        scratch_shapes=[
            pltpu.VMEM(stacked.shape, jnp.bfloat16),
            pltpu.VMEM((cells + 1, orb, orb), jnp.float32),
            pltpu.SemaphoreType.DMA((chunks,)),
        ],
        out_shape=jax.ShapeDtypeStruct((cells, orb, orb), jnp.bfloat16),
        compiler_params=pltpu.CompilerParams(vmem_limit_bytes=need + SPARE),
        name="build_tile",
    )(rows, cols, count, stacked)


def finish(total, first, orb, current_ref, previous_ref, center_ref, halfwidth_ref, outs):
    scale = (1.0 if first else 2.0) / jnp.full((1, total.shape[1]), halfwidth_ref[0])
    own = (total[:orb] - center_ref[0] * current_ref[...]) * scale
    outs[0][...] = own if first else own - previous_ref[...]
    for d in range(1, len(outs)):
        outs[d][...] = total[d * orb : (d + 1) * orb] * scale


def merge_apply(sources, targets, dense, received, pieces, current, center, halfwidth):
    cells, orb, _ = dense.shape
    grid_rows = sources.shape[0]
    grid_cols = targets.shape[0]
    vectors = current.shape[1]
    count = len(pieces)

    def kernel(sources_ref, targets_ref, center_ref, halfwidth_ref, dense_ref, received_ref, current_ref, *refs):
        piece_refs = refs[:count]
        tile_ref, *outs = refs[count:]
        total = None
        at = 0
        for ref in piece_refs:
            depth = ref.shape[0]
            for k in range(at // orb, (at + depth) // orb):
                first = sources_ref[k] * grid_cols
                for d in range(grid_cols):
                    cell = first + targets_ref[d]
                    turned = received_ref[cell].T.astype(jnp.float32)
                    block = (dense_ref[cell].astype(jnp.float32) + turned).astype(jnp.bfloat16)
                    tile_ref[d * orb : (d + 1) * orb, k * orb : (k + 1) * orb] = block
            part = jnp.dot(
                tile_ref[:, at : at + depth], ref[...], preferred_element_type=jnp.float32
            )
            total = part if total is None else total + part
            at += depth
        finish(total, True, orb, current_ref, None, center_ref, halfwidth_ref, outs)

    block = jax.ShapeDtypeStruct((orb, vectors), jnp.float32)
    return pl.pallas_call(
        kernel,
        in_specs=[SMEM] * 4 + [VMEM] * (3 + count),
        out_specs=[VMEM] * (1 + grid_cols),
        out_shape=[jax.ShapeDtypeStruct((grid_cols * orb, grid_rows * orb), jnp.bfloat16)]
        + [block] * grid_cols,
        compiler_params=pltpu.CompilerParams(vmem_limit_bytes=dense.size * 6 + 2 * SPARE),
        name="merge_apply",
    )(sources, targets, center, halfwidth, dense, received, current, *pieces)


def apply_tile(tile, pieces, current, previous, center, halfwidth, grid_cols):
    height, _ = tile.shape
    orb = height // grid_cols
    vectors = current.shape[1]
    count = len(pieces)

    def kernel(center_ref, halfwidth_ref, tile_ref, current_ref, previous_ref, *refs):
        total = None
        at = 0
        for ref in refs[:count]:
            depth = ref.shape[0]
            part = jnp.dot(
                tile_ref[:, at : at + depth], ref[...], preferred_element_type=jnp.float32
            )
            total = part if total is None else total + part
            at += depth
        finish(total, False, orb, current_ref, previous_ref, center_ref, halfwidth_ref, refs[count:])

    return pl.pallas_call(
        kernel,
        in_specs=[SMEM] * 2 + [VMEM] * (3 + count),
        out_specs=[VMEM] * grid_cols,
        out_shape=[jax.ShapeDtypeStruct((orb, vectors), jnp.float32)] * grid_cols,
        compiler_params=pltpu.CompilerParams(vmem_limit_bytes=tile.size * 2 + 2 * SPARE),
        name="apply_tile",
    )(center, halfwidth, tile, current, previous, *pieces)


def body(hamiltonian_blocks, block_rows, block_cols, block_counts, initial, center, halfwidth):
    grid_rows = lax.axis_size("row")
    grid_cols = lax.axis_size("col")
    strides = stage_strides(grid_rows)

    def gather(panel):
        gathered = panel
        for index, (stride, radix) in enumerate(strides):
            parts = [gathered] + [
                swap(gathered, "row", grid_rows, k * stride) for k in range(1, radix)
            ]
            if index < len(strides) - 1:
                gathered = jnp.concatenate(parts, axis=0)
        return parts

    sources = jnp.array(arrival_order(strides), jnp.int32) ^ lax.axis_index("row")
    targets = jnp.arange(grid_cols, dtype=jnp.int32) ^ lax.axis_index("col")
    pieces = gather(initial.astype(jnp.bfloat16))
    dense = build_tile(
        block_rows[0, 0], block_cols[0, 0], block_counts[0], hamiltonian_blocks[0, 0],
        grid_rows, grid_cols,
    )
    received = lax.all_to_all(dense, ("row", "col"), 0, 0)
    tile, base, *others = merge_apply(
        sources, targets, dense, received, pieces, initial, center, halfwidth
    )

    previous = initial
    current = initial
    for degree_step in range(DEGREE):
        if degree_step > 0:
            pieces = gather(current.astype(jnp.bfloat16))
            base, *others = apply_tile(
                tile, pieces, current, previous, center, halfwidth, grid_cols
            )
        following = base
        for d, other in enumerate(others, start=1):
            following = following + swap(other, "col", grid_cols, d)
        previous = current
        current = following
    return current


def solution(mesh):
    in_specs = (
        P("row", "col", None, None, None),
        P("row", "col", None),
        P("row", "col", None),
        P("row", "col"),
        P(("row", "col"), None),
        P(),
        P(),
    )
    out_specs = P(("row", "col"), None)
    return jax.shard_map(body, mesh=mesh, in_specs=in_specs, out_specs=out_specs, check_vma=False)
```

time: 108 us -> 90 us (0.83)
  Pallas kernels: 21.9 us -> 5.24 us
  other arithmetic: 4.3 us -> 0.7 us
  waiting for transfers between devices: 43.8 us -> 47.2 us
  local copies, waits for them, and re-layouts: 4.3 us -> 2.9 us
    pallas_call x5 -> x4, Pallas kernels: 21.9 us -> 5.24 us  [the longest x1 2.56 us: build_tile(): pl.pallas_call(kernel, in_specs=[SMEM, SMEM, SMEM, HBM], out_specs=VMEM,...]
    ppermute x21, waiting for transfers between devices: 43.8 us -> 47.2 us  [swap(): lax.ppermute(x, axis, [(source, source ^ offset) for source in range(size)])]
    convert_element_type x3 -> x2, other arithmetic: 1.73 us -> 0.02 us  [body(): pieces = gather(current.astype(jnp.bfloat16))]
    sub x1 -> x0, other arithmetic: 1.49 us -> none  [body(): following = shifted if degree_step == 0 else 2.0 * shifted - previous]
    unnamed x30 -> x10, local copies, waits for them, and re-layouts: 4.3 us -> 2.9 us
  transfers between devices with their start and end apart: 22 -> 22, of which waited for: 14 -> 18; matrix products, arithmetic and copies ran while one was open for 1% -> 0% of each run, Pallas kernels for 8% -> 0%
where the time goes in v2:
time: 90 us; the launch traced here: 89.7 us
  waiting for transfers between devices  47.2 us (52%)
  starting transfers between devices  31.5 us (35%)
  Pallas kernels  5.24 us (6%)
  local copies, waits for them, and re-layouts  2.9 us (3%)
  between operations  2.09 us (2%)
    ppermute x21, waiting for transfers between devices, swap(): lax.ppermute(x, axis, [(source, source ^ offset) for source in range(size)])  47.2 us
    ppermute x21, starting transfers between devices, swap(): lax.ppermute(x, axis, [(source, source ^ offset) for source in range(size)])  24.2 us
    all_to_all x1, starting transfers between devices, body(): received = lax.all_to_all(dense, ('row', 'col'), 0, 0)  7.29 us
    unnamed x10, local copies, waits for them, and re-layouts  2.9 us
    pallas_call x1, Pallas kernels, build_tile(): pl.pallas_call(kernel, in_specs=[SMEM, SMEM, SMEM, HBM], out_specs=VMEM,...  2.56 us
    pallas_call x1, Pallas kernels, merge_apply(): pl.pallas_call(kernel, in_specs=[SMEM] * 4 + [VMEM] * (3 + count), out_sp...  1.83 us
  transfers between devices with their start and end apart: 22, of which 18 were waited for; matrix products, arithmetic and copies ran while one was open for 0% of the time, Pallas kernels for 0%

profile of v2, /device:TPU:0, one launch (start us, length us, event | category | flops | bytes accessed | tf_op | source)
XLA Modules:
  0.0 89.7 jit_solution(1655717343181861639)
XLA Ops:
  0.7 1.6 %copy-done = bf16[1,1,64,128,128]{4,3,2,1,0:T(8,128)(2,1)S(1)} copy-done((bf16[1,1,64,128,128]{4,3,2,1,0:T(8,128)(2,1)S(1)}, bf16[1,1,64,128,128]{4,3,2,1,0:T(8,128)(2,1)}, u32[]{:S(2)}) %copy-start) | copy-done | bytes 2097176
  2.2 0.7 copy-done.2
  2.9 0.7 copy-done.3
  3.6 2.6 %build_tile.1.dense_ref = bf16[32,128,128]{2,1,0:T(8,128)(2,1)} custom-call(s32[64]{0:T(128)S(1)} %bitcast.6, s32[64]{0:T(128)S(1)} %bitcast.7, s32[1]{0:T(128)} %bitcast.4.count_ref, bf16[64,128,128]{2,1,0:T(8,128)(2,1)S(1)} %bitcast.5), custom_call_target="tpu_custom_call" | custom-call | tf_op jit(solution)/shard_map/build_tile/pallas_call | solution.py:69
  6.1 7.3 %all-to-all-start = ((bf16[32,128,128]{2,1,0:T(8,128)(2,1)}), bf16[32,128,128]{2,1,0:T(8,128)(2,1)S(1)}, u32[]{:S(2)}, u32[]{:S(2)}) async-start(bf16[32,128,128]{2,1,0:T(8,128)(2,1)} %build_tile.1.dense_ref), calls=%async_computation | async-start | bytes 2097152 | tf_op jit(solution)/shard_map/all_to_all | solution.py:182
  13.5 3.7 %collective-permute-start.2 = (bf16[128,128]{1,0:T(8,128)(2,1)S(1)}, bf16[128,128]{1,0:T(8,128)(2,1)S(1)}, u32[]{:S(2)}, u32[]{:S(2)}) collective-permute-start(bf16[128,128]{1,0:T(8,128)(2,1)S(1)} %convert_element_type.9), channel_id=1, source_target_pairs={{0,24},{2,26},{4,28},{6,30},{8,16},{10,18},{12,20},{14,22},{16,8},... | collective-permute-start | bytes 98312 | tf_op jit(solution)/shard_map/ppermute | solution.py:36
  17.1 0.8 collective-permute-start
  17.9 18.3 %collective-permute-done.2 = bf16[128,128]{1,0:T(8,128)(2,1)S(1)} collective-permute-done((bf16[128,128]{1,0:T(8,128)(2,1)S(1)}, bf16[128,128]{1,0:T(8,128)(2,1)S(1)}, u32[]{:S(2)}, u32[]{:S(2)}) %collective-permute-start.2) | collective-permute-done | bytes 32800 | tf_op jit(solution)/shard_map/ppermute | solution.py:36
  36.2 6.3 %collective-permute-done.1 = bf16[128,128]{1,0:T(8,128)(2,1)S(1)} collective-permute-done((bf16[128,128]{1,0:T(8,128)(2,1)S(1)}, bf16[128,128]{1,0:T(8,128)(2,1)S(1)}, u32[]{:S(2)}, u32[]{:S(2)}) %collective-permute-start.1) | collective-permute-done | bytes 32800 | tf_op jit(solution)/shard_map/ppermute | solution.py:36
  42.5 2.5 %collective-permute-start.5 = (bf16[512,128]{1,0:T(8,128)(2,1)S(1)}, bf16[512,128]{1,0:T(8,128)(2,1)S(1)}, u32[]{:S(2)}, u32[]{:S(2)}) collective-permute-start(bf16[512,128]{1,0:T(8,128)(2,1)S(1)} %pad_maximum_fusion.refs_0_), channel_id=1, source_target_pairs={{0,6},{2,4},{4,2},{6,0},{8,14},{10,12},{12,10},{14,8},{16,22},{18,... | collective-permute-start | bytes 393224 | tf_op jit(solution)/shard_map/ppermute | solution.py:36
  44.9 0.5 collective-permute-start.4
  45.5 0.6 collective-permute-start.3
  47.4 1.7 %collective-permute-done.5.refs_3_ = bf16[512,128]{1,0:T(8,128)(2,1)S(1)} collective-permute-done((bf16[512,128]{1,0:T(8,128)(2,1)S(1)}, bf16[512,128]{1,0:T(8,128)(2,1)S(1)}, u32[]{:S(2)}, u32[]{:S(2)}) %collective-permute-start.5) | collective-permute-done | bytes 131104 | tf_op jit(solution)/shard_map/ppermute | solution.py:36
  49.1 1.9 %collective-permute-done.4.refs_2_ = bf16[512,128]{1,0:T(8,128)(2,1)S(1)} collective-permute-done((bf16[512,128]{1,0:T(8,128)(2,1)S(1)}, bf16[512,128]{1,0:T(8,128)(2,1)S(1)}, u32[]{:S(2)}, u32[]{:S(2)}) %collective-permute-start.4) | collective-permute-done | bytes 131104 | tf_op jit(solution)/shard_map/ppermute | solution.py:36
  51.0 0.1 collective-permute-done.3.refs_1_
  51.1 0.0 all-to-all-done.received_ref
  51.1 1.8 %merge_apply.1 = (bf16[256,2048]{1,0:T(8,128)(2,1)S(1)}, f32[128,128]{1,0:T(8,128)S(1)}, f32[128,128]{1,0:T(8,128)S(1)}) custom-call(s32[16]{0:T(128)S(1)} %broadcast_xor_fusion.sources_ref, s32[2]{0:T(128)S(1)} %iota_xor_fusion.targets_ref, f32[1]{0:T(128)S(6)} %copy.10.center_ref, f32[1]{0:T(128)S(6)} %copy.11.halfwidth_ref, ...), custom_call_target="tpu_custom_call" | custom-call | tf_op jit(solution)/shard_map/merge_apply/pallas_call | solution.py:121
  52.9 0.1 collective-permute-start.6
  53.0 1.2 %collective-permute-done.6 = f32[128,128]{1,0:T(8,128)S(1)} collective-permute-done((f32[128,128]{1,0:T(8,128)S(1)}, f32[128,128]{1,0:T(8,128)S(1)}, u32[]{:S(2)}, u32[]{:S(2)}) %collective-permute-start.6) | collective-permute-done | bytes 65568 | tf_op jit(solution)/shard_map/ppermute | solution.py:36
  54.3 2.3 %collective-permute-start.9 = (bf16[128,128]{1,0:T(8,128)(2,1)S(1)}, bf16[128,128]{1,0:T(8,128)(2,1)S(1)}, u32[]{:S(2)}, u32[]{:S(2)}) collective-permute-start(bf16[128,128]{1,0:T(8,128)(2,1)S(1)} %get-tuple-element.21), channel_id=1, source_target_pairs={{0,24},{2,26},{4,28},{6,30},{8,16},{10,18},{12,20},{14,22},{16,8},... | collective-permute-start | bytes 98312 | tf_op jit(solution)/shard_map/ppermute | solution.py:36
  56.5 2.2 %collective-permute-start.7 = (bf16[128,128]{1,0:T(8,128)(2,1)S(1)}, bf16[128,128]{1,0:T(8,128)(2,1)S(1)}, u32[]{:S(2)}, u32[]{:S(2)}) collective-permute-start(bf16[128,128]{1,0:T(8,128)(2,1)S(1)} %get-tuple-element.21), channel_id=1, source_target_pairs={{0,8},{2,10},{4,12},{6,14},{8,0},{10,2},{12,4},{14,6},{16,24},{18,... | collective-permute-start | bytes 98312 | tf_op jit(solution)/shard_map/ppermute | solution.py:36
  58.7 1.3 %collective-permute-done.9 = bf16[128,128]{1,0:T(8,128)(2,1)S(1)} collective-permute-done((bf16[128,128]{1,0:T(8,128)(2,1)S(1)}, bf16[128,128]{1,0:T(8,128)(2,1)S(1)}, u32[]{:S(2)}, u32[]{:S(2)}) %collective-permute-start.9) | collective-permute-done | bytes 32800 | tf_op jit(solution)/shard_map/ppermute | solution.py:36
  60.0 1.3 %collective-permute-done.8 = bf16[128,128]{1,0:T(8,128)(2,1)S(1)} collective-permute-done((bf16[128,128]{1,0:T(8,128)(2,1)S(1)}, bf16[128,128]{1,0:T(8,128)(2,1)S(1)}, u32[]{:S(2)}, u32[]{:S(2)}) %collective-permute-start.8) | collective-permute-done | bytes 32800 | tf_op jit(solution)/shard_map/ppermute | solution.py:36
  61.3 0.0 collective-permute-done.7
  61.4 1.6 %collective-permute-start.12 = (bf16[512,128]{1,0:T(8,128)(2,1)S(1)}, bf16[512,128]{1,0:T(8,128)(2,1)S(1)}, u32[]{:S(2)}, u32[]{:S(2)}) collective-permute-start(bf16[512,128]{1,0:T(8,128)(2,1)S(1)} %pad_maximum_fusion.1.refs_0_), channel_id=1, source_target_pairs={{0,6},{2,4},{4,2},{6,0},{8,14},{10,12},{12,10},{14,8},{16,22},{18,... | collective-permute-start | bytes 393224 | tf_op jit(solution)/shard_map/ppermute | solution.py:36
  62.9 1.4 %collective-permute-start.11 = (bf16[512,128]{1,0:T(8,128)(2,1)S(1)}, bf16[512,128]{1,0:T(8,128)(2,1)S(1)}, u32[]{:S(2)}, u32[]{:S(2)}) collective-permute-start(bf16[512,128]{1,0:T(8,128)(2,1)S(1)} %pad_maximum_fusion.1.refs_0_), channel_id=1, source_target_pairs={{0,4},{2,6},{4,0},{6,2},{8,12},{10,14},{12,8},{14,10},{16,20},{18,... | collective-permute-start | bytes 393224 | tf_op jit(solution)/shard_map/ppermute | solution.py:36
  64.3 0.6 collective-permute-start.10
  64.9 3.7 %collective-permute-done.12.refs_3_ = bf16[512,128]{1,0:T(8,128)(2,1)S(1)} collective-permute-done((bf16[512,128]{1,0:T(8,128)(2,1)S(1)}, bf16[512,128]{1,0:T(8,128)(2,1)S(1)}, u32[]{:S(2)}, u32[]{:S(2)}) %collective-permute-start.12) | collective-permute-done | bytes 131104 | tf_op jit(solution)/shard_map/ppermute | solution.py:36
  68.6 1.2 %collective-permute-done.11.refs_2_ = bf16[512,128]{1,0:T(8,128)(2,1)S(1)} collective-permute-done((bf16[512,128]{1,0:T(8,128)(2,1)S(1)}, bf16[512,128]{1,0:T(8,128)(2,1)S(1)}, u32[]{:S(2)}, u32[]{:S(2)}) %collective-permute-start.11) | collective-permute-done | bytes 131104 | tf_op jit(solution)/shard_map/ppermute | solution.py:36
  69.9 0.1 collective-permute-done.10.refs_1_
  69.9 0.4 apply_tile.2
  70.4 0.1 collective-permute-start.13
  70.4 1.2 %collective-permute-done.13 = f32[128,128]{1,0:T(8,128)S(1)} collective-permute-done((f32[128,128]{1,0:T(8,128)S(1)}, f32[128,128]{1,0:T(8,128)S(1)}, u32[]{:S(2)}, u32[]{:S(2)}) %collective-permute-start.13) | collective-permute-done | bytes 65568 | tf_op jit(solution)/shard_map/ppermute | solution.py:36
  71.7 2.4 %collective-permute-start.16 = (bf16[128,128]{1,0:T(8,128)(2,1)S(1)}, bf16[128,128]{1,0:T(8,128)(2,1)S(1)}, u32[]{:S(2)}, u32[]{:S(2)}) collective-permute-start(bf16[128,128]{1,0:T(8,128)(2,1)S(1)} %get-tuple-element.19), channel_id=1, source_target_pairs={{0,24},{2,26},{4,28},{6,30},{8,16},{10,18},{12,20},{14,22},{16,8},... | collective-permute-start | bytes 98312 | tf_op jit(solution)/shard_map/ppermute | solution.py:36
  74.1 0.0 collective-permute-start.15
  74.1 2.0 %collective-permute-start.14 = (bf16[128,128]{1,0:T(8,128)(2,1)S(1)}, bf16[128,128]{1,0:T(8,128)(2,1)S(1)}, u32[]{:S(2)}, u32[]{:S(2)}) collective-permute-start(bf16[128,128]{1,0:T(8,128)(2,1)S(1)} %get-tuple-element.19), channel_id=1, source_target_pairs={{0,8},{2,10},{4,12},{6,14},{8,0},{10,2},{12,4},{14,6},{16,24},{18,... | collective-permute-start | bytes 98312 | tf_op jit(solution)/shard_map/ppermute | solution.py:36
  76.1 1.3 %collective-permute-done.16 = bf16[128,128]{1,0:T(8,128)(2,1)S(1)} collective-permute-done((bf16[128,128]{1,0:T(8,128)(2,1)S(1)}, bf16[128,128]{1,0:T(8,128)(2,1)S(1)}, u32[]{:S(2)}, u32[]{:S(2)}) %collective-permute-start.16) | collective-permute-done | bytes 32800 | tf_op jit(solution)/shard_map/ppermute | solution.py:36
  77.5 1.4 %collective-permute-done.15 = bf16[128,128]{1,0:T(8,128)(2,1)S(1)} collective-permute-done((bf16[128,128]{1,0:T(8,128)(2,1)S(1)}, bf16[128,128]{1,0:T(8,128)(2,1)S(1)}, u32[]{:S(2)}, u32[]{:S(2)}) %collective-permute-start.15) | collective-permute-done | bytes 32800 | tf_op jit(solution)/shard_map/ppermute | solution.py:36
  78.9 1.5 %collective-permute-start.19 = (bf16[512,128]{1,0:T(8,128)(2,1)S(1)}, bf16[512,128]{1,0:T(8,128)(2,1)S(1)}, u32[]{:S(2)}, u32[]{:S(2)}) collective-permute-start(bf16[512,128]{1,0:T(8,128)(2,1)S(1)} %pad_maximum_fusion.2.refs_0_), channel_id=1, source_target_pairs={{0,6},{2,4},{4,2},{6,0},{8,14},{10,12},{12,10},{14,8},{16,22},{18,... | collective-permute-start | bytes 393224 | tf_op jit(solution)/shard_map/ppermute | solution.py:36
  80.4 1.5 %collective-permute-start.18 = (bf16[512,128]{1,0:T(8,128)(2,1)S(1)}, bf16[512,128]{1,0:T(8,128)(2,1)S(1)}, u32[]{:S(2)}, u32[]{:S(2)}) collective-permute-start(bf16[512,128]{1,0:T(8,128)(2,1)S(1)} %pad_maximum_fusion.2.refs_0_), channel_id=1, source_target_pairs={{0,4},{2,6},{4,0},{6,2},{8,12},{10,14},{12,8},{14,10},{16,20},{18,... | collective-permute-start | bytes 393224 | tf_op jit(solution)/shard_map/ppermute | solution.py:36
  81.9 0.6 collective-permute-start.17
  82.5 3.5 %collective-permute-done.19.refs_3_ = bf16[512,128]{1,0:T(8,128)(2,1)S(1)} collective-permute-done((bf16[512,128]{1,0:T(8,128)(2,1)S(1)}, bf16[512,128]{1,0:T(8,128)(2,1)S(1)}, u32[]{:S(2)}, u32[]{:S(2)}) %collective-permute-start.19) | collective-permute-done | bytes 131104 | tf_op jit(solution)/shard_map/ppermute | solution.py:36
  86.0 1.2 %collective-permute-done.18.refs_2_ = bf16[512,128]{1,0:T(8,128)(2,1)S(1)} collective-permute-done((bf16[512,128]{1,0:T(8,128)(2,1)S(1)}, bf16[512,128]{1,0:T(8,128)(2,1)S(1)}, u32[]{:S(2)}, u32[]{:S(2)}) %collective-permute-start.18) | collective-permute-done | bytes 131104 | tf_op jit(solution)/shard_map/ppermute | solution.py:36
  87.2 0.1 collective-permute-done.17.refs_1_
  87.3 0.4 apply_tile.3
  87.7 0.1 collective-permute-start.20
  87.8 1.2 %collective-permute-done.20 = f32[128,128]{1,0:T(8,128)S(1)} collective-permute-done((f32[128,128]{1,0:T(8,128)S(1)}, f32[128,128]{1,0:T(8,128)S(1)}, u32[]{:S(2)}, u32[]{:S(2)}) %collective-permute-start.20) | collective-permute-done | bytes 65568 | tf_op jit(solution)/shard_map/ppermute | solution.py:36
  89.0 0.6 add.11
  (19 shorter events, 0.1 us)
Async XLA Ops:
  0.7 1.6 %copy-start = (bf16[1,1,64,128,128]{4,3,2,1,0:T(8,128)(2,1)S(1)}, bf16[1,1,64,128,128]{4,3,2,1,0:T(8,128)(2,1)}, u32[]{:S(2)}) copy-start(bf16[1,1,64,128,128]{4,3,2,1,0:T(8,128)(2,1)} %param.8) | copy-start | bytes 6291460
  2.2 0.7 copy-start.2
  2.9 0.7 copy-start.3
  3.6 9.9 %copy-start.1 = (f32[128,128]{1,0:T(8,128)S(1)}, f32[128,128]{1,0:T(8,128)}, u32[]{:S(2)}) copy-start(f32[128,128]{1,0:T(8,128)} %previous_ref.1) | copy-start | bytes 196612
  3.6 42.5 %copy-start.4 = (s32[16]{0:T(128)S(1)}, s32[16]{0:T(128)}, u32[]{:S(2)}) copy-start(s32[16]{0:T(128)} %constant.10.clone) | copy-start | bytes 196
  6.1 44.9 %all-to-all-start = ((bf16[32,128,128]{2,1,0:T(8,128)(2,1)}), bf16[32,128,128]{2,1,0:T(8,128)(2,1)S(1)}, u32[]{:S(2)}, u32[]{:S(2)}) async-start(bf16[32,128,128]{2,1,0:T(8,128)(2,1)} %build_tile.1.dense_ref), calls=%async_computation | async-start | bytes 2097152 | tf_op jit(solution)/shard_map/all_to_all | solution.py:182
  13.5 22.7 %collective-permute-start.2 = (bf16[128,128]{1,0:T(8,128)(2,1)S(1)}, bf16[128,128]{1,0:T(8,128)(2,1)S(1)}, u32[]{:S(2)}, u32[]{:S(2)}) collective-permute-start(bf16[128,128]{1,0:T(8,128)(2,1)S(1)} %convert_element_type.9), channel_id=1, source_target_pairs={{0,24},{2,26},{4,28},{6,30},{8,16},{10,18},{12,20},{14,22},{16,8},... | collective-permute-start | bytes 98312 | tf_op jit(solution)/shard_map/ppermute | solution.py:36
  17.1 25.3 %collective-permute-start.1 = (bf16[128,128]{1,0:T(8,128)(2,1)S(1)}, bf16[128,128]{1,0:T(8,128)(2,1)S(1)}, u32[]{:S(2)}, u32[]{:S(2)}) collective-permute-start(bf16[128,128]{1,0:T(8,128)(2,1)S(1)} %convert_element_type.9), channel_id=1, source_target_pairs={{0,16},{2,18},{4,20},{6,22},{8,24},{10,26},{12,28},{14,30},{16,0},... | collective-permute-start | bytes 98312 | tf_op jit(solution)/shard_map/ppermute | solution.py:36
  17.1 25.3 %collective-permute-start = (bf16[128,128]{1,0:T(8,128)(2,1)S(1)}, bf16[128,128]{1,0:T(8,128)(2,1)S(1)}, u32[]{:S(2)}, u32[]{:S(2)}) collective-permute-start(bf16[128,128]{1,0:T(8,128)(2,1)S(1)} %convert_element_type.9), channel_id=1, source_target_pairs={{0,8},{2,10},{4,12},{6,14},{8,0},{10,2},{12,4},{14,6},{16,24},{18,... | collective-permute-start | bytes 98312 | tf_op jit(solution)/shard_map/ppermute | solution.py:36
  42.5 6.6 %collective-permute-start.5 = (bf16[512,128]{1,0:T(8,128)(2,1)S(1)}, bf16[512,128]{1,0:T(8,128)(2,1)S(1)}, u32[]{:S(2)}, u32[]{:S(2)}) collective-permute-start(bf16[512,128]{1,0:T(8,128)(2,1)S(1)} %pad_maximum_fusion.refs_0_), channel_id=1, source_target_pairs={{0,6},{2,4},{4,2},{6,0},{8,14},{10,12},{12,10},{14,8},{16,22},{18,... | collective-permute-start | bytes 393224 | tf_op jit(solution)/shard_map/ppermute | solution.py:36
  44.9 6.1 %collective-permute-start.4 = (bf16[512,128]{1,0:T(8,128)(2,1)S(1)}, bf16[512,128]{1,0:T(8,128)(2,1)S(1)}, u32[]{:S(2)}, u32[]{:S(2)}) collective-permute-start(bf16[512,128]{1,0:T(8,128)(2,1)S(1)} %pad_maximum_fusion.refs_0_), channel_id=1, source_target_pairs={{0,4},{2,6},{4,0},{6,2},{8,12},{10,14},{12,8},{14,10},{16,20},{18,... | collective-permute-start | bytes 393224 | tf_op jit(solution)/shard_map/ppermute | solution.py:36
  45.5 5.6 %collective-permute-start.3 = (bf16[512,128]{1,0:T(8,128)(2,1)S(1)}, bf16[512,128]{1,0:T(8,128)(2,1)S(1)}, u32[]{:S(2)}, u32[]{:S(2)}) collective-permute-start(bf16[512,128]{1,0:T(8,128)(2,1)S(1)} %pad_maximum_fusion.refs_0_), channel_id=1, source_target_pairs={{0,2},{2,0},{4,6},{6,4},{8,10},{10,8},{12,14},{14,12},{16,18},{18,... | collective-permute-start | bytes 393224 | tf_op jit(solution)/shard_map/ppermute | solution.py:36
  52.9 1.3 %collective-permute-start.6 = (f32[128,128]{1,0:T(8,128)S(1)}, f32[128,128]{1,0:T(8,128)S(1)}, u32[]{:S(2)}, u32[]{:S(2)}) collective-permute-start(f32[128,128]{1,0:T(8,128)S(1)} %get-tuple-element.14), channel_id=1, source_target_pairs={{0,1},{1,0},{2,3},{3,2},{4,5},{5,4},{6,7},{7,6},{8,9},{9,8},{10,11... | collective-permute-start | bytes 196616 | tf_op jit(solution)/shard_map/ppermute | solution.py:36
  54.3 5.8 %collective-permute-start.9 = (bf16[128,128]{1,0:T(8,128)(2,1)S(1)}, bf16[128,128]{1,0:T(8,128)(2,1)S(1)}, u32[]{:S(2)}, u32[]{:S(2)}) collective-permute-start(bf16[128,128]{1,0:T(8,128)(2,1)S(1)} %get-tuple-element.21), channel_id=1, source_target_pairs={{0,24},{2,26},{4,28},{6,30},{8,16},{10,18},{12,20},{14,22},{16,8},... | collective-permute-start | bytes 98312 | tf_op jit(solution)/shard_map/ppermute | solution.py:36
  56.5 4.8 %collective-permute-start.8 = (bf16[128,128]{1,0:T(8,128)(2,1)S(1)}, bf16[128,128]{1,0:T(8,128)(2,1)S(1)}, u32[]{:S(2)}, u32[]{:S(2)}) collective-permute-start(bf16[128,128]{1,0:T(8,128)(2,1)S(1)} %get-tuple-element.21), channel_id=1, source_target_pairs={{0,16},{2,18},{4,20},{6,22},{8,24},{10,26},{12,28},{14,30},{16,0},... | collective-permute-start | bytes 98312 | tf_op jit(solution)/shard_map/ppermute | solution.py:36
  56.5 4.8 %collective-permute-start.7 = (bf16[128,128]{1,0:T(8,128)(2,1)S(1)}, bf16[128,128]{1,0:T(8,128)(2,1)S(1)}, u32[]{:S(2)}, u32[]{:S(2)}) collective-permute-start(bf16[128,128]{1,0:T(8,128)(2,1)S(1)} %get-tuple-element.21), channel_id=1, source_target_pairs={{0,8},{2,10},{4,12},{6,14},{8,0},{10,2},{12,4},{14,6},{16,24},{18,... | collective-permute-start | bytes 98312 | tf_op jit(solution)/shard_map/ppermute | solution.py:36
  61.4 7.3 %collective-permute-start.12 = (bf16[512,128]{1,0:T(8,128)(2,1)S(1)}, bf16[512,128]{1,0:T(8,128)(2,1)S(1)}, u32[]{:S(2)}, u32[]{:S(2)}) collective-permute-start(bf16[512,128]{1,0:T(8,128)(2,1)S(1)} %pad_maximum_fusion.1.refs_0_), channel_id=1, source_target_pairs={{0,6},{2,4},{4,2},{6,0},{8,14},{10,12},{12,10},{14,8},{16,22},{18,... | collective-permute-start | bytes 393224 | tf_op jit(solution)/shard_map/ppermute | solution.py:36
  62.9 6.9 %collective-permute-start.11 = (bf16[512,128]{1,0:T(8,128)(2,1)S(1)}, bf16[512,128]{1,0:T(8,128)(2,1)S(1)}, u32[]{:S(2)}, u32[]{:S(2)}) collective-permute-start(bf16[512,128]{1,0:T(8,128)(2,1)S(1)} %pad_maximum_fusion.1.refs_0_), channel_id=1, source_target_pairs={{0,4},{2,6},{4,0},{6,2},{8,12},{10,14},{12,8},{14,10},{16,20},{18,... | collective-permute-start | bytes 393224 | tf_op jit(solution)/shard_map/ppermute | solution.py:36
  64.3 5.6 %collective-permute-start.10 = (bf16[512,128]{1,0:T(8,128)(2,1)S(1)}, bf16[512,128]{1,0:T(8,128)(2,1)S(1)}, u32[]{:S(2)}, u32[]{:S(2)}) collective-permute-start(bf16[512,128]{1,0:T(8,128)(2,1)S(1)} %pad_maximum_fusion.1.refs_0_), channel_id=1, source_target_pairs={{0,2},{2,0},{4,6},{6,4},{8,10},{10,8},{12,14},{14,12},{16,18},{18,... | collective-permute-start | bytes 393224 | tf_op jit(solution)/shard_map/ppermute | solution.py:36
  70.4 1.3 %collective-permute-start.13 = (f32[128,128]{1,0:T(8,128)S(1)}, f32[128,128]{1,0:T(8,128)S(1)}, u32[]{:S(2)}, u32[]{:S(2)}) collective-permute-start(f32[128,128]{1,0:T(8,128)S(1)} %get-tuple-element.16), channel_id=1, source_target_pairs={{0,1},{1,0},{2,3},{3,2},{4,5},{5,4},{6,7},{7,6},{8,9},{9,8},{10,11... | collective-permute-start | bytes 196616 | tf_op jit(solution)/shard_map/ppermute | solution.py:36
  71.7 5.8 %collective-permute-start.16 = (bf16[128,128]{1,0:T(8,128)(2,1)S(1)}, bf16[128,128]{1,0:T(8,128)(2,1)S(1)}, u32[]{:S(2)}, u32[]{:S(2)}) collective-permute-start(bf16[128,128]{1,0:T(8,128)(2,1)S(1)} %get-tuple-element.19), channel_id=1, source_target_pairs={{0,24},{2,26},{4,28},{6,30},{8,16},{10,18},{12,20},{14,22},{16,8},... | collective-permute-start | bytes 98312 | tf_op jit(solution)/shard_map/ppermute | solution.py:36
  74.1 4.8 %collective-permute-start.15 = (bf16[128,128]{1,0:T(8,128)(2,1)S(1)}, bf16[128,128]{1,0:T(8,128)(2,1)S(1)}, u32[]{:S(2)}, u32[]{:S(2)}) collective-permute-start(bf16[128,128]{1,0:T(8,128)(2,1)S(1)} %get-tuple-element.19), channel_id=1, source_target_pairs={{0,16},{2,18},{4,20},{6,22},{8,24},{10,26},{12,28},{14,30},{16,0},... | collective-permute-start | bytes 98312 | tf_op jit(solution)/shard_map/ppermute | solution.py:36
  74.1 4.8 %collective-permute-start.14 = (bf16[128,128]{1,0:T(8,128)(2,1)S(1)}, bf16[128,128]{1,0:T(8,128)(2,1)S(1)}, u32[]{:S(2)}, u32[]{:S(2)}) collective-permute-start(bf16[128,128]{1,0:T(8,128)(2,1)S(1)} %get-tuple-element.19), channel_id=1, source_target_pairs={{0,8},{2,10},{4,12},{6,14},{8,0},{10,2},{12,4},{14,6},{16,24},{18,... | collective-permute-start | bytes 98312 | tf_op jit(solution)/shard_map/ppermute | solution.py:36
  78.9 7.1 %collective-permute-start.19 = (bf16[512,128]{1,0:T(8,128)(2,1)S(1)}, bf16[512,128]{1,0:T(8,128)(2,1)S(1)}, u32[]{:S(2)}, u32[]{:S(2)}) collective-permute-start(bf16[512,128]{1,0:T(8,128)(2,1)S(1)} %pad_maximum_fusion.2.refs_0_), channel_id=1, source_target_pairs={{0,6},{2,4},{4,2},{6,0},{8,14},{10,12},{12,10},{14,8},{16,22},{18,... | collective-permute-start | bytes 393224 | tf_op jit(solution)/shard_map/ppermute | solution.py:36
  80.4 6.7 %collective-permute-start.18 = (bf16[512,128]{1,0:T(8,128)(2,1)S(1)}, bf16[512,128]{1,0:T(8,128)(2,1)S(1)}, u32[]{:S(2)}, u32[]{:S(2)}) collective-permute-start(bf16[512,128]{1,0:T(8,128)(2,1)S(1)} %pad_maximum_fusion.2.refs_0_), channel_id=1, source_target_pairs={{0,4},{2,6},{4,0},{6,2},{8,12},{10,14},{12,8},{14,10},{16,20},{18,... | collective-permute-start | bytes 393224 | tf_op jit(solution)/shard_map/ppermute | solution.py:36
  81.9 5.4 %collective-permute-start.17 = (bf16[512,128]{1,0:T(8,128)(2,1)S(1)}, bf16[512,128]{1,0:T(8,128)(2,1)S(1)}, u32[]{:S(2)}, u32[]{:S(2)}) collective-permute-start(bf16[512,128]{1,0:T(8,128)(2,1)S(1)} %pad_maximum_fusion.2.refs_0_), channel_id=1, source_target_pairs={{0,2},{2,0},{4,6},{6,4},{8,10},{10,8},{12,14},{14,12},{16,18},{18,... | collective-permute-start | bytes 393224 | tf_op jit(solution)/shard_map/ppermute | solution.py:36
  87.7 1.3 %collective-permute-start.20 = (f32[128,128]{1,0:T(8,128)S(1)}, f32[128,128]{1,0:T(8,128)S(1)}, u32[]{:S(2)}, u32[]{:S(2)}) collective-permute-start(f32[128,128]{1,0:T(8,128)S(1)} %get-tuple-element.18), channel_id=1, source_target_pairs={{0,1},{1,0},{2,3},{3,2},{4,5},{5,4},{6,7},{7,6},{8,9},{9,8},{10,11... | collective-permute-start | bytes 196616 | tf_op jit(solution)/shard_map/ppermute | solution.py:36

commit v3 on v2

--- a/solution.py
+++ b/solution.py
@@ -9,6 +9,8 @@
 RADIX = 4
 CHUNK = 8
 SPARE = 4 * 2**20
+BUILD_VMEM = 62 * 2**20
+AFTER_VMEM = 60 * 2**20
 
 VMEM = pl.BlockSpec(memory_space=pltpu.VMEM)
 SMEM = pl.BlockSpec(memory_space=pltpu.SMEM)
@@ -65,20 +67,40 @@
 
         lax.fori_loop(0, cells, put, 0, unroll=4 if cells % 4 == 0 else 1)
 
-    need = stacked.size * 2 + (cells + 1) * orb * orb * 4 + cells * orb * orb * 2
-    return pl.pallas_call(
-        kernel,
-        in_specs=[SMEM, SMEM, SMEM, HBM],
-        out_specs=VMEM,
-        scratch_shapes=[
-            pltpu.VMEM(stacked.shape, jnp.bfloat16),
-            pltpu.VMEM((cells + 1, orb, orb), jnp.float32),
-            pltpu.SemaphoreType.DMA((chunks,)),
-        ],
+    return pl.pallas_call(
+        kernel,
+        grid_spec=pltpu.PrefetchScalarGridSpec(
+            num_scalar_prefetch=3,
+            grid=(1,),
+            in_specs=[HBM],
+            out_specs=VMEM,
+            scratch_shapes=[
+                pltpu.VMEM(stacked.shape, jnp.bfloat16),
+                pltpu.VMEM((cells + 1, orb, orb), jnp.float32),
+                pltpu.SemaphoreType.DMA((chunks,)),
+            ],
+        ),
         out_shape=jax.ShapeDtypeStruct((cells, orb, orb), jnp.bfloat16),
-        compiler_params=pltpu.CompilerParams(vmem_limit_bytes=need + SPARE),
+        compiler_params=pltpu.CompilerParams(vmem_limit_bytes=BUILD_VMEM),
         name="build_tile",
     )(rows, cols, count, stacked)
+
+
+def after(x, others):
+    token = sum(other[:16] for other in others)
+
+    def kernel(*refs):
+        pass
+
+    return pl.pallas_call(
+        kernel,
+        in_specs=[HBM, HBM],
+        out_specs=HBM,
+        out_shape=jax.ShapeDtypeStruct(x.shape, x.dtype),
+        input_output_aliases={0: 0},
+        compiler_params=pltpu.CompilerParams(vmem_limit_bytes=AFTER_VMEM),
+        name="after",
+    )(x, token)
 
 
 def finish(total, first, orb, current_ref, previous_ref, center_ref, halfwidth_ref, outs):
@@ -162,24 +184,24 @@
     grid_cols = lax.axis_size("col")
     strides = stage_strides(grid_rows)
 
-    def gather(panel):
-        gathered = panel
-        for index, (stride, radix) in enumerate(strides):
-            parts = [gathered] + [
-                swap(gathered, "row", grid_rows, k * stride) for k in range(1, radix)
-            ]
-            if index < len(strides) - 1:
-                gathered = jnp.concatenate(parts, axis=0)
+    def stage(gathered, stride, radix):
+        return [gathered] + [swap(gathered, "row", grid_rows, k * stride) for k in range(1, radix)]
+
+    def gather(parts, stages):
+        for stride, radix in stages:
+            parts = stage(jnp.concatenate(parts, axis=0), stride, radix)
         return parts
 
     sources = jnp.array(arrival_order(strides), jnp.int32) ^ lax.axis_index("row")
     targets = jnp.arange(grid_cols, dtype=jnp.int32) ^ lax.axis_index("col")
-    pieces = gather(initial.astype(jnp.bfloat16))
+    pieces = gather([initial.astype(jnp.bfloat16)], strides[:1])
     dense = build_tile(
         block_rows[0, 0], block_cols[0, 0], block_counts[0], hamiltonian_blocks[0, 0],
         grid_rows, grid_cols,
     )
+    dense = after(dense, pieces[1:])
     received = lax.all_to_all(dense, ("row", "col"), 0, 0)
+    pieces = gather(pieces, strides[1:])
     tile, base, *others = merge_apply(
         sources, targets, dense, received, pieces, initial, center, halfwidth
     )
@@ -188,7 +210,7 @@
     current = initial
     for degree_step in range(DEGREE):
         if degree_step > 0:
-            pieces = gather(current.astype(jnp.bfloat16))
+            pieces = gather([current.astype(jnp.bfloat16)], strides)
             base, *others = apply_tile(
                 tile, pieces, current, previous, center, halfwidth, grid_cols
             )

time: 90 us -> 82.2 us (0.913)
  waiting for transfers between devices: 47.2 us -> 40.9 us
  local copies, waits for them, and re-layouts: 2.9 us -> 0.01 us
  other arithmetic: 0.7 us -> 2.14 us
    ppermute x21, waiting for transfers between devices: 47.2 us -> 33 us  [swap(): lax.ppermute(x, axis, [(source, source ^ offset) for source in range(size)])]
    all_to_all x1, waiting for transfers between devices: 0.01 us -> 7.87 us  [body(): received = lax.all_to_all(dense, ('row', 'col'), 0, 0)]
    unnamed x10 -> x6, local copies, waits for them, and re-layouts: 2.9 us -> 0.01 us
    all_to_all x1, starting transfers between devices: 7.29 us -> 5.95 us  [body(): received = lax.all_to_all(dense, ('row', 'col'), 0, 0)]
    ppermute x21, starting transfers between devices: 24.2 us -> 25.4 us  [swap(): lax.ppermute(x, axis, [(source, source ^ offset) for source in range(size)])]
    pallas_call x1 -> x2, Pallas kernels: 2.56 us -> 3.44 us  [the longest x1 3.44 us: build_tile(): pl.pallas_call(kernel, grid_spec=pltpu.PrefetchScalarGridSpec(num_scalar_...]
  transfers between devices with their start and end apart: 22 -> 22, of which waited for: 18 -> 17; matrix products, arithmetic and copies ran while one was open for 0% -> 0% of each run, Pallas kernels for 0% -> 4%
where the time goes in v3:
time: 82.2 us; the launch traced here: 81.9 us
  waiting for transfers between devices  40.9 us (50%)
  starting transfers between devices  31.3 us (38%)
  Pallas kernels  5.41 us (7%)
  other arithmetic  2.14 us (3%)
  between operations  2.07 us (3%)
    ppermute x21, waiting for transfers between devices, swap(): lax.ppermute(x, axis, [(source, source ^ offset) for source in range(size)])  33 us
    ppermute x21, starting transfers between devices, swap(): lax.ppermute(x, axis, [(source, source ^ offset) for source in range(size)])  25.4 us
    all_to_all x1, waiting for transfers between devices, body(): received = lax.all_to_all(dense, ('row', 'col'), 0, 0)  7.87 us
    all_to_all x1, starting transfers between devices, body(): received = lax.all_to_all(dense, ('row', 'col'), 0, 0)  5.95 us
    pallas_call x1, Pallas kernels, build_tile(): pl.pallas_call(kernel, grid_spec=pltpu.PrefetchScalarGridSpec(num_scalar_...  3.44 us
  transfers between devices with their start and end apart: 22, of which 17 were waited for; matrix products, arithmetic and copies ran while one was open for 0% of the time, Pallas kernels for 4%

profile of v3, /device:TPU:0, one launch (start us, length us, event | category | flops | bytes accessed | tf_op | source)
XLA Modules:
  0.0 81.9 jit_solution(9377563696449153065)
XLA Ops:
  0.0 0.8 %convert_element_type.9 = bf16[128,128]{1,0:T(8,128)(2,1)S(1)} convert(f32[128,128]{1,0:T(8,128)} %previous_ref.1) | non-fusion elementwise | flops 16384 | bytes 98304 | tf_op jit(solution)/shard_map/convert_element_type | solution.py:197
  0.8 5.0 %collective-permute-start.2 = (bf16[128,128]{1,0:T(8,128)(2,1)S(1)}, bf16[128,128]{1,0:T(8,128)(2,1)S(1)}, u32[]{:S(2)}, u32[]{:S(2)}) collective-permute-start(bf16[128,128]{1,0:T(8,128)(2,1)S(1)} %convert_element_type.9), channel_id=1, source_target_pairs={{0,24},{2,26},{4,28},{6,30},{8,16},{10,18},{12,20},{14,22},{16,8},... | collective-permute-start | bytes 98312 | tf_op jit(solution)/shard_map/ppermute | solution.py:38
  5.9 0.6 collective-permute-start
  7.1 3.4 %build_tile.1.refs_0_ = bf16[32,128,128]{2,1,0:T(8,128)(2,1)} custom-call(s32[64]{0:T(128)} %bitcast.6, s32[64]{0:T(128)} %bitcast.7, s32[1]{0:T(128)} %bitcast.4.count_ref, bf16[64,128,128]{2,1,0:T(8,128)(2,1)} %bitcast.5), custom_call_target="tpu_custom_call" | custom-call | tf_op jit(solution)/shard_map/build_tile/pallas_call | solution.py:70
  10.6 0.0 collective-permute-done.2
  10.6 0.1 collective-permute-done.1
  10.7 0.6 slice_add_fusion.refs_1_
  11.3 5.9 %all-to-all-start = ((bf16[32,128,128]{2,1,0:T(8,128)(2,1)}), bf16[32,128,128]{2,1,0:T(8,128)(2,1)S(1)}, u32[]{:S(2)}, u32[]{:S(2)}) async-start(bf16[32,128,128]{2,1,0:T(8,128)(2,1)} %after.1.dense_ref), calls=%async_computation | async-start | bytes 2097152 | tf_op jit(solution)/shard_map/all_to_all | solution.py:203
  17.3 2.7 %collective-permute-start.5 = (bf16[512,128]{1,0:T(8,128)(2,1)S(1)}, bf16[512,128]{1,0:T(8,128)(2,1)S(1)}, u32[]{:S(2)}, u32[]{:S(2)}) collective-permute-start(bf16[512,128]{1,0:T(8,128)(2,1)S(1)} %pad_maximum_fusion.refs_0_), channel_id=1, source_target_pairs={{0,6},{2,4},{4,2},{6,0},{8,14},{10,12},{12,10},{14,8},{16,22},{18,... | collective-permute-start | bytes 393224 | tf_op jit(solution)/shard_map/ppermute | solution.py:38
  20.0 0.6 collective-permute-start.4
  20.6 0.3 collective-permute-start.3
  22.2 11.2 %collective-permute-done.5.refs_3_ = bf16[512,128]{1,0:T(8,128)(2,1)S(1)} collective-permute-done((bf16[512,128]{1,0:T(8,128)(2,1)S(1)}, bf16[512,128]{1,0:T(8,128)(2,1)S(1)}, u32[]{:S(2)}, u32[]{:S(2)}) %collective-permute-start.5) | collective-permute-done | bytes 131104 | tf_op jit(solution)/shard_map/ppermute | solution.py:38
  33.3 1.3 %collective-permute-done.4.refs_2_ = bf16[512,128]{1,0:T(8,128)(2,1)S(1)} collective-permute-done((bf16[512,128]{1,0:T(8,128)(2,1)S(1)}, bf16[512,128]{1,0:T(8,128)(2,1)S(1)}, u32[]{:S(2)}, u32[]{:S(2)}) %collective-permute-start.4) | collective-permute-done | bytes 131104 | tf_op jit(solution)/shard_map/ppermute | solution.py:38
  34.6 1.0 %collective-permute-done.3.refs_1_ = bf16[512,128]{1,0:T(8,128)(2,1)S(1)} collective-permute-done((bf16[512,128]{1,0:T(8,128)(2,1)S(1)}, bf16[512,128]{1,0:T(8,128)(2,1)S(1)}, u32[]{:S(2)}, u32[]{:S(2)}) %collective-permute-start.3) | collective-permute-done | bytes 131104 | tf_op jit(solution)/shard_map/ppermute | solution.py:38
  35.6 7.9 %all-to-all-done.received_ref = bf16[32,128,128]{2,1,0:T(8,128)(2,1)S(1)} async-done(((bf16[32,128,128]{2,1,0:T(8,128)(2,1)}), bf16[32,128,128]{2,1,0:T(8,128)(2,1)S(1)}, u32[]{:S(2)}, u32[]{:S(2)}) %all-to-all-start) | async-done | bytes 1048608 | tf_op jit(solution)/shard_map/all_to_all | solution.py:203
  43.5 1.1 %merge_apply.1 = (bf16[256,2048]{1,0:T(8,128)(2,1)S(1)}, f32[128,128]{1,0:T(8,128)S(1)}, f32[128,128]{1,0:T(8,128)S(1)}) custom-call(s32[16]{0:T(128)S(1)} %broadcast_xor_fusion.sources_ref, s32[2]{0:T(128)S(1)} %iota_xor_fusion.targets_ref, f32[1]{0:T(128)S(6)} %copy.12.center_ref, f32[1]{0:T(128)S(6)} %copy.13.halfwidth_ref, ...), custom_call_target="tpu_custom_call" | custom-call | tf_op jit(solution)/shard_map/merge_apply/pallas_call | solution.py:143
  44.6 0.1 collective-permute-start.6
  44.7 1.2 %collective-permute-done.6 = f32[128,128]{1,0:T(8,128)S(1)} collective-permute-done((f32[128,128]{1,0:T(8,128)S(1)}, f32[128,128]{1,0:T(8,128)S(1)}, u32[]{:S(2)}, u32[]{:S(2)}) %collective-permute-start.6) | collective-permute-done | bytes 65568 | tf_op jit(solution)/shard_map/ppermute | solution.py:38
  46.0 1.4 %collective-permute-start.9 = (bf16[128,128]{1,0:T(8,128)(2,1)S(1)}, bf16[128,128]{1,0:T(8,128)(2,1)S(1)}, u32[]{:S(2)}, u32[]{:S(2)}) collective-permute-start(bf16[128,128]{1,0:T(8,128)(2,1)S(1)} %get-tuple-element.21), channel_id=1, source_target_pairs={{0,24},{2,26},{4,28},{6,30},{8,16},{10,18},{12,20},{14,22},{16,8},... | collective-permute-start | bytes 98312 | tf_op jit(solution)/shard_map/ppermute | solution.py:38
  47.3 0.9 %collective-permute-start.8 = (bf16[128,128]{1,0:T(8,128)(2,1)S(1)}, bf16[128,128]{1,0:T(8,128)(2,1)S(1)}, u32[]{:S(2)}, u32[]{:S(2)}) collective-permute-start(bf16[128,128]{1,0:T(8,128)(2,1)S(1)} %get-tuple-element.21), channel_id=1, source_target_pairs={{0,16},{2,18},{4,20},{6,22},{8,24},{10,26},{12,28},{14,30},{16,0},... | collective-permute-start | bytes 98312 | tf_op jit(solution)/shard_map/ppermute | solution.py:38
  48.3 2.2 %collective-permute-start.7 = (bf16[128,128]{1,0:T(8,128)(2,1)S(1)}, bf16[128,128]{1,0:T(8,128)(2,1)S(1)}, u32[]{:S(2)}, u32[]{:S(2)}) collective-permute-start(bf16[128,128]{1,0:T(8,128)(2,1)S(1)} %get-tuple-element.21), channel_id=1, source_target_pairs={{0,8},{2,10},{4,12},{6,14},{8,0},{10,2},{12,4},{14,6},{16,24},{18,... | collective-permute-start | bytes 98312 | tf_op jit(solution)/shard_map/ppermute | solution.py:38
  50.4 1.3 %collective-permute-done.9 = bf16[128,128]{1,0:T(8,128)(2,1)S(1)} collective-permute-done((bf16[128,128]{1,0:T(8,128)(2,1)S(1)}, bf16[128,128]{1,0:T(8,128)(2,1)S(1)}, u32[]{:S(2)}, u32[]{:S(2)}) %collective-permute-start.9) | collective-permute-done | bytes 32800 | tf_op jit(solution)/shard_map/ppermute | solution.py:38
  51.8 1.0 %collective-permute-done.8 = bf16[128,128]{1,0:T(8,128)(2,1)S(1)} collective-permute-done((bf16[128,128]{1,0:T(8,128)(2,1)S(1)}, bf16[128,128]{1,0:T(8,128)(2,1)S(1)}, u32[]{:S(2)}, u32[]{:S(2)}) %collective-permute-start.8) | collective-permute-done | bytes 32800 | tf_op jit(solution)/shard_map/ppermute | solution.py:38
  52.7 0.1 collective-permute-done.7
  52.9 2.5 %collective-permute-start.12 = (bf16[512,128]{1,0:T(8,128)(2,1)S(1)}, bf16[512,128]{1,0:T(8,128)(2,1)S(1)}, u32[]{:S(2)}, u32[]{:S(2)}) collective-permute-start(bf16[512,128]{1,0:T(8,128)(2,1)S(1)} %pad_maximum_fusion.1.refs_0_), channel_id=1, source_target_pairs={{0,6},{2,4},{4,2},{6,0},{8,14},{10,12},{12,10},{14,8},{16,22},{18,... | collective-permute-start | bytes 393224 | tf_op jit(solution)/shard_map/ppermute | solution.py:38
  55.4 0.5 collective-permute-start.11
  55.9 0.5 collective-permute-start.10
  56.4 3.1 %collective-permute-done.12.refs_3_ = bf16[512,128]{1,0:T(8,128)(2,1)S(1)} collective-permute-done((bf16[512,128]{1,0:T(8,128)(2,1)S(1)}, bf16[512,128]{1,0:T(8,128)(2,1)S(1)}, u32[]{:S(2)}, u32[]{:S(2)}) %collective-permute-start.12) | collective-permute-done | bytes 131104 | tf_op jit(solution)/shard_map/ppermute | solution.py:38
  59.5 2.4 %collective-permute-done.11.refs_2_ = bf16[512,128]{1,0:T(8,128)(2,1)S(1)} collective-permute-done((bf16[512,128]{1,0:T(8,128)(2,1)S(1)}, bf16[512,128]{1,0:T(8,128)(2,1)S(1)}, u32[]{:S(2)}, u32[]{:S(2)}) %collective-permute-start.11) | collective-permute-done | bytes 131104 | tf_op jit(solution)/shard_map/ppermute | solution.py:38
  61.9 0.0 collective-permute-done.10.refs_1_
  61.9 0.4 apply_tile.2
  62.3 0.1 collective-permute-start.13
  62.4 1.2 %collective-permute-done.13 = f32[128,128]{1,0:T(8,128)S(1)} collective-permute-done((f32[128,128]{1,0:T(8,128)S(1)}, f32[128,128]{1,0:T(8,128)S(1)}, u32[]{:S(2)}, u32[]{:S(2)}) %collective-permute-start.13) | collective-permute-done | bytes 65568 | tf_op jit(solution)/shard_map/ppermute | solution.py:38
  63.7 1.2 %collective-permute-start.16 = (bf16[128,128]{1,0:T(8,128)(2,1)S(1)}, bf16[128,128]{1,0:T(8,128)(2,1)S(1)}, u32[]{:S(2)}, u32[]{:S(2)}) collective-permute-start(bf16[128,128]{1,0:T(8,128)(2,1)S(1)} %get-tuple-element.19), channel_id=1, source_target_pairs={{0,24},{2,26},{4,28},{6,30},{8,16},{10,18},{12,20},{14,22},{16,8},... | collective-permute-start | bytes 98312 | tf_op jit(solution)/shard_map/ppermute | solution.py:38
  64.9 0.8 %collective-permute-start.15 = (bf16[128,128]{1,0:T(8,128)(2,1)S(1)}, bf16[128,128]{1,0:T(8,128)(2,1)S(1)}, u32[]{:S(2)}, u32[]{:S(2)}) collective-permute-start(bf16[128,128]{1,0:T(8,128)(2,1)S(1)} %get-tuple-element.19), channel_id=1, source_target_pairs={{0,16},{2,18},{4,20},{6,22},{8,24},{10,26},{12,28},{14,30},{16,0},... | collective-permute-start | bytes 98312 | tf_op jit(solution)/shard_map/ppermute | solution.py:38
  65.7 2.4 %collective-permute-start.14 = (bf16[128,128]{1,0:T(8,128)(2,1)S(1)}, bf16[128,128]{1,0:T(8,128)(2,1)S(1)}, u32[]{:S(2)}, u32[]{:S(2)}) collective-permute-start(bf16[128,128]{1,0:T(8,128)(2,1)S(1)} %get-tuple-element.19), channel_id=1, source_target_pairs={{0,8},{2,10},{4,12},{6,14},{8,0},{10,2},{12,4},{14,6},{16,24},{18,... | collective-permute-start | bytes 98312 | tf_op jit(solution)/shard_map/ppermute | solution.py:38
  68.1 1.3 %collective-permute-done.16 = bf16[128,128]{1,0:T(8,128)(2,1)S(1)} collective-permute-done((bf16[128,128]{1,0:T(8,128)(2,1)S(1)}, bf16[128,128]{1,0:T(8,128)(2,1)S(1)}, u32[]{:S(2)}, u32[]{:S(2)}) %collective-permute-start.16) | collective-permute-done | bytes 32800 | tf_op jit(solution)/shard_map/ppermute | solution.py:38
  69.5 0.9 %collective-permute-done.15 = bf16[128,128]{1,0:T(8,128)(2,1)S(1)} collective-permute-done((bf16[128,128]{1,0:T(8,128)(2,1)S(1)}, bf16[128,128]{1,0:T(8,128)(2,1)S(1)}, u32[]{:S(2)}, u32[]{:S(2)}) %collective-permute-start.15) | collective-permute-done | bytes 32800 | tf_op jit(solution)/shard_map/ppermute | solution.py:38
  70.4 0.0 collective-permute-done.14
  70.4 1.5 %collective-permute-start.19 = (bf16[512,128]{1,0:T(8,128)(2,1)S(1)}, bf16[512,128]{1,0:T(8,128)(2,1)S(1)}, u32[]{:S(2)}, u32[]{:S(2)}) collective-permute-start(bf16[512,128]{1,0:T(8,128)(2,1)S(1)} %pad_maximum_fusion.2.refs_0_), channel_id=1, source_target_pairs={{0,6},{2,4},{4,2},{6,0},{8,14},{10,12},{12,10},{14,8},{16,22},{18,... | collective-permute-start | bytes 393224 | tf_op jit(solution)/shard_map/ppermute | solution.py:38
  72.0 1.5 %collective-permute-start.18 = (bf16[512,128]{1,0:T(8,128)(2,1)S(1)}, bf16[512,128]{1,0:T(8,128)(2,1)S(1)}, u32[]{:S(2)}, u32[]{:S(2)}) collective-permute-start(bf16[512,128]{1,0:T(8,128)(2,1)S(1)} %pad_maximum_fusion.2.refs_0_), channel_id=1, source_target_pairs={{0,4},{2,6},{4,0},{6,2},{8,12},{10,14},{12,8},{14,10},{16,20},{18,... | collective-permute-start | bytes 393224 | tf_op jit(solution)/shard_map/ppermute | solution.py:38
  73.5 0.5 collective-permute-start.17
  74.0 3.8 %collective-permute-done.19.refs_3_ = bf16[512,128]{1,0:T(8,128)(2,1)S(1)} collective-permute-done((bf16[512,128]{1,0:T(8,128)(2,1)S(1)}, bf16[512,128]{1,0:T(8,128)(2,1)S(1)}, u32[]{:S(2)}, u32[]{:S(2)}) %collective-permute-start.19) | collective-permute-done | bytes 131104 | tf_op jit(solution)/shard_map/ppermute | solution.py:38
  77.8 1.7 %collective-permute-done.18.refs_2_ = bf16[512,128]{1,0:T(8,128)(2,1)S(1)} collective-permute-done((bf16[512,128]{1,0:T(8,128)(2,1)S(1)}, bf16[512,128]{1,0:T(8,128)(2,1)S(1)}, u32[]{:S(2)}, u32[]{:S(2)}) %collective-permute-start.18) | collective-permute-done | bytes 131104 | tf_op jit(solution)/shard_map/ppermute | solution.py:38
  79.5 0.4 apply_tile.3
  79.9 0.1 collective-permute-start.20
  80.0 1.2 %collective-permute-done.20 = f32[128,128]{1,0:T(8,128)S(1)} collective-permute-done((f32[128,128]{1,0:T(8,128)S(1)}, f32[128,128]{1,0:T(8,128)S(1)}, u32[]{:S(2)}, u32[]{:S(2)}) %collective-permute-start.20) | collective-permute-done | bytes 65568 | tf_op jit(solution)/shard_map/ppermute | solution.py:38
  81.2 0.6 add.19
  (17 shorter events, 0.1 us)
Async XLA Ops:
  0.8 9.7 %collective-permute-start.2 = (bf16[128,128]{1,0:T(8,128)(2,1)S(1)}, bf16[128,128]{1,0:T(8,128)(2,1)S(1)}, u32[]{:S(2)}, u32[]{:S(2)}) collective-permute-start(bf16[128,128]{1,0:T(8,128)(2,1)S(1)} %convert_element_type.9), channel_id=1, source_target_pairs={{0,24},{2,26},{4,28},{6,30},{8,16},{10,18},{12,20},{14,22},{16,8},... | collective-permute-start | bytes 98312 | tf_op jit(solution)/shard_map/ppermute | solution.py:38
  5.9 4.8 %collective-permute-start.1 = (bf16[128,128]{1,0:T(8,128)(2,1)S(1)}, bf16[128,128]{1,0:T(8,128)(2,1)S(1)}, u32[]{:S(2)}, u32[]{:S(2)}) collective-permute-start(bf16[128,128]{1,0:T(8,128)(2,1)S(1)} %convert_element_type.9), channel_id=1, source_target_pairs={{0,16},{2,18},{4,20},{6,22},{8,24},{10,26},{12,28},{14,30},{16,0},... | collective-permute-start | bytes 98312 | tf_op jit(solution)/shard_map/ppermute | solution.py:38
  5.9 4.8 %collective-permute-start = (bf16[128,128]{1,0:T(8,128)(2,1)S(1)}, bf16[128,128]{1,0:T(8,128)(2,1)S(1)}, u32[]{:S(2)}, u32[]{:S(2)}) collective-permute-start(bf16[128,128]{1,0:T(8,128)(2,1)S(1)} %convert_element_type.9), channel_id=1, source_target_pairs={{0,8},{2,10},{4,12},{6,14},{8,0},{10,2},{12,4},{14,6},{16,24},{18,... | collective-permute-start | bytes 98312 | tf_op jit(solution)/shard_map/ppermute | solution.py:38
  11.3 9.5 %copy-start.2 = (s32[16]{0:T(128)S(1)}, s32[16]{0:T(128)}, u32[]{:S(2)}) copy-start(s32[16]{0:T(128)} %constant.10.clone) | copy-start | bytes 196
  11.3 32.2 %copy-start.1 = (f32[128,128]{1,0:T(8,128)S(1)}, f32[128,128]{1,0:T(8,128)}, u32[]{:S(2)}) copy-start(f32[128,128]{1,0:T(8,128)} %previous_ref.1) | copy-start | bytes 196612
  11.3 32.2 %copy-start = (bf16[32,128,128]{2,1,0:T(8,128)(2,1)S(1)}, bf16[32,128,128]{2,1,0:T(8,128)(2,1)}, u32[]{:S(2)}) copy-start(bf16[32,128,128]{2,1,0:T(8,128)(2,1)} %after.1.dense_ref) | copy-start | bytes 3145732
  11.3 32.2 %all-to-all-start = ((bf16[32,128,128]{2,1,0:T(8,128)(2,1)}), bf16[32,128,128]{2,1,0:T(8,128)(2,1)S(1)}, u32[]{:S(2)}, u32[]{:S(2)}) async-start(bf16[32,128,128]{2,1,0:T(8,128)(2,1)} %after.1.dense_ref), calls=%async_computation | async-start | bytes 2097152 | tf_op jit(solution)/shard_map/all_to_all | solution.py:203
  17.3 16.0 %collective-permute-start.5 = (bf16[512,128]{1,0:T(8,128)(2,1)S(1)}, bf16[512,128]{1,0:T(8,128)(2,1)S(1)}, u32[]{:S(2)}, u32[]{:S(2)}) collective-permute-start(bf16[512,128]{1,0:T(8,128)(2,1)S(1)} %pad_maximum_fusion.refs_0_), channel_id=1, source_target_pairs={{0,6},{2,4},{4,2},{6,0},{8,14},{10,12},{12,10},{14,8},{16,22},{18,... | collective-permute-start | bytes 393224 | tf_op jit(solution)/shard_map/ppermute | solution.py:38
  20.0 14.6 %collective-permute-start.4 = (bf16[512,128]{1,0:T(8,128)(2,1)S(1)}, bf16[512,128]{1,0:T(8,128)(2,1)S(1)}, u32[]{:S(2)}, u32[]{:S(2)}) collective-permute-start(bf16[512,128]{1,0:T(8,128)(2,1)S(1)} %pad_maximum_fusion.refs_0_), channel_id=1, source_target_pairs={{0,4},{2,6},{4,0},{6,2},{8,12},{10,14},{12,8},{14,10},{16,20},{18,... | collective-permute-start | bytes 393224 | tf_op jit(solution)/shard_map/ppermute | solution.py:38
  20.6 15.0 %collective-permute-start.3 = (bf16[512,128]{1,0:T(8,128)(2,1)S(1)}, bf16[512,128]{1,0:T(8,128)(2,1)S(1)}, u32[]{:S(2)}, u32[]{:S(2)}) collective-permute-start(bf16[512,128]{1,0:T(8,128)(2,1)S(1)} %pad_maximum_fusion.refs_0_), channel_id=1, source_target_pairs={{0,2},{2,0},{4,6},{6,4},{8,10},{10,8},{12,14},{14,12},{16,18},{18,... | collective-permute-start | bytes 393224 | tf_op jit(solution)/shard_map/ppermute | solution.py:38
  44.6 1.3 %collective-permute-start.6 = (f32[128,128]{1,0:T(8,128)S(1)}, f32[128,128]{1,0:T(8,128)S(1)}, u32[]{:S(2)}, u32[]{:S(2)}) collective-permute-start(f32[128,128]{1,0:T(8,128)S(1)} %get-tuple-element.14), channel_id=1, source_target_pairs={{0,1},{1,0},{2,3},{3,2},{4,5},{5,4},{6,7},{7,6},{8,9},{9,8},{10,11... | collective-permute-start | bytes 196616 | tf_op jit(solution)/shard_map/ppermute | solution.py:38
  46.0 5.8 %collective-permute-start.9 = (bf16[128,128]{1,0:T(8,128)(2,1)S(1)}, bf16[128,128]{1,0:T(8,128)(2,1)S(1)}, u32[]{:S(2)}, u32[]{:S(2)}) collective-permute-start(bf16[128,128]{1,0:T(8,128)(2,1)S(1)} %get-tuple-element.21), channel_id=1, source_target_pairs={{0,24},{2,26},{4,28},{6,30},{8,16},{10,18},{12,20},{14,22},{16,8},... | collective-permute-start | bytes 98312 | tf_op jit(solution)/shard_map/ppermute | solution.py:38
  47.3 5.4 %collective-permute-start.8 = (bf16[128,128]{1,0:T(8,128)(2,1)S(1)}, bf16[128,128]{1,0:T(8,128)(2,1)S(1)}, u32[]{:S(2)}, u32[]{:S(2)}) collective-permute-start(bf16[128,128]{1,0:T(8,128)(2,1)S(1)} %get-tuple-element.21), channel_id=1, source_target_pairs={{0,16},{2,18},{4,20},{6,22},{8,24},{10,26},{12,28},{14,30},{16,0},... | collective-permute-start | bytes 98312 | tf_op jit(solution)/shard_map/ppermute | solution.py:38
  48.3 4.6 %collective-permute-start.7 = (bf16[128,128]{1,0:T(8,128)(2,1)S(1)}, bf16[128,128]{1,0:T(8,128)(2,1)S(1)}, u32[]{:S(2)}, u32[]{:S(2)}) collective-permute-start(bf16[128,128]{1,0:T(8,128)(2,1)S(1)} %get-tuple-element.21), channel_id=1, source_target_pairs={{0,8},{2,10},{4,12},{6,14},{8,0},{10,2},{12,4},{14,6},{16,24},{18,... | collective-permute-start | bytes 98312 | tf_op jit(solution)/shard_map/ppermute | solution.py:38
  52.9 6.6 %collective-permute-start.12 = (bf16[512,128]{1,0:T(8,128)(2,1)S(1)}, bf16[512,128]{1,0:T(8,128)(2,1)S(1)}, u32[]{:S(2)}, u32[]{:S(2)}) collective-permute-start(bf16[512,128]{1,0:T(8,128)(2,1)S(1)} %pad_maximum_fusion.1.refs_0_), channel_id=1, source_target_pairs={{0,6},{2,4},{4,2},{6,0},{8,14},{10,12},{12,10},{14,8},{16,22},{18,... | collective-permute-start | bytes 393224 | tf_op jit(solution)/shard_map/ppermute | solution.py:38
  55.4 6.5 %collective-permute-start.11 = (bf16[512,128]{1,0:T(8,128)(2,1)S(1)}, bf16[512,128]{1,0:T(8,128)(2,1)S(1)}, u32[]{:S(2)}, u32[]{:S(2)}) collective-permute-start(bf16[512,128]{1,0:T(8,128)(2,1)S(1)} %pad_maximum_fusion.1.refs_0_), channel_id=1, source_target_pairs={{0,4},{2,6},{4,0},{6,2},{8,12},{10,14},{12,8},{14,10},{16,20},{18,... | collective-permute-start | bytes 393224 | tf_op jit(solution)/shard_map/ppermute | solution.py:38
  55.9 6.0 %collective-permute-start.10 = (bf16[512,128]{1,0:T(8,128)(2,1)S(1)}, bf16[512,128]{1,0:T(8,128)(2,1)S(1)}, u32[]{:S(2)}, u32[]{:S(2)}) collective-permute-start(bf16[512,128]{1,0:T(8,128)(2,1)S(1)} %pad_maximum_fusion.1.refs_0_), channel_id=1, source_target_pairs={{0,2},{2,0},{4,6},{6,4},{8,10},{10,8},{12,14},{14,12},{16,18},{18,... | collective-permute-start | bytes 393224 | tf_op jit(solution)/shard_map/ppermute | solution.py:38
  62.3 1.3 %collective-permute-start.13 = (f32[128,128]{1,0:T(8,128)S(1)}, f32[128,128]{1,0:T(8,128)S(1)}, u32[]{:S(2)}, u32[]{:S(2)}) collective-permute-start(f32[128,128]{1,0:T(8,128)S(1)} %get-tuple-element.16), channel_id=1, source_target_pairs={{0,1},{1,0},{2,3},{3,2},{4,5},{5,4},{6,7},{7,6},{8,9},{9,8},{10,11... | collective-permute-start | bytes 196616 | tf_op jit(solution)/shard_map/ppermute | solution.py:38
  63.7 5.8 %collective-permute-start.16 = (bf16[128,128]{1,0:T(8,128)(2,1)S(1)}, bf16[128,128]{1,0:T(8,128)(2,1)S(1)}, u32[]{:S(2)}, u32[]{:S(2)}) collective-permute-start(bf16[128,128]{1,0:T(8,128)(2,1)S(1)} %get-tuple-element.19), channel_id=1, source_target_pairs={{0,24},{2,26},{4,28},{6,30},{8,16},{10,18},{12,20},{14,22},{16,8},... | collective-permute-start | bytes 98312 | tf_op jit(solution)/shard_map/ppermute | solution.py:38
  64.9 5.5 %collective-permute-start.15 = (bf16[128,128]{1,0:T(8,128)(2,1)S(1)}, bf16[128,128]{1,0:T(8,128)(2,1)S(1)}, u32[]{:S(2)}, u32[]{:S(2)}) collective-permute-start(bf16[128,128]{1,0:T(8,128)(2,1)S(1)} %get-tuple-element.19), channel_id=1, source_target_pairs={{0,16},{2,18},{4,20},{6,22},{8,24},{10,26},{12,28},{14,30},{16,0},... | collective-permute-start | bytes 98312 | tf_op jit(solution)/shard_map/ppermute | solution.py:38
  65.7 4.7 %collective-permute-start.14 = (bf16[128,128]{1,0:T(8,128)(2,1)S(1)}, bf16[128,128]{1,0:T(8,128)(2,1)S(1)}, u32[]{:S(2)}, u32[]{:S(2)}) collective-permute-start(bf16[128,128]{1,0:T(8,128)(2,1)S(1)} %get-tuple-element.19), channel_id=1, source_target_pairs={{0,8},{2,10},{4,12},{6,14},{8,0},{10,2},{12,4},{14,6},{16,24},{18,... | collective-permute-start | bytes 98312 | tf_op jit(solution)/shard_map/ppermute | solution.py:38
  70.4 7.3 %collective-permute-start.19 = (bf16[512,128]{1,0:T(8,128)(2,1)S(1)}, bf16[512,128]{1,0:T(8,128)(2,1)S(1)}, u32[]{:S(2)}, u32[]{:S(2)}) collective-permute-start(bf16[512,128]{1,0:T(8,128)(2,1)S(1)} %pad_maximum_fusion.2.refs_0_), channel_id=1, source_target_pairs={{0,6},{2,4},{4,2},{6,0},{8,14},{10,12},{12,10},{14,8},{16,22},{18,... | collective-permute-start | bytes 393224 | tf_op jit(solution)/shard_map/ppermute | solution.py:38
  72.0 7.5 %collective-permute-start.18 = (bf16[512,128]{1,0:T(8,128)(2,1)S(1)}, bf16[512,128]{1,0:T(8,128)(2,1)S(1)}, u32[]{:S(2)}, u32[]{:S(2)}) collective-permute-start(bf16[512,128]{1,0:T(8,128)(2,1)S(1)} %pad_maximum_fusion.2.refs_0_), channel_id=1, source_target_pairs={{0,4},{2,6},{4,0},{6,2},{8,12},{10,14},{12,8},{14,10},{16,20},{18,... | collective-permute-start | bytes 393224 | tf_op jit(solution)/shard_map/ppermute | solution.py:38
  73.5 6.0 %collective-permute-start.17 = (bf16[512,128]{1,0:T(8,128)(2,1)S(1)}, bf16[512,128]{1,0:T(8,128)(2,1)S(1)}, u32[]{:S(2)}, u32[]{:S(2)}) collective-permute-start(bf16[512,128]{1,0:T(8,128)(2,1)S(1)} %pad_maximum_fusion.2.refs_0_), channel_id=1, source_target_pairs={{0,2},{2,0},{4,6},{6,4},{8,10},{10,8},{12,14},{14,12},{16,18},{18,... | collective-permute-start | bytes 393224 | tf_op jit(solution)/shard_map/ppermute | solution.py:38
  79.9 1.3 %collective-permute-start.20 = (f32[128,128]{1,0:T(8,128)S(1)}, f32[128,128]{1,0:T(8,128)S(1)}, u32[]{:S(2)}, u32[]{:S(2)}) collective-permute-start(f32[128,128]{1,0:T(8,128)S(1)} %get-tuple-element.18), channel_id=1, source_target_pairs={{0,1},{1,0},{2,3},{3,2},{4,5},{5,4},{6,7},{7,6},{8,9},{9,8},{10,11... | collective-permute-start | bytes 196616 | tf_op jit(solution)/shard_map/ppermute | solution.py:38

commit v4 on v3

--- a/solution.py
+++ b/solution.py
@@ -30,8 +30,18 @@
 def arrival_order(strides):
     order = [0]
     for stride, radix in strides:
-        order = [k * stride ^ offset for k in range(radix) for offset in order]
+        order = [k * stride + offset for k in range(radix) for offset in order]
     return order
+
+
+def spread(x, axis, size, stride, radix):
+    groups = [
+        [first + k * stride for k in range(radix)]
+        for first in range(size)
+        if first // stride % radix == 0
+    ]
+    copies = jnp.broadcast_to(x[None], (radix, *x.shape))
+    return lax.all_to_all(copies, axis, 0, 0, axis_index_groups=groups)
 
 
 def swap(x, axis, size, offset):
@@ -86,8 +96,8 @@
     )(rows, cols, count, stacked)
 
 
-def after(x, others):
-    token = sum(other[:16] for other in others)
+def after(x, other):
+    token = other[:16]
 
     def kernel(*refs):
         pass
@@ -111,72 +121,56 @@
         outs[d][...] = total[d * orb : (d + 1) * orb] * scale
 
 
-def merge_apply(sources, targets, dense, received, pieces, current, center, halfwidth):
+def merge_apply(sources, targets, dense, received, panel, current, center, halfwidth):
     cells, orb, _ = dense.shape
-    grid_rows = sources.shape[0]
+    grid_rows = len(sources)
     grid_cols = targets.shape[0]
     vectors = current.shape[1]
-    count = len(pieces)
-
-    def kernel(sources_ref, targets_ref, center_ref, halfwidth_ref, dense_ref, received_ref, current_ref, *refs):
-        piece_refs = refs[:count]
-        tile_ref, *outs = refs[count:]
+    step = min(4, grid_rows)
+
+    def kernel(targets_ref, center_ref, halfwidth_ref, dense_ref, received_ref, current_ref, panel_ref, tile_ref, *outs):
         total = None
-        at = 0
-        for ref in piece_refs:
-            depth = ref.shape[0]
-            for k in range(at // orb, (at + depth) // orb):
-                first = sources_ref[k] * grid_cols
+        for start in range(0, grid_rows, step):
+            for k in range(start, start + step):
                 for d in range(grid_cols):
-                    cell = first + targets_ref[d]
+                    cell = sources[k] * grid_cols + targets_ref[d]
                     turned = received_ref[cell].T.astype(jnp.float32)
                     block = (dense_ref[cell].astype(jnp.float32) + turned).astype(jnp.bfloat16)
                     tile_ref[d * orb : (d + 1) * orb, k * orb : (k + 1) * orb] = block
-            part = jnp.dot(
-                tile_ref[:, at : at + depth], ref[...], preferred_element_type=jnp.float32
-            )
+            held = slice(start * orb, (start + step) * orb)
+            part = jnp.dot(tile_ref[:, held], panel_ref[held], preferred_element_type=jnp.float32)
             total = part if total is None else total + part
-            at += depth
         finish(total, True, orb, current_ref, None, center_ref, halfwidth_ref, outs)
 
     block = jax.ShapeDtypeStruct((orb, vectors), jnp.float32)
     return pl.pallas_call(
         kernel,
-        in_specs=[SMEM] * 4 + [VMEM] * (3 + count),
+        in_specs=[SMEM] * 3 + [VMEM] * 4,
         out_specs=[VMEM] * (1 + grid_cols),
         out_shape=[jax.ShapeDtypeStruct((grid_cols * orb, grid_rows * orb), jnp.bfloat16)]
         + [block] * grid_cols,
         compiler_params=pltpu.CompilerParams(vmem_limit_bytes=dense.size * 6 + 2 * SPARE),
         name="merge_apply",
-    )(sources, targets, center, halfwidth, dense, received, current, *pieces)
-
-
-def apply_tile(tile, pieces, current, previous, center, halfwidth, grid_cols):
+    )(targets, center, halfwidth, dense, received, current, panel)
+
+
+def apply_tile(tile, panel, current, previous, center, halfwidth, grid_cols):
     height, _ = tile.shape
     orb = height // grid_cols
     vectors = current.shape[1]
-    count = len(pieces)
-
-    def kernel(center_ref, halfwidth_ref, tile_ref, current_ref, previous_ref, *refs):
-        total = None
-        at = 0
-        for ref in refs[:count]:
-            depth = ref.shape[0]
-            part = jnp.dot(
-                tile_ref[:, at : at + depth], ref[...], preferred_element_type=jnp.float32
-            )
-            total = part if total is None else total + part
-            at += depth
-        finish(total, False, orb, current_ref, previous_ref, center_ref, halfwidth_ref, refs[count:])
-
-    return pl.pallas_call(
-        kernel,
-        in_specs=[SMEM] * 2 + [VMEM] * (3 + count),
+
+    def kernel(center_ref, halfwidth_ref, tile_ref, current_ref, previous_ref, panel_ref, *outs):
+        total = jnp.dot(tile_ref[...], panel_ref[...], preferred_element_type=jnp.float32)
+        finish(total, False, orb, current_ref, previous_ref, center_ref, halfwidth_ref, outs)
+
+    return pl.pallas_call(
+        kernel,
+        in_specs=[SMEM] * 2 + [VMEM] * 4,
         out_specs=[VMEM] * grid_cols,
         out_shape=[jax.ShapeDtypeStruct((orb, vectors), jnp.float32)] * grid_cols,
         compiler_params=pltpu.CompilerParams(vmem_limit_bytes=tile.size * 2 + 2 * SPARE),
         name="apply_tile",
-    )(center, halfwidth, tile, current, previous, *pieces)
+    )(center, halfwidth, tile, current, previous, panel)
 
 
 def body(hamiltonian_blocks, block_rows, block_cols, block_counts, initial, center, halfwidth):
@@ -184,35 +178,33 @@
     grid_cols = lax.axis_size("col")
     strides = stage_strides(grid_rows)
 
-    def stage(gathered, stride, radix):
-        return [gathered] + [swap(gathered, "row", grid_rows, k * stride) for k in range(1, radix)]
-
-    def gather(parts, stages):
+    def gather(panel, stages):
         for stride, radix in stages:
-            parts = stage(jnp.concatenate(parts, axis=0), stride, radix)
-        return parts
-
-    sources = jnp.array(arrival_order(strides), jnp.int32) ^ lax.axis_index("row")
+            spreaded = spread(panel, "row", grid_rows, stride, radix)
+            panel = spreaded.reshape(-1, panel.shape[1])
+        return panel
+
+    sources = arrival_order(strides)
     targets = jnp.arange(grid_cols, dtype=jnp.int32) ^ lax.axis_index("col")
-    pieces = gather([initial.astype(jnp.bfloat16)], strides[:1])
+    panel = gather(initial.astype(jnp.bfloat16), strides[:1])
     dense = build_tile(
         block_rows[0, 0], block_cols[0, 0], block_counts[0], hamiltonian_blocks[0, 0],
         grid_rows, grid_cols,
     )
-    dense = after(dense, pieces[1:])
+    dense = after(dense, panel)
     received = lax.all_to_all(dense, ("row", "col"), 0, 0)
-    pieces = gather(pieces, strides[1:])
+    panel = gather(panel, strides[1:])
     tile, base, *others = merge_apply(
-        sources, targets, dense, received, pieces, initial, center, halfwidth
+        sources, targets, dense, received, panel, initial, center, halfwidth
     )
 
     previous = initial
     current = initial
     for degree_step in range(DEGREE):
         if degree_step > 0:
-            pieces = gather([current.astype(jnp.bfloat16)], strides)
+            panel = gather(current.astype(jnp.bfloat16), strides)
             base, *others = apply_tile(
-                tile, pieces, current, previous, center, halfwidth, grid_cols
+                tile, panel, current, previous, center, halfwidth, grid_cols
             )
         following = base
         for d, other in enumerate(others, start=1):

time: 82.2 us -> 101 us (1.23)
  blocking collectives: 0 us -> 51.4 us
  starting transfers between devices: 31.3 us -> 7.47 us
  waiting for transfers between devices: 40.9 us -> 30.6 us
  local copies, waits for them, and re-layouts: 0.01 us -> 1.69 us
    all_to_all x0 -> x5, blocking collectives: none -> 51.4 us  [spread(): return lax.all_to_all(copies, axis, 0, 0, axis_index_groups=groups)]
    ppermute x21 -> x3, waiting for transfers between devices: 33 us -> 3.72 us  [swap(): lax.ppermute(x, axis, [(source, source ^ offset) for source in range(size)])]
    ppermute x21 -> x3, starting transfers between devices: 25.4 us -> 0.21 us  [swap(): lax.ppermute(x, axis, [(source, source ^ offset) for source in range(size)])]
    all_to_all x1, waiting for transfers between devices: 7.87 us -> 24.9 us  [body(): received = lax.all_to_all(dense, ('row', 'col'), 0, 0)]
    all_to_all x0 -> x1, starting transfers between devices: none -> 3.72 us  [spread(): return lax.all_to_all(copies, axis, 0, 0, axis_index_groups=groups)]
    all_to_all x1, starting transfers between devices: 5.95 us -> 3.54 us  [body(): received = lax.all_to_all(dense, ('row', 'col'), 0, 0)]
    all_to_all x0 -> x1, waiting for transfers between devices: none -> 1.95 us  [spread(): return lax.all_to_all(copies, axis, 0, 0, axis_index_groups=groups)]
    broadcast_in_dim x0 -> x6, local copies, waits for them, and re-layouts: none -> 1.09 us  [spread(): copies = jnp.broadcast_to(x[None], (radix, *x.shape))]
  transfers between devices with their start and end apart: 22 -> 5, of which waited for: 17 -> 5; matrix products, arithmetic and copies ran while one was open for 0% -> 1% of each run, Pallas kernels for 4% -> 3%
where the time goes in v4:
time: 101 us; the launch traced here: 100 us
  blocking collectives  51.4 us (51%)
  waiting for transfers between devices  30.6 us (30%)
  starting transfers between devices  7.47 us (7%)
  Pallas kernels  5.42 us (5%)
  between operations  2.05 us (2%)
  local copies, waits for them, and re-layouts  1.69 us (2%)
  other arithmetic  1.51 us (1%)
    all_to_all x5, blocking collectives, spread(): return lax.all_to_all(copies, axis, 0, 0, axis_index_groups=groups)  51.4 us
    all_to_all x1, waiting for transfers between devices, body(): received = lax.all_to_all(dense, ('row', 'col'), 0, 0)  24.9 us
    ppermute x3, waiting for transfers between devices, swap(): lax.ppermute(x, axis, [(source, source ^ offset) for source in range(size)])  3.72 us
    all_to_all x1, starting transfers between devices, spread(): return lax.all_to_all(copies, axis, 0, 0, axis_index_groups=groups)  3.72 us
    all_to_all x1, starting transfers between devices, body(): received = lax.all_to_all(dense, ('row', 'col'), 0, 0)  3.54 us
    pallas_call x1, Pallas kernels, build_tile(): pl.pallas_call(kernel, grid_spec=pltpu.PrefetchScalarGridSpec(num_scalar_...  3.42 us
  transfers between devices with their start and end apart: 5, of which 5 were waited for; matrix products, arithmetic and copies ran while one was open for 1% of the time, Pallas kernels for 3%

profile of v4, /device:TPU:0, one launch (start us, length us, event | category | flops | bytes accessed | tf_op | source)
XLA Modules:
  0.0 100.1 jit_solution(15972775799439657883)
XLA Ops:
  0.0 0.8 convert_element_type.9
  0.9 12.2 %all_to_all.35 = bf16[4,128,128]{2,1,0:T(8,128)(2,1)S(1)} all-to-all(bf16[4,128,128]{2,1,0:T(8,128)(2,1)S(1)} %broadcast_in_dim.16), channel_id=1, replica_groups={{0,8,16,24},{2,10,18,26},{4,12,20,28},{6,14,22,30},{1,9,17,25},{3,11,19..., dimensions={0} | all-to-all | bytes 262144 | tf_op jit(solution)/shard_map/all_to_all | solution.py:44
  13.1 0.9 broadcast_in_dim.17
  14.0 3.7 %all-to-all-start.2 = ((bf16[4,512,128]{2,1,0:T(8,128)(2,1)}), bf16[4,512,128]{2,1,0:T(8,128)(2,1)S(1)}, u32[]{:S(2)}, u32[]{:S(2)}) async-start(bf16[4,512,128]{2,1,0:T(8,128)(2,1)} %broadcast_in_dim.17), calls=%async_computation.2 | async-start | bytes 1048576 | tf_op jit(solution)/shard_map/all_to_all | solution.py:44
  18.3 3.4 %build_tile.1.refs_0_ = bf16[32,128,128]{2,1,0:T(8,128)(2,1)} custom-call(s32[64]{0:T(128)} %bitcast.19, s32[64]{0:T(128)} %bitcast.20, s32[1]{0:T(128)} %bitcast.10.count_ref, bf16[64,128,128]{2,1,0:T(8,128)(2,1)} %bitcast.14), custom_call_target="tpu_custom_call" | custom-call | tf_op jit(solution)/shard_map/build_tile/pallas_call | solution.py:80
  21.8 0.6 slice.4.refs_1_
  22.3 0.0 copy-start.1
  22.4 0.0 copy-start
  22.4 1.9 %all-to-all-done.2 = bf16[4,512,128]{2,1,0:T(8,128)(2,1)S(1)} async-done(((bf16[4,512,128]{2,1,0:T(8,128)(2,1)}), bf16[4,512,128]{2,1,0:T(8,128)(2,1)S(1)}, u32[]{:S(2)}, u32[]{:S(2)}) %all-to-all-start.2) | async-done | bytes 524320 | tf_op jit(solution)/shard_map/all_to_all | solution.py:44
  24.3 3.5 %all-to-all-start.1 = ((bf16[32,128,128]{2,1,0:T(8,128)(2,1)}), bf16[32,128,128]{2,1,0:T(8,128)(2,1)S(1)}, u32[]{:S(2)}, u32[]{:S(2)}) async-start(bf16[32,128,128]{2,1,0:T(8,128)(2,1)} %after.1.dense_ref), calls=%async_computation.1 | async-start | bytes 2097152 | tf_op jit(solution)/shard_map/all_to_all | solution.py:195
  29.2 24.9 %all-to-all-done.1.received_ref = bf16[32,128,128]{2,1,0:T(8,128)(2,1)S(1)} async-done(((bf16[32,128,128]{2,1,0:T(8,128)(2,1)}), bf16[32,128,128]{2,1,0:T(8,128)(2,1)S(1)}, u32[]{:S(2)}, u32[]{:S(2)}) %all-to-all-start.1) | async-done | bytes 1048608 | tf_op jit(solution)/shard_map/all_to_all | solution.py:195
  54.1 0.0 copy-done.1
  54.1 0.0 copy-done
  54.1 1.1 %merge_apply.1 = (bf16[256,2048]{1,0:T(8,128)(2,1)S(1)}, f32[128,128]{1,0:T(8,128)S(1)}, f32[128,128]{1,0:T(8,128)S(1)}) custom-call(s32[2]{0:T(128)S(1)} %iota_xor_fusion.targets_ref, f32[1]{0:T(128)S(6)} %copy.11.center_ref, f32[1]{0:T(128)S(6)} %copy.12.halfwidth_ref, bf16[32,128,128]{2,1,0:T(8,128)(2,1)S(1)} %copy-done, ...), custom_call_target="tpu_custom_call" | custom-call | tf_op jit(solution)/shard_map/merge_apply/pallas_call | solution.py:146
  55.2 0.1 collective-permute-start
  55.3 1.2 %collective-permute-done = f32[128,128]{1,0:T(8,128)S(1)} collective-permute-done((f32[128,128]{1,0:T(8,128)S(1)}, f32[128,128]{1,0:T(8,128)S(1)}, u32[]{:S(2)}, u32[]{:S(2)}) %collective-permute-start) | collective-permute-done | bytes 65568 | tf_op jit(solution)/shard_map/ppermute | solution.py:48
  56.6 8.8 %all_to_all.36 = bf16[4,128,128]{2,1,0:T(8,128)(2,1)S(1)} all-to-all(bf16[4,128,128]{2,1,0:T(8,128)(2,1)S(1)} %broadcast_in_dim.18), channel_id=1, replica_groups={{0,8,16,24},{2,10,18,26},{4,12,20,28},{6,14,22,30},{1,9,17,25},{3,11,19..., dimensions={0} | all-to-all | bytes 262144 | tf_op jit(solution)/shard_map/all_to_all | solution.py:44
  65.4 0.1 broadcast_in_dim.20
  65.5 10.7 %all_to_all.37 = bf16[4,512,128]{2,1,0:T(8,128)(2,1)S(1)} all-to-all(bf16[4,512,128]{2,1,0:T(8,128)(2,1)S(1)} %broadcast_in_dim.20), channel_id=1, replica_groups={{0,2,4,6},{8,10,12,14},{16,18,20,22},{24,26,28,30},{1,3,5,7},{9,11,13,1..., dimensions={0} | all-to-all | bytes 1048576 | tf_op jit(solution)/shard_map/all_to_all | solution.py:44
  76.2 0.4 apply_tile.2
  76.6 0.1 collective-permute-start.1
  76.7 1.2 %collective-permute-done.1 = f32[128,128]{1,0:T(8,128)S(1)} collective-permute-done((f32[128,128]{1,0:T(8,128)S(1)}, f32[128,128]{1,0:T(8,128)S(1)}, u32[]{:S(2)}, u32[]{:S(2)}) %collective-permute-start.1) | collective-permute-done | bytes 65568 | tf_op jit(solution)/shard_map/ppermute | solution.py:48
  78.0 9.9 %all_to_all.38 = bf16[4,128,128]{2,1,0:T(8,128)(2,1)S(1)} all-to-all(bf16[4,128,128]{2,1,0:T(8,128)(2,1)S(1)} %broadcast_in_dim.42), channel_id=1, replica_groups={{0,8,16,24},{2,10,18,26},{4,12,20,28},{6,14,22,30},{1,9,17,25},{3,11,19..., dimensions={0} | all-to-all | bytes 262144 | tf_op jit(solution)/shard_map/all_to_all | solution.py:44
  87.9 0.1 broadcast_in_dim.44
  88.0 9.8 %all_to_all.39 = bf16[4,512,128]{2,1,0:T(8,128)(2,1)S(1)} all-to-all(bf16[4,512,128]{2,1,0:T(8,128)(2,1)S(1)} %broadcast_in_dim.44), channel_id=1, replica_groups={{0,2,4,6},{8,10,12,14},{16,18,20,22},{24,26,28,30},{1,3,5,7},{9,11,13,1..., dimensions={0} | all-to-all | bytes 1048576 | tf_op jit(solution)/shard_map/all_to_all | solution.py:44
  97.7 0.4 apply_tile.3
  98.2 0.1 collective-permute-start.2
  98.3 1.2 %collective-permute-done.2 = f32[128,128]{1,0:T(8,128)S(1)} collective-permute-done((f32[128,128]{1,0:T(8,128)S(1)}, f32[128,128]{1,0:T(8,128)S(1)}, u32[]{:S(2)}, u32[]{:S(2)}) %collective-permute-start.2) | collective-permute-done | bytes 65568 | tf_op jit(solution)/shard_map/ppermute | solution.py:48
  99.5 0.6 add.11
  (7 shorter events, 0.1 us)
Async XLA Ops:
  14.0 10.3 %all-to-all-start.2 = ((bf16[4,512,128]{2,1,0:T(8,128)(2,1)}), bf16[4,512,128]{2,1,0:T(8,128)(2,1)S(1)}, u32[]{:S(2)}, u32[]{:S(2)}) async-start(bf16[4,512,128]{2,1,0:T(8,128)(2,1)} %broadcast_in_dim.17), calls=%async_computation.2 | async-start | bytes 1048576 | tf_op jit(solution)/shard_map/all_to_all | solution.py:44
  22.3 31.7 %copy-start.1 = (f32[128,128]{1,0:T(8,128)S(1)}, f32[128,128]{1,0:T(8,128)}, u32[]{:S(2)}) copy-start(f32[128,128]{1,0:T(8,128)} %previous_ref.1) | copy-start | bytes 196612
  22.4 31.7 %copy-start = (bf16[32,128,128]{2,1,0:T(8,128)(2,1)S(1)}, bf16[32,128,128]{2,1,0:T(8,128)(2,1)}, u32[]{:S(2)}) copy-start(bf16[32,128,128]{2,1,0:T(8,128)(2,1)} %after.1.dense_ref) | copy-start | bytes 3145732
  24.3 29.8 %all-to-all-start.1 = ((bf16[32,128,128]{2,1,0:T(8,128)(2,1)}), bf16[32,128,128]{2,1,0:T(8,128)(2,1)S(1)}, u32[]{:S(2)}, u32[]{:S(2)}) async-start(bf16[32,128,128]{2,1,0:T(8,128)(2,1)} %after.1.dense_ref), calls=%async_computation.1 | async-start | bytes 2097152 | tf_op jit(solution)/shard_map/all_to_all | solution.py:195
  55.2 1.3 %collective-permute-start = (f32[128,128]{1,0:T(8,128)S(1)}, f32[128,128]{1,0:T(8,128)S(1)}, u32[]{:S(2)}, u32[]{:S(2)}) collective-permute-start(f32[128,128]{1,0:T(8,128)S(1)} %get-tuple-element.14), channel_id=1, source_target_pairs={{0,1},{1,0},{2,3},{3,2},{4,5},{5,4},{6,7},{7,6},{8,9},{9,8},{10,11... | collective-permute-start | bytes 196616 | tf_op jit(solution)/shard_map/ppermute | solution.py:48
  76.6 1.3 %collective-permute-start.1 = (f32[128,128]{1,0:T(8,128)S(1)}, f32[128,128]{1,0:T(8,128)S(1)}, u32[]{:S(2)}, u32[]{:S(2)}) collective-permute-start(f32[128,128]{1,0:T(8,128)S(1)} %get-tuple-element.16), channel_id=1, source_target_pairs={{0,1},{1,0},{2,3},{3,2},{4,5},{5,4},{6,7},{7,6},{8,9},{9,8},{10,11... | collective-permute-start | bytes 196616 | tf_op jit(solution)/shard_map/ppermute | solution.py:48
  98.2 1.3 %collective-permute-start.2 = (f32[128,128]{1,0:T(8,128)S(1)}, f32[128,128]{1,0:T(8,128)S(1)}, u32[]{:S(2)}, u32[]{:S(2)}) collective-permute-start(f32[128,128]{1,0:T(8,128)S(1)} %get-tuple-element.18), channel_id=1, source_target_pairs={{0,1},{1,0},{2,3},{3,2},{4,5},{5,4},{6,7},{7,6},{8,9},{9,8},{10,11... | collective-permute-start | bytes 196616 | tf_op jit(solution)/shard_map/ppermute | solution.py:48

commit v5 on v3

--- a/solution.py
+++ b/solution.py
@@ -36,6 +36,15 @@
 
 def swap(x, axis, size, offset):
     return lax.ppermute(x, axis, [(source, source ^ offset) for source in range(size)])
+
+
+def swap_rows(x, grid_rows, grid_cols, offsets):
+    pairs = [
+        (row * grid_cols + col, (row ^ offsets[col % 2]) * grid_cols + col)
+        for row in range(grid_rows)
+        for col in range(grid_cols)
+    ]
+    return lax.ppermute(x, ("row", "col"), pairs)
 
 
 def build_tile(rows, cols, count, stacked, grid_rows, grid_cols):
@@ -111,44 +120,42 @@
         outs[d][...] = total[d * orb : (d + 1) * orb] * scale
 
 
-def merge_apply(sources, targets, dense, received, pieces, current, center, halfwidth):
+def merge_apply(sources, places, targets, dense, received, panel, current, center, halfwidth):
     cells, orb, _ = dense.shape
     grid_rows = sources.shape[0]
     grid_cols = targets.shape[0]
     vectors = current.shape[1]
-    count = len(pieces)
-
-    def kernel(sources_ref, targets_ref, center_ref, halfwidth_ref, dense_ref, received_ref, current_ref, *refs):
-        piece_refs = refs[:count]
-        tile_ref, *outs = refs[count:]
+
+    def kernel(
+        sources_ref, places_ref, targets_ref, center_ref, halfwidth_ref,
+        dense_ref, received_ref, panel_ref, current_ref, tile_ref, *outs,
+    ):
         total = None
-        at = 0
-        for ref in piece_refs:
-            depth = ref.shape[0]
-            for k in range(at // orb, (at + depth) // orb):
-                first = sources_ref[k] * grid_cols
-                for d in range(grid_cols):
-                    cell = first + targets_ref[d]
-                    turned = received_ref[cell].T.astype(jnp.float32)
-                    block = (dense_ref[cell].astype(jnp.float32) + turned).astype(jnp.bfloat16)
-                    tile_ref[d * orb : (d + 1) * orb, k * orb : (k + 1) * orb] = block
+        for k in range(grid_rows):
+            held = slice(k * orb, (k + 1) * orb)
+            first = sources_ref[k] * grid_cols
+            for d in range(grid_cols):
+                cell = first + targets_ref[d]
+                turned = received_ref[cell].T.astype(jnp.float32)
+                block = (dense_ref[cell].astype(jnp.float32) + turned).astype(jnp.bfloat16)
+                tile_ref[d * orb : (d + 1) * orb, held] = block
+            place = pl.ds(pl.multiple_of(places_ref[k] * orb, orb), orb)
             part = jnp.dot(
-                tile_ref[:, at : at + depth], ref[...], preferred_element_type=jnp.float32
+                tile_ref[:, held], panel_ref[place, :], preferred_element_type=jnp.float32
             )
             total = part if total is None else total + part
-            at += depth
         finish(total, True, orb, current_ref, None, center_ref, halfwidth_ref, outs)
 
     block = jax.ShapeDtypeStruct((orb, vectors), jnp.float32)
     return pl.pallas_call(
         kernel,
-        in_specs=[SMEM] * 4 + [VMEM] * (3 + count),
+        in_specs=[SMEM] * 5 + [VMEM] * 4,
         out_specs=[VMEM] * (1 + grid_cols),
         out_shape=[jax.ShapeDtypeStruct((grid_cols * orb, grid_rows * orb), jnp.bfloat16)]
         + [block] * grid_cols,
         compiler_params=pltpu.CompilerParams(vmem_limit_bytes=dense.size * 6 + 2 * SPARE),
         name="merge_apply",
-    )(sources, targets, center, halfwidth, dense, received, current, *pieces)
+    )(sources, places, targets, center, halfwidth, dense, received, panel, current)
 
 
 def apply_tile(tile, pieces, current, previous, center, halfwidth, grid_cols):
@@ -183,34 +190,45 @@
     grid_rows = lax.axis_size("row")
     grid_cols = lax.axis_size("col")
     strides = stage_strides(grid_rows)
-
-    def stage(gathered, stride, radix):
-        return [gathered] + [swap(gathered, "row", grid_rows, k * stride) for k in range(1, radix)]
-
-    def gather(parts, stages):
-        for stride, radix in stages:
-            parts = stage(jnp.concatenate(parts, axis=0), stride, radix)
+    same = [strides, strides]
+    turned = [strides, strides[::-1]]
+    if [radix for _, radix in turned[0]] != [radix for _, radix in turned[1]]:
+        turned = same
+
+    def gather(parts, orders, first=0, last=None):
+        for (stride, radix), (odd_stride, _) in list(zip(*orders))[first:last]:
+            panel = jnp.concatenate(parts, axis=0)
+            parts = [panel] + [
+                swap_rows(panel, grid_rows, grid_cols, (k * stride, k * odd_stride))
+                for k in range(1, radix)
+            ]
         return parts
 
-    sources = jnp.array(arrival_order(strides), jnp.int32) ^ lax.axis_index("row")
-    targets = jnp.arange(grid_cols, dtype=jnp.int32) ^ lax.axis_index("col")
-    pieces = gather([initial.astype(jnp.bfloat16)], strides[:1])
+    row = lax.axis_index("row")
+    col = lax.axis_index("col")
+    early = arrival_order(strides)
+    late = [arrival_order(order) for order in turned]
+    places = [[early.index(offset) for offset in order] for order in late]
+    sources = jnp.array(late, jnp.int32)[col % 2] ^ row
+    places = jnp.array(places, jnp.int32)[col % 2]
+    targets = jnp.arange(grid_cols, dtype=jnp.int32) ^ col
+    pieces = gather([initial.astype(jnp.bfloat16)], same, last=1)
     dense = build_tile(
         block_rows[0, 0], block_cols[0, 0], block_counts[0], hamiltonian_blocks[0, 0],
         grid_rows, grid_cols,
     )
     dense = after(dense, pieces[1:])
     received = lax.all_to_all(dense, ("row", "col"), 0, 0)
-    pieces = gather(pieces, strides[1:])
+    panel = jnp.concatenate(gather(pieces, same, first=1), axis=0)
     tile, base, *others = merge_apply(
-        sources, targets, dense, received, pieces, initial, center, halfwidth
+        sources, places, targets, dense, received, panel, initial, center, halfwidth
     )
 
     previous = initial
     current = initial
     for degree_step in range(DEGREE):
         if degree_step > 0:
-            pieces = gather([current.astype(jnp.bfloat16)], strides)
+            pieces = gather([current.astype(jnp.bfloat16)], turned)
             base, *others = apply_tile(
                 tile, pieces, current, previous, center, halfwidth, grid_cols
             )

time: 82.2 us -> 80.1 us (0.974)
  waiting for transfers between devices: 40.9 us -> 38.5 us
    ppermute x21 -> x3, waiting for transfers between devices: 33 us -> 3.72 us  [swap(): lax.ppermute(x, axis, [(source, source ^ offset) for source in range(size)])]
    ppermute x0 -> x18, waiting for transfers between devices: none -> 27 us  [swap_rows(): return lax.ppermute(x, ('row', 'col'), pairs)]
    ppermute x0 -> x18, starting transfers between devices: none -> 25.3 us  [swap_rows(): return lax.ppermute(x, ('row', 'col'), pairs)]
    ppermute x21 -> x3, starting transfers between devices: 25.4 us -> 0.21 us  [swap(): lax.ppermute(x, axis, [(source, source ^ offset) for source in range(size)])]
    unnamed x0 -> x1, other arithmetic: none -> 0.85 us
    convert_element_type x3 -> x2, other arithmetic: 0.87 us -> 0.02 us  [body(): pieces = gather([current.astype(jnp.bfloat16)], turned)]
  transfers between devices with their start and end apart: 22 -> 22, of which waited for: 17 -> 18; matrix products, arithmetic and copies ran while one was open for 0% -> 0% of each run, Pallas kernels for 4% -> 4%
where the time goes in v5:
time: 80.1 us; the launch traced here: 79.8 us
  waiting for transfers between devices  38.5 us (48%)
  starting transfers between devices  31.5 us (39%)
  Pallas kernels  5.43 us (7%)
  other arithmetic  2.16 us (3%)
  between operations  2.15 us (3%)
    ppermute x18, waiting for transfers between devices, swap_rows(): return lax.ppermute(x, ('row', 'col'), pairs)  27 us
    ppermute x18, starting transfers between devices, swap_rows(): return lax.ppermute(x, ('row', 'col'), pairs)  25.3 us
    all_to_all x1, waiting for transfers between devices, body(): received = lax.all_to_all(dense, ('row', 'col'), 0, 0)  7.78 us
    all_to_all x1, starting transfers between devices, body(): received = lax.all_to_all(dense, ('row', 'col'), 0, 0)  5.94 us
    ppermute x3, waiting for transfers between devices, swap(): lax.ppermute(x, axis, [(source, source ^ offset) for source in range(size)])  3.72 us
    pallas_call x1, Pallas kernels, build_tile(): pl.pallas_call(kernel, grid_spec=pltpu.PrefetchScalarGridSpec(num_scalar_...  3.43 us
  transfers between devices with their start and end apart: 22, of which 18 were waited for; matrix products, arithmetic and copies ran while one was open for 0% of the time, Pallas kernels for 4%

profile of v5, /device:TPU:0, one launch (start us, length us, event | category | flops | bytes accessed | tf_op | source)
XLA Modules:
  0.0 79.8 jit_solution(16796171303570303532)
XLA Ops:
  0.0 0.8 %constant_dynamic-update-slice_fusion.6 = (bf16[2048,128]{1,0:T(8,128)(2,1)S(1)}, bf16[128,128]{1,0:T(8,128)(2,1)S(1)}) fusion(f32[128,128]{1,0:T(8,128)} %previous_ref.1), kind=kLoop, calls=%fused_computation.9 | loop fusion | flops 16383 | bytes 131072
  0.9 5.1 %collective-permute-start.2 = (bf16[128,128]{1,0:T(8,128)(2,1)S(1)}, bf16[128,128]{1,0:T(8,128)(2,1)S(1)}, u32[]{:S(2)}, u32[]{:S(2)}) collective-permute-start(bf16[128,128]{1,0:T(8,128)(2,1)S(1)} %get-tuple-element.24), channel_id=1, source_target_pairs={{0,24},{1,25},{2,26},{3,27},{4,28},{5,29},{6,30},{7,31},{8,16},{9,... | collective-permute-start | bytes 98312 | tf_op jit(solution)/shard_map/ppermute | solution.py:47
  6.0 0.0 collective-permute-start.1
  6.0 0.6 collective-permute-start
  7.3 3.4 %build_tile.1.refs_0_ = bf16[32,128,128]{2,1,0:T(8,128)(2,1)} custom-call(s32[64]{0:T(128)} %bitcast.10, s32[64]{0:T(128)} %bitcast.11, s32[1]{0:T(128)} %bitcast.8.count_ref, bf16[64,128,128]{2,1,0:T(8,128)(2,1)} %bitcast.9), custom_call_target="tpu_custom_call" | custom-call | tf_op jit(solution)/shard_map/build_tile/pallas_call | solution.py:79
  10.7 0.1 collective-permute-done.1
  10.8 0.6 slice_add_fusion.refs_1_
  11.4 5.9 %all-to-all-start = ((bf16[32,128,128]{2,1,0:T(8,128)(2,1)}), bf16[32,128,128]{2,1,0:T(8,128)(2,1)S(1)}, u32[]{:S(2)}, u32[]{:S(2)}) async-start(bf16[32,128,128]{2,1,0:T(8,128)(2,1)} %after.1.dense_ref), calls=%async_computation | async-start | bytes 2097152 | tf_op jit(solution)/shard_map/all_to_all | solution.py:221
  18.7 2.7 %collective-permute-start.5 = (bf16[512,128]{1,0:T(8,128)(2,1)S(1)}, bf16[512,128]{1,0:T(8,128)(2,1)S(1)}, u32[]{:S(2)}, u32[]{:S(2)}) collective-permute-start(bf16[512,128]{1,0:T(8,128)(2,1)S(1)} %pad_maximum_fusion), channel_id=1, source_target_pairs={{0,6},{1,7},{2,4},{3,5},{4,2},{5,3},{6,0},{7,1},{8,14},{9,15},{10,... | collective-permute-start | bytes 393224 | tf_op jit(solution)/shard_map/ppermute | solution.py:47
  21.5 0.6 collective-permute-start.4
  22.0 0.3 collective-permute-start.3
  22.3 13.4 %collective-permute-done.3 = bf16[512,128]{1,0:T(8,128)(2,1)S(1)} collective-permute-done((bf16[512,128]{1,0:T(8,128)(2,1)S(1)}, bf16[512,128]{1,0:T(8,128)(2,1)S(1)}, u32[]{:S(2)}, u32[]{:S(2)}) %collective-permute-start.3) | collective-permute-done | bytes 131104 | tf_op jit(solution)/shard_map/ppermute | solution.py:47
  35.8 0.0 collective-permute-done.5
  35.8 7.8 %all-to-all-done.received_ref = bf16[32,128,128]{2,1,0:T(8,128)(2,1)S(1)} async-done(((bf16[32,128,128]{2,1,0:T(8,128)(2,1)}), bf16[32,128,128]{2,1,0:T(8,128)(2,1)S(1)}, u32[]{:S(2)}, u32[]{:S(2)}) %all-to-all-start) | async-done | bytes 1048608 | tf_op jit(solution)/shard_map/all_to_all | solution.py:221
  43.6 1.2 %merge_apply.1 = (bf16[256,2048]{1,0:T(8,128)(2,1)S(1)}, f32[128,128]{1,0:T(8,128)S(1)}, f32[128,128]{1,0:T(8,128)S(1)}) custom-call(s32[16]{0:T(128)S(1)} %get-tuple-element.26.sources_ref, s32[16]{0:T(128)S(1)} %get-tuple-element.25.places_ref, s32[2]{0:T(128)S(1)} %iota_xor_fusion.targets_ref, f32[1]{0:T(128)S(6)} %copy.19.center_ref, ...), custom_call_target="tpu_custom_call" | custom-call | tf_op jit(solution)/shard_map/merge_apply/pallas_call | solution.py:150
  44.8 0.1 collective-permute-start.6
  44.8 1.2 %collective-permute-done.6 = f32[128,128]{1,0:T(8,128)S(1)} collective-permute-done((f32[128,128]{1,0:T(8,128)S(1)}, f32[128,128]{1,0:T(8,128)S(1)}, u32[]{:S(2)}, u32[]{:S(2)}) %collective-permute-start.6) | collective-permute-done | bytes 65568 | tf_op jit(solution)/shard_map/ppermute | solution.py:38
  46.1 1.4 %collective-permute-start.9 = (bf16[128,128]{1,0:T(8,128)(2,1)S(1)}, bf16[128,128]{1,0:T(8,128)(2,1)S(1)}, u32[]{:S(2)}, u32[]{:S(2)}) collective-permute-start(bf16[128,128]{1,0:T(8,128)(2,1)S(1)} %get-tuple-element.21), channel_id=1, source_target_pairs={{0,24},{1,7},{2,26},{3,5},{4,28},{5,3},{6,30},{7,1},{8,16},{9,15},... | collective-permute-start | bytes 98312 | tf_op jit(solution)/shard_map/ppermute | solution.py:47
  47.4 0.9 %collective-permute-start.8 = (bf16[128,128]{1,0:T(8,128)(2,1)S(1)}, bf16[128,128]{1,0:T(8,128)(2,1)S(1)}, u32[]{:S(2)}, u32[]{:S(2)}) collective-permute-start(bf16[128,128]{1,0:T(8,128)(2,1)S(1)} %get-tuple-element.21), channel_id=1, source_target_pairs={{0,16},{1,5},{2,18},{3,7},{4,20},{5,1},{6,22},{7,3},{8,24},{9,13},... | collective-permute-start | bytes 98312 | tf_op jit(solution)/shard_map/ppermute | solution.py:47
  48.4 2.2 %collective-permute-start.7 = (bf16[128,128]{1,0:T(8,128)(2,1)S(1)}, bf16[128,128]{1,0:T(8,128)(2,1)S(1)}, u32[]{:S(2)}, u32[]{:S(2)}) collective-permute-start(bf16[128,128]{1,0:T(8,128)(2,1)S(1)} %get-tuple-element.21), channel_id=1, source_target_pairs={{0,8},{1,3},{2,10},{3,1},{4,12},{5,7},{6,14},{7,5},{8,0},{9,11},{1... | collective-permute-start | bytes 98312 | tf_op jit(solution)/shard_map/ppermute | solution.py:47
  50.5 1.3 %collective-permute-done.9 = bf16[128,128]{1,0:T(8,128)(2,1)S(1)} collective-permute-done((bf16[128,128]{1,0:T(8,128)(2,1)S(1)}, bf16[128,128]{1,0:T(8,128)(2,1)S(1)}, u32[]{:S(2)}, u32[]{:S(2)}) %collective-permute-start.9) | collective-permute-done | bytes 32800 | tf_op jit(solution)/shard_map/ppermute | solution.py:47
  51.9 0.8 %collective-permute-done.8 = bf16[128,128]{1,0:T(8,128)(2,1)S(1)} collective-permute-done((bf16[128,128]{1,0:T(8,128)(2,1)S(1)}, bf16[128,128]{1,0:T(8,128)(2,1)S(1)}, u32[]{:S(2)}, u32[]{:S(2)}) %collective-permute-start.8) | collective-permute-done | bytes 32800 | tf_op jit(solution)/shard_map/ppermute | solution.py:47
  52.7 0.1 collective-permute-done.7
  52.8 2.5 %collective-permute-start.12 = (bf16[512,128]{1,0:T(8,128)(2,1)S(1)}, bf16[512,128]{1,0:T(8,128)(2,1)S(1)}, u32[]{:S(2)}, u32[]{:S(2)}) collective-permute-start(bf16[512,128]{1,0:T(8,128)(2,1)S(1)} %pad_maximum_fusion.1.refs_0_), channel_id=1, source_target_pairs={{0,6},{1,25},{2,4},{3,27},{4,2},{5,29},{6,0},{7,31},{8,14},{9,17},... | collective-permute-start | bytes 393224 | tf_op jit(solution)/shard_map/ppermute | solution.py:47
  55.3 0.5 collective-permute-start.11
  55.8 0.5 collective-permute-start.10
  56.3 2.4 %collective-permute-done.12.refs_3_ = bf16[512,128]{1,0:T(8,128)(2,1)S(1)} collective-permute-done((bf16[512,128]{1,0:T(8,128)(2,1)S(1)}, bf16[512,128]{1,0:T(8,128)(2,1)S(1)}, u32[]{:S(2)}, u32[]{:S(2)}) %collective-permute-start.12) | collective-permute-done | bytes 131104 | tf_op jit(solution)/shard_map/ppermute | solution.py:47
  58.7 1.5 %collective-permute-done.11.refs_2_ = bf16[512,128]{1,0:T(8,128)(2,1)S(1)} collective-permute-done((bf16[512,128]{1,0:T(8,128)(2,1)S(1)}, bf16[512,128]{1,0:T(8,128)(2,1)S(1)}, u32[]{:S(2)}, u32[]{:S(2)}) %collective-permute-start.11) | collective-permute-done | bytes 131104 | tf_op jit(solution)/shard_map/ppermute | solution.py:47
  60.2 0.5 collective-permute-done.10.refs_1_
  60.8 0.4 apply_tile.2
  61.2 0.1 collective-permute-start.13
  61.3 1.2 %collective-permute-done.13 = f32[128,128]{1,0:T(8,128)S(1)} collective-permute-done((f32[128,128]{1,0:T(8,128)S(1)}, f32[128,128]{1,0:T(8,128)S(1)}, u32[]{:S(2)}, u32[]{:S(2)}) %collective-permute-start.13) | collective-permute-done | bytes 65568 | tf_op jit(solution)/shard_map/ppermute | solution.py:38
  62.5 2.1 %collective-permute-start.16 = (bf16[128,128]{1,0:T(8,128)(2,1)S(1)}, bf16[128,128]{1,0:T(8,128)(2,1)S(1)}, u32[]{:S(2)}, u32[]{:S(2)}) collective-permute-start(bf16[128,128]{1,0:T(8,128)(2,1)S(1)} %get-tuple-element.19), channel_id=1, source_target_pairs={{0,24},{1,7},{2,26},{3,5},{4,28},{5,3},{6,30},{7,1},{8,16},{9,15},... | collective-permute-start | bytes 98312 | tf_op jit(solution)/shard_map/ppermute | solution.py:47
  64.6 1.1 %collective-permute-start.15 = (bf16[128,128]{1,0:T(8,128)(2,1)S(1)}, bf16[128,128]{1,0:T(8,128)(2,1)S(1)}, u32[]{:S(2)}, u32[]{:S(2)}) collective-permute-start(bf16[128,128]{1,0:T(8,128)(2,1)S(1)} %get-tuple-element.19), channel_id=1, source_target_pairs={{0,16},{1,5},{2,18},{3,7},{4,20},{5,1},{6,22},{7,3},{8,24},{9,13},... | collective-permute-start | bytes 98312 | tf_op jit(solution)/shard_map/ppermute | solution.py:47
  65.7 1.3 %collective-permute-start.14 = (bf16[128,128]{1,0:T(8,128)(2,1)S(1)}, bf16[128,128]{1,0:T(8,128)(2,1)S(1)}, u32[]{:S(2)}, u32[]{:S(2)}) collective-permute-start(bf16[128,128]{1,0:T(8,128)(2,1)S(1)} %get-tuple-element.19), channel_id=1, source_target_pairs={{0,8},{1,3},{2,10},{3,1},{4,12},{5,7},{6,14},{7,5},{8,0},{9,11},{1... | collective-permute-start | bytes 98312 | tf_op jit(solution)/shard_map/ppermute | solution.py:47
  67.0 1.3 %collective-permute-done.16 = bf16[128,128]{1,0:T(8,128)(2,1)S(1)} collective-permute-done((bf16[128,128]{1,0:T(8,128)(2,1)S(1)}, bf16[128,128]{1,0:T(8,128)(2,1)S(1)}, u32[]{:S(2)}, u32[]{:S(2)}) %collective-permute-start.16) | collective-permute-done | bytes 32800 | tf_op jit(solution)/shard_map/ppermute | solution.py:47
  68.3 1.1 %collective-permute-done.15 = bf16[128,128]{1,0:T(8,128)(2,1)S(1)} collective-permute-done((bf16[128,128]{1,0:T(8,128)(2,1)S(1)}, bf16[128,128]{1,0:T(8,128)(2,1)S(1)}, u32[]{:S(2)}, u32[]{:S(2)}) %collective-permute-start.15) | collective-permute-done | bytes 32800 | tf_op jit(solution)/shard_map/ppermute | solution.py:47
  69.4 0.3 collective-permute-done.14
  69.8 1.6 %collective-permute-start.19 = (bf16[512,128]{1,0:T(8,128)(2,1)S(1)}, bf16[512,128]{1,0:T(8,128)(2,1)S(1)}, u32[]{:S(2)}, u32[]{:S(2)}) collective-permute-start(bf16[512,128]{1,0:T(8,128)(2,1)S(1)} %pad_maximum_fusion.2.refs_0_), channel_id=1, source_target_pairs={{0,6},{1,25},{2,4},{3,27},{4,2},{5,29},{6,0},{7,31},{8,14},{9,17},... | collective-permute-start | bytes 393224 | tf_op jit(solution)/shard_map/ppermute | solution.py:47
  71.4 1.0 %collective-permute-start.18 = (bf16[512,128]{1,0:T(8,128)(2,1)S(1)}, bf16[512,128]{1,0:T(8,128)(2,1)S(1)}, u32[]{:S(2)}, u32[]{:S(2)}) collective-permute-start(bf16[512,128]{1,0:T(8,128)(2,1)S(1)} %pad_maximum_fusion.2.refs_0_), channel_id=1, source_target_pairs={{0,4},{1,17},{2,6},{3,19},{4,0},{5,21},{6,2},{7,23},{8,12},{9,25},... | collective-permute-start | bytes 393224 | tf_op jit(solution)/shard_map/ppermute | solution.py:47
  72.4 0.9 %collective-permute-start.17 = (bf16[512,128]{1,0:T(8,128)(2,1)S(1)}, bf16[512,128]{1,0:T(8,128)(2,1)S(1)}, u32[]{:S(2)}, u32[]{:S(2)}) collective-permute-start(bf16[512,128]{1,0:T(8,128)(2,1)S(1)} %pad_maximum_fusion.2.refs_0_), channel_id=1, source_target_pairs={{0,2},{1,9},{2,0},{3,11},{4,6},{5,13},{6,4},{7,15},{8,10},{9,1},{1... | collective-permute-start | bytes 393224 | tf_op jit(solution)/shard_map/ppermute | solution.py:47
  73.3 2.5 %collective-permute-done.19.refs_3_ = bf16[512,128]{1,0:T(8,128)(2,1)S(1)} collective-permute-done((bf16[512,128]{1,0:T(8,128)(2,1)S(1)}, bf16[512,128]{1,0:T(8,128)(2,1)S(1)}, u32[]{:S(2)}, u32[]{:S(2)}) %collective-permute-start.19) | collective-permute-done | bytes 131104 | tf_op jit(solution)/shard_map/ppermute | solution.py:47
  75.8 1.3 %collective-permute-done.18.refs_2_ = bf16[512,128]{1,0:T(8,128)(2,1)S(1)} collective-permute-done((bf16[512,128]{1,0:T(8,128)(2,1)S(1)}, bf16[512,128]{1,0:T(8,128)(2,1)S(1)}, u32[]{:S(2)}, u32[]{:S(2)}) %collective-permute-start.18) | collective-permute-done | bytes 131104 | tf_op jit(solution)/shard_map/ppermute | solution.py:47
  77.1 0.3 collective-permute-done.17.refs_1_
  77.4 0.4 apply_tile.3
  77.8 0.1 collective-permute-start.20
  77.9 1.2 %collective-permute-done.20 = f32[128,128]{1,0:T(8,128)S(1)} collective-permute-done((f32[128,128]{1,0:T(8,128)S(1)}, f32[128,128]{1,0:T(8,128)S(1)}, u32[]{:S(2)}, u32[]{:S(2)}) %collective-permute-start.20) | collective-permute-done | bytes 65568 | tf_op jit(solution)/shard_map/ppermute | solution.py:38
  79.2 0.6 add.30
  (25 shorter events, 0.2 us)
Async XLA Ops:
  0.9 9.8 %collective-permute-start.2 = (bf16[128,128]{1,0:T(8,128)(2,1)S(1)}, bf16[128,128]{1,0:T(8,128)(2,1)S(1)}, u32[]{:S(2)}, u32[]{:S(2)}) collective-permute-start(bf16[128,128]{1,0:T(8,128)(2,1)S(1)} %get-tuple-element.24), channel_id=1, source_target_pairs={{0,24},{1,25},{2,26},{3,27},{4,28},{5,29},{6,30},{7,31},{8,16},{9,... | collective-permute-start | bytes 98312 | tf_op jit(solution)/shard_map/ppermute | solution.py:47
  6.0 4.8 %collective-permute-start.1 = (bf16[128,128]{1,0:T(8,128)(2,1)S(1)}, bf16[128,128]{1,0:T(8,128)(2,1)S(1)}, u32[]{:S(2)}, u32[]{:S(2)}) collective-permute-start(bf16[128,128]{1,0:T(8,128)(2,1)S(1)} %get-tuple-element.24), channel_id=1, source_target_pairs={{0,16},{1,17},{2,18},{3,19},{4,20},{5,21},{6,22},{7,23},{8,24},{9,... | collective-permute-start | bytes 98312 | tf_op jit(solution)/shard_map/ppermute | solution.py:47
  6.0 4.8 %collective-permute-start = (bf16[128,128]{1,0:T(8,128)(2,1)S(1)}, bf16[128,128]{1,0:T(8,128)(2,1)S(1)}, u32[]{:S(2)}, u32[]{:S(2)}) collective-permute-start(bf16[128,128]{1,0:T(8,128)(2,1)S(1)} %get-tuple-element.24), channel_id=1, source_target_pairs={{0,8},{1,9},{2,10},{3,11},{4,12},{5,13},{6,14},{7,15},{8,0},{9,1},... | collective-permute-start | bytes 98312 | tf_op jit(solution)/shard_map/ppermute | solution.py:47
  11.4 7.3 %copy-start.2 = (s32[2,16]{1,0:T(2,128)S(1)}, s32[2,16]{1,0:T(2,128)}, u32[]{:S(2)}) copy-start(s32[2,16]{1,0:T(2,128)} %constant.29.clone) | copy-start | bytes 388
  11.4 7.3 %copy-start.3 = (s32[2,16]{1,0:T(2,128)S(1)}, s32[2,16]{1,0:T(2,128)}, u32[]{:S(2)}) copy-start(s32[2,16]{1,0:T(2,128)} %constant.28.clone) | copy-start | bytes 388
  11.4 32.2 %copy-start = (bf16[32,128,128]{2,1,0:T(8,128)(2,1)S(1)}, bf16[32,128,128]{2,1,0:T(8,128)(2,1)}, u32[]{:S(2)}) copy-start(bf16[32,128,128]{2,1,0:T(8,128)(2,1)} %after.1.dense_ref) | copy-start | bytes 3145732
  11.4 32.2 %copy-start.1 = (f32[128,128]{1,0:T(8,128)S(1)}, f32[128,128]{1,0:T(8,128)}, u32[]{:S(2)}) copy-start(f32[128,128]{1,0:T(8,128)} %previous_ref.1) | copy-start | bytes 196612
  11.4 32.2 %all-to-all-start = ((bf16[32,128,128]{2,1,0:T(8,128)(2,1)}), bf16[32,128,128]{2,1,0:T(8,128)(2,1)S(1)}, u32[]{:S(2)}, u32[]{:S(2)}) async-start(bf16[32,128,128]{2,1,0:T(8,128)(2,1)} %after.1.dense_ref), calls=%async_computation | async-start | bytes 2097152 | tf_op jit(solution)/shard_map/all_to_all | solution.py:221
  18.7 17.0 %collective-permute-start.5 = (bf16[512,128]{1,0:T(8,128)(2,1)S(1)}, bf16[512,128]{1,0:T(8,128)(2,1)S(1)}, u32[]{:S(2)}, u32[]{:S(2)}) collective-permute-start(bf16[512,128]{1,0:T(8,128)(2,1)S(1)} %pad_maximum_fusion), channel_id=1, source_target_pairs={{0,6},{1,7},{2,4},{3,5},{4,2},{5,3},{6,0},{7,1},{8,14},{9,15},{10,... | collective-permute-start | bytes 393224 | tf_op jit(solution)/shard_map/ppermute | solution.py:47
  21.5 14.3 %collective-permute-start.4 = (bf16[512,128]{1,0:T(8,128)(2,1)S(1)}, bf16[512,128]{1,0:T(8,128)(2,1)S(1)}, u32[]{:S(2)}, u32[]{:S(2)}) collective-permute-start(bf16[512,128]{1,0:T(8,128)(2,1)S(1)} %pad_maximum_fusion), channel_id=1, source_target_pairs={{0,4},{1,5},{2,6},{3,7},{4,0},{5,1},{6,2},{7,3},{8,12},{9,13},{10,... | collective-permute-start | bytes 393224 | tf_op jit(solution)/shard_map/ppermute | solution.py:47
  22.0 13.7 %collective-permute-start.3 = (bf16[512,128]{1,0:T(8,128)(2,1)S(1)}, bf16[512,128]{1,0:T(8,128)(2,1)S(1)}, u32[]{:S(2)}, u32[]{:S(2)}) collective-permute-start(bf16[512,128]{1,0:T(8,128)(2,1)S(1)} %pad_maximum_fusion), channel_id=1, source_target_pairs={{0,2},{1,3},{2,0},{3,1},{4,6},{5,7},{6,4},{7,5},{8,10},{9,11},{10,... | collective-permute-start | bytes 393224 | tf_op jit(solution)/shard_map/ppermute | solution.py:47
  44.8 1.3 %collective-permute-start.6 = (f32[128,128]{1,0:T(8,128)S(1)}, f32[128,128]{1,0:T(8,128)S(1)}, u32[]{:S(2)}, u32[]{:S(2)}) collective-permute-start(f32[128,128]{1,0:T(8,128)S(1)} %get-tuple-element.14), channel_id=1, source_target_pairs={{0,1},{1,0},{2,3},{3,2},{4,5},{5,4},{6,7},{7,6},{8,9},{9,8},{10,11... | collective-permute-start | bytes 196616 | tf_op jit(solution)/shard_map/ppermute | solution.py:38
  46.1 5.8 %collective-permute-start.9 = (bf16[128,128]{1,0:T(8,128)(2,1)S(1)}, bf16[128,128]{1,0:T(8,128)(2,1)S(1)}, u32[]{:S(2)}, u32[]{:S(2)}) collective-permute-start(bf16[128,128]{1,0:T(8,128)(2,1)S(1)} %get-tuple-element.21), channel_id=1, source_target_pairs={{0,24},{1,7},{2,26},{3,5},{4,28},{5,3},{6,30},{7,1},{8,16},{9,15},... | collective-permute-start | bytes 98312 | tf_op jit(solution)/shard_map/ppermute | solution.py:47
  47.4 5.2 %collective-permute-start.8 = (bf16[128,128]{1,0:T(8,128)(2,1)S(1)}, bf16[128,128]{1,0:T(8,128)(2,1)S(1)}, u32[]{:S(2)}, u32[]{:S(2)}) collective-permute-start(bf16[128,128]{1,0:T(8,128)(2,1)S(1)} %get-tuple-element.21), channel_id=1, source_target_pairs={{0,16},{1,5},{2,18},{3,7},{4,20},{5,1},{6,22},{7,3},{8,24},{9,13},... | collective-permute-start | bytes 98312 | tf_op jit(solution)/shard_map/ppermute | solution.py:47
  48.4 4.4 %collective-permute-start.7 = (bf16[128,128]{1,0:T(8,128)(2,1)S(1)}, bf16[128,128]{1,0:T(8,128)(2,1)S(1)}, u32[]{:S(2)}, u32[]{:S(2)}) collective-permute-start(bf16[128,128]{1,0:T(8,128)(2,1)S(1)} %get-tuple-element.21), channel_id=1, source_target_pairs={{0,8},{1,3},{2,10},{3,1},{4,12},{5,7},{6,14},{7,5},{8,0},{9,11},{1... | collective-permute-start | bytes 98312 | tf_op jit(solution)/shard_map/ppermute | solution.py:47
  52.8 5.9 %collective-permute-start.12 = (bf16[512,128]{1,0:T(8,128)(2,1)S(1)}, bf16[512,128]{1,0:T(8,128)(2,1)S(1)}, u32[]{:S(2)}, u32[]{:S(2)}) collective-permute-start(bf16[512,128]{1,0:T(8,128)(2,1)S(1)} %pad_maximum_fusion.1.refs_0_), channel_id=1, source_target_pairs={{0,6},{1,25},{2,4},{3,27},{4,2},{5,29},{6,0},{7,31},{8,14},{9,17},... | collective-permute-start | bytes 393224 | tf_op jit(solution)/shard_map/ppermute | solution.py:47
  55.3 5.0 %collective-permute-start.11 = (bf16[512,128]{1,0:T(8,128)(2,1)S(1)}, bf16[512,128]{1,0:T(8,128)(2,1)S(1)}, u32[]{:S(2)}, u32[]{:S(2)}) collective-permute-start(bf16[512,128]{1,0:T(8,128)(2,1)S(1)} %pad_maximum_fusion.1.refs_0_), channel_id=1, source_target_pairs={{0,4},{1,17},{2,6},{3,19},{4,0},{5,21},{6,2},{7,23},{8,12},{9,25},... | collective-permute-start | bytes 393224 | tf_op jit(solution)/shard_map/ppermute | solution.py:47
  55.8 5.0 %collective-permute-start.10 = (bf16[512,128]{1,0:T(8,128)(2,1)S(1)}, bf16[512,128]{1,0:T(8,128)(2,1)S(1)}, u32[]{:S(2)}, u32[]{:S(2)}) collective-permute-start(bf16[512,128]{1,0:T(8,128)(2,1)S(1)} %pad_maximum_fusion.1.refs_0_), channel_id=1, source_target_pairs={{0,2},{1,9},{2,0},{3,11},{4,6},{5,13},{6,4},{7,15},{8,10},{9,1},{1... | collective-permute-start | bytes 393224 | tf_op jit(solution)/shard_map/ppermute | solution.py:47
  61.2 1.3 %collective-permute-start.13 = (f32[128,128]{1,0:T(8,128)S(1)}, f32[128,128]{1,0:T(8,128)S(1)}, u32[]{:S(2)}, u32[]{:S(2)}) collective-permute-start(f32[128,128]{1,0:T(8,128)S(1)} %get-tuple-element.16), channel_id=1, source_target_pairs={{0,1},{1,0},{2,3},{3,2},{4,5},{5,4},{6,7},{7,6},{8,9},{9,8},{10,11... | collective-permute-start | bytes 196616 | tf_op jit(solution)/shard_map/ppermute | solution.py:38
  62.5 5.8 %collective-permute-start.16 = (bf16[128,128]{1,0:T(8,128)(2,1)S(1)}, bf16[128,128]{1,0:T(8,128)(2,1)S(1)}, u32[]{:S(2)}, u32[]{:S(2)}) collective-permute-start(bf16[128,128]{1,0:T(8,128)(2,1)S(1)} %get-tuple-element.19), channel_id=1, source_target_pairs={{0,24},{1,7},{2,26},{3,5},{4,28},{5,3},{6,30},{7,1},{8,16},{9,15},... | collective-permute-start | bytes 98312 | tf_op jit(solution)/shard_map/ppermute | solution.py:47
  64.6 4.8 %collective-permute-start.15 = (bf16[128,128]{1,0:T(8,128)(2,1)S(1)}, bf16[128,128]{1,0:T(8,128)(2,1)S(1)}, u32[]{:S(2)}, u32[]{:S(2)}) collective-permute-start(bf16[128,128]{1,0:T(8,128)(2,1)S(1)} %get-tuple-element.19), channel_id=1, source_target_pairs={{0,16},{1,5},{2,18},{3,7},{4,20},{5,1},{6,22},{7,3},{8,24},{9,13},... | collective-permute-start | bytes 98312 | tf_op jit(solution)/shard_map/ppermute | solution.py:47
  65.7 4.0 %collective-permute-start.14 = (bf16[128,128]{1,0:T(8,128)(2,1)S(1)}, bf16[128,128]{1,0:T(8,128)(2,1)S(1)}, u32[]{:S(2)}, u32[]{:S(2)}) collective-permute-start(bf16[128,128]{1,0:T(8,128)(2,1)S(1)} %get-tuple-element.19), channel_id=1, source_target_pairs={{0,8},{1,3},{2,10},{3,1},{4,12},{5,7},{6,14},{7,5},{8,0},{9,11},{1... | collective-permute-start | bytes 98312 | tf_op jit(solution)/shard_map/ppermute | solution.py:47
  69.8 6.0 %collective-permute-start.19 = (bf16[512,128]{1,0:T(8,128)(2,1)S(1)}, bf16[512,128]{1,0:T(8,128)(2,1)S(1)}, u32[]{:S(2)}, u32[]{:S(2)}) collective-permute-start(bf16[512,128]{1,0:T(8,128)(2,1)S(1)} %pad_maximum_fusion.2.refs_0_), channel_id=1, source_target_pairs={{0,6},{1,25},{2,4},{3,27},{4,2},{5,29},{6,0},{7,31},{8,14},{9,17},... | collective-permute-start | bytes 393224 | tf_op jit(solution)/shard_map/ppermute | solution.py:47
  71.4 5.7 %collective-permute-start.18 = (bf16[512,128]{1,0:T(8,128)(2,1)S(1)}, bf16[512,128]{1,0:T(8,128)(2,1)S(1)}, u32[]{:S(2)}, u32[]{:S(2)}) collective-permute-start(bf16[512,128]{1,0:T(8,128)(2,1)S(1)} %pad_maximum_fusion.2.refs_0_), channel_id=1, source_target_pairs={{0,4},{1,17},{2,6},{3,19},{4,0},{5,21},{6,2},{7,23},{8,12},{9,25},... | collective-permute-start | bytes 393224 | tf_op jit(solution)/shard_map/ppermute | solution.py:47
  72.4 5.0 %collective-permute-start.17 = (bf16[512,128]{1,0:T(8,128)(2,1)S(1)}, bf16[512,128]{1,0:T(8,128)(2,1)S(1)}, u32[]{:S(2)}, u32[]{:S(2)}) collective-permute-start(bf16[512,128]{1,0:T(8,128)(2,1)S(1)} %pad_maximum_fusion.2.refs_0_), channel_id=1, source_target_pairs={{0,2},{1,9},{2,0},{3,11},{4,6},{5,13},{6,4},{7,15},{8,10},{9,1},{1... | collective-permute-start | bytes 393224 | tf_op jit(solution)/shard_map/ppermute | solution.py:47
  77.8 1.3 %collective-permute-start.20 = (f32[128,128]{1,0:T(8,128)S(1)}, f32[128,128]{1,0:T(8,128)S(1)}, u32[]{:S(2)}, u32[]{:S(2)}) collective-permute-start(f32[128,128]{1,0:T(8,128)S(1)} %get-tuple-element.18), channel_id=1, source_target_pairs={{0,1},{1,0},{2,3},{3,2},{4,5},{5,4},{6,7},{7,6},{8,9},{9,8},{10,11... | collective-permute-start | bytes 196616 | tf_op jit(solution)/shard_map/ppermute | solution.py:38

commit v6 on v5

--- a/solution.py
+++ b/solution.py
@@ -6,7 +6,6 @@
 from jax.sharding import PartitionSpec as P
 
 DEGREE = 3
-RADIX = 4
 CHUNK = 8
 SPARE = 4 * 2**20
 BUILD_VMEM = 62 * 2**20
@@ -17,14 +16,13 @@
 HBM = pl.BlockSpec(memory_space=pltpu.HBM)
 
 
-def stage_strides(size):
+def stage_strides(bits, radices):
     found = []
-    stride = 1
-    while stride < size:
-        radix = RADIX if size % (stride * RADIX) == 0 else size // stride
-        found.append((stride, radix))
-        stride *= radix
-    return found[::-1]
+    for radix in radices:
+        width = radix.bit_length() - 1
+        found.append((1 << min(bits[:width]), radix))
+        bits = bits[width:]
+    return found
 
 
 def arrival_order(strides):
@@ -62,7 +60,7 @@
         ]
         for copy in copies:
             copy.start()
-        count = count_ref[0]
+        count = count_ref[0, 0]
         acc_ref[...] = jnp.zeros_like(acc_ref)
         for n, copy in enumerate(copies):
             copy.wait()
@@ -189,11 +187,11 @@
 def body(hamiltonian_blocks, block_rows, block_cols, block_counts, initial, center, halfwidth):
     grid_rows = lax.axis_size("row")
     grid_cols = lax.axis_size("col")
-    strides = stage_strides(grid_rows)
-    same = [strides, strides]
-    turned = [strides, strides[::-1]]
-    if [radix for _, radix in turned[0]] != [radix for _, radix in turned[1]]:
-        turned = same
+    bits = list(range(grid_rows.bit_length() - 1))
+    few = [2] * (len(bits) % 2) + [4] * (len(bits) // 2)
+    many = [2] * (len(bits) - 2) + [4] * (len(bits) >= 2) + [2] * (len(bits) == 1)
+    same = [stage_strides(bits[::-1], few)] * 2
+    turned = [stage_strides(bits[::-1], many), stage_strides(bits, many)]
 
     def gather(parts, orders, first=0, last=None):
         for (stride, radix), (odd_stride, _) in list(zip(*orders))[first:last]:
@@ -206,7 +204,7 @@
 
     row = lax.axis_index("row")
     col = lax.axis_index("col")
-    early = arrival_order(strides)
+    early = arrival_order(same[0])
     late = [arrival_order(order) for order in turned]
     places = [[early.index(offset) for offset in order] for order in late]
     sources = jnp.array(late, jnp.int32)[col % 2] ^ row
@@ -214,7 +212,7 @@
     targets = jnp.arange(grid_cols, dtype=jnp.int32) ^ col
     pieces = gather([initial.astype(jnp.bfloat16)], same, last=1)
     dense = build_tile(
-        block_rows[0, 0], block_cols[0, 0], block_counts[0], hamiltonian_blocks[0, 0],
+        block_rows[0, 0], block_cols[0, 0], block_counts, hamiltonian_blocks[0, 0],
         grid_rows, grid_cols,
     )
     dense = after(dense, pieces[1:])

time: 80.1 us -> 84.7 us (1.057)
  waiting for transfers between devices: 38.5 us -> 49.5 us
  starting transfers between devices: 31.5 us -> 25.1 us
    ppermute x18 -> x16, waiting for transfers between devices: 27 us -> 38 us  [swap_rows(): return lax.ppermute(x, ('row', 'col'), pairs)]
    ppermute x18 -> x16, starting transfers between devices: 25.3 us -> 18.9 us  [swap_rows(): return lax.ppermute(x, ('row', 'col'), pairs)]
  transfers between devices with their start and end apart: 22 -> 20, of which waited for: 18 -> 15; matrix products, arithmetic and copies ran while one was open for 0% -> 0% of each run, Pallas kernels for 4% -> 4%
where the time goes in v6:
time: 84.7 us; the launch traced here: 84.4 us
  waiting for transfers between devices  49.5 us (58%)
  starting transfers between devices  25.1 us (30%)
  Pallas kernels  5.44 us (6%)
  other arithmetic  2.17 us (3%)
  between operations  2.15 us (3%)
    ppermute x16, waiting for transfers between devices, swap_rows(): return lax.ppermute(x, ('row', 'col'), pairs)  38 us
    ppermute x16, starting transfers between devices, swap_rows(): return lax.ppermute(x, ('row', 'col'), pairs)  18.9 us
    all_to_all x1, waiting for transfers between devices, body(): received = lax.all_to_all(dense, ('row', 'col'), 0, 0)  7.78 us
    all_to_all x1, starting transfers between devices, body(): received = lax.all_to_all(dense, ('row', 'col'), 0, 0)  5.95 us
    ppermute x3, waiting for transfers between devices, swap(): lax.ppermute(x, axis, [(source, source ^ offset) for source in range(size)])  3.72 us
    pallas_call x1, Pallas kernels, build_tile(): pl.pallas_call(kernel, grid_spec=pltpu.PrefetchScalarGridSpec(num_scalar_...  3.44 us
  transfers between devices with their start and end apart: 20, of which 15 were waited for; matrix products, arithmetic and copies ran while one was open for 0% of the time, Pallas kernels for 4%

profile of v6, /device:TPU:0, one launch (start us, length us, event | category | flops | bytes accessed | tf_op | source)
XLA Modules:
  0.0 84.4 jit_solution(4337959402690113005)
XLA Ops:
  0.0 0.8 %constant_dynamic-update-slice_fusion.6 = (bf16[2048,128]{1,0:T(8,128)(2,1)S(1)}, bf16[128,128]{1,0:T(8,128)(2,1)S(1)}) fusion(f32[128,128]{1,0:T(8,128)} %previous_ref.1), kind=kLoop, calls=%fused_computation.11 | loop fusion | flops 16383 | bytes 131072
  0.9 5.1 %collective-permute-start.2 = (bf16[128,128]{1,0:T(8,128)(2,1)S(1)}, bf16[128,128]{1,0:T(8,128)(2,1)S(1)}, u32[]{:S(2)}, u32[]{:S(2)}) collective-permute-start(bf16[128,128]{1,0:T(8,128)(2,1)S(1)} %get-tuple-element.24), channel_id=1, source_target_pairs={{0,24},{1,25},{2,26},{3,27},{4,28},{5,29},{6,30},{7,31},{8,16},{9,... | collective-permute-start | bytes 98312 | tf_op jit(solution)/shard_map/ppermute | solution.py:45
  6.0 0.0 collective-permute-start.1
  6.0 0.6 collective-permute-start
  7.3 3.4 %build_tile.1.refs_0_ = bf16[32,128,128]{2,1,0:T(8,128)(2,1)} custom-call(s32[64]{0:T(128)} %bitcast.8, s32[64]{0:T(128)} %bitcast.9, s32[1,1]{1,0:T(1,128)S(6)} %copy.18.count_ref, bf16[64,128,128]{2,1,0:T(8,128)(2,1)} %bitcast.7), custom_call_target="tpu_custom_call" | custom-call | tf_op jit(solution)/shard_map/build_tile/pallas_call | solution.py:77
  10.7 0.0 collective-permute-done.2
  10.7 0.1 collective-permute-done.1
  10.8 0.0 collective-permute-done
  10.8 0.6 slice_add_fusion.refs_1_
  11.4 6.0 %all-to-all-start = ((bf16[32,128,128]{2,1,0:T(8,128)(2,1)}), bf16[32,128,128]{2,1,0:T(8,128)(2,1)S(1)}, u32[]{:S(2)}, u32[]{:S(2)}) async-start(bf16[32,128,128]{2,1,0:T(8,128)(2,1)} %after.1.dense_ref), calls=%async_computation | async-start | bytes 2097152 | tf_op jit(solution)/shard_map/all_to_all | solution.py:219
  18.7 2.7 %collective-permute-start.5 = (bf16[512,128]{1,0:T(8,128)(2,1)S(1)}, bf16[512,128]{1,0:T(8,128)(2,1)S(1)}, u32[]{:S(2)}, u32[]{:S(2)}) collective-permute-start(bf16[512,128]{1,0:T(8,128)(2,1)S(1)} %pad_maximum_fusion), channel_id=1, source_target_pairs={{0,6},{1,7},{2,4},{3,5},{4,2},{5,3},{6,0},{7,1},{8,14},{9,15},{10,... | collective-permute-start | bytes 393224 | tf_op jit(solution)/shard_map/ppermute | solution.py:45
  21.5 0.6 collective-permute-start.4
  22.0 0.3 collective-permute-start.3
  22.3 13.4 %collective-permute-done.3 = bf16[512,128]{1,0:T(8,128)(2,1)S(1)} collective-permute-done((bf16[512,128]{1,0:T(8,128)(2,1)S(1)}, bf16[512,128]{1,0:T(8,128)(2,1)S(1)}, u32[]{:S(2)}, u32[]{:S(2)}) %collective-permute-start.3) | collective-permute-done | bytes 131104 | tf_op jit(solution)/shard_map/ppermute | solution.py:45
  35.7 0.0 collective-permute-done.4
  35.8 0.0 collective-permute-done.5
  35.8 7.8 %all-to-all-done.received_ref = bf16[32,128,128]{2,1,0:T(8,128)(2,1)S(1)} async-done(((bf16[32,128,128]{2,1,0:T(8,128)(2,1)}), bf16[32,128,128]{2,1,0:T(8,128)(2,1)S(1)}, u32[]{:S(2)}, u32[]{:S(2)}) %all-to-all-start) | async-done | bytes 1048608 | tf_op jit(solution)/shard_map/all_to_all | solution.py:219
  43.6 0.0 copy-done
  43.6 1.2 %merge_apply.1 = (bf16[256,2048]{1,0:T(8,128)(2,1)S(1)}, f32[128,128]{1,0:T(8,128)S(1)}, f32[128,128]{1,0:T(8,128)S(1)}) custom-call(s32[16]{0:T(128)S(1)} %get-tuple-element.26.sources_ref, s32[16]{0:T(128)S(1)} %get-tuple-element.25.places_ref, s32[2]{0:T(128)S(1)} %iota_xor_fusion.targets_ref, f32[1]{0:T(128)S(6)} %copy.19.center_ref, ...), custom_call_target="tpu_custom_call" | custom-call | tf_op jit(solution)/shard_map/merge_apply/pallas_call | solution.py:148
  44.8 0.1 collective-permute-start.6
  44.8 1.2 %collective-permute-done.6 = f32[128,128]{1,0:T(8,128)S(1)} collective-permute-done((f32[128,128]{1,0:T(8,128)S(1)}, f32[128,128]{1,0:T(8,128)S(1)}, u32[]{:S(2)}, u32[]{:S(2)}) %collective-permute-start.6) | collective-permute-done | bytes 65568 | tf_op jit(solution)/shard_map/ppermute | solution.py:36
  46.1 1.2 %collective-permute-start.7 = (bf16[128,128]{1,0:T(8,128)(2,1)S(1)}, bf16[128,128]{1,0:T(8,128)(2,1)S(1)}, u32[]{:S(2)}, u32[]{:S(2)}) collective-permute-start(bf16[128,128]{1,0:T(8,128)(2,1)S(1)} %get-tuple-element.21), channel_id=1, source_target_pairs={{0,16},{1,3},{2,18},{3,1},{4,20},{5,7},{6,22},{7,5},{8,24},{9,11},... | collective-permute-start | bytes 98312 | tf_op jit(solution)/shard_map/ppermute | solution.py:45
  47.3 4.0 %collective-permute-done.7 = bf16[128,128]{1,0:T(8,128)(2,1)S(1)} collective-permute-done((bf16[128,128]{1,0:T(8,128)(2,1)S(1)}, bf16[128,128]{1,0:T(8,128)(2,1)S(1)}, u32[]{:S(2)}, u32[]{:S(2)}) %collective-permute-start.7) | collective-permute-done | bytes 32800 | tf_op jit(solution)/shard_map/ppermute | solution.py:45
  51.3 0.5 collective-permute-start.8
  51.8 3.8 %collective-permute-done.8 = bf16[256,128]{1,0:T(8,128)(2,1)S(1)} collective-permute-done((bf16[256,128]{1,0:T(8,128)(2,1)S(1)}, bf16[256,128]{1,0:T(8,128)(2,1)S(1)}, u32[]{:S(2)}, u32[]{:S(2)}) %collective-permute-start.8) | collective-permute-done | bytes 65568 | tf_op jit(solution)/shard_map/ppermute | solution.py:45
  55.6 2.1 %collective-permute-start.11 = (bf16[512,128]{1,0:T(8,128)(2,1)S(1)}, bf16[512,128]{1,0:T(8,128)(2,1)S(1)}, u32[]{:S(2)}, u32[]{:S(2)}) collective-permute-start(bf16[512,128]{1,0:T(8,128)(2,1)S(1)} %pad_maximum_fusion.1.refs_0_), channel_id=1, source_target_pairs={{0,6},{1,25},{2,4},{3,27},{4,2},{5,29},{6,0},{7,31},{8,14},{9,17},... | collective-permute-start | bytes 393224 | tf_op jit(solution)/shard_map/ppermute | solution.py:45
  57.7 0.9 %collective-permute-start.10 = (bf16[512,128]{1,0:T(8,128)(2,1)S(1)}, bf16[512,128]{1,0:T(8,128)(2,1)S(1)}, u32[]{:S(2)}, u32[]{:S(2)}) collective-permute-start(bf16[512,128]{1,0:T(8,128)(2,1)S(1)} %pad_maximum_fusion.1.refs_0_), channel_id=1, source_target_pairs={{0,4},{1,17},{2,6},{3,19},{4,0},{5,21},{6,2},{7,23},{8,12},{9,25},... | collective-permute-start | bytes 393224 | tf_op jit(solution)/shard_map/ppermute | solution.py:45
  58.6 0.6 collective-permute-start.9
  59.2 2.4 %collective-permute-done.11.refs_3_ = bf16[512,128]{1,0:T(8,128)(2,1)S(1)} collective-permute-done((bf16[512,128]{1,0:T(8,128)(2,1)S(1)}, bf16[512,128]{1,0:T(8,128)(2,1)S(1)}, u32[]{:S(2)}, u32[]{:S(2)}) %collective-permute-start.11) | collective-permute-done | bytes 131104 | tf_op jit(solution)/shard_map/ppermute | solution.py:45
  61.6 1.4 %collective-permute-done.10.refs_2_ = bf16[512,128]{1,0:T(8,128)(2,1)S(1)} collective-permute-done((bf16[512,128]{1,0:T(8,128)(2,1)S(1)}, bf16[512,128]{1,0:T(8,128)(2,1)S(1)}, u32[]{:S(2)}, u32[]{:S(2)}) %collective-permute-start.10) | collective-permute-done | bytes 131104 | tf_op jit(solution)/shard_map/ppermute | solution.py:45
  63.0 0.6 collective-permute-done.9.refs_1_
  63.6 0.4 apply_tile.2
  64.0 0.1 collective-permute-start.12
  64.1 1.2 %collective-permute-done.12 = f32[128,128]{1,0:T(8,128)S(1)} collective-permute-done((f32[128,128]{1,0:T(8,128)S(1)}, f32[128,128]{1,0:T(8,128)S(1)}, u32[]{:S(2)}, u32[]{:S(2)}) %collective-permute-start.12) | collective-permute-done | bytes 65568 | tf_op jit(solution)/shard_map/ppermute | solution.py:36
  65.3 0.5 collective-permute-start.13
  65.9 4.5 %collective-permute-done.13 = bf16[128,128]{1,0:T(8,128)(2,1)S(1)} collective-permute-done((bf16[128,128]{1,0:T(8,128)(2,1)S(1)}, bf16[128,128]{1,0:T(8,128)(2,1)S(1)}, u32[]{:S(2)}, u32[]{:S(2)}) %collective-permute-start.13) | collective-permute-done | bytes 32800 | tf_op jit(solution)/shard_map/ppermute | solution.py:45
  70.4 0.2 collective-permute-start.14
  70.6 4.0 %collective-permute-done.14 = bf16[256,128]{1,0:T(8,128)(2,1)S(1)} collective-permute-done((bf16[256,128]{1,0:T(8,128)(2,1)S(1)}, bf16[256,128]{1,0:T(8,128)(2,1)S(1)}, u32[]{:S(2)}, u32[]{:S(2)}) %collective-permute-start.14) | collective-permute-done | bytes 65568 | tf_op jit(solution)/shard_map/ppermute | solution.py:45
  74.6 1.4 %collective-permute-start.17 = (bf16[512,128]{1,0:T(8,128)(2,1)S(1)}, bf16[512,128]{1,0:T(8,128)(2,1)S(1)}, u32[]{:S(2)}, u32[]{:S(2)}) collective-permute-start(bf16[512,128]{1,0:T(8,128)(2,1)S(1)} %pad_maximum_fusion.2.refs_0_), channel_id=1, source_target_pairs={{0,6},{1,25},{2,4},{3,27},{4,2},{5,29},{6,0},{7,31},{8,14},{9,17},... | collective-permute-start | bytes 393224 | tf_op jit(solution)/shard_map/ppermute | solution.py:45
  76.0 1.0 %collective-permute-start.16 = (bf16[512,128]{1,0:T(8,128)(2,1)S(1)}, bf16[512,128]{1,0:T(8,128)(2,1)S(1)}, u32[]{:S(2)}, u32[]{:S(2)}) collective-permute-start(bf16[512,128]{1,0:T(8,128)(2,1)S(1)} %pad_maximum_fusion.2.refs_0_), channel_id=1, source_target_pairs={{0,4},{1,17},{2,6},{3,19},{4,0},{5,21},{6,2},{7,23},{8,12},{9,25},... | collective-permute-start | bytes 393224 | tf_op jit(solution)/shard_map/ppermute | solution.py:45
  77.0 1.2 %collective-permute-start.15 = (bf16[512,128]{1,0:T(8,128)(2,1)S(1)}, bf16[512,128]{1,0:T(8,128)(2,1)S(1)}, u32[]{:S(2)}, u32[]{:S(2)}) collective-permute-start(bf16[512,128]{1,0:T(8,128)(2,1)S(1)} %pad_maximum_fusion.2.refs_0_), channel_id=1, source_target_pairs={{0,2},{1,9},{2,0},{3,11},{4,6},{5,13},{6,4},{7,15},{8,10},{9,1},{1... | collective-permute-start | bytes 393224 | tf_op jit(solution)/shard_map/ppermute | solution.py:45
  78.2 2.5 %collective-permute-done.17.refs_3_ = bf16[512,128]{1,0:T(8,128)(2,1)S(1)} collective-permute-done((bf16[512,128]{1,0:T(8,128)(2,1)S(1)}, bf16[512,128]{1,0:T(8,128)(2,1)S(1)}, u32[]{:S(2)}, u32[]{:S(2)}) %collective-permute-start.17) | collective-permute-done | bytes 131104 | tf_op jit(solution)/shard_map/ppermute | solution.py:45
  80.7 1.3 %collective-permute-done.16.refs_2_ = bf16[512,128]{1,0:T(8,128)(2,1)S(1)} collective-permute-done((bf16[512,128]{1,0:T(8,128)(2,1)S(1)}, bf16[512,128]{1,0:T(8,128)(2,1)S(1)}, u32[]{:S(2)}, u32[]{:S(2)}) %collective-permute-start.16) | collective-permute-done | bytes 131104 | tf_op jit(solution)/shard_map/ppermute | solution.py:45
  82.0 0.0 collective-permute-done.15.refs_1_
  82.0 0.4 apply_tile.3
  82.4 0.1 collective-permute-start.18
  82.5 1.2 %collective-permute-done.18 = f32[128,128]{1,0:T(8,128)S(1)} collective-permute-done((f32[128,128]{1,0:T(8,128)S(1)}, f32[128,128]{1,0:T(8,128)S(1)}, u32[]{:S(2)}, u32[]{:S(2)}) %collective-permute-start.18) | collective-permute-done | bytes 65568 | tf_op jit(solution)/shard_map/ppermute | solution.py:36
  83.7 0.6 add.30
  (23 shorter events, 0.2 us)
Async XLA Ops:
  0.9 9.9 %collective-permute-start.2 = (bf16[128,128]{1,0:T(8,128)(2,1)S(1)}, bf16[128,128]{1,0:T(8,128)(2,1)S(1)}, u32[]{:S(2)}, u32[]{:S(2)}) collective-permute-start(bf16[128,128]{1,0:T(8,128)(2,1)S(1)} %get-tuple-element.24), channel_id=1, source_target_pairs={{0,24},{1,25},{2,26},{3,27},{4,28},{5,29},{6,30},{7,31},{8,16},{9,... | collective-permute-start | bytes 98312 | tf_op jit(solution)/shard_map/ppermute | solution.py:45
  6.0 4.8 %collective-permute-start.1 = (bf16[128,128]{1,0:T(8,128)(2,1)S(1)}, bf16[128,128]{1,0:T(8,128)(2,1)S(1)}, u32[]{:S(2)}, u32[]{:S(2)}) collective-permute-start(bf16[128,128]{1,0:T(8,128)(2,1)S(1)} %get-tuple-element.24), channel_id=1, source_target_pairs={{0,16},{1,17},{2,18},{3,19},{4,20},{5,21},{6,22},{7,23},{8,24},{9,... | collective-permute-start | bytes 98312 | tf_op jit(solution)/shard_map/ppermute | solution.py:45
  6.0 4.8 %collective-permute-start = (bf16[128,128]{1,0:T(8,128)(2,1)S(1)}, bf16[128,128]{1,0:T(8,128)(2,1)S(1)}, u32[]{:S(2)}, u32[]{:S(2)}) collective-permute-start(bf16[128,128]{1,0:T(8,128)(2,1)S(1)} %get-tuple-element.24), channel_id=1, source_target_pairs={{0,8},{1,9},{2,10},{3,11},{4,12},{5,13},{6,14},{7,15},{8,0},{9,1},... | collective-permute-start | bytes 98312 | tf_op jit(solution)/shard_map/ppermute | solution.py:45
  11.4 7.3 %copy-start.2 = (s32[2,16]{1,0:T(2,128)S(1)}, s32[2,16]{1,0:T(2,128)}, u32[]{:S(2)}) copy-start(s32[2,16]{1,0:T(2,128)} %constant.29.clone) | copy-start | bytes 388
  11.4 7.3 %copy-start.3 = (s32[2,16]{1,0:T(2,128)S(1)}, s32[2,16]{1,0:T(2,128)}, u32[]{:S(2)}) copy-start(s32[2,16]{1,0:T(2,128)} %constant.28.clone) | copy-start | bytes 388
  11.4 32.2 %copy-start = (bf16[32,128,128]{2,1,0:T(8,128)(2,1)S(1)}, bf16[32,128,128]{2,1,0:T(8,128)(2,1)}, u32[]{:S(2)}) copy-start(bf16[32,128,128]{2,1,0:T(8,128)(2,1)} %after.1.dense_ref) | copy-start | bytes 3145732
  11.4 32.2 %copy-start.1 = (f32[128,128]{1,0:T(8,128)S(1)}, f32[128,128]{1,0:T(8,128)}, u32[]{:S(2)}) copy-start(f32[128,128]{1,0:T(8,128)} %previous_ref.1) | copy-start | bytes 196612
  11.4 32.2 %all-to-all-start = ((bf16[32,128,128]{2,1,0:T(8,128)(2,1)}), bf16[32,128,128]{2,1,0:T(8,128)(2,1)S(1)}, u32[]{:S(2)}, u32[]{:S(2)}) async-start(bf16[32,128,128]{2,1,0:T(8,128)(2,1)} %after.1.dense_ref), calls=%async_computation | async-start | bytes 2097152 | tf_op jit(solution)/shard_map/all_to_all | solution.py:219
  18.7 17.0 %collective-permute-start.5 = (bf16[512,128]{1,0:T(8,128)(2,1)S(1)}, bf16[512,128]{1,0:T(8,128)(2,1)S(1)}, u32[]{:S(2)}, u32[]{:S(2)}) collective-permute-start(bf16[512,128]{1,0:T(8,128)(2,1)S(1)} %pad_maximum_fusion), channel_id=1, source_target_pairs={{0,6},{1,7},{2,4},{3,5},{4,2},{5,3},{6,0},{7,1},{8,14},{9,15},{10,... | collective-permute-start | bytes 393224 | tf_op jit(solution)/shard_map/ppermute | solution.py:45
  21.5 14.3 %collective-permute-start.4 = (bf16[512,128]{1,0:T(8,128)(2,1)S(1)}, bf16[512,128]{1,0:T(8,128)(2,1)S(1)}, u32[]{:S(2)}, u32[]{:S(2)}) collective-permute-start(bf16[512,128]{1,0:T(8,128)(2,1)S(1)} %pad_maximum_fusion), channel_id=1, source_target_pairs={{0,4},{1,5},{2,6},{3,7},{4,0},{5,1},{6,2},{7,3},{8,12},{9,13},{10,... | collective-permute-start | bytes 393224 | tf_op jit(solution)/shard_map/ppermute | solution.py:45
  22.0 13.7 %collective-permute-start.3 = (bf16[512,128]{1,0:T(8,128)(2,1)S(1)}, bf16[512,128]{1,0:T(8,128)(2,1)S(1)}, u32[]{:S(2)}, u32[]{:S(2)}) collective-permute-start(bf16[512,128]{1,0:T(8,128)(2,1)S(1)} %pad_maximum_fusion), channel_id=1, source_target_pairs={{0,2},{1,3},{2,0},{3,1},{4,6},{5,7},{6,4},{7,5},{8,10},{9,11},{10,... | collective-permute-start | bytes 393224 | tf_op jit(solution)/shard_map/ppermute | solution.py:45
  44.8 1.3 %collective-permute-start.6 = (f32[128,128]{1,0:T(8,128)S(1)}, f32[128,128]{1,0:T(8,128)S(1)}, u32[]{:S(2)}, u32[]{:S(2)}) collective-permute-start(f32[128,128]{1,0:T(8,128)S(1)} %get-tuple-element.14), channel_id=1, source_target_pairs={{0,1},{1,0},{2,3},{3,2},{4,5},{5,4},{6,7},{7,6},{8,9},{9,8},{10,11... | collective-permute-start | bytes 196616 | tf_op jit(solution)/shard_map/ppermute | solution.py:36
  46.1 5.2 %collective-permute-start.7 = (bf16[128,128]{1,0:T(8,128)(2,1)S(1)}, bf16[128,128]{1,0:T(8,128)(2,1)S(1)}, u32[]{:S(2)}, u32[]{:S(2)}) collective-permute-start(bf16[128,128]{1,0:T(8,128)(2,1)S(1)} %get-tuple-element.21), channel_id=1, source_target_pairs={{0,16},{1,3},{2,18},{3,1},{4,20},{5,7},{6,22},{7,5},{8,24},{9,11},... | collective-permute-start | bytes 98312 | tf_op jit(solution)/shard_map/ppermute | solution.py:45
  51.3 4.3 %collective-permute-start.8 = (bf16[256,128]{1,0:T(8,128)(2,1)S(1)}, bf16[256,128]{1,0:T(8,128)(2,1)S(1)}, u32[]{:S(2)}, u32[]{:S(2)}) collective-permute-start(bf16[256,128]{1,0:T(8,128)(2,1)S(1)} %pad_maximum_fusion.3), channel_id=1, source_target_pairs={{0,8},{1,5},{2,10},{3,7},{4,12},{5,1},{6,14},{7,3},{8,0},{9,13},{1... | collective-permute-start | bytes 196616 | tf_op jit(solution)/shard_map/ppermute | solution.py:45
  55.6 6.0 %collective-permute-start.11 = (bf16[512,128]{1,0:T(8,128)(2,1)S(1)}, bf16[512,128]{1,0:T(8,128)(2,1)S(1)}, u32[]{:S(2)}, u32[]{:S(2)}) collective-permute-start(bf16[512,128]{1,0:T(8,128)(2,1)S(1)} %pad_maximum_fusion.1.refs_0_), channel_id=1, source_target_pairs={{0,6},{1,25},{2,4},{3,27},{4,2},{5,29},{6,0},{7,31},{8,14},{9,17},... | collective-permute-start | bytes 393224 | tf_op jit(solution)/shard_map/ppermute | solution.py:45
  57.7 5.2 %collective-permute-start.10 = (bf16[512,128]{1,0:T(8,128)(2,1)S(1)}, bf16[512,128]{1,0:T(8,128)(2,1)S(1)}, u32[]{:S(2)}, u32[]{:S(2)}) collective-permute-start(bf16[512,128]{1,0:T(8,128)(2,1)S(1)} %pad_maximum_fusion.1.refs_0_), channel_id=1, source_target_pairs={{0,4},{1,17},{2,6},{3,19},{4,0},{5,21},{6,2},{7,23},{8,12},{9,25},... | collective-permute-start | bytes 393224 | tf_op jit(solution)/shard_map/ppermute | solution.py:45
  58.6 5.0 %collective-permute-start.9 = (bf16[512,128]{1,0:T(8,128)(2,1)S(1)}, bf16[512,128]{1,0:T(8,128)(2,1)S(1)}, u32[]{:S(2)}, u32[]{:S(2)}) collective-permute-start(bf16[512,128]{1,0:T(8,128)(2,1)S(1)} %pad_maximum_fusion.1.refs_0_), channel_id=1, source_target_pairs={{0,2},{1,9},{2,0},{3,11},{4,6},{5,13},{6,4},{7,15},{8,10},{9,1},{1... | collective-permute-start | bytes 393224 | tf_op jit(solution)/shard_map/ppermute | solution.py:45
  64.0 1.3 %collective-permute-start.12 = (f32[128,128]{1,0:T(8,128)S(1)}, f32[128,128]{1,0:T(8,128)S(1)}, u32[]{:S(2)}, u32[]{:S(2)}) collective-permute-start(f32[128,128]{1,0:T(8,128)S(1)} %get-tuple-element.16), channel_id=1, source_target_pairs={{0,1},{1,0},{2,3},{3,2},{4,5},{5,4},{6,7},{7,6},{8,9},{9,8},{10,11... | collective-permute-start | bytes 196616 | tf_op jit(solution)/shard_map/ppermute | solution.py:36
  65.3 5.0 %collective-permute-start.13 = (bf16[128,128]{1,0:T(8,128)(2,1)S(1)}, bf16[128,128]{1,0:T(8,128)(2,1)S(1)}, u32[]{:S(2)}, u32[]{:S(2)}) collective-permute-start(bf16[128,128]{1,0:T(8,128)(2,1)S(1)} %get-tuple-element.19), channel_id=1, source_target_pairs={{0,16},{1,3},{2,18},{3,1},{4,20},{5,7},{6,22},{7,5},{8,24},{9,11},... | collective-permute-start | bytes 98312 | tf_op jit(solution)/shard_map/ppermute | solution.py:45
  70.4 4.3 %collective-permute-start.14 = (bf16[256,128]{1,0:T(8,128)(2,1)S(1)}, bf16[256,128]{1,0:T(8,128)(2,1)S(1)}, u32[]{:S(2)}, u32[]{:S(2)}) collective-permute-start(bf16[256,128]{1,0:T(8,128)(2,1)S(1)} %pad_maximum_fusion.4), channel_id=1, source_target_pairs={{0,8},{1,5},{2,10},{3,7},{4,12},{5,1},{6,14},{7,3},{8,0},{9,13},{1... | collective-permute-start | bytes 196616 | tf_op jit(solution)/shard_map/ppermute | solution.py:45
  74.6 6.0 %collective-permute-start.17 = (bf16[512,128]{1,0:T(8,128)(2,1)S(1)}, bf16[512,128]{1,0:T(8,128)(2,1)S(1)}, u32[]{:S(2)}, u32[]{:S(2)}) collective-permute-start(bf16[512,128]{1,0:T(8,128)(2,1)S(1)} %pad_maximum_fusion.2.refs_0_), channel_id=1, source_target_pairs={{0,6},{1,25},{2,4},{3,27},{4,2},{5,29},{6,0},{7,31},{8,14},{9,17},... | collective-permute-start | bytes 393224 | tf_op jit(solution)/shard_map/ppermute | solution.py:45
  76.0 6.0 %collective-permute-start.16 = (bf16[512,128]{1,0:T(8,128)(2,1)S(1)}, bf16[512,128]{1,0:T(8,128)(2,1)S(1)}, u32[]{:S(2)}, u32[]{:S(2)}) collective-permute-start(bf16[512,128]{1,0:T(8,128)(2,1)S(1)} %pad_maximum_fusion.2.refs_0_), channel_id=1, source_target_pairs={{0,4},{1,17},{2,6},{3,19},{4,0},{5,21},{6,2},{7,23},{8,12},{9,25},... | collective-permute-start | bytes 393224 | tf_op jit(solution)/shard_map/ppermute | solution.py:45
  77.0 5.0 %collective-permute-start.15 = (bf16[512,128]{1,0:T(8,128)(2,1)S(1)}, bf16[512,128]{1,0:T(8,128)(2,1)S(1)}, u32[]{:S(2)}, u32[]{:S(2)}) collective-permute-start(bf16[512,128]{1,0:T(8,128)(2,1)S(1)} %pad_maximum_fusion.2.refs_0_), channel_id=1, source_target_pairs={{0,2},{1,9},{2,0},{3,11},{4,6},{5,13},{6,4},{7,15},{8,10},{9,1},{1... | collective-permute-start | bytes 393224 | tf_op jit(solution)/shard_map/ppermute | solution.py:45
  82.4 1.3 %collective-permute-start.18 = (f32[128,128]{1,0:T(8,128)S(1)}, f32[128,128]{1,0:T(8,128)S(1)}, u32[]{:S(2)}, u32[]{:S(2)}) collective-permute-start(f32[128,128]{1,0:T(8,128)S(1)} %get-tuple-element.18), channel_id=1, source_target_pairs={{0,1},{1,0},{2,3},{3,2},{4,5},{5,4},{6,7},{7,6},{8,9},{9,8},{10,11... | collective-permute-start | bytes 196616 | tf_op jit(solution)/shard_map/ppermute | solution.py:36

commit v7 on v5

--- a/solution.py
+++ b/solution.py
@@ -10,7 +10,6 @@
 CHUNK = 8
 SPARE = 4 * 2**20
 BUILD_VMEM = 62 * 2**20
-AFTER_VMEM = 60 * 2**20
 
 VMEM = pl.BlockSpec(memory_space=pltpu.VMEM)
 SMEM = pl.BlockSpec(memory_space=pltpu.SMEM)
@@ -53,7 +52,16 @@
     chunks = slots // chunk
     cells = grid_rows * grid_cols
 
-    def kernel(rows_ref, cols_ref, count_ref, stack_ref, dense_ref, held_ref, acc_ref, sems):
+    def kernel(
+        rows_hbm, cols_hbm, count_ref, stack_ref, dense_ref,
+        held_ref, acc_ref, rows_ref, cols_ref, sems, index_sems,
+    ):
+        indices = [
+            pltpu.make_async_copy(source, target, index_sems.at[n])
+            for n, (source, target) in enumerate([(rows_hbm, rows_ref), (cols_hbm, cols_ref)])
+        ]
+        for copy in indices:
+            copy.start()
         copies = [
             pltpu.make_async_copy(
                 stack_ref.at[pl.ds(n * chunk, chunk)], held_ref.at[pl.ds(n * chunk, chunk)], sems.at[n]
@@ -62,12 +70,14 @@
         ]
         for copy in copies:
             copy.start()
-        count = count_ref[0]
         acc_ref[...] = jnp.zeros_like(acc_ref)
+        for copy in indices:
+            copy.wait()
+        count = count_ref[0, 0]
         for n, copy in enumerate(copies):
             copy.wait()
             for s in range(n * chunk, (n + 1) * chunk):
-                cell = jnp.where(s < count, cols_ref[s] * grid_cols + rows_ref[s], cells)
+                cell = jnp.where(s < count, cols_ref[0, s] * grid_cols + rows_ref[0, s], cells)
                 acc_ref[cell] += held_ref[s].astype(jnp.float32)
 
         def put(cell, carry):
@@ -78,38 +88,40 @@
 
     return pl.pallas_call(
         kernel,
-        grid_spec=pltpu.PrefetchScalarGridSpec(
-            num_scalar_prefetch=3,
-            grid=(1,),
-            in_specs=[HBM],
-            out_specs=VMEM,
-            scratch_shapes=[
-                pltpu.VMEM(stacked.shape, jnp.bfloat16),
-                pltpu.VMEM((cells + 1, orb, orb), jnp.float32),
-                pltpu.SemaphoreType.DMA((chunks,)),
-            ],
-        ),
+        in_specs=[HBM, HBM, SMEM, HBM],
+        out_specs=VMEM,
+        scratch_shapes=[
+            pltpu.VMEM(stacked.shape, jnp.bfloat16),
+            pltpu.VMEM((cells + 1, orb, orb), jnp.float32),
+            pltpu.SMEM(rows.shape, jnp.int32),
+            pltpu.SMEM(cols.shape, jnp.int32),
+            pltpu.SemaphoreType.DMA((chunks,)),
+            pltpu.SemaphoreType.DMA((2,)),
+        ],
         out_shape=jax.ShapeDtypeStruct((cells, orb, orb), jnp.bfloat16),
         compiler_params=pltpu.CompilerParams(vmem_limit_bytes=BUILD_VMEM),
         name="build_tile",
-    )(rows, cols, count, stacked)
+    )(
+        pltpu.with_memory_space_constraint(rows, pltpu.HBM),
+        pltpu.with_memory_space_constraint(cols, pltpu.HBM),
+        count,
+        pltpu.with_memory_space_constraint(stacked, pltpu.HBM),
+    )
 
 
 def after(x, others):
-    token = sum(other[:16] for other in others)
-
     def kernel(*refs):
         pass
 
     return pl.pallas_call(
         kernel,
-        in_specs=[HBM, HBM],
+        in_specs=[HBM] + [VMEM] * len(others),
         out_specs=HBM,
-        out_shape=jax.ShapeDtypeStruct(x.shape, x.dtype),
+        out_shape=pltpu.HBM(x.shape, x.dtype),
         input_output_aliases={0: 0},
-        compiler_params=pltpu.CompilerParams(vmem_limit_bytes=AFTER_VMEM),
+        compiler_params=pltpu.CompilerParams(vmem_limit_bytes=SPARE),
         name="after",
-    )(x, token)
+    )(pltpu.with_memory_space_constraint(x, pltpu.HBM), *others)
 
 
 def finish(total, first, orb, current_ref, previous_ref, center_ref, halfwidth_ref, outs):
@@ -214,7 +226,7 @@
     targets = jnp.arange(grid_cols, dtype=jnp.int32) ^ col
     pieces = gather([initial.astype(jnp.bfloat16)], same, last=1)
     dense = build_tile(
-        block_rows[0, 0], block_cols[0, 0], block_counts[0], hamiltonian_blocks[0, 0],
+        block_rows[0], block_cols[0], block_counts, hamiltonian_blocks[0, 0],
         grid_rows, grid_cols,
     )
     dense = after(dense, pieces[1:])

time: 80.1 us -> 78.9 us (0.985)
  no operation moved by 1% of the time
where the time goes in v7:
time: 78.9 us; the launch traced here: 78.6 us
  waiting for transfers between devices  39.1 us (50%)
  starting transfers between devices  30.9 us (39%)
  Pallas kernels  4.78 us (6%)
  between operations  2.16 us (3%)
  other arithmetic  1.56 us (2%)
    ppermute x18, waiting for transfers between devices, swap_rows(): return lax.ppermute(x, ('row', 'col'), pairs)  27.6 us
    ppermute x18, starting transfers between devices, swap_rows(): return lax.ppermute(x, ('row', 'col'), pairs)  25.3 us
    all_to_all x1, waiting for transfers between devices, body(): received = lax.all_to_all(dense, ('row', 'col'), 0, 0)  7.78 us
    all_to_all x1, starting transfers between devices, body(): received = lax.all_to_all(dense, ('row', 'col'), 0, 0)  5.33 us
    ppermute x3, waiting for transfers between devices, swap(): lax.ppermute(x, axis, [(source, source ^ offset) for source in range(size)])  3.72 us
    pallas_call x1, Pallas kernels, build_tile(): pl.pallas_call(kernel, in_specs=[HBM, HBM, SMEM, HBM], out_specs=VMEM, sc...  2.78 us
  transfers between devices with their start and end apart: 22, of which 18 were waited for; matrix products, arithmetic and copies ran while one was open for 0% of the time, Pallas kernels for 4%

profile of v7, /device:TPU:0, one launch (start us, length us, event | category | flops | bytes accessed | tf_op | source)
XLA Modules:
  0.0 78.6 jit_solution(13195605977723519658)
XLA Ops:
  0.0 0.8 %constant_dynamic-update-slice_fusion.6 = (bf16[2048,128]{1,0:T(8,128)(2,1)S(1)}, bf16[128,128]{1,0:T(8,128)(2,1)S(1)}) fusion(f32[128,128]{1,0:T(8,128)} %previous_ref.1), kind=kLoop, calls=%fused_computation.9 | loop fusion | flops 16383 | bytes 131072
  0.9 5.1 %collective-permute-start.2 = (bf16[128,128]{1,0:T(8,128)(2,1)S(1)}, bf16[128,128]{1,0:T(8,128)(2,1)S(1)}, u32[]{:S(2)}, u32[]{:S(2)}) collective-permute-start(bf16[128,128]{1,0:T(8,128)(2,1)S(1)} %get-tuple-element.24), channel_id=1, source_target_pairs={{0,24},{1,25},{2,26},{3,27},{4,28},{5,29},{6,30},{7,31},{8,16},{9,... | collective-permute-start | bytes 98312 | tf_op jit(solution)/shard_map/ppermute | solution.py:46
  6.0 0.0 collective-permute-start.1
  6.0 0.6 collective-permute-start
  7.3 2.8 %build_tile.1.refs_0_ = bf16[32,128,128]{2,1,0:T(8,128)(2,1)} custom-call(s32[1,64]{1,0:T(1,128)} %bitcast.8, s32[1,64]{1,0:T(1,128)} %bitcast.9, s32[1,1]{1,0:T(1,128)S(6)} %copy.18.count_ref, bf16[64,128,128]{2,1,0:T(8,128)(2,1)} %bitcast.7), custom_call_target="tpu_custom_call" | custom-call | tf_op jit(solution)/shard_map/build_tile/pallas_call | solution.py:89
  10.0 0.0 copy-start.2
  10.1 0.0 copy-start.3
  10.1 0.7 collective-permute-done.1.refs_2_
  10.8 5.3 %all-to-all-start = ((bf16[32,128,128]{2,1,0:T(8,128)(2,1)}), bf16[32,128,128]{2,1,0:T(8,128)(2,1)S(1)}, u32[]{:S(2)}, u32[]{:S(2)}) async-start(bf16[32,128,128]{2,1,0:T(8,128)(2,1)} %after.1.dense_ref), calls=%async_computation | async-start | bytes 2097152 | tf_op jit(solution)/shard_map/all_to_all | solution.py:233
  17.5 2.7 %collective-permute-start.5 = (bf16[512,128]{1,0:T(8,128)(2,1)S(1)}, bf16[512,128]{1,0:T(8,128)(2,1)S(1)}, u32[]{:S(2)}, u32[]{:S(2)}) collective-permute-start(bf16[512,128]{1,0:T(8,128)(2,1)S(1)} %pad_maximum_fusion), channel_id=1, source_target_pairs={{0,6},{1,7},{2,4},{3,5},{4,2},{5,3},{6,0},{7,1},{8,14},{9,15},{10,... | collective-permute-start | bytes 393224 | tf_op jit(solution)/shard_map/ppermute | solution.py:46
  20.2 0.6 collective-permute-start.4
  20.8 0.3 collective-permute-start.3
  21.1 13.4 %collective-permute-done.3 = bf16[512,128]{1,0:T(8,128)(2,1)S(1)} collective-permute-done((bf16[512,128]{1,0:T(8,128)(2,1)S(1)}, bf16[512,128]{1,0:T(8,128)(2,1)S(1)}, u32[]{:S(2)}, u32[]{:S(2)}) %collective-permute-start.3) | collective-permute-done | bytes 131104 | tf_op jit(solution)/shard_map/ppermute | solution.py:46
  34.6 7.8 %all-to-all-done.received_ref = bf16[32,128,128]{2,1,0:T(8,128)(2,1)S(1)} async-done(((bf16[32,128,128]{2,1,0:T(8,128)(2,1)}), bf16[32,128,128]{2,1,0:T(8,128)(2,1)S(1)}, u32[]{:S(2)}, u32[]{:S(2)}) %all-to-all-start) | async-done | bytes 1048608 | tf_op jit(solution)/shard_map/all_to_all | solution.py:233
  42.4 1.2 %merge_apply.1 = (bf16[256,2048]{1,0:T(8,128)(2,1)S(1)}, f32[128,128]{1,0:T(8,128)S(1)}, f32[128,128]{1,0:T(8,128)S(1)}) custom-call(s32[16]{0:T(128)S(1)} %get-tuple-element.26.sources_ref, s32[16]{0:T(128)S(1)} %get-tuple-element.25.places_ref, s32[2]{0:T(128)S(1)} %iota_xor_fusion.targets_ref, f32[1]{0:T(128)S(6)} %copy.19.center_ref, ...), custom_call_target="tpu_custom_call" | custom-call | tf_op jit(solution)/shard_map/merge_apply/pallas_call | solution.py:162
  43.5 0.1 collective-permute-start.6
  43.6 1.2 %collective-permute-done.6 = f32[128,128]{1,0:T(8,128)S(1)} collective-permute-done((f32[128,128]{1,0:T(8,128)S(1)}, f32[128,128]{1,0:T(8,128)S(1)}, u32[]{:S(2)}, u32[]{:S(2)}) %collective-permute-start.6) | collective-permute-done | bytes 65568 | tf_op jit(solution)/shard_map/ppermute | solution.py:37
  44.9 1.4 %collective-permute-start.9 = (bf16[128,128]{1,0:T(8,128)(2,1)S(1)}, bf16[128,128]{1,0:T(8,128)(2,1)S(1)}, u32[]{:S(2)}, u32[]{:S(2)}) collective-permute-start(bf16[128,128]{1,0:T(8,128)(2,1)S(1)} %get-tuple-element.21), channel_id=1, source_target_pairs={{0,24},{1,7},{2,26},{3,5},{4,28},{5,3},{6,30},{7,1},{8,16},{9,15},... | collective-permute-start | bytes 98312 | tf_op jit(solution)/shard_map/ppermute | solution.py:46
  46.2 0.9 %collective-permute-start.8 = (bf16[128,128]{1,0:T(8,128)(2,1)S(1)}, bf16[128,128]{1,0:T(8,128)(2,1)S(1)}, u32[]{:S(2)}, u32[]{:S(2)}) collective-permute-start(bf16[128,128]{1,0:T(8,128)(2,1)S(1)} %get-tuple-element.21), channel_id=1, source_target_pairs={{0,16},{1,5},{2,18},{3,7},{4,20},{5,1},{6,22},{7,3},{8,24},{9,13},... | collective-permute-start | bytes 98312 | tf_op jit(solution)/shard_map/ppermute | solution.py:46
  47.2 2.2 %collective-permute-start.7 = (bf16[128,128]{1,0:T(8,128)(2,1)S(1)}, bf16[128,128]{1,0:T(8,128)(2,1)S(1)}, u32[]{:S(2)}, u32[]{:S(2)}) collective-permute-start(bf16[128,128]{1,0:T(8,128)(2,1)S(1)} %get-tuple-element.21), channel_id=1, source_target_pairs={{0,8},{1,3},{2,10},{3,1},{4,12},{5,7},{6,14},{7,5},{8,0},{9,11},{1... | collective-permute-start | bytes 98312 | tf_op jit(solution)/shard_map/ppermute | solution.py:46
  49.3 1.3 %collective-permute-done.9 = bf16[128,128]{1,0:T(8,128)(2,1)S(1)} collective-permute-done((bf16[128,128]{1,0:T(8,128)(2,1)S(1)}, bf16[128,128]{1,0:T(8,128)(2,1)S(1)}, u32[]{:S(2)}, u32[]{:S(2)}) %collective-permute-start.9) | collective-permute-done | bytes 32800 | tf_op jit(solution)/shard_map/ppermute | solution.py:46
  50.7 0.8 %collective-permute-done.8 = bf16[128,128]{1,0:T(8,128)(2,1)S(1)} collective-permute-done((bf16[128,128]{1,0:T(8,128)(2,1)S(1)}, bf16[128,128]{1,0:T(8,128)(2,1)S(1)}, u32[]{:S(2)}, u32[]{:S(2)}) %collective-permute-start.8) | collective-permute-done | bytes 32800 | tf_op jit(solution)/shard_map/ppermute | solution.py:46
  51.5 0.1 collective-permute-done.7
  51.6 2.5 %collective-permute-start.12 = (bf16[512,128]{1,0:T(8,128)(2,1)S(1)}, bf16[512,128]{1,0:T(8,128)(2,1)S(1)}, u32[]{:S(2)}, u32[]{:S(2)}) collective-permute-start(bf16[512,128]{1,0:T(8,128)(2,1)S(1)} %pad_maximum_fusion.1.refs_0_), channel_id=1, source_target_pairs={{0,6},{1,25},{2,4},{3,27},{4,2},{5,29},{6,0},{7,31},{8,14},{9,17},... | collective-permute-start | bytes 393224 | tf_op jit(solution)/shard_map/ppermute | solution.py:46
  54.0 0.5 collective-permute-start.11
  54.6 0.5 collective-permute-start.10
  55.1 2.4 %collective-permute-done.12.refs_3_ = bf16[512,128]{1,0:T(8,128)(2,1)S(1)} collective-permute-done((bf16[512,128]{1,0:T(8,128)(2,1)S(1)}, bf16[512,128]{1,0:T(8,128)(2,1)S(1)}, u32[]{:S(2)}, u32[]{:S(2)}) %collective-permute-start.12) | collective-permute-done | bytes 131104 | tf_op jit(solution)/shard_map/ppermute | solution.py:46
  57.5 1.5 %collective-permute-done.11.refs_2_ = bf16[512,128]{1,0:T(8,128)(2,1)S(1)} collective-permute-done((bf16[512,128]{1,0:T(8,128)(2,1)S(1)}, bf16[512,128]{1,0:T(8,128)(2,1)S(1)}, u32[]{:S(2)}, u32[]{:S(2)}) %collective-permute-start.11) | collective-permute-done | bytes 131104 | tf_op jit(solution)/shard_map/ppermute | solution.py:46
  59.0 0.5 collective-permute-done.10.refs_1_
  59.5 0.4 apply_tile.2
  60.0 0.1 collective-permute-start.13
  60.1 1.2 %collective-permute-done.13 = f32[128,128]{1,0:T(8,128)S(1)} collective-permute-done((f32[128,128]{1,0:T(8,128)S(1)}, f32[128,128]{1,0:T(8,128)S(1)}, u32[]{:S(2)}, u32[]{:S(2)}) %collective-permute-start.13) | collective-permute-done | bytes 65568 | tf_op jit(solution)/shard_map/ppermute | solution.py:37
  61.3 2.1 %collective-permute-start.16 = (bf16[128,128]{1,0:T(8,128)(2,1)S(1)}, bf16[128,128]{1,0:T(8,128)(2,1)S(1)}, u32[]{:S(2)}, u32[]{:S(2)}) collective-permute-start(bf16[128,128]{1,0:T(8,128)(2,1)S(1)} %get-tuple-element.19), channel_id=1, source_target_pairs={{0,24},{1,7},{2,26},{3,5},{4,28},{5,3},{6,30},{7,1},{8,16},{9,15},... | collective-permute-start | bytes 98312 | tf_op jit(solution)/shard_map/ppermute | solution.py:46
  63.4 1.1 %collective-permute-start.15 = (bf16[128,128]{1,0:T(8,128)(2,1)S(1)}, bf16[128,128]{1,0:T(8,128)(2,1)S(1)}, u32[]{:S(2)}, u32[]{:S(2)}) collective-permute-start(bf16[128,128]{1,0:T(8,128)(2,1)S(1)} %get-tuple-element.19), channel_id=1, source_target_pairs={{0,16},{1,5},{2,18},{3,7},{4,20},{5,1},{6,22},{7,3},{8,24},{9,13},... | collective-permute-start | bytes 98312 | tf_op jit(solution)/shard_map/ppermute | solution.py:46
  64.5 1.3 %collective-permute-start.14 = (bf16[128,128]{1,0:T(8,128)(2,1)S(1)}, bf16[128,128]{1,0:T(8,128)(2,1)S(1)}, u32[]{:S(2)}, u32[]{:S(2)}) collective-permute-start(bf16[128,128]{1,0:T(8,128)(2,1)S(1)} %get-tuple-element.19), channel_id=1, source_target_pairs={{0,8},{1,3},{2,10},{3,1},{4,12},{5,7},{6,14},{7,5},{8,0},{9,11},{1... | collective-permute-start | bytes 98312 | tf_op jit(solution)/shard_map/ppermute | solution.py:46
  65.8 1.3 %collective-permute-done.16 = bf16[128,128]{1,0:T(8,128)(2,1)S(1)} collective-permute-done((bf16[128,128]{1,0:T(8,128)(2,1)S(1)}, bf16[128,128]{1,0:T(8,128)(2,1)S(1)}, u32[]{:S(2)}, u32[]{:S(2)}) %collective-permute-start.16) | collective-permute-done | bytes 32800 | tf_op jit(solution)/shard_map/ppermute | solution.py:46
  67.1 1.1 %collective-permute-done.15 = bf16[128,128]{1,0:T(8,128)(2,1)S(1)} collective-permute-done((bf16[128,128]{1,0:T(8,128)(2,1)S(1)}, bf16[128,128]{1,0:T(8,128)(2,1)S(1)}, u32[]{:S(2)}, u32[]{:S(2)}) %collective-permute-start.15) | collective-permute-done | bytes 32800 | tf_op jit(solution)/shard_map/ppermute | solution.py:46
  68.2 0.3 collective-permute-done.14
  68.6 1.6 %collective-permute-start.19 = (bf16[512,128]{1,0:T(8,128)(2,1)S(1)}, bf16[512,128]{1,0:T(8,128)(2,1)S(1)}, u32[]{:S(2)}, u32[]{:S(2)}) collective-permute-start(bf16[512,128]{1,0:T(8,128)(2,1)S(1)} %pad_maximum_fusion.2.refs_0_), channel_id=1, source_target_pairs={{0,6},{1,25},{2,4},{3,27},{4,2},{5,29},{6,0},{7,31},{8,14},{9,17},... | collective-permute-start | bytes 393224 | tf_op jit(solution)/shard_map/ppermute | solution.py:46
  70.2 1.0 %collective-permute-start.18 = (bf16[512,128]{1,0:T(8,128)(2,1)S(1)}, bf16[512,128]{1,0:T(8,128)(2,1)S(1)}, u32[]{:S(2)}, u32[]{:S(2)}) collective-permute-start(bf16[512,128]{1,0:T(8,128)(2,1)S(1)} %pad_maximum_fusion.2.refs_0_), channel_id=1, source_target_pairs={{0,4},{1,17},{2,6},{3,19},{4,0},{5,21},{6,2},{7,23},{8,12},{9,25},... | collective-permute-start | bytes 393224 | tf_op jit(solution)/shard_map/ppermute | solution.py:46
  71.2 0.9 %collective-permute-start.17 = (bf16[512,128]{1,0:T(8,128)(2,1)S(1)}, bf16[512,128]{1,0:T(8,128)(2,1)S(1)}, u32[]{:S(2)}, u32[]{:S(2)}) collective-permute-start(bf16[512,128]{1,0:T(8,128)(2,1)S(1)} %pad_maximum_fusion.2.refs_0_), channel_id=1, source_target_pairs={{0,2},{1,9},{2,0},{3,11},{4,6},{5,13},{6,4},{7,15},{8,10},{9,1},{1... | collective-permute-start | bytes 393224 | tf_op jit(solution)/shard_map/ppermute | solution.py:46
  72.1 2.5 %collective-permute-done.19.refs_3_ = bf16[512,128]{1,0:T(8,128)(2,1)S(1)} collective-permute-done((bf16[512,128]{1,0:T(8,128)(2,1)S(1)}, bf16[512,128]{1,0:T(8,128)(2,1)S(1)}, u32[]{:S(2)}, u32[]{:S(2)}) %collective-permute-start.19) | collective-permute-done | bytes 131104 | tf_op jit(solution)/shard_map/ppermute | solution.py:46
  74.6 1.3 %collective-permute-done.18.refs_2_ = bf16[512,128]{1,0:T(8,128)(2,1)S(1)} collective-permute-done((bf16[512,128]{1,0:T(8,128)(2,1)S(1)}, bf16[512,128]{1,0:T(8,128)(2,1)S(1)}, u32[]{:S(2)}, u32[]{:S(2)}) %collective-permute-start.18) | collective-permute-done | bytes 131104 | tf_op jit(solution)/shard_map/ppermute | solution.py:46
  75.9 0.3 collective-permute-done.17.refs_1_
  76.2 0.4 apply_tile.3
  76.6 0.1 collective-permute-start.20
  76.7 1.2 %collective-permute-done.20 = f32[128,128]{1,0:T(8,128)S(1)} collective-permute-done((f32[128,128]{1,0:T(8,128)S(1)}, f32[128,128]{1,0:T(8,128)S(1)}, u32[]{:S(2)}, u32[]{:S(2)}) %collective-permute-start.20) | collective-permute-done | bytes 65568 | tf_op jit(solution)/shard_map/ppermute | solution.py:37
  77.9 0.6 add.22
  (24 shorter events, 0.2 us)
Async XLA Ops:
  0.9 9.2 %collective-permute-start.2 = (bf16[128,128]{1,0:T(8,128)(2,1)S(1)}, bf16[128,128]{1,0:T(8,128)(2,1)S(1)}, u32[]{:S(2)}, u32[]{:S(2)}) collective-permute-start(bf16[128,128]{1,0:T(8,128)(2,1)S(1)} %get-tuple-element.24), channel_id=1, source_target_pairs={{0,24},{1,25},{2,26},{3,27},{4,28},{5,29},{6,30},{7,31},{8,16},{9,... | collective-permute-start | bytes 98312 | tf_op jit(solution)/shard_map/ppermute | solution.py:46
  6.0 4.8 %collective-permute-start.1 = (bf16[128,128]{1,0:T(8,128)(2,1)S(1)}, bf16[128,128]{1,0:T(8,128)(2,1)S(1)}, u32[]{:S(2)}, u32[]{:S(2)}) collective-permute-start(bf16[128,128]{1,0:T(8,128)(2,1)S(1)} %get-tuple-element.24), channel_id=1, source_target_pairs={{0,16},{1,17},{2,18},{3,19},{4,20},{5,21},{6,22},{7,23},{8,24},{9,... | collective-permute-start | bytes 98312 | tf_op jit(solution)/shard_map/ppermute | solution.py:46
  6.0 4.8 %collective-permute-start = (bf16[128,128]{1,0:T(8,128)(2,1)S(1)}, bf16[128,128]{1,0:T(8,128)(2,1)S(1)}, u32[]{:S(2)}, u32[]{:S(2)}) collective-permute-start(bf16[128,128]{1,0:T(8,128)(2,1)S(1)} %get-tuple-element.24), channel_id=1, source_target_pairs={{0,8},{1,9},{2,10},{3,11},{4,12},{5,13},{6,14},{7,15},{8,0},{9,1},... | collective-permute-start | bytes 98312 | tf_op jit(solution)/shard_map/ppermute | solution.py:46
  10.0 7.4 %copy-start.2 = (s32[2,16]{1,0:T(2,128)S(1)}, s32[2,16]{1,0:T(2,128)}, u32[]{:S(2)}) copy-start(s32[2,16]{1,0:T(2,128)} %constant.29.clone) | copy-start | bytes 388
  10.1 7.4 %copy-start.3 = (s32[2,16]{1,0:T(2,128)S(1)}, s32[2,16]{1,0:T(2,128)}, u32[]{:S(2)}) copy-start(s32[2,16]{1,0:T(2,128)} %constant.28.clone) | copy-start | bytes 388
  10.8 31.6 %copy-start = (bf16[32,128,128]{2,1,0:T(8,128)(2,1)S(1)}, bf16[32,128,128]{2,1,0:T(8,128)(2,1)}, u32[]{:S(2)}) copy-start(bf16[32,128,128]{2,1,0:T(8,128)(2,1)} %after.1.dense_ref) | copy-start | bytes 3145732
  10.8 31.6 %copy-start.1 = (f32[128,128]{1,0:T(8,128)S(1)}, f32[128,128]{1,0:T(8,128)}, u32[]{:S(2)}) copy-start(f32[128,128]{1,0:T(8,128)} %previous_ref.1) | copy-start | bytes 196612
  10.8 31.6 %all-to-all-start = ((bf16[32,128,128]{2,1,0:T(8,128)(2,1)}), bf16[32,128,128]{2,1,0:T(8,128)(2,1)S(1)}, u32[]{:S(2)}, u32[]{:S(2)}) async-start(bf16[32,128,128]{2,1,0:T(8,128)(2,1)} %after.1.dense_ref), calls=%async_computation | async-start | bytes 2097152 | tf_op jit(solution)/shard_map/all_to_all | solution.py:233
  17.5 17.0 %collective-permute-start.5 = (bf16[512,128]{1,0:T(8,128)(2,1)S(1)}, bf16[512,128]{1,0:T(8,128)(2,1)S(1)}, u32[]{:S(2)}, u32[]{:S(2)}) collective-permute-start(bf16[512,128]{1,0:T(8,128)(2,1)S(1)} %pad_maximum_fusion), channel_id=1, source_target_pairs={{0,6},{1,7},{2,4},{3,5},{4,2},{5,3},{6,0},{7,1},{8,14},{9,15},{10,... | collective-permute-start | bytes 393224 | tf_op jit(solution)/shard_map/ppermute | solution.py:46
  20.2 14.3 %collective-permute-start.4 = (bf16[512,128]{1,0:T(8,128)(2,1)S(1)}, bf16[512,128]{1,0:T(8,128)(2,1)S(1)}, u32[]{:S(2)}, u32[]{:S(2)}) collective-permute-start(bf16[512,128]{1,0:T(8,128)(2,1)S(1)} %pad_maximum_fusion), channel_id=1, source_target_pairs={{0,4},{1,5},{2,6},{3,7},{4,0},{5,1},{6,2},{7,3},{8,12},{9,13},{10,... | collective-permute-start | bytes 393224 | tf_op jit(solution)/shard_map/ppermute | solution.py:46
  20.8 13.7 %collective-permute-start.3 = (bf16[512,128]{1,0:T(8,128)(2,1)S(1)}, bf16[512,128]{1,0:T(8,128)(2,1)S(1)}, u32[]{:S(2)}, u32[]{:S(2)}) collective-permute-start(bf16[512,128]{1,0:T(8,128)(2,1)S(1)} %pad_maximum_fusion), channel_id=1, source_target_pairs={{0,2},{1,3},{2,0},{3,1},{4,6},{5,7},{6,4},{7,5},{8,10},{9,11},{10,... | collective-permute-start | bytes 393224 | tf_op jit(solution)/shard_map/ppermute | solution.py:46
  43.5 1.3 %collective-permute-start.6 = (f32[128,128]{1,0:T(8,128)S(1)}, f32[128,128]{1,0:T(8,128)S(1)}, u32[]{:S(2)}, u32[]{:S(2)}) collective-permute-start(f32[128,128]{1,0:T(8,128)S(1)} %get-tuple-element.14), channel_id=1, source_target_pairs={{0,1},{1,0},{2,3},{3,2},{4,5},{5,4},{6,7},{7,6},{8,9},{9,8},{10,11... | collective-permute-start | bytes 196616 | tf_op jit(solution)/shard_map/ppermute | solution.py:37
  44.9 5.8 %collective-permute-start.9 = (bf16[128,128]{1,0:T(8,128)(2,1)S(1)}, bf16[128,128]{1,0:T(8,128)(2,1)S(1)}, u32[]{:S(2)}, u32[]{:S(2)}) collective-permute-start(bf16[128,128]{1,0:T(8,128)(2,1)S(1)} %get-tuple-element.21), channel_id=1, source_target_pairs={{0,24},{1,7},{2,26},{3,5},{4,28},{5,3},{6,30},{7,1},{8,16},{9,15},... | collective-permute-start | bytes 98312 | tf_op jit(solution)/shard_map/ppermute | solution.py:46
  46.2 5.2 %collective-permute-start.8 = (bf16[128,128]{1,0:T(8,128)(2,1)S(1)}, bf16[128,128]{1,0:T(8,128)(2,1)S(1)}, u32[]{:S(2)}, u32[]{:S(2)}) collective-permute-start(bf16[128,128]{1,0:T(8,128)(2,1)S(1)} %get-tuple-element.21), channel_id=1, source_target_pairs={{0,16},{1,5},{2,18},{3,7},{4,20},{5,1},{6,22},{7,3},{8,24},{9,13},... | collective-permute-start | bytes 98312 | tf_op jit(solution)/shard_map/ppermute | solution.py:46
  47.2 4.4 %collective-permute-start.7 = (bf16[128,128]{1,0:T(8,128)(2,1)S(1)}, bf16[128,128]{1,0:T(8,128)(2,1)S(1)}, u32[]{:S(2)}, u32[]{:S(2)}) collective-permute-start(bf16[128,128]{1,0:T(8,128)(2,1)S(1)} %get-tuple-element.21), channel_id=1, source_target_pairs={{0,8},{1,3},{2,10},{3,1},{4,12},{5,7},{6,14},{7,5},{8,0},{9,11},{1... | collective-permute-start | bytes 98312 | tf_op jit(solution)/shard_map/ppermute | solution.py:46
  51.6 5.9 %collective-permute-start.12 = (bf16[512,128]{1,0:T(8,128)(2,1)S(1)}, bf16[512,128]{1,0:T(8,128)(2,1)S(1)}, u32[]{:S(2)}, u32[]{:S(2)}) collective-permute-start(bf16[512,128]{1,0:T(8,128)(2,1)S(1)} %pad_maximum_fusion.1.refs_0_), channel_id=1, source_target_pairs={{0,6},{1,25},{2,4},{3,27},{4,2},{5,29},{6,0},{7,31},{8,14},{9,17},... | collective-permute-start | bytes 393224 | tf_op jit(solution)/shard_map/ppermute | solution.py:46
  54.0 5.0 %collective-permute-start.11 = (bf16[512,128]{1,0:T(8,128)(2,1)S(1)}, bf16[512,128]{1,0:T(8,128)(2,1)S(1)}, u32[]{:S(2)}, u32[]{:S(2)}) collective-permute-start(bf16[512,128]{1,0:T(8,128)(2,1)S(1)} %pad_maximum_fusion.1.refs_0_), channel_id=1, source_target_pairs={{0,4},{1,17},{2,6},{3,19},{4,0},{5,21},{6,2},{7,23},{8,12},{9,25},... | collective-permute-start | bytes 393224 | tf_op jit(solution)/shard_map/ppermute | solution.py:46
  54.6 5.0 %collective-permute-start.10 = (bf16[512,128]{1,0:T(8,128)(2,1)S(1)}, bf16[512,128]{1,0:T(8,128)(2,1)S(1)}, u32[]{:S(2)}, u32[]{:S(2)}) collective-permute-start(bf16[512,128]{1,0:T(8,128)(2,1)S(1)} %pad_maximum_fusion.1.refs_0_), channel_id=1, source_target_pairs={{0,2},{1,9},{2,0},{3,11},{4,6},{5,13},{6,4},{7,15},{8,10},{9,1},{1... | collective-permute-start | bytes 393224 | tf_op jit(solution)/shard_map/ppermute | solution.py:46
  60.0 1.3 %collective-permute-start.13 = (f32[128,128]{1,0:T(8,128)S(1)}, f32[128,128]{1,0:T(8,128)S(1)}, u32[]{:S(2)}, u32[]{:S(2)}) collective-permute-start(f32[128,128]{1,0:T(8,128)S(1)} %get-tuple-element.16), channel_id=1, source_target_pairs={{0,1},{1,0},{2,3},{3,2},{4,5},{5,4},{6,7},{7,6},{8,9},{9,8},{10,11... | collective-permute-start | bytes 196616 | tf_op jit(solution)/shard_map/ppermute | solution.py:37
  61.3 5.8 %collective-permute-start.16 = (bf16[128,128]{1,0:T(8,128)(2,1)S(1)}, bf16[128,128]{1,0:T(8,128)(2,1)S(1)}, u32[]{:S(2)}, u32[]{:S(2)}) collective-permute-start(bf16[128,128]{1,0:T(8,128)(2,1)S(1)} %get-tuple-element.19), channel_id=1, source_target_pairs={{0,24},{1,7},{2,26},{3,5},{4,28},{5,3},{6,30},{7,1},{8,16},{9,15},... | collective-permute-start | bytes 98312 | tf_op jit(solution)/shard_map/ppermute | solution.py:46
  63.4 4.8 %collective-permute-start.15 = (bf16[128,128]{1,0:T(8,128)(2,1)S(1)}, bf16[128,128]{1,0:T(8,128)(2,1)S(1)}, u32[]{:S(2)}, u32[]{:S(2)}) collective-permute-start(bf16[128,128]{1,0:T(8,128)(2,1)S(1)} %get-tuple-element.19), channel_id=1, source_target_pairs={{0,16},{1,5},{2,18},{3,7},{4,20},{5,1},{6,22},{7,3},{8,24},{9,13},... | collective-permute-start | bytes 98312 | tf_op jit(solution)/shard_map/ppermute | solution.py:46
  64.5 4.0 %collective-permute-start.14 = (bf16[128,128]{1,0:T(8,128)(2,1)S(1)}, bf16[128,128]{1,0:T(8,128)(2,1)S(1)}, u32[]{:S(2)}, u32[]{:S(2)}) collective-permute-start(bf16[128,128]{1,0:T(8,128)(2,1)S(1)} %get-tuple-element.19), channel_id=1, source_target_pairs={{0,8},{1,3},{2,10},{3,1},{4,12},{5,7},{6,14},{7,5},{8,0},{9,11},{1... | collective-permute-start | bytes 98312 | tf_op jit(solution)/shard_map/ppermute | solution.py:46
  68.6 6.0 %collective-permute-start.19 = (bf16[512,128]{1,0:T(8,128)(2,1)S(1)}, bf16[512,128]{1,0:T(8,128)(2,1)S(1)}, u32[]{:S(2)}, u32[]{:S(2)}) collective-permute-start(bf16[512,128]{1,0:T(8,128)(2,1)S(1)} %pad_maximum_fusion.2.refs_0_), channel_id=1, source_target_pairs={{0,6},{1,25},{2,4},{3,27},{4,2},{5,29},{6,0},{7,31},{8,14},{9,17},... | collective-permute-start | bytes 393224 | tf_op jit(solution)/shard_map/ppermute | solution.py:46
  70.2 5.7 %collective-permute-start.18 = (bf16[512,128]{1,0:T(8,128)(2,1)S(1)}, bf16[512,128]{1,0:T(8,128)(2,1)S(1)}, u32[]{:S(2)}, u32[]{:S(2)}) collective-permute-start(bf16[512,128]{1,0:T(8,128)(2,1)S(1)} %pad_maximum_fusion.2.refs_0_), channel_id=1, source_target_pairs={{0,4},{1,17},{2,6},{3,19},{4,0},{5,21},{6,2},{7,23},{8,12},{9,25},... | collective-permute-start | bytes 393224 | tf_op jit(solution)/shard_map/ppermute | solution.py:46
  71.2 5.0 %collective-permute-start.17 = (bf16[512,128]{1,0:T(8,128)(2,1)S(1)}, bf16[512,128]{1,0:T(8,128)(2,1)S(1)}, u32[]{:S(2)}, u32[]{:S(2)}) collective-permute-start(bf16[512,128]{1,0:T(8,128)(2,1)S(1)} %pad_maximum_fusion.2.refs_0_), channel_id=1, source_target_pairs={{0,2},{1,9},{2,0},{3,11},{4,6},{5,13},{6,4},{7,15},{8,10},{9,1},{1... | collective-permute-start | bytes 393224 | tf_op jit(solution)/shard_map/ppermute | solution.py:46
  76.6 1.3 %collective-permute-start.20 = (f32[128,128]{1,0:T(8,128)S(1)}, f32[128,128]{1,0:T(8,128)S(1)}, u32[]{:S(2)}, u32[]{:S(2)}) collective-permute-start(f32[128,128]{1,0:T(8,128)S(1)} %get-tuple-element.18), channel_id=1, source_target_pairs={{0,1},{1,0},{2,3},{3,2},{4,5},{5,4},{6,7},{7,6},{8,9},{9,8},{10,11... | collective-permute-start | bytes 196616 | tf_op jit(solution)/shard_map/ppermute | solution.py:37

commit v8 on v7

--- a/solution.py
+++ b/solution.py
@@ -46,7 +46,11 @@
     return lax.ppermute(x, ("row", "col"), pairs)
 
 
-def build_tile(rows, cols, count, stacked, grid_rows, grid_cols):
+def cell_of(col_slot, row_slot, grid_rows, grid_cols, low):
+    return (col_slot % low * grid_cols + row_slot) * (grid_rows // low) + col_slot // low
+
+
+def build_tile(rows, cols, count, stacked, grid_rows, grid_cols, low):
     slots, orb, _ = stacked.shape
     chunk = CHUNK if slots % CHUNK == 0 else slots
     chunks = slots // chunk
@@ -77,7 +81,10 @@
         for n, copy in enumerate(copies):
             copy.wait()
             for s in range(n * chunk, (n + 1) * chunk):
-                cell = jnp.where(s < count, cols_ref[0, s] * grid_cols + rows_ref[0, s], cells)
+                col_slot = cols_ref[0, s]
+                fast = lax.shift_right_logical(col_slot, low.bit_length() - 1)
+                slow = (col_slot & (low - 1)) * grid_cols + rows_ref[0, s]
+                cell = jnp.where(s < count, slow * (grid_rows // low) + fast, cells)
                 acc_ref[cell] += held_ref[s].astype(jnp.float32)
 
         def put(cell, carry):
@@ -132,22 +139,21 @@
         outs[d][...] = total[d * orb : (d + 1) * orb] * scale
 
 
-def merge_apply(sources, places, targets, dense, received, panel, current, center, halfwidth):
-    cells, orb, _ = dense.shape
-    grid_rows = sources.shape[0]
-    grid_cols = targets.shape[0]
+def merge_apply(cells, places, dense, received, panel, current, center, halfwidth):
+    _, orb, _ = dense.shape
+    grid_rows = places.shape[0]
+    grid_cols = cells.shape[0] // grid_rows
     vectors = current.shape[1]
 
     def kernel(
-        sources_ref, places_ref, targets_ref, center_ref, halfwidth_ref,
+        cells_ref, places_ref, center_ref, halfwidth_ref,
         dense_ref, received_ref, panel_ref, current_ref, tile_ref, *outs,
     ):
         total = None
         for k in range(grid_rows):
             held = slice(k * orb, (k + 1) * orb)
-            first = sources_ref[k] * grid_cols
             for d in range(grid_cols):
-                cell = first + targets_ref[d]
+                cell = cells_ref[k * grid_cols + d]
                 turned = received_ref[cell].T.astype(jnp.float32)
                 block = (dense_ref[cell].astype(jnp.float32) + turned).astype(jnp.bfloat16)
                 tile_ref[d * orb : (d + 1) * orb, held] = block
@@ -161,13 +167,13 @@
     block = jax.ShapeDtypeStruct((orb, vectors), jnp.float32)
     return pl.pallas_call(
         kernel,
-        in_specs=[SMEM] * 5 + [VMEM] * 4,
+        in_specs=[SMEM] * 4 + [VMEM] * 4,
         out_specs=[VMEM] * (1 + grid_cols),
         out_shape=[jax.ShapeDtypeStruct((grid_cols * orb, grid_rows * orb), jnp.bfloat16)]
         + [block] * grid_cols,
         compiler_params=pltpu.CompilerParams(vmem_limit_bytes=dense.size * 6 + 2 * SPARE),
         name="merge_apply",
-    )(sources, places, targets, center, halfwidth, dense, received, panel, current)
+    )(cells, places, center, halfwidth, dense, received, panel, current)
 
 
 def apply_tile(tile, pieces, current, previous, center, halfwidth, grid_cols):
@@ -224,16 +230,22 @@
     sources = jnp.array(late, jnp.int32)[col % 2] ^ row
     places = jnp.array(places, jnp.int32)[col % 2]
     targets = jnp.arange(grid_cols, dtype=jnp.int32) ^ col
+    low = same[0][0][0]
+    cells = cell_of(sources[:, None], targets[None, :], grid_rows, grid_cols, low).reshape(-1)
+    everyone = [0] * (grid_rows * grid_cols)
+    for device in range(grid_rows * grid_cols):
+        cell = cell_of(device // grid_cols, device % grid_cols, grid_rows, grid_cols, low)
+        everyone[cell] = device
     pieces = gather([initial.astype(jnp.bfloat16)], same, last=1)
     dense = build_tile(
         block_rows[0], block_cols[0], block_counts, hamiltonian_blocks[0, 0],
-        grid_rows, grid_cols,
+        grid_rows, grid_cols, low,
     )
     dense = after(dense, pieces[1:])
-    received = lax.all_to_all(dense, ("row", "col"), 0, 0)
+    received = lax.all_to_all(dense, ("row", "col"), 0, 0, axis_index_groups=[everyone], tiled=True)
     panel = jnp.concatenate(gather(pieces, same, first=1), axis=0)
     tile, base, *others = merge_apply(
-        sources, places, targets, dense, received, panel, initial, center, halfwidth
+        cells, places, dense, received, panel, initial, center, halfwidth
     )
 
     previous = initial

time: 78.9 us -> 78.6 us (level)
  waiting for transfers between devices: 39.1 us -> 37.1 us
  starting transfers between devices: 30.9 us -> 32.4 us
    ppermute x3, starting transfers between devices: 0.21 us -> 1.75 us  [swap(): lax.ppermute(x, axis, [(source, source ^ offset) for source in range(size)])]
    ppermute x18, waiting for transfers between devices: 27.6 us -> 26.6 us  [swap_rows(): return lax.ppermute(x, ('row', 'col'), pairs)]
  transfers between devices with their start and end apart: 22 -> 22, of which waited for: 18 -> 16; matrix products, arithmetic and copies ran while one was open for 0% -> 0% of each run, Pallas kernels for 4% -> 4%
where the time goes in v8:
time: 78.6 us; the launch traced here: 78.3 us
  waiting for transfers between devices  37.1 us (47%)
  starting transfers between devices  32.4 us (41%)
  Pallas kernels  4.76 us (6%)
  between operations  2.16 us (3%)
  other arithmetic  1.66 us (2%)
    ppermute x18, waiting for transfers between devices, swap_rows(): return lax.ppermute(x, ('row', 'col'), pairs)  26.6 us
    ppermute x18, starting transfers between devices, swap_rows(): return lax.ppermute(x, ('row', 'col'), pairs)  25.3 us
    all_to_all x1, waiting for transfers between devices, body(): lax.all_to_all(dense, ('row', 'col'), 0, 0, axis_index_groups=[everyone],...  7.15 us
    all_to_all x1, starting transfers between devices, body(): lax.all_to_all(dense, ('row', 'col'), 0, 0, axis_index_groups=[everyone],...  5.34 us
    ppermute x3, waiting for transfers between devices, swap(): lax.ppermute(x, axis, [(source, source ^ offset) for source in range(size)])  3.38 us
    pallas_call x1, Pallas kernels, build_tile(): pl.pallas_call(kernel, in_specs=[HBM, HBM, SMEM, HBM], out_specs=VMEM, sc...  2.78 us
    ppermute x3, starting transfers between devices, swap(): lax.ppermute(x, axis, [(source, source ^ offset) for source in range(size)])  1.75 us
  transfers between devices with their start and end apart: 22, of which 16 were waited for; matrix products, arithmetic and copies ran while one was open for 0% of the time, Pallas kernels for 4%

profile of v8, /device:TPU:0, one launch (start us, length us, event | category | flops | bytes accessed | tf_op | source)
XLA Modules:
  0.0 78.3 jit_solution(3338323026329611049)
XLA Ops:
  0.0 0.8 %constant_dynamic-update-slice_fusion.6 = (bf16[2048,128]{1,0:T(8,128)(2,1)S(1)}, bf16[128,128]{1,0:T(8,128)(2,1)S(1)}) fusion(f32[128,128]{1,0:T(8,128)} %previous_ref.1), kind=kLoop, calls=%fused_computation.9 | loop fusion | flops 16383 | bytes 131072
  0.9 5.1 %collective-permute-start.2 = (bf16[128,128]{1,0:T(8,128)(2,1)S(1)}, bf16[128,128]{1,0:T(8,128)(2,1)S(1)}, u32[]{:S(2)}, u32[]{:S(2)}) collective-permute-start(bf16[128,128]{1,0:T(8,128)(2,1)S(1)} %get-tuple-element.24), channel_id=1, source_target_pairs={{0,24},{1,25},{2,26},{3,27},{4,28},{5,29},{6,30},{7,31},{8,16},{9,... | collective-permute-start | bytes 98312 | tf_op jit(solution)/shard_map/ppermute | solution.py:46
  6.0 0.6 collective-permute-start
  7.3 2.8 %build_tile.1.refs_0_ = bf16[32,128,128]{2,1,0:T(8,128)(2,1)} custom-call(s32[1,64]{1,0:T(1,128)} %bitcast.18, s32[1,64]{1,0:T(1,128)} %bitcast.19, s32[1,1]{1,0:T(1,128)S(6)} %copy.18.count_ref, bf16[64,128,128]{2,1,0:T(8,128)(2,1)} %bitcast.17), custom_call_target="tpu_custom_call" | custom-call | tf_op jit(solution)/shard_map/build_tile/pallas_call | solution.py:96
  10.0 0.0 copy-start.2
  10.1 0.0 copy-start.3
  10.1 0.7 collective-permute-done.1.refs_2_
  10.8 5.3 %all-to-all-start = ((bf16[32,128,128]{2,1,0:T(8,128)(2,1)}), bf16[32,128,128]{2,1,0:T(8,128)(2,1)S(1)}, u32[]{:S(2)}, u32[]{:S(2)}) async-start(bf16[32,128,128]{2,1,0:T(8,128)(2,1)} %after.1.dense_ref), calls=%async_computation | async-start | bytes 2097152 | tf_op jit(solution)/shard_map/all_to_all | solution.py:245
  17.5 0.1 multiply_add_fusion
  17.6 0.1 add.70.cells_ref
  17.7 2.7 %collective-permute-start.5 = (bf16[512,128]{1,0:T(8,128)(2,1)S(1)}, bf16[512,128]{1,0:T(8,128)(2,1)S(1)}, u32[]{:S(2)}, u32[]{:S(2)}) collective-permute-start(bf16[512,128]{1,0:T(8,128)(2,1)S(1)} %pad_maximum_fusion), channel_id=1, source_target_pairs={{0,6},{1,7},{2,4},{3,5},{4,2},{5,3},{6,0},{7,1},{8,14},{9,15},{10,... | collective-permute-start | bytes 393224 | tf_op jit(solution)/shard_map/ppermute | solution.py:46
  20.5 0.6 collective-permute-start.4
  21.0 0.3 collective-permute-start.3
  21.3 12.6 %collective-permute-done.3 = bf16[512,128]{1,0:T(8,128)(2,1)S(1)} collective-permute-done((bf16[512,128]{1,0:T(8,128)(2,1)S(1)}, bf16[512,128]{1,0:T(8,128)(2,1)S(1)}, u32[]{:S(2)}, u32[]{:S(2)}) %collective-permute-start.3) | collective-permute-done | bytes 131104 | tf_op jit(solution)/shard_map/ppermute | solution.py:46
  34.1 7.1 %all-to-all-done.received_ref = bf16[32,128,128]{2,1,0:T(8,128)(2,1)S(1)} async-done(((bf16[32,128,128]{2,1,0:T(8,128)(2,1)}), bf16[32,128,128]{2,1,0:T(8,128)(2,1)S(1)}, u32[]{:S(2)}, u32[]{:S(2)}) %all-to-all-start) | async-done | bytes 1048608 | tf_op jit(solution)/shard_map/all_to_all | solution.py:245
  41.2 1.1 %merge_apply.1 = (bf16[256,2048]{1,0:T(8,128)(2,1)S(1)}, f32[128,128]{1,0:T(8,128)S(1)}, f32[128,128]{1,0:T(8,128)S(1)}) custom-call(s32[32]{0:T(128)S(1)} %add.70.cells_ref, s32[16]{0:T(128)S(1)} %dynamic-slice_bitcast_fusion.places_ref, f32[1]{0:T(128)S(6)} %copy.19.center_ref, f32[1]{0:T(128)S(6)} %copy.20.halfwidth_ref, ...), custom_call_target="tpu_custom_call" | custom-call | tf_op jit(solution)/shard_map/merge_apply/pallas_call | solution.py:168
  42.4 1.6 %collective-permute-start.6 = (f32[128,128]{1,0:T(8,128)S(1)}, f32[128,128]{1,0:T(8,128)S(1)}, u32[]{:S(2)}, u32[]{:S(2)}) collective-permute-start(f32[128,128]{1,0:T(8,128)S(1)} %get-tuple-element.14), channel_id=1, source_target_pairs={{0,1},{1,0},{2,3},{3,2},{4,5},{5,4},{6,7},{7,6},{8,9},{9,8},{10,11... | collective-permute-start | bytes 196616 | tf_op jit(solution)/shard_map/ppermute | solution.py:37
  44.0 0.9 %collective-permute-done.6 = f32[128,128]{1,0:T(8,128)S(1)} collective-permute-done((f32[128,128]{1,0:T(8,128)S(1)}, f32[128,128]{1,0:T(8,128)S(1)}, u32[]{:S(2)}, u32[]{:S(2)}) %collective-permute-start.6) | collective-permute-done | bytes 65568 | tf_op jit(solution)/shard_map/ppermute | solution.py:37
  44.9 2.1 %collective-permute-start.9 = (bf16[128,128]{1,0:T(8,128)(2,1)S(1)}, bf16[128,128]{1,0:T(8,128)(2,1)S(1)}, u32[]{:S(2)}, u32[]{:S(2)}) collective-permute-start(bf16[128,128]{1,0:T(8,128)(2,1)S(1)} %get-tuple-element.21), channel_id=1, source_target_pairs={{0,24},{1,7},{2,26},{3,5},{4,28},{5,3},{6,30},{7,1},{8,16},{9,15},... | collective-permute-start | bytes 98312 | tf_op jit(solution)/shard_map/ppermute | solution.py:46
  46.9 1.4 %collective-permute-start.8 = (bf16[128,128]{1,0:T(8,128)(2,1)S(1)}, bf16[128,128]{1,0:T(8,128)(2,1)S(1)}, u32[]{:S(2)}, u32[]{:S(2)}) collective-permute-start(bf16[128,128]{1,0:T(8,128)(2,1)S(1)} %get-tuple-element.21), channel_id=1, source_target_pairs={{0,16},{1,5},{2,18},{3,7},{4,20},{5,1},{6,22},{7,3},{8,24},{9,13},... | collective-permute-start | bytes 98312 | tf_op jit(solution)/shard_map/ppermute | solution.py:46
  48.3 1.0 %collective-permute-start.7 = (bf16[128,128]{1,0:T(8,128)(2,1)S(1)}, bf16[128,128]{1,0:T(8,128)(2,1)S(1)}, u32[]{:S(2)}, u32[]{:S(2)}) collective-permute-start(bf16[128,128]{1,0:T(8,128)(2,1)S(1)} %get-tuple-element.21), channel_id=1, source_target_pairs={{0,8},{1,3},{2,10},{3,1},{4,12},{5,7},{6,14},{7,5},{8,0},{9,11},{1... | collective-permute-start | bytes 98312 | tf_op jit(solution)/shard_map/ppermute | solution.py:46
  49.3 1.3 %collective-permute-done.9 = bf16[128,128]{1,0:T(8,128)(2,1)S(1)} collective-permute-done((bf16[128,128]{1,0:T(8,128)(2,1)S(1)}, bf16[128,128]{1,0:T(8,128)(2,1)S(1)}, u32[]{:S(2)}, u32[]{:S(2)}) %collective-permute-start.9) | collective-permute-done | bytes 32800 | tf_op jit(solution)/shard_map/ppermute | solution.py:46
  50.7 1.1 %collective-permute-done.8 = bf16[128,128]{1,0:T(8,128)(2,1)S(1)} collective-permute-done((bf16[128,128]{1,0:T(8,128)(2,1)S(1)}, bf16[128,128]{1,0:T(8,128)(2,1)S(1)}, u32[]{:S(2)}, u32[]{:S(2)}) %collective-permute-start.8) | collective-permute-done | bytes 32800 | tf_op jit(solution)/shard_map/ppermute | solution.py:46
  51.8 0.5 collective-permute-done.7
  52.2 1.0 %collective-permute-start.12 = (bf16[512,128]{1,0:T(8,128)(2,1)S(1)}, bf16[512,128]{1,0:T(8,128)(2,1)S(1)}, u32[]{:S(2)}, u32[]{:S(2)}) collective-permute-start(bf16[512,128]{1,0:T(8,128)(2,1)S(1)} %pad_maximum_fusion.1.refs_0_), channel_id=1, source_target_pairs={{0,6},{1,25},{2,4},{3,27},{4,2},{5,29},{6,0},{7,31},{8,14},{9,17},... | collective-permute-start | bytes 393224 | tf_op jit(solution)/shard_map/ppermute | solution.py:46
  53.2 1.5 %collective-permute-start.11 = (bf16[512,128]{1,0:T(8,128)(2,1)S(1)}, bf16[512,128]{1,0:T(8,128)(2,1)S(1)}, u32[]{:S(2)}, u32[]{:S(2)}) collective-permute-start(bf16[512,128]{1,0:T(8,128)(2,1)S(1)} %pad_maximum_fusion.1.refs_0_), channel_id=1, source_target_pairs={{0,4},{1,17},{2,6},{3,19},{4,0},{5,21},{6,2},{7,23},{8,12},{9,25},... | collective-permute-start | bytes 393224 | tf_op jit(solution)/shard_map/ppermute | solution.py:46
  54.8 1.0 %collective-permute-start.10 = (bf16[512,128]{1,0:T(8,128)(2,1)S(1)}, bf16[512,128]{1,0:T(8,128)(2,1)S(1)}, u32[]{:S(2)}, u32[]{:S(2)}) collective-permute-start(bf16[512,128]{1,0:T(8,128)(2,1)S(1)} %pad_maximum_fusion.1.refs_0_), channel_id=1, source_target_pairs={{0,2},{1,9},{2,0},{3,11},{4,6},{5,13},{6,4},{7,15},{8,10},{9,1},{1... | collective-permute-start | bytes 393224 | tf_op jit(solution)/shard_map/ppermute | solution.py:46
  55.8 2.5 %collective-permute-done.12.refs_3_ = bf16[512,128]{1,0:T(8,128)(2,1)S(1)} collective-permute-done((bf16[512,128]{1,0:T(8,128)(2,1)S(1)}, bf16[512,128]{1,0:T(8,128)(2,1)S(1)}, u32[]{:S(2)}, u32[]{:S(2)}) %collective-permute-start.12) | collective-permute-done | bytes 131104 | tf_op jit(solution)/shard_map/ppermute | solution.py:46
  58.3 1.3 %collective-permute-done.11.refs_2_ = bf16[512,128]{1,0:T(8,128)(2,1)S(1)} collective-permute-done((bf16[512,128]{1,0:T(8,128)(2,1)S(1)}, bf16[512,128]{1,0:T(8,128)(2,1)S(1)}, u32[]{:S(2)}, u32[]{:S(2)}) %collective-permute-start.11) | collective-permute-done | bytes 131104 | tf_op jit(solution)/shard_map/ppermute | solution.py:46
  59.6 0.2 collective-permute-done.10.refs_1_
  59.7 0.4 apply_tile.2
  60.2 0.1 collective-permute-start.13
  60.2 1.2 %collective-permute-done.13 = f32[128,128]{1,0:T(8,128)S(1)} collective-permute-done((f32[128,128]{1,0:T(8,128)S(1)}, f32[128,128]{1,0:T(8,128)S(1)}, u32[]{:S(2)}, u32[]{:S(2)}) %collective-permute-start.13) | collective-permute-done | bytes 65568 | tf_op jit(solution)/shard_map/ppermute | solution.py:37
  61.5 1.9 %collective-permute-start.16 = (bf16[128,128]{1,0:T(8,128)(2,1)S(1)}, bf16[128,128]{1,0:T(8,128)(2,1)S(1)}, u32[]{:S(2)}, u32[]{:S(2)}) collective-permute-start(bf16[128,128]{1,0:T(8,128)(2,1)S(1)} %get-tuple-element.19), channel_id=1, source_target_pairs={{0,24},{1,7},{2,26},{3,5},{4,28},{5,3},{6,30},{7,1},{8,16},{9,15},... | collective-permute-start | bytes 98312 | tf_op jit(solution)/shard_map/ppermute | solution.py:46
  63.4 1.1 %collective-permute-start.15 = (bf16[128,128]{1,0:T(8,128)(2,1)S(1)}, bf16[128,128]{1,0:T(8,128)(2,1)S(1)}, u32[]{:S(2)}, u32[]{:S(2)}) collective-permute-start(bf16[128,128]{1,0:T(8,128)(2,1)S(1)} %get-tuple-element.19), channel_id=1, source_target_pairs={{0,16},{1,5},{2,18},{3,7},{4,20},{5,1},{6,22},{7,3},{8,24},{9,13},... | collective-permute-start | bytes 98312 | tf_op jit(solution)/shard_map/ppermute | solution.py:46
  64.5 1.4 %collective-permute-start.14 = (bf16[128,128]{1,0:T(8,128)(2,1)S(1)}, bf16[128,128]{1,0:T(8,128)(2,1)S(1)}, u32[]{:S(2)}, u32[]{:S(2)}) collective-permute-start(bf16[128,128]{1,0:T(8,128)(2,1)S(1)} %get-tuple-element.19), channel_id=1, source_target_pairs={{0,8},{1,3},{2,10},{3,1},{4,12},{5,7},{6,14},{7,5},{8,0},{9,11},{1... | collective-permute-start | bytes 98312 | tf_op jit(solution)/shard_map/ppermute | solution.py:46
  65.9 1.3 %collective-permute-done.16 = bf16[128,128]{1,0:T(8,128)(2,1)S(1)} collective-permute-done((bf16[128,128]{1,0:T(8,128)(2,1)S(1)}, bf16[128,128]{1,0:T(8,128)(2,1)S(1)}, u32[]{:S(2)}, u32[]{:S(2)}) %collective-permute-start.16) | collective-permute-done | bytes 32800 | tf_op jit(solution)/shard_map/ppermute | solution.py:46
  67.3 1.3 %collective-permute-done.15 = bf16[128,128]{1,0:T(8,128)(2,1)S(1)} collective-permute-done((bf16[128,128]{1,0:T(8,128)(2,1)S(1)}, bf16[128,128]{1,0:T(8,128)(2,1)S(1)}, u32[]{:S(2)}, u32[]{:S(2)}) %collective-permute-start.15) | collective-permute-done | bytes 32800 | tf_op jit(solution)/shard_map/ppermute | solution.py:46
  68.6 0.0 collective-permute-done.14
  68.6 1.5 %collective-permute-start.19 = (bf16[512,128]{1,0:T(8,128)(2,1)S(1)}, bf16[512,128]{1,0:T(8,128)(2,1)S(1)}, u32[]{:S(2)}, u32[]{:S(2)}) collective-permute-start(bf16[512,128]{1,0:T(8,128)(2,1)S(1)} %pad_maximum_fusion.2.refs_0_), channel_id=1, source_target_pairs={{0,6},{1,25},{2,4},{3,27},{4,2},{5,29},{6,0},{7,31},{8,14},{9,17},... | collective-permute-start | bytes 393224 | tf_op jit(solution)/shard_map/ppermute | solution.py:46
  70.1 0.8 %collective-permute-start.18 = (bf16[512,128]{1,0:T(8,128)(2,1)S(1)}, bf16[512,128]{1,0:T(8,128)(2,1)S(1)}, u32[]{:S(2)}, u32[]{:S(2)}) collective-permute-start(bf16[512,128]{1,0:T(8,128)(2,1)S(1)} %pad_maximum_fusion.2.refs_0_), channel_id=1, source_target_pairs={{0,4},{1,17},{2,6},{3,19},{4,0},{5,21},{6,2},{7,23},{8,12},{9,25},... | collective-permute-start | bytes 393224 | tf_op jit(solution)/shard_map/ppermute | solution.py:46
  71.0 1.2 %collective-permute-start.17 = (bf16[512,128]{1,0:T(8,128)(2,1)S(1)}, bf16[512,128]{1,0:T(8,128)(2,1)S(1)}, u32[]{:S(2)}, u32[]{:S(2)}) collective-permute-start(bf16[512,128]{1,0:T(8,128)(2,1)S(1)} %pad_maximum_fusion.2.refs_0_), channel_id=1, source_target_pairs={{0,2},{1,9},{2,0},{3,11},{4,6},{5,13},{6,4},{7,15},{8,10},{9,1},{1... | collective-permute-start | bytes 393224 | tf_op jit(solution)/shard_map/ppermute | solution.py:46
  72.1 2.5 %collective-permute-done.19.refs_3_ = bf16[512,128]{1,0:T(8,128)(2,1)S(1)} collective-permute-done((bf16[512,128]{1,0:T(8,128)(2,1)S(1)}, bf16[512,128]{1,0:T(8,128)(2,1)S(1)}, u32[]{:S(2)}, u32[]{:S(2)}) %collective-permute-start.19) | collective-permute-done | bytes 131104 | tf_op jit(solution)/shard_map/ppermute | solution.py:46
  74.6 1.3 %collective-permute-done.18.refs_2_ = bf16[512,128]{1,0:T(8,128)(2,1)S(1)} collective-permute-done((bf16[512,128]{1,0:T(8,128)(2,1)S(1)}, bf16[512,128]{1,0:T(8,128)(2,1)S(1)}, u32[]{:S(2)}, u32[]{:S(2)}) %collective-permute-start.18) | collective-permute-done | bytes 131104 | tf_op jit(solution)/shard_map/ppermute | solution.py:46
  75.9 0.4 apply_tile.3
  76.4 0.1 collective-permute-start.20
  76.4 1.2 %collective-permute-done.20 = f32[128,128]{1,0:T(8,128)S(1)} collective-permute-done((f32[128,128]{1,0:T(8,128)S(1)}, f32[128,128]{1,0:T(8,128)S(1)}, u32[]{:S(2)}, u32[]{:S(2)}) %collective-permute-start.20) | collective-permute-done | bytes 65568 | tf_op jit(solution)/shard_map/ppermute | solution.py:37
  77.7 0.6 add.73
  (28 shorter events, 0.2 us)
Async XLA Ops:
  0.9 9.2 %collective-permute-start.2 = (bf16[128,128]{1,0:T(8,128)(2,1)S(1)}, bf16[128,128]{1,0:T(8,128)(2,1)S(1)}, u32[]{:S(2)}, u32[]{:S(2)}) collective-permute-start(bf16[128,128]{1,0:T(8,128)(2,1)S(1)} %get-tuple-element.24), channel_id=1, source_target_pairs={{0,24},{1,25},{2,26},{3,27},{4,28},{5,29},{6,30},{7,31},{8,16},{9,... | collective-permute-start | bytes 98312 | tf_op jit(solution)/shard_map/ppermute | solution.py:46
  6.0 4.8 %collective-permute-start.1 = (bf16[128,128]{1,0:T(8,128)(2,1)S(1)}, bf16[128,128]{1,0:T(8,128)(2,1)S(1)}, u32[]{:S(2)}, u32[]{:S(2)}) collective-permute-start(bf16[128,128]{1,0:T(8,128)(2,1)S(1)} %get-tuple-element.24), channel_id=1, source_target_pairs={{0,16},{1,17},{2,18},{3,19},{4,20},{5,21},{6,22},{7,23},{8,24},{9,... | collective-permute-start | bytes 98312 | tf_op jit(solution)/shard_map/ppermute | solution.py:46
  6.0 4.8 %collective-permute-start = (bf16[128,128]{1,0:T(8,128)(2,1)S(1)}, bf16[128,128]{1,0:T(8,128)(2,1)S(1)}, u32[]{:S(2)}, u32[]{:S(2)}) collective-permute-start(bf16[128,128]{1,0:T(8,128)(2,1)S(1)} %get-tuple-element.24), channel_id=1, source_target_pairs={{0,8},{1,9},{2,10},{3,11},{4,12},{5,13},{6,14},{7,15},{8,0},{9,1},... | collective-permute-start | bytes 98312 | tf_op jit(solution)/shard_map/ppermute | solution.py:46
  10.0 7.4 %copy-start.2 = (s32[2,16]{1,0:T(2,128)S(1)}, s32[2,16]{1,0:T(2,128)}, u32[]{:S(2)}) copy-start(s32[2,16]{1,0:T(2,128)} %constant.55.clone) | copy-start | bytes 388
  10.1 7.6 %copy-start.3 = (s32[2,16]{1,0:T(2,128)S(1)}, s32[2,16]{1,0:T(2,128)}, u32[]{:S(2)}) copy-start(s32[2,16]{1,0:T(2,128)} %constant.56.clone) | copy-start | bytes 388
  10.8 30.4 %copy-start = (bf16[32,128,128]{2,1,0:T(8,128)(2,1)S(1)}, bf16[32,128,128]{2,1,0:T(8,128)(2,1)}, u32[]{:S(2)}) copy-start(bf16[32,128,128]{2,1,0:T(8,128)(2,1)} %after.1.dense_ref) | copy-start | bytes 3145732
  10.8 30.4 %copy-start.1 = (f32[128,128]{1,0:T(8,128)S(1)}, f32[128,128]{1,0:T(8,128)}, u32[]{:S(2)}) copy-start(f32[128,128]{1,0:T(8,128)} %previous_ref.1) | copy-start | bytes 196612
  10.8 30.4 %all-to-all-start = ((bf16[32,128,128]{2,1,0:T(8,128)(2,1)}), bf16[32,128,128]{2,1,0:T(8,128)(2,1)S(1)}, u32[]{:S(2)}, u32[]{:S(2)}) async-start(bf16[32,128,128]{2,1,0:T(8,128)(2,1)} %after.1.dense_ref), calls=%async_computation | async-start | bytes 2097152 | tf_op jit(solution)/shard_map/all_to_all | solution.py:245
  17.7 16.3 %collective-permute-start.5 = (bf16[512,128]{1,0:T(8,128)(2,1)S(1)}, bf16[512,128]{1,0:T(8,128)(2,1)S(1)}, u32[]{:S(2)}, u32[]{:S(2)}) collective-permute-start(bf16[512,128]{1,0:T(8,128)(2,1)S(1)} %pad_maximum_fusion), channel_id=1, source_target_pairs={{0,6},{1,7},{2,4},{3,5},{4,2},{5,3},{6,0},{7,1},{8,14},{9,15},{10,... | collective-permute-start | bytes 393224 | tf_op jit(solution)/shard_map/ppermute | solution.py:46
  20.5 13.5 %collective-permute-start.4 = (bf16[512,128]{1,0:T(8,128)(2,1)S(1)}, bf16[512,128]{1,0:T(8,128)(2,1)S(1)}, u32[]{:S(2)}, u32[]{:S(2)}) collective-permute-start(bf16[512,128]{1,0:T(8,128)(2,1)S(1)} %pad_maximum_fusion), channel_id=1, source_target_pairs={{0,4},{1,5},{2,6},{3,7},{4,0},{5,1},{6,2},{7,3},{8,12},{9,13},{10,... | collective-permute-start | bytes 393224 | tf_op jit(solution)/shard_map/ppermute | solution.py:46
  21.0 12.9 %collective-permute-start.3 = (bf16[512,128]{1,0:T(8,128)(2,1)S(1)}, bf16[512,128]{1,0:T(8,128)(2,1)S(1)}, u32[]{:S(2)}, u32[]{:S(2)}) collective-permute-start(bf16[512,128]{1,0:T(8,128)(2,1)S(1)} %pad_maximum_fusion), channel_id=1, source_target_pairs={{0,2},{1,3},{2,0},{3,1},{4,6},{5,7},{6,4},{7,5},{8,10},{9,11},{10,... | collective-permute-start | bytes 393224 | tf_op jit(solution)/shard_map/ppermute | solution.py:46
  42.4 2.5 %collective-permute-start.6 = (f32[128,128]{1,0:T(8,128)S(1)}, f32[128,128]{1,0:T(8,128)S(1)}, u32[]{:S(2)}, u32[]{:S(2)}) collective-permute-start(f32[128,128]{1,0:T(8,128)S(1)} %get-tuple-element.14), channel_id=1, source_target_pairs={{0,1},{1,0},{2,3},{3,2},{4,5},{5,4},{6,7},{7,6},{8,9},{9,8},{10,11... | collective-permute-start | bytes 196616 | tf_op jit(solution)/shard_map/ppermute | solution.py:37
  44.9 5.8 %collective-permute-start.9 = (bf16[128,128]{1,0:T(8,128)(2,1)S(1)}, bf16[128,128]{1,0:T(8,128)(2,1)S(1)}, u32[]{:S(2)}, u32[]{:S(2)}) collective-permute-start(bf16[128,128]{1,0:T(8,128)(2,1)S(1)} %get-tuple-element.21), channel_id=1, source_target_pairs={{0,24},{1,7},{2,26},{3,5},{4,28},{5,3},{6,30},{7,1},{8,16},{9,15},... | collective-permute-start | bytes 98312 | tf_op jit(solution)/shard_map/ppermute | solution.py:46
  46.9 4.8 %collective-permute-start.8 = (bf16[128,128]{1,0:T(8,128)(2,1)S(1)}, bf16[128,128]{1,0:T(8,128)(2,1)S(1)}, u32[]{:S(2)}, u32[]{:S(2)}) collective-permute-start(bf16[128,128]{1,0:T(8,128)(2,1)S(1)} %get-tuple-element.21), channel_id=1, source_target_pairs={{0,16},{1,5},{2,18},{3,7},{4,20},{5,1},{6,22},{7,3},{8,24},{9,13},... | collective-permute-start | bytes 98312 | tf_op jit(solution)/shard_map/ppermute | solution.py:46
  48.3 3.9 %collective-permute-start.7 = (bf16[128,128]{1,0:T(8,128)(2,1)S(1)}, bf16[128,128]{1,0:T(8,128)(2,1)S(1)}, u32[]{:S(2)}, u32[]{:S(2)}) collective-permute-start(bf16[128,128]{1,0:T(8,128)(2,1)S(1)} %get-tuple-element.21), channel_id=1, source_target_pairs={{0,8},{1,3},{2,10},{3,1},{4,12},{5,7},{6,14},{7,5},{8,0},{9,11},{1... | collective-permute-start | bytes 98312 | tf_op jit(solution)/shard_map/ppermute | solution.py:46
  52.2 6.0 %collective-permute-start.12 = (bf16[512,128]{1,0:T(8,128)(2,1)S(1)}, bf16[512,128]{1,0:T(8,128)(2,1)S(1)}, u32[]{:S(2)}, u32[]{:S(2)}) collective-permute-start(bf16[512,128]{1,0:T(8,128)(2,1)S(1)} %pad_maximum_fusion.1.refs_0_), channel_id=1, source_target_pairs={{0,6},{1,25},{2,4},{3,27},{4,2},{5,29},{6,0},{7,31},{8,14},{9,17},... | collective-permute-start | bytes 393224 | tf_op jit(solution)/shard_map/ppermute | solution.py:46
  53.2 6.3 %collective-permute-start.11 = (bf16[512,128]{1,0:T(8,128)(2,1)S(1)}, bf16[512,128]{1,0:T(8,128)(2,1)S(1)}, u32[]{:S(2)}, u32[]{:S(2)}) collective-permute-start(bf16[512,128]{1,0:T(8,128)(2,1)S(1)} %pad_maximum_fusion.1.refs_0_), channel_id=1, source_target_pairs={{0,4},{1,17},{2,6},{3,19},{4,0},{5,21},{6,2},{7,23},{8,12},{9,25},... | collective-permute-start | bytes 393224 | tf_op jit(solution)/shard_map/ppermute | solution.py:46
  54.8 5.0 %collective-permute-start.10 = (bf16[512,128]{1,0:T(8,128)(2,1)S(1)}, bf16[512,128]{1,0:T(8,128)(2,1)S(1)}, u32[]{:S(2)}, u32[]{:S(2)}) collective-permute-start(bf16[512,128]{1,0:T(8,128)(2,1)S(1)} %pad_maximum_fusion.1.refs_0_), channel_id=1, source_target_pairs={{0,2},{1,9},{2,0},{3,11},{4,6},{5,13},{6,4},{7,15},{8,10},{9,1},{1... | collective-permute-start | bytes 393224 | tf_op jit(solution)/shard_map/ppermute | solution.py:46
  60.2 1.3 %collective-permute-start.13 = (f32[128,128]{1,0:T(8,128)S(1)}, f32[128,128]{1,0:T(8,128)S(1)}, u32[]{:S(2)}, u32[]{:S(2)}) collective-permute-start(f32[128,128]{1,0:T(8,128)S(1)} %get-tuple-element.16), channel_id=1, source_target_pairs={{0,1},{1,0},{2,3},{3,2},{4,5},{5,4},{6,7},{7,6},{8,9},{9,8},{10,11... | collective-permute-start | bytes 196616 | tf_op jit(solution)/shard_map/ppermute | solution.py:37
  61.5 5.8 %collective-permute-start.16 = (bf16[128,128]{1,0:T(8,128)(2,1)S(1)}, bf16[128,128]{1,0:T(8,128)(2,1)S(1)}, u32[]{:S(2)}, u32[]{:S(2)}) collective-permute-start(bf16[128,128]{1,0:T(8,128)(2,1)S(1)} %get-tuple-element.19), channel_id=1, source_target_pairs={{0,24},{1,7},{2,26},{3,5},{4,28},{5,3},{6,30},{7,1},{8,16},{9,15},... | collective-permute-start | bytes 98312 | tf_op jit(solution)/shard_map/ppermute | solution.py:46
  63.4 5.2 %collective-permute-start.15 = (bf16[128,128]{1,0:T(8,128)(2,1)S(1)}, bf16[128,128]{1,0:T(8,128)(2,1)S(1)}, u32[]{:S(2)}, u32[]{:S(2)}) collective-permute-start(bf16[128,128]{1,0:T(8,128)(2,1)S(1)} %get-tuple-element.19), channel_id=1, source_target_pairs={{0,16},{1,5},{2,18},{3,7},{4,20},{5,1},{6,22},{7,3},{8,24},{9,13},... | collective-permute-start | bytes 98312 | tf_op jit(solution)/shard_map/ppermute | solution.py:46
  64.5 4.0 %collective-permute-start.14 = (bf16[128,128]{1,0:T(8,128)(2,1)S(1)}, bf16[128,128]{1,0:T(8,128)(2,1)S(1)}, u32[]{:S(2)}, u32[]{:S(2)}) collective-permute-start(bf16[128,128]{1,0:T(8,128)(2,1)S(1)} %get-tuple-element.19), channel_id=1, source_target_pairs={{0,8},{1,3},{2,10},{3,1},{4,12},{5,7},{6,14},{7,5},{8,0},{9,11},{1... | collective-permute-start | bytes 98312 | tf_op jit(solution)/shard_map/ppermute | solution.py:46
  68.6 6.0 %collective-permute-start.19 = (bf16[512,128]{1,0:T(8,128)(2,1)S(1)}, bf16[512,128]{1,0:T(8,128)(2,1)S(1)}, u32[]{:S(2)}, u32[]{:S(2)}) collective-permute-start(bf16[512,128]{1,0:T(8,128)(2,1)S(1)} %pad_maximum_fusion.2.refs_0_), channel_id=1, source_target_pairs={{0,6},{1,25},{2,4},{3,27},{4,2},{5,29},{6,0},{7,31},{8,14},{9,17},... | collective-permute-start | bytes 393224 | tf_op jit(solution)/shard_map/ppermute | solution.py:46
  70.1 5.8 %collective-permute-start.18 = (bf16[512,128]{1,0:T(8,128)(2,1)S(1)}, bf16[512,128]{1,0:T(8,128)(2,1)S(1)}, u32[]{:S(2)}, u32[]{:S(2)}) collective-permute-start(bf16[512,128]{1,0:T(8,128)(2,1)S(1)} %pad_maximum_fusion.2.refs_0_), channel_id=1, source_target_pairs={{0,4},{1,17},{2,6},{3,19},{4,0},{5,21},{6,2},{7,23},{8,12},{9,25},... | collective-permute-start | bytes 393224 | tf_op jit(solution)/shard_map/ppermute | solution.py:46
  71.0 5.0 %collective-permute-start.17 = (bf16[512,128]{1,0:T(8,128)(2,1)S(1)}, bf16[512,128]{1,0:T(8,128)(2,1)S(1)}, u32[]{:S(2)}, u32[]{:S(2)}) collective-permute-start(bf16[512,128]{1,0:T(8,128)(2,1)S(1)} %pad_maximum_fusion.2.refs_0_), channel_id=1, source_target_pairs={{0,2},{1,9},{2,0},{3,11},{4,6},{5,13},{6,4},{7,15},{8,10},{9,1},{1... | collective-permute-start | bytes 393224 | tf_op jit(solution)/shard_map/ppermute | solution.py:46
  76.4 1.3 %collective-permute-start.20 = (f32[128,128]{1,0:T(8,128)S(1)}, f32[128,128]{1,0:T(8,128)S(1)}, u32[]{:S(2)}, u32[]{:S(2)}) collective-permute-start(f32[128,128]{1,0:T(8,128)S(1)} %get-tuple-element.18), channel_id=1, source_target_pairs={{0,1},{1,0},{2,3},{3,2},{4,5},{5,4},{6,7},{7,6},{8,9},{9,8},{10,11... | collective-permute-start | bytes 196616 | tf_op jit(solution)/shard_map/ppermute | solution.py:37

commit v9 on v7

--- a/solution.py
+++ b/solution.py
@@ -124,50 +124,138 @@
     )(pltpu.with_memory_space_constraint(x, pltpu.HBM), *others)
 
 
-def finish(total, first, orb, current_ref, previous_ref, center_ref, halfwidth_ref, outs):
-    scale = (1.0 if first else 2.0) / jnp.full((1, total.shape[1]), halfwidth_ref[0])
-    own = (total[:orb] - center_ref[0] * current_ref[...]) * scale
-    outs[0][...] = own if first else own - previous_ref[...]
-    for d in range(1, len(outs)):
-        outs[d][...] = total[d * orb : (d + 1) * orb] * scale
-
-
-def merge_apply(sources, places, targets, dense, received, panel, current, center, halfwidth):
+def finish(own, first, current_ref, previous_ref, center_ref, halfwidth_ref):
+    scale = (1.0 if first else 2.0) / jnp.full((1, own.shape[1]), halfwidth_ref[0])
+    own = (own - center_ref[0] * current_ref[...]) * scale
+    return own if first else own - previous_ref[...], scale
+
+
+def forward_first(sources, targets, dense, panel, current, center, halfwidth):
     cells, orb, _ = dense.shape
     grid_rows = sources.shape[0]
     grid_cols = targets.shape[0]
     vectors = current.shape[1]
 
     def kernel(
-        sources_ref, places_ref, targets_ref, center_ref, halfwidth_ref,
-        dense_ref, received_ref, panel_ref, current_ref, tile_ref, *outs,
+        sources_ref, targets_ref, center_ref, halfwidth_ref,
+        dense_ref, panel_ref, current_ref, *refs,
     ):
+        *outs, total_ref = refs
         total = None
         for k in range(grid_rows):
-            held = slice(k * orb, (k + 1) * orb)
-            first = sources_ref[k] * grid_cols
-            for d in range(grid_cols):
-                cell = first + targets_ref[d]
-                turned = received_ref[cell].T.astype(jnp.float32)
-                block = (dense_ref[cell].astype(jnp.float32) + turned).astype(jnp.bfloat16)
-                tile_ref[d * orb : (d + 1) * orb, held] = block
-            place = pl.ds(pl.multiple_of(places_ref[k] * orb, orb), orb)
+            blocks = dense_ref[pl.ds(sources_ref[k] * grid_cols, grid_cols)]
             part = jnp.dot(
-                tile_ref[:, held], panel_ref[place, :], preferred_element_type=jnp.float32
+                blocks.reshape(grid_cols * orb, orb), panel_ref[k * orb : (k + 1) * orb],
+                preferred_element_type=jnp.float32,
             )
             total = part if total is None else total + part
-        finish(total, True, orb, current_ref, None, center_ref, halfwidth_ref, outs)
-
-    block = jax.ShapeDtypeStruct((orb, vectors), jnp.float32)
-    return pl.pallas_call(
-        kernel,
-        in_specs=[SMEM] * 5 + [VMEM] * 4,
-        out_specs=[VMEM] * (1 + grid_cols),
-        out_shape=[jax.ShapeDtypeStruct((grid_cols * orb, grid_rows * orb), jnp.bfloat16)]
-        + [block] * grid_cols,
-        compiler_params=pltpu.CompilerParams(vmem_limit_bytes=dense.size * 6 + 2 * SPARE),
-        name="merge_apply",
-    )(sources, places, targets, center, halfwidth, dense, received, panel, current)
+        total_ref[...] = total.reshape(grid_cols, orb, vectors)
+        base, scale = finish(
+            total_ref[targets_ref[0]], True, current_ref, None, center_ref, halfwidth_ref
+        )
+        outs[0][...] = base
+        for d in range(1, grid_cols):
+            outs[d][...] = total_ref[targets_ref[d]] * scale
+
+    return pl.pallas_call(
+        kernel,
+        in_specs=[SMEM] * 4 + [VMEM] * 3,
+        out_specs=[VMEM] * grid_cols,
+        out_shape=[jax.ShapeDtypeStruct((orb, vectors), jnp.float32)] * grid_cols,
+        scratch_shapes=[pltpu.VMEM((grid_cols, orb, vectors), jnp.float32)],
+        compiler_params=pltpu.CompilerParams(vmem_limit_bytes=dense.size * 2 + 2 * SPARE),
+        name="forward_first",
+    )(sources, targets, center, halfwidth, dense, panel, current)
+
+
+def turn_panels(sources, targets, panels, orb):
+    grid_rows = sources.shape[0]
+    grid_cols = targets.shape[0]
+    vectors = panels[0].shape[1]
+
+    def kernel(sources_ref, targets_ref, *refs):
+        *panel_refs, turned_ref = refs
+        for d, panel_ref in enumerate(panel_refs):
+            for k in range(grid_rows):
+                at = (sources_ref[k] * grid_cols + targets_ref[d]) * orb
+                turned = panel_ref[k * orb : (k + 1) * orb].T
+                turned_ref[:, pl.ds(pl.multiple_of(at, orb), orb)] = turned
+
+    return pl.pallas_call(
+        kernel,
+        in_specs=[SMEM] * 2 + [VMEM] * grid_cols,
+        out_specs=VMEM,
+        out_shape=jax.ShapeDtypeStruct((vectors, grid_rows * grid_cols * orb), jnp.bfloat16),
+        compiler_params=pltpu.CompilerParams(vmem_limit_bytes=panels[0].size * 4 * grid_cols + SPARE),
+        name="turn_panels",
+    )(sources, targets, *panels)
+
+
+def backward_first(turned_panels, received, base, halfwidth):
+    cells, orb, _ = received.shape
+    vectors = base.shape[1]
+
+    def kernel(halfwidth_ref, turned_ref, received_ref, base_ref, out_ref, panel_ref):
+        blocks = received_ref[...].reshape(cells * orb, orb)
+        total = jnp.dot(turned_ref[...], blocks, preferred_element_type=jnp.float32)
+        out = base_ref[...] + total.T / jnp.full((1, vectors), halfwidth_ref[0])
+        out_ref[...] = out
+        panel_ref[...] = out.astype(jnp.bfloat16)
+
+    return pl.pallas_call(
+        kernel,
+        in_specs=[SMEM] + [VMEM] * 3,
+        out_specs=[VMEM] * 2,
+        out_shape=[
+            jax.ShapeDtypeStruct((orb, vectors), jnp.float32),
+            jax.ShapeDtypeStruct((orb, vectors), jnp.bfloat16),
+        ],
+        compiler_params=pltpu.CompilerParams(vmem_limit_bytes=received.size * 4 + 2 * SPARE),
+        name="backward_first",
+    )(halfwidth, turned_panels, received, base)
+
+
+def turn_blocks(targets, received, panel, grid_rows):
+    _, orb, _ = received.shape
+    grid_cols = targets.shape[0]
+
+    def kernel(targets_ref, received_ref, panel_ref, *outs):
+        for d, out in enumerate(outs):
+            for c in range(grid_rows):
+                out[c] = received_ref[c * grid_cols + targets_ref[d]].T
+
+    return pl.pallas_call(
+        kernel,
+        in_specs=[SMEM, VMEM, VMEM],
+        out_specs=[VMEM] * grid_cols,
+        out_shape=[jax.ShapeDtypeStruct((grid_rows, orb, orb), jnp.bfloat16)] * grid_cols,
+        compiler_params=pltpu.CompilerParams(vmem_limit_bytes=received.size * 4 + SPARE),
+        name="turn_blocks",
+    )(targets, received, panel)
+
+
+def merge_tile(sources, targets, dense, stacks):
+    _, orb, _ = dense.shape
+    grid_rows = sources.shape[0]
+    grid_cols = targets.shape[0]
+
+    def kernel(sources_ref, targets_ref, dense_ref, *refs):
+        *stack_refs, tile_ref = refs
+        for k in range(grid_rows):
+            source = sources_ref[k]
+            for d, stack_ref in enumerate(stack_refs):
+                own = dense_ref[source * grid_cols + targets_ref[d]].astype(jnp.float32)
+                block = (own + stack_ref[source].astype(jnp.float32)).astype(jnp.bfloat16)
+                tile_ref[d * orb : (d + 1) * orb, k * orb : (k + 1) * orb] = block
+
+    return pl.pallas_call(
+        kernel,
+        in_specs=[SMEM] * 2 + [VMEM] * (1 + grid_cols),
+        out_specs=VMEM,
+        out_shape=jax.ShapeDtypeStruct((grid_cols * orb, grid_rows * orb), jnp.bfloat16),
+        compiler_params=pltpu.CompilerParams(vmem_limit_bytes=dense.size * 6 + SPARE),
+        name="merge_tile",
+    )(sources, targets, dense, *stacks)
 
 
 def apply_tile(tile, pieces, current, previous, center, halfwidth, grid_cols):
@@ -177,6 +265,7 @@
     count = len(pieces)
 
     def kernel(center_ref, halfwidth_ref, tile_ref, current_ref, previous_ref, *refs):
+        outs = refs[count:]
         total = None
         at = 0
         for ref in refs[:count]:
@@ -186,7 +275,12 @@
             )
             total = part if total is None else total + part
             at += depth
-        finish(total, False, orb, current_ref, previous_ref, center_ref, halfwidth_ref, refs[count:])
+        base, scale = finish(
+            total[:orb], False, current_ref, previous_ref, center_ref, halfwidth_ref
+        )
+        outs[0][...] = base
+        for d in range(1, grid_cols):
+            outs[d][...] = total[d * orb : (d + 1) * orb] * scale
 
     return pl.pallas_call(
         kernel,
@@ -220,9 +314,8 @@
     col = lax.axis_index("col")
     early = arrival_order(strides)
     late = [arrival_order(order) for order in turned]
-    places = [[early.index(offset) for offset in order] for order in late]
+    early_sources = jnp.array(early, jnp.int32) ^ row
     sources = jnp.array(late, jnp.int32)[col % 2] ^ row
-    places = jnp.array(places, jnp.int32)[col % 2]
     targets = jnp.arange(grid_cols, dtype=jnp.int32) ^ col
     pieces = gather([initial.astype(jnp.bfloat16)], same, last=1)
     dense = build_tile(
@@ -230,25 +323,30 @@
         grid_rows, grid_cols,
     )
     dense = after(dense, pieces[1:])
-    received = lax.all_to_all(dense, ("row", "col"), 0, 0)
+    received = lax.all_to_all(dense, "row", 0, 0, tiled=True)
     panel = jnp.concatenate(gather(pieces, same, first=1), axis=0)
-    tile, base, *others = merge_apply(
-        sources, places, targets, dense, received, panel, initial, center, halfwidth
+    panels = [panel] + [swap(panel, "col", grid_cols, d) for d in range(1, grid_cols)]
+    base, *others = forward_first(
+        early_sources, targets, dense, panel, initial, center, halfwidth
     )
+    for d, other in enumerate(others, start=1):
+        base = base + swap(other, "col", grid_cols, d)
+    turned_panels = turn_panels(early_sources, targets, panels, dense.shape[1])
 
     previous = initial
-    current = initial
-    for degree_step in range(DEGREE):
-        if degree_step > 0:
-            pieces = gather([current.astype(jnp.bfloat16)], turned)
-            base, *others = apply_tile(
-                tile, pieces, current, previous, center, halfwidth, grid_cols
-            )
+    current, panel = backward_first(turned_panels, received, base, halfwidth)
+    stacks = turn_blocks(targets, received, panel, grid_rows)
+    stacks = [stacks[0]] + [swap(stacks[d], "col", grid_cols, d) for d in range(1, grid_cols)]
+    tile = merge_tile(sources, targets, dense, stacks)
+    for degree_step in range(1, DEGREE):
+        pieces = gather([panel], turned)
+        base, *others = apply_tile(tile, pieces, current, previous, center, halfwidth, grid_cols)
         following = base
         for d, other in enumerate(others, start=1):
             following = following + swap(other, "col", grid_cols, d)
         previous = current
         current = following
+        panel = current.astype(jnp.bfloat16)
     return current
 
 

time: 78.9 us -> 76.6 us (0.971)
  waiting for transfers between devices: 39.1 us -> 28.2 us
  Pallas kernels: 4.78 us -> 8.54 us
  local copies, waits for them, and re-layouts: 0.11 us -> 3.01 us
  starting transfers between devices: 30.9 us -> 32.6 us
    all_to_all x1, waiting for transfers between devices: 7.78 us -> 0.31 us  [body(): received = lax.all_to_all(dense, 'row', 0, 0, tiled=True)]
    pallas_call x1 -> x5, Pallas kernels: 1.15 us -> 4.91 us  [the longest x1 1.66 us: turn_blocks(): pl.pallas_call(kernel, in_specs=[SMEM, VMEM, VMEM], out_specs=[VMEM] * gr...]
    ppermute x18, waiting for transfers between devices: 27.6 us -> 24.5 us  [swap_rows(): return lax.ppermute(x, ('row', 'col'), pairs)]
    unnamed x13 -> x24, local copies, waits for them, and re-layouts: 0.09 us -> 2.98 us
    all_to_all x1, starting transfers between devices: 5.33 us -> 6.48 us  [body(): received = lax.all_to_all(dense, 'row', 0, 0, tiled=True)]
    ppermute x3 -> x5, waiting for transfers between devices: 3.72 us -> 3.39 us  [swap(): lax.ppermute(x, axis, [(source, source ^ offset) for source in range(size)])]
  transfers between devices with their start and end apart: 22 -> 24, of which waited for: 18 -> 18; matrix products, arithmetic and copies ran while one was open for 0% -> 0% of each run, Pallas kernels for 4% -> 9%
where the time goes in v9:
time: 76.6 us; the launch traced here: 76.2 us
  starting transfers between devices  32.6 us (43%)
  waiting for transfers between devices  28.2 us (37%)
  Pallas kernels  8.54 us (11%)
  local copies, waits for them, and re-layouts  3.01 us (4%)
  between operations  2.26 us (3%)
  other arithmetic  1.55 us (2%)
    ppermute x18, starting transfers between devices, swap_rows(): return lax.ppermute(x, ('row', 'col'), pairs)  25.4 us
    ppermute x18, waiting for transfers between devices, swap_rows(): return lax.ppermute(x, ('row', 'col'), pairs)  24.5 us
    all_to_all x1, starting transfers between devices, body(): received = lax.all_to_all(dense, 'row', 0, 0, tiled=True)  6.48 us
    ppermute x5, waiting for transfers between devices, swap(): lax.ppermute(x, axis, [(source, source ^ offset) for source in range(size)])  3.39 us
    unnamed x24, local copies, waits for them, and re-layouts  2.98 us
    pallas_call x1, Pallas kernels, build_tile(): pl.pallas_call(kernel, in_specs=[HBM, HBM, SMEM, HBM], out_specs=VMEM, sc...  2.78 us
    pallas_call x1, Pallas kernels, turn_blocks(): pl.pallas_call(kernel, in_specs=[SMEM, VMEM, VMEM], out_specs=[VMEM] * gr...  1.66 us
  transfers between devices with their start and end apart: 24, of which 18 were waited for; matrix products, arithmetic and copies ran while one was open for 0% of the time, Pallas kernels for 9%

profile of v9, /device:TPU:0, one launch (start us, length us, event | category | flops | bytes accessed | tf_op | source)
XLA Modules:
  0.0 76.2 jit_solution(210292624994124152)
XLA Ops:
  0.0 0.8 %constant_dynamic-update-slice_fusion.6 = (bf16[2048,128]{1,0:T(8,128)(2,1)S(1)}, bf16[128,128]{1,0:T(8,128)(2,1)S(1)}) fusion(f32[128,128]{1,0:T(8,128)} %previous_ref.1), kind=kLoop, calls=%fused_computation.8 | loop fusion | flops 16383 | bytes 131072
  0.9 5.1 %collective-permute-start.2 = (bf16[128,128]{1,0:T(8,128)(2,1)S(1)}, bf16[128,128]{1,0:T(8,128)(2,1)S(1)}, u32[]{:S(2)}, u32[]{:S(2)}) collective-permute-start(bf16[128,128]{1,0:T(8,128)(2,1)S(1)} %get-tuple-element.28), channel_id=1, source_target_pairs={{0,24},{1,25},{2,26},{3,27},{4,28},{5,29},{6,30},{7,31},{8,16},{9,... | collective-permute-start | bytes 98312 | tf_op jit(solution)/shard_map/ppermute | solution.py:46
  6.0 0.6 collective-permute-start
  7.3 2.8 %build_tile.1.refs_0_ = bf16[32,128,128]{2,1,0:T(8,128)(2,1)} custom-call(s32[1,64]{1,0:T(1,128)} %bitcast.6, s32[1,64]{1,0:T(1,128)} %bitcast.7, s32[1,1]{1,0:T(1,128)S(6)} %copy.21.count_ref, bf16[64,128,128]{2,1,0:T(8,128)(2,1)} %bitcast.5), custom_call_target="tpu_custom_call" | custom-call | tf_op jit(solution)/shard_map/build_tile/pallas_call | solution.py:89
  10.1 0.7 collective-permute-done.1.refs_2_
  10.8 6.5 %all-to-all-start = ((bf16[32,128,128]{2,1,0:T(8,128)(2,1)}), bf16[32,128,128]{2,1,0:T(8,128)(2,1)S(1)}, u32[]{:S(2)}, u32[]{:S(2)}) async-start(bf16[32,128,128]{2,1,0:T(8,128)(2,1)} %after.1.dense_ref), calls=%async_computation | async-start | bytes 2097152 | tf_op jit(solution)/shard_map/all_to_all | solution.py:326
  17.3 2.9 %collective-permute-start.5 = (bf16[512,128]{1,0:T(8,128)(2,1)S(1)}, bf16[512,128]{1,0:T(8,128)(2,1)S(1)}, u32[]{:S(2)}, u32[]{:S(2)}) collective-permute-start(bf16[512,128]{1,0:T(8,128)(2,1)S(1)} %pad_maximum_fusion), channel_id=1, source_target_pairs={{0,6},{1,7},{2,4},{3,5},{4,2},{5,3},{6,0},{7,1},{8,14},{9,15},{10,... | collective-permute-start | bytes 393224 | tf_op jit(solution)/shard_map/ppermute | solution.py:46
  20.2 0.6 collective-permute-start.4
  20.8 0.1 collective-permute-start.3
  20.9 9.8 %collective-permute-done.3 = bf16[512,128]{1,0:T(8,128)(2,1)S(1)} collective-permute-done((bf16[512,128]{1,0:T(8,128)(2,1)S(1)}, bf16[512,128]{1,0:T(8,128)(2,1)S(1)}, u32[]{:S(2)}, u32[]{:S(2)}) %collective-permute-start.3) | collective-permute-done | bytes 131104 | tf_op jit(solution)/shard_map/ppermute | solution.py:46
  30.7 2.1 %collective-permute-done.4 = bf16[512,128]{1,0:T(8,128)(2,1)S(1)} collective-permute-done((bf16[512,128]{1,0:T(8,128)(2,1)S(1)}, bf16[512,128]{1,0:T(8,128)(2,1)S(1)}, u32[]{:S(2)}, u32[]{:S(2)}) %collective-permute-start.4) | collective-permute-done | bytes 131104 | tf_op jit(solution)/shard_map/ppermute | solution.py:46
  34.4 1.0 %forward_first.1 = (f32[128,128]{1,0:T(8,128)S(1)}, f32[128,128]{1,0:T(8,128)S(1)}) custom-call(s32[16]{0:T(128)S(1)} %broadcast_xor_fusion.sources_ref, s32[2]{0:T(128)S(1)} %iota_xor_fusion.targets_ref, f32[1]{0:T(128)S(6)} %copy.22.center_ref, f32[1]{0:T(128)S(6)} %copy.23.halfwidth_ref, bf16[32,128,128]{2,1,0:T(8,128)(2,1)S(1)} %copy-done, ...), custom_call_target="tpu_custom_call" | custom-call | tf_op jit(solution)/shard_map/forward_first/pallas_call | solution.py:160
  35.4 0.5 collective-permute-start.7
  35.9 0.9 %collective-permute-done.7 = f32[128,128]{1,0:T(8,128)S(1)} collective-permute-done((f32[128,128]{1,0:T(8,128)S(1)}, f32[128,128]{1,0:T(8,128)S(1)}, u32[]{:S(2)}, u32[]{:S(2)}) %collective-permute-start.7) | collective-permute-done | bytes 65568 | tf_op jit(solution)/shard_map/ppermute | solution.py:37
  36.8 0.8 %copy-done.4 = bf16[2048,128]{1,0:T(8,128)(2,1)} copy-done((bf16[2048,128]{1,0:T(8,128)(2,1)}, bf16[2048,128]{1,0:T(8,128)(2,1)S(1)}, u32[]{:S(2)}) %copy-start.4) | copy-done | bytes 524312
  37.6 1.0 %copy-done.2 = bf16[2048,128]{1,0:T(8,128)(2,1)S(1)} copy-done((bf16[2048,128]{1,0:T(8,128)(2,1)S(1)}, bf16[2048,128]{1,0:T(8,128)(2,1)}, u32[]{:S(2)}) %copy-start.2) | copy-done | bytes 524312
  38.7 1.0 %copy-done.5 = bf16[2048,128]{1,0:T(8,128)(2,1)S(1)} copy-done((bf16[2048,128]{1,0:T(8,128)(2,1)S(1)}, bf16[2048,128]{1,0:T(8,128)(2,1)}, u32[]{:S(2)}) %copy-start.5) | copy-done | bytes 524312
  39.7 0.9 %turn_panels.1.turned_ref = bf16[128,4096]{1,0:T(8,128)(2,1)S(1)} custom-call(s32[16]{0:T(128)S(1)} %broadcast_xor_fusion.sources_ref, s32[2]{0:T(128)S(1)} %iota_xor_fusion.targets_ref, bf16[2048,128]{1,0:T(8,128)(2,1)S(1)} %copy-done.2, bf16[2048,128]{1,0:T(8,128)(2,1)S(1)} %copy-done.5), custom_call_target="tpu_custom_call" | custom-call | tf_op jit(solution)/shard_map/turn_panels/pallas_call | solution.py:184
  40.6 0.3 all-to-all-done.received_ref
  41.0 0.5 backward_first.1
  41.5 3.9 %collective-permute-start.11 = (bf16[128,128]{1,0:T(8,128)(2,1)S(1)}, bf16[128,128]{1,0:T(8,128)(2,1)S(1)}, u32[]{:S(2)}, u32[]{:S(2)}) collective-permute-start(bf16[128,128]{1,0:T(8,128)(2,1)S(1)} %get-tuple-element.17.panel_ref), channel_id=1, source_target_pairs={{0,24},{1,7},{2,26},{3,5},{4,28},{5,3},{6,30},{7,1},{8,16},{9,15},... | collective-permute-start | bytes 98312 | tf_op jit(solution)/shard_map/ppermute | solution.py:46
  45.3 0.6 collective-permute-start.10
  46.0 1.7 %turn_blocks.1 = (bf16[16,128,128]{2,1,0:T(8,128)(2,1)S(1)}, bf16[16,128,128]{2,1,0:T(8,128)(2,1)}) custom-call(s32[2]{0:T(128)S(1)} %iota_xor_fusion.targets_ref, bf16[32,128,128]{2,1,0:T(8,128)(2,1)S(1)} %all-to-all-done.received_ref, bf16[128,128]{1,0:T(8,128)(2,1)S(1)} %get-tuple-element.17.panel_ref), custom_call_target="tpu_custom_call" | custom-call | tf_op jit(solution)/shard_map/turn_blocks/pallas_call | solution.py:227
  47.7 2.3 %collective-permute-done.9 = bf16[128,128]{1,0:T(8,128)(2,1)S(1)} collective-permute-done((bf16[128,128]{1,0:T(8,128)(2,1)S(1)}, bf16[128,128]{1,0:T(8,128)(2,1)S(1)}, u32[]{:S(2)}, u32[]{:S(2)}) %collective-permute-start.9) | collective-permute-done | bytes 32800 | tf_op jit(solution)/shard_map/ppermute | solution.py:46
  49.9 0.3 collective-permute-done.10
  50.3 1.3 %collective-permute-start.14 = (bf16[512,128]{1,0:T(8,128)(2,1)S(1)}, bf16[512,128]{1,0:T(8,128)(2,1)S(1)}, u32[]{:S(2)}, u32[]{:S(2)}) collective-permute-start(bf16[512,128]{1,0:T(8,128)(2,1)S(1)} %constant_dynamic-update-slice_fusion.7.refs_0_), channel_id=1, source_target_pairs={{0,6},{1,25},{2,4},{3,27},{4,2},{5,29},{6,0},{7,31},{8,14},{9,17},... | collective-permute-start | bytes 393224 | tf_op jit(solution)/shard_map/ppermute | solution.py:46
  51.6 1.3 %collective-permute-start.13 = (bf16[512,128]{1,0:T(8,128)(2,1)S(1)}, bf16[512,128]{1,0:T(8,128)(2,1)S(1)}, u32[]{:S(2)}, u32[]{:S(2)}) collective-permute-start(bf16[512,128]{1,0:T(8,128)(2,1)S(1)} %constant_dynamic-update-slice_fusion.7.refs_0_), channel_id=1, source_target_pairs={{0,4},{1,17},{2,6},{3,19},{4,0},{5,21},{6,2},{7,23},{8,12},{9,25},... | collective-permute-start | bytes 393224 | tf_op jit(solution)/shard_map/ppermute | solution.py:46
  52.9 0.9 %collective-permute-start.12 = (bf16[512,128]{1,0:T(8,128)(2,1)S(1)}, bf16[512,128]{1,0:T(8,128)(2,1)S(1)}, u32[]{:S(2)}, u32[]{:S(2)}) collective-permute-start(bf16[512,128]{1,0:T(8,128)(2,1)S(1)} %constant_dynamic-update-slice_fusion.7.refs_0_), channel_id=1, source_target_pairs={{0,2},{1,9},{2,0},{3,11},{4,6},{5,13},{6,4},{7,15},{8,10},{9,1},{1... | collective-permute-start | bytes 393224 | tf_op jit(solution)/shard_map/ppermute | solution.py:46
  53.9 0.9 %merge_tile.1.tile_ref = bf16[256,2048]{1,0:T(8,128)(2,1)S(1)} custom-call(s32[16]{0:T(128)S(1)} %xor_bitcast_fusion.sources_ref, s32[2]{0:T(128)S(1)} %iota_xor_fusion.targets_ref, bf16[32,128,128]{2,1,0:T(8,128)(2,1)S(1)} %copy-done, bf16[16,128,128]{2,1,0:T(8,128)(2,1)S(1)} %get-tuple-element.18.refs_0_, ...), custom_call_target="tpu_custom_call" | custom-call | tf_op jit(solution)/shard_map/merge_tile/pallas_call | solution.py:251
  54.7 1.6 %collective-permute-done.14.refs_3_ = bf16[512,128]{1,0:T(8,128)(2,1)S(1)} collective-permute-done((bf16[512,128]{1,0:T(8,128)(2,1)S(1)}, bf16[512,128]{1,0:T(8,128)(2,1)S(1)}, u32[]{:S(2)}, u32[]{:S(2)}) %collective-permute-start.14) | collective-permute-done | bytes 131104 | tf_op jit(solution)/shard_map/ppermute | solution.py:46
  56.3 1.3 %collective-permute-done.13.refs_2_ = bf16[512,128]{1,0:T(8,128)(2,1)S(1)} collective-permute-done((bf16[512,128]{1,0:T(8,128)(2,1)S(1)}, bf16[512,128]{1,0:T(8,128)(2,1)S(1)}, u32[]{:S(2)}, u32[]{:S(2)}) %collective-permute-start.13) | collective-permute-done | bytes 131104 | tf_op jit(solution)/shard_map/ppermute | solution.py:46
  57.6 0.3 collective-permute-done.12.refs_1_
  57.9 0.4 apply_tile.2
  58.4 1.2 %collective-permute-done.15 = f32[128,128]{1,0:T(8,128)S(1)} collective-permute-done((f32[128,128]{1,0:T(8,128)S(1)}, f32[128,128]{1,0:T(8,128)S(1)}, u32[]{:S(2)}, u32[]{:S(2)}) %collective-permute-start.15) | collective-permute-done | bytes 65568 | tf_op jit(solution)/shard_map/ppermute | solution.py:37
  59.7 1.6 %collective-permute-start.18 = (bf16[128,128]{1,0:T(8,128)(2,1)S(1)}, bf16[128,128]{1,0:T(8,128)(2,1)S(1)}, u32[]{:S(2)}, u32[]{:S(2)}) collective-permute-start(bf16[128,128]{1,0:T(8,128)(2,1)S(1)} %get-tuple-element.25), channel_id=1, source_target_pairs={{0,24},{1,7},{2,26},{3,5},{4,28},{5,3},{6,30},{7,1},{8,16},{9,15},... | collective-permute-start | bytes 98312 | tf_op jit(solution)/shard_map/ppermute | solution.py:46
  61.2 0.6 collective-permute-start.17
  61.9 2.3 %collective-permute-start.16 = (bf16[128,128]{1,0:T(8,128)(2,1)S(1)}, bf16[128,128]{1,0:T(8,128)(2,1)S(1)}, u32[]{:S(2)}, u32[]{:S(2)}) collective-permute-start(bf16[128,128]{1,0:T(8,128)(2,1)S(1)} %get-tuple-element.25), channel_id=1, source_target_pairs={{0,8},{1,3},{2,10},{3,1},{4,12},{5,7},{6,14},{7,5},{8,0},{9,11},{1... | collective-permute-start | bytes 98312 | tf_op jit(solution)/shard_map/ppermute | solution.py:46
  64.1 1.3 %collective-permute-done.18 = bf16[128,128]{1,0:T(8,128)(2,1)S(1)} collective-permute-done((bf16[128,128]{1,0:T(8,128)(2,1)S(1)}, bf16[128,128]{1,0:T(8,128)(2,1)S(1)}, u32[]{:S(2)}, u32[]{:S(2)}) %collective-permute-start.18) | collective-permute-done | bytes 32800 | tf_op jit(solution)/shard_map/ppermute | solution.py:46
  65.4 0.7 collective-permute-done.17
  66.1 0.2 collective-permute-done.16
  66.4 1.6 %collective-permute-start.21 = (bf16[512,128]{1,0:T(8,128)(2,1)S(1)}, bf16[512,128]{1,0:T(8,128)(2,1)S(1)}, u32[]{:S(2)}, u32[]{:S(2)}) collective-permute-start(bf16[512,128]{1,0:T(8,128)(2,1)S(1)} %pad_maximum_fusion.1.refs_0_), channel_id=1, source_target_pairs={{0,6},{1,25},{2,4},{3,27},{4,2},{5,29},{6,0},{7,31},{8,14},{9,17},... | collective-permute-start | bytes 393224 | tf_op jit(solution)/shard_map/ppermute | solution.py:46
  68.0 0.9 %collective-permute-start.20 = (bf16[512,128]{1,0:T(8,128)(2,1)S(1)}, bf16[512,128]{1,0:T(8,128)(2,1)S(1)}, u32[]{:S(2)}, u32[]{:S(2)}) collective-permute-start(bf16[512,128]{1,0:T(8,128)(2,1)S(1)} %pad_maximum_fusion.1.refs_0_), channel_id=1, source_target_pairs={{0,4},{1,17},{2,6},{3,19},{4,0},{5,21},{6,2},{7,23},{8,12},{9,25},... | collective-permute-start | bytes 393224 | tf_op jit(solution)/shard_map/ppermute | solution.py:46
  68.8 1.1 %collective-permute-start.19 = (bf16[512,128]{1,0:T(8,128)(2,1)S(1)}, bf16[512,128]{1,0:T(8,128)(2,1)S(1)}, u32[]{:S(2)}, u32[]{:S(2)}) collective-permute-start(bf16[512,128]{1,0:T(8,128)(2,1)S(1)} %pad_maximum_fusion.1.refs_0_), channel_id=1, source_target_pairs={{0,2},{1,9},{2,0},{3,11},{4,6},{5,13},{6,4},{7,15},{8,10},{9,1},{1... | collective-permute-start | bytes 393224 | tf_op jit(solution)/shard_map/ppermute | solution.py:46
  69.9 2.5 %collective-permute-done.21.refs_3_ = bf16[512,128]{1,0:T(8,128)(2,1)S(1)} collective-permute-done((bf16[512,128]{1,0:T(8,128)(2,1)S(1)}, bf16[512,128]{1,0:T(8,128)(2,1)S(1)}, u32[]{:S(2)}, u32[]{:S(2)}) %collective-permute-start.21) | collective-permute-done | bytes 131104 | tf_op jit(solution)/shard_map/ppermute | solution.py:46
  72.4 1.3 %collective-permute-done.20.refs_2_ = bf16[512,128]{1,0:T(8,128)(2,1)S(1)} collective-permute-done((bf16[512,128]{1,0:T(8,128)(2,1)S(1)}, bf16[512,128]{1,0:T(8,128)(2,1)S(1)}, u32[]{:S(2)}, u32[]{:S(2)}) %collective-permute-start.20) | collective-permute-done | bytes 131104 | tf_op jit(solution)/shard_map/ppermute | solution.py:46
  73.8 0.4 apply_tile.3
  74.3 1.2 %collective-permute-done.22 = f32[128,128]{1,0:T(8,128)S(1)} collective-permute-done((f32[128,128]{1,0:T(8,128)S(1)}, f32[128,128]{1,0:T(8,128)S(1)}, u32[]{:S(2)}, u32[]{:S(2)}) %collective-permute-start.22) | collective-permute-done | bytes 65568 | tf_op jit(solution)/shard_map/ppermute | solution.py:37
  75.5 0.6 add.20
  (44 shorter events, 0.5 us)
Async XLA Ops:
  0.9 9.2 %collective-permute-start.2 = (bf16[128,128]{1,0:T(8,128)(2,1)S(1)}, bf16[128,128]{1,0:T(8,128)(2,1)S(1)}, u32[]{:S(2)}, u32[]{:S(2)}) collective-permute-start(bf16[128,128]{1,0:T(8,128)(2,1)S(1)} %get-tuple-element.28), channel_id=1, source_target_pairs={{0,24},{1,25},{2,26},{3,27},{4,28},{5,29},{6,30},{7,31},{8,16},{9,... | collective-permute-start | bytes 98312 | tf_op jit(solution)/shard_map/ppermute | solution.py:46
  6.0 4.8 %collective-permute-start.1 = (bf16[128,128]{1,0:T(8,128)(2,1)S(1)}, bf16[128,128]{1,0:T(8,128)(2,1)S(1)}, u32[]{:S(2)}, u32[]{:S(2)}) collective-permute-start(bf16[128,128]{1,0:T(8,128)(2,1)S(1)} %get-tuple-element.28), channel_id=1, source_target_pairs={{0,16},{1,17},{2,18},{3,19},{4,20},{5,21},{6,22},{7,23},{8,24},{9,... | collective-permute-start | bytes 98312 | tf_op jit(solution)/shard_map/ppermute | solution.py:46
  6.0 4.8 %collective-permute-start = (bf16[128,128]{1,0:T(8,128)(2,1)S(1)}, bf16[128,128]{1,0:T(8,128)(2,1)S(1)}, u32[]{:S(2)}, u32[]{:S(2)}) collective-permute-start(bf16[128,128]{1,0:T(8,128)(2,1)S(1)} %get-tuple-element.28), channel_id=1, source_target_pairs={{0,8},{1,9},{2,10},{3,11},{4,12},{5,13},{6,14},{7,15},{8,0},{9,1},... | collective-permute-start | bytes 98312 | tf_op jit(solution)/shard_map/ppermute | solution.py:46
  10.8 23.6 %copy-start.7 = (s32[16]{0:T(128)S(1)}, s32[16]{0:T(128)}, u32[]{:S(2)}) copy-start(s32[16]{0:T(128)} %constant.26.clone) | copy-start | bytes 196
  10.8 23.6 %copy-start = (bf16[32,128,128]{2,1,0:T(8,128)(2,1)S(1)}, bf16[32,128,128]{2,1,0:T(8,128)(2,1)}, u32[]{:S(2)}) copy-start(bf16[32,128,128]{2,1,0:T(8,128)(2,1)} %after.1.dense_ref) | copy-start | bytes 3145732
  10.8 23.6 %copy-start.3 = (f32[128,128]{1,0:T(8,128)S(1)}, f32[128,128]{1,0:T(8,128)}, u32[]{:S(2)}) copy-start(f32[128,128]{1,0:T(8,128)} %previous_ref.1) | copy-start | bytes 196612
  10.8 30.2 %all-to-all-start = ((bf16[32,128,128]{2,1,0:T(8,128)(2,1)}), bf16[32,128,128]{2,1,0:T(8,128)(2,1)S(1)}, u32[]{:S(2)}, u32[]{:S(2)}) async-start(bf16[32,128,128]{2,1,0:T(8,128)(2,1)} %after.1.dense_ref), calls=%async_computation | async-start | bytes 2097152 | tf_op jit(solution)/shard_map/all_to_all | solution.py:326
  17.3 15.6 %collective-permute-start.5 = (bf16[512,128]{1,0:T(8,128)(2,1)S(1)}, bf16[512,128]{1,0:T(8,128)(2,1)S(1)}, u32[]{:S(2)}, u32[]{:S(2)}) collective-permute-start(bf16[512,128]{1,0:T(8,128)(2,1)S(1)} %pad_maximum_fusion), channel_id=1, source_target_pairs={{0,6},{1,7},{2,4},{3,5},{4,2},{5,3},{6,0},{7,1},{8,14},{9,15},{10,... | collective-permute-start | bytes 393224 | tf_op jit(solution)/shard_map/ppermute | solution.py:46
  20.2 12.6 %collective-permute-start.4 = (bf16[512,128]{1,0:T(8,128)(2,1)S(1)}, bf16[512,128]{1,0:T(8,128)(2,1)S(1)}, u32[]{:S(2)}, u32[]{:S(2)}) collective-permute-start(bf16[512,128]{1,0:T(8,128)(2,1)S(1)} %pad_maximum_fusion), channel_id=1, source_target_pairs={{0,4},{1,5},{2,6},{3,7},{4,0},{5,1},{6,2},{7,3},{8,12},{9,13},{10,... | collective-permute-start | bytes 393224 | tf_op jit(solution)/shard_map/ppermute | solution.py:46
  20.8 9.9 %collective-permute-start.3 = (bf16[512,128]{1,0:T(8,128)(2,1)S(1)}, bf16[512,128]{1,0:T(8,128)(2,1)S(1)}, u32[]{:S(2)}, u32[]{:S(2)}) collective-permute-start(bf16[512,128]{1,0:T(8,128)(2,1)S(1)} %pad_maximum_fusion), channel_id=1, source_target_pairs={{0,2},{1,3},{2,0},{3,1},{4,6},{5,7},{6,4},{7,5},{8,10},{9,11},{10,... | collective-permute-start | bytes 393224 | tf_op jit(solution)/shard_map/ppermute | solution.py:46
  32.9 3.9 %copy-start.1 = (bf16[2048,128]{1,0:T(8,128)(2,1)}, bf16[2048,128]{1,0:T(8,128)(2,1)S(1)}, u32[]{:S(2)}) copy-start(bf16[2048,128]{1,0:T(8,128)(2,1)S(1)} %constant_dynamic-update-slice_fusion.refs_0_.panel_ref) | copy-start | bytes 1572868
  32.9 3.9 %collective-permute-start.6 = (bf16[2048,128]{1,0:T(8,128)(2,1)S(1)}, bf16[2048,128]{1,0:T(8,128)(2,1)S(1)}, u32[]{:S(2)}, u32[]{:S(2)}) collective-permute-start(bf16[2048,128]{1,0:T(8,128)(2,1)S(1)} %constant_dynamic-update-slice_fusion.refs_0_.panel_ref), channel_id=1, source_target_pairs={{0,1},{1,0},{2,3},{3,2},{4,5},{5,4},{6,7},{7,6},{8,9},{9,8},{10,11... | collective-permute-start | bytes 1572872 | tf_op jit(solution)/shard_map/ppermute | solution.py:37
  35.4 1.4 %collective-permute-start.7 = (f32[128,128]{1,0:T(8,128)S(1)}, f32[128,128]{1,0:T(8,128)S(1)}, u32[]{:S(2)}, u32[]{:S(2)}) collective-permute-start(f32[128,128]{1,0:T(8,128)S(1)} %get-tuple-element.16), channel_id=1, source_target_pairs={{0,1},{1,0},{2,3},{3,2},{4,5},{5,4},{6,7},{7,6},{8,9},{9,8},{10,11... | collective-permute-start | bytes 196616 | tf_op jit(solution)/shard_map/ppermute | solution.py:37
  36.8 0.8 %copy-start.4 = (bf16[2048,128]{1,0:T(8,128)(2,1)}, bf16[2048,128]{1,0:T(8,128)(2,1)S(1)}, u32[]{:S(2)}) copy-start(bf16[2048,128]{1,0:T(8,128)(2,1)S(1)} %collective-permute-done.6.refs_1_) | copy-start | bytes 1572868
  37.6 1.0 %copy-start.2 = (bf16[2048,128]{1,0:T(8,128)(2,1)S(1)}, bf16[2048,128]{1,0:T(8,128)(2,1)}, u32[]{:S(2)}) copy-start(bf16[2048,128]{1,0:T(8,128)(2,1)} %copy-done.1) | copy-start | bytes 1572868
  38.7 1.0 %copy-start.5 = (bf16[2048,128]{1,0:T(8,128)(2,1)S(1)}, bf16[2048,128]{1,0:T(8,128)(2,1)}, u32[]{:S(2)}) copy-start(bf16[2048,128]{1,0:T(8,128)(2,1)} %copy-done.4) | copy-start | bytes 1572868
  40.6 13.2 %copy-start.6 = (s32[2,16]{1,0:T(2,128)S(1)}, s32[2,16]{1,0:T(2,128)}, u32[]{:S(2)}) copy-start(s32[2,16]{1,0:T(2,128)} %constant.27.clone) | copy-start | bytes 388
  41.5 8.8 %collective-permute-start.11 = (bf16[128,128]{1,0:T(8,128)(2,1)S(1)}, bf16[128,128]{1,0:T(8,128)(2,1)S(1)}, u32[]{:S(2)}, u32[]{:S(2)}) collective-permute-start(bf16[128,128]{1,0:T(8,128)(2,1)S(1)} %get-tuple-element.17.panel_ref), channel_id=1, source_target_pairs={{0,24},{1,7},{2,26},{3,5},{4,28},{5,3},{6,30},{7,1},{8,16},{9,15},... | collective-permute-start | bytes 98312 | tf_op jit(solution)/shard_map/ppermute | solution.py:46
  45.3 4.9 %collective-permute-start.10 = (bf16[128,128]{1,0:T(8,128)(2,1)S(1)}, bf16[128,128]{1,0:T(8,128)(2,1)S(1)}, u32[]{:S(2)}, u32[]{:S(2)}) collective-permute-start(bf16[128,128]{1,0:T(8,128)(2,1)S(1)} %get-tuple-element.17.panel_ref), channel_id=1, source_target_pairs={{0,16},{1,5},{2,18},{3,7},{4,20},{5,1},{6,22},{7,3},{8,24},{9,13},... | collective-permute-start | bytes 98312 | tf_op jit(solution)/shard_map/ppermute | solution.py:46
  46.0 3.9 %collective-permute-start.9 = (bf16[128,128]{1,0:T(8,128)(2,1)S(1)}, bf16[128,128]{1,0:T(8,128)(2,1)S(1)}, u32[]{:S(2)}, u32[]{:S(2)}) collective-permute-start(bf16[128,128]{1,0:T(8,128)(2,1)S(1)} %get-tuple-element.17.panel_ref), channel_id=1, source_target_pairs={{0,8},{1,3},{2,10},{3,1},{4,12},{5,7},{6,14},{7,5},{8,0},{9,11},{1... | collective-permute-start | bytes 98312 | tf_op jit(solution)/shard_map/ppermute | solution.py:46
  47.7 6.2 %collective-permute-start.8 = (bf16[16,128,128]{2,1,0:T(8,128)(2,1)}, bf16[16,128,128]{2,1,0:T(8,128)(2,1)S(1)}, u32[]{:S(2)}, u32[]{:S(2)}) collective-permute-start(bf16[16,128,128]{2,1,0:T(8,128)(2,1)} %get-tuple-element.19), channel_id=1, source_target_pairs={{0,1},{1,0},{2,3},{3,2},{4,5},{5,4},{6,7},{7,6},{8,9},{9,8},{10,11... | collective-permute-start | bytes 1572872 | tf_op jit(solution)/shard_map/ppermute | solution.py:37
  50.3 6.0 %collective-permute-start.14 = (bf16[512,128]{1,0:T(8,128)(2,1)S(1)}, bf16[512,128]{1,0:T(8,128)(2,1)S(1)}, u32[]{:S(2)}, u32[]{:S(2)}) collective-permute-start(bf16[512,128]{1,0:T(8,128)(2,1)S(1)} %constant_dynamic-update-slice_fusion.7.refs_0_), channel_id=1, source_target_pairs={{0,6},{1,25},{2,4},{3,27},{4,2},{5,29},{6,0},{7,31},{8,14},{9,17},... | collective-permute-start | bytes 393224 | tf_op jit(solution)/shard_map/ppermute | solution.py:46
  51.6 6.0 %collective-permute-start.13 = (bf16[512,128]{1,0:T(8,128)(2,1)S(1)}, bf16[512,128]{1,0:T(8,128)(2,1)S(1)}, u32[]{:S(2)}, u32[]{:S(2)}) collective-permute-start(bf16[512,128]{1,0:T(8,128)(2,1)S(1)} %constant_dynamic-update-slice_fusion.7.refs_0_), channel_id=1, source_target_pairs={{0,4},{1,17},{2,6},{3,19},{4,0},{5,21},{6,2},{7,23},{8,12},{9,25},... | collective-permute-start | bytes 393224 | tf_op jit(solution)/shard_map/ppermute | solution.py:46
  52.9 5.0 %collective-permute-start.12 = (bf16[512,128]{1,0:T(8,128)(2,1)S(1)}, bf16[512,128]{1,0:T(8,128)(2,1)S(1)}, u32[]{:S(2)}, u32[]{:S(2)}) collective-permute-start(bf16[512,128]{1,0:T(8,128)(2,1)S(1)} %constant_dynamic-update-slice_fusion.7.refs_0_), channel_id=1, source_target_pairs={{0,2},{1,9},{2,0},{3,11},{4,6},{5,13},{6,4},{7,15},{8,10},{9,1},{1... | collective-permute-start | bytes 393224 | tf_op jit(solution)/shard_map/ppermute | solution.py:46
  58.3 1.3 %collective-permute-start.15 = (f32[128,128]{1,0:T(8,128)S(1)}, f32[128,128]{1,0:T(8,128)S(1)}, u32[]{:S(2)}, u32[]{:S(2)}) collective-permute-start(f32[128,128]{1,0:T(8,128)S(1)} %get-tuple-element.22), channel_id=1, source_target_pairs={{0,1},{1,0},{2,3},{3,2},{4,5},{5,4},{6,7},{7,6},{8,9},{9,8},{10,11... | collective-permute-start | bytes 196616 | tf_op jit(solution)/shard_map/ppermute | solution.py:37
  59.7 5.8 %collective-permute-start.18 = (bf16[128,128]{1,0:T(8,128)(2,1)S(1)}, bf16[128,128]{1,0:T(8,128)(2,1)S(1)}, u32[]{:S(2)}, u32[]{:S(2)}) collective-permute-start(bf16[128,128]{1,0:T(8,128)(2,1)S(1)} %get-tuple-element.25), channel_id=1, source_target_pairs={{0,24},{1,7},{2,26},{3,5},{4,28},{5,3},{6,30},{7,1},{8,16},{9,15},... | collective-permute-start | bytes 98312 | tf_op jit(solution)/shard_map/ppermute | solution.py:46
  61.2 4.9 %collective-permute-start.17 = (bf16[128,128]{1,0:T(8,128)(2,1)S(1)}, bf16[128,128]{1,0:T(8,128)(2,1)S(1)}, u32[]{:S(2)}, u32[]{:S(2)}) collective-permute-start(bf16[128,128]{1,0:T(8,128)(2,1)S(1)} %get-tuple-element.25), channel_id=1, source_target_pairs={{0,16},{1,5},{2,18},{3,7},{4,20},{5,1},{6,22},{7,3},{8,24},{9,13},... | collective-permute-start | bytes 98312 | tf_op jit(solution)/shard_map/ppermute | solution.py:46
  61.9 4.5 %collective-permute-start.16 = (bf16[128,128]{1,0:T(8,128)(2,1)S(1)}, bf16[128,128]{1,0:T(8,128)(2,1)S(1)}, u32[]{:S(2)}, u32[]{:S(2)}) collective-permute-start(bf16[128,128]{1,0:T(8,128)(2,1)S(1)} %get-tuple-element.25), channel_id=1, source_target_pairs={{0,8},{1,3},{2,10},{3,1},{4,12},{5,7},{6,14},{7,5},{8,0},{9,11},{1... | collective-permute-start | bytes 98312 | tf_op jit(solution)/shard_map/ppermute | solution.py:46
  66.4 6.0 %collective-permute-start.21 = (bf16[512,128]{1,0:T(8,128)(2,1)S(1)}, bf16[512,128]{1,0:T(8,128)(2,1)S(1)}, u32[]{:S(2)}, u32[]{:S(2)}) collective-permute-start(bf16[512,128]{1,0:T(8,128)(2,1)S(1)} %pad_maximum_fusion.1.refs_0_), channel_id=1, source_target_pairs={{0,6},{1,25},{2,4},{3,27},{4,2},{5,29},{6,0},{7,31},{8,14},{9,17},... | collective-permute-start | bytes 393224 | tf_op jit(solution)/shard_map/ppermute | solution.py:46
  68.0 5.8 %collective-permute-start.20 = (bf16[512,128]{1,0:T(8,128)(2,1)S(1)}, bf16[512,128]{1,0:T(8,128)(2,1)S(1)}, u32[]{:S(2)}, u32[]{:S(2)}) collective-permute-start(bf16[512,128]{1,0:T(8,128)(2,1)S(1)} %pad_maximum_fusion.1.refs_0_), channel_id=1, source_target_pairs={{0,4},{1,17},{2,6},{3,19},{4,0},{5,21},{6,2},{7,23},{8,12},{9,25},... | collective-permute-start | bytes 393224 | tf_op jit(solution)/shard_map/ppermute | solution.py:46
  68.8 5.0 %collective-permute-start.19 = (bf16[512,128]{1,0:T(8,128)(2,1)S(1)}, bf16[512,128]{1,0:T(8,128)(2,1)S(1)}, u32[]{:S(2)}, u32[]{:S(2)}) collective-permute-start(bf16[512,128]{1,0:T(8,128)(2,1)S(1)} %pad_maximum_fusion.1.refs_0_), channel_id=1, source_target_pairs={{0,2},{1,9},{2,0},{3,11},{4,6},{5,13},{6,4},{7,15},{8,10},{9,1},{1... | collective-permute-start | bytes 393224 | tf_op jit(solution)/shard_map/ppermute | solution.py:46
  74.2 1.3 %collective-permute-start.22 = (f32[128,128]{1,0:T(8,128)S(1)}, f32[128,128]{1,0:T(8,128)S(1)}, u32[]{:S(2)}, u32[]{:S(2)}) collective-permute-start(f32[128,128]{1,0:T(8,128)S(1)} %get-tuple-element.24), channel_id=1, source_target_pairs={{0,1},{1,0},{2,3},{3,2},{4,5},{5,4},{6,7},{7,6},{8,9},{9,8},{10,11... | collective-permute-start | bytes 196616 | tf_op jit(solution)/shard_map/ppermute | solution.py:37

commit v10 on v9

--- a/solution.py
+++ b/solution.py
@@ -168,43 +168,47 @@
     )(sources, targets, center, halfwidth, dense, panel, current)
 
 
-def turn_panels(sources, targets, panels, orb):
+def turn_panel(sources, panel, orb):
     grid_rows = sources.shape[0]
+    vectors = panel.shape[1]
+
+    def kernel(sources_ref, panel_ref, turned_ref):
+        for k in range(grid_rows):
+            turned = panel_ref[k * orb : (k + 1) * orb].T
+            turned_ref[:, pl.ds(pl.multiple_of(sources_ref[k] * orb, orb), orb)] = turned
+
+    return pl.pallas_call(
+        kernel,
+        in_specs=[SMEM, VMEM],
+        out_specs=VMEM,
+        out_shape=jax.ShapeDtypeStruct((vectors, grid_rows * orb), jnp.bfloat16),
+        compiler_params=pltpu.CompilerParams(vmem_limit_bytes=panel.size * 4 + SPARE),
+        name="turn_panel",
+    )(sources, panel)
+
+
+def backward_first(targets, turned_panels, received, base, halfwidth):
+    cells, orb, _ = received.shape
     grid_cols = targets.shape[0]
-    vectors = panels[0].shape[1]
-
-    def kernel(sources_ref, targets_ref, *refs):
-        *panel_refs, turned_ref = refs
-        for d, panel_ref in enumerate(panel_refs):
-            for k in range(grid_rows):
-                at = (sources_ref[k] * grid_cols + targets_ref[d]) * orb
-                turned = panel_ref[k * orb : (k + 1) * orb].T
-                turned_ref[:, pl.ds(pl.multiple_of(at, orb), orb)] = turned
-
-    return pl.pallas_call(
-        kernel,
-        in_specs=[SMEM] * 2 + [VMEM] * grid_cols,
-        out_specs=VMEM,
-        out_shape=jax.ShapeDtypeStruct((vectors, grid_rows * grid_cols * orb), jnp.bfloat16),
-        compiler_params=pltpu.CompilerParams(vmem_limit_bytes=panels[0].size * 4 * grid_cols + SPARE),
-        name="turn_panels",
-    )(sources, targets, *panels)
-
-
-def backward_first(turned_panels, received, base, halfwidth):
-    cells, orb, _ = received.shape
     vectors = base.shape[1]
 
-    def kernel(halfwidth_ref, turned_ref, received_ref, base_ref, out_ref, panel_ref):
-        blocks = received_ref[...].reshape(cells * orb, orb)
-        total = jnp.dot(turned_ref[...], blocks, preferred_element_type=jnp.float32)
+    def kernel(targets_ref, halfwidth_ref, received_ref, base_ref, *refs):
+        turned_refs = refs[:grid_cols]
+        out_ref, panel_ref = refs[grid_cols:]
+        total = None
+        for d, turned_ref in enumerate(turned_refs):
+            blocks = jnp.concatenate(
+                [received_ref[c + targets_ref[d]] for c in range(0, cells, grid_cols)], axis=0
+            )
+            part = jnp.dot(turned_ref[...], blocks, preferred_element_type=jnp.float32)
+            total = part if total is None else total + part
         out = base_ref[...] + total.T / jnp.full((1, vectors), halfwidth_ref[0])
         out_ref[...] = out
         panel_ref[...] = out.astype(jnp.bfloat16)
 
     return pl.pallas_call(
         kernel,
-        in_specs=[SMEM] + [VMEM] * 3,
+        in_specs=[SMEM] * 2 + [VMEM] * (2 + grid_cols),
         out_specs=[VMEM] * 2,
         out_shape=[
             jax.ShapeDtypeStruct((orb, vectors), jnp.float32),
@@ -212,40 +216,42 @@
         ],
         compiler_params=pltpu.CompilerParams(vmem_limit_bytes=received.size * 4 + 2 * SPARE),
         name="backward_first",
-    )(halfwidth, turned_panels, received, base)
-
-
-def turn_blocks(targets, received, panel, grid_rows):
+    )(targets, halfwidth, received, base, *turned_panels)
+
+
+def pick_blocks(targets, received, panel, grid_rows):
     _, orb, _ = received.shape
     grid_cols = targets.shape[0]
 
     def kernel(targets_ref, received_ref, panel_ref, *outs):
-        for d, out in enumerate(outs):
+        for d, out in enumerate(outs, start=1):
             for c in range(grid_rows):
-                out[c] = received_ref[c * grid_cols + targets_ref[d]].T
+                out[c] = received_ref[c * grid_cols + targets_ref[d]]
 
     return pl.pallas_call(
         kernel,
         in_specs=[SMEM, VMEM, VMEM],
-        out_specs=[VMEM] * grid_cols,
-        out_shape=[jax.ShapeDtypeStruct((grid_rows, orb, orb), jnp.bfloat16)] * grid_cols,
+        out_specs=[VMEM] * (grid_cols - 1),
+        out_shape=[jax.ShapeDtypeStruct((grid_rows, orb, orb), jnp.bfloat16)] * (grid_cols - 1),
         compiler_params=pltpu.CompilerParams(vmem_limit_bytes=received.size * 4 + SPARE),
-        name="turn_blocks",
+        name="pick_blocks",
     )(targets, received, panel)
 
 
-def merge_tile(sources, targets, dense, stacks):
+def merge_tile(sources, targets, dense, received, stacks):
     _, orb, _ = dense.shape
     grid_rows = sources.shape[0]
     grid_cols = targets.shape[0]
 
-    def kernel(sources_ref, targets_ref, dense_ref, *refs):
+    def kernel(sources_ref, targets_ref, dense_ref, received_ref, *refs):
         *stack_refs, tile_ref = refs
         for k in range(grid_rows):
             source = sources_ref[k]
-            for d, stack_ref in enumerate(stack_refs):
-                own = dense_ref[source * grid_cols + targets_ref[d]].astype(jnp.float32)
-                block = (own + stack_ref[source].astype(jnp.float32)).astype(jnp.bfloat16)
+            for d in range(grid_cols):
+                cell = source * grid_cols + targets_ref[d]
+                turned = received_ref[cell] if d == 0 else stack_refs[d - 1][source]
+                own = dense_ref[cell].astype(jnp.float32)
+                block = (own + turned.T.astype(jnp.float32)).astype(jnp.bfloat16)
                 tile_ref[d * orb : (d + 1) * orb, k * orb : (k + 1) * orb] = block
 
     return pl.pallas_call(
@@ -253,9 +259,9 @@
         in_specs=[SMEM] * 2 + [VMEM] * (1 + grid_cols),
         out_specs=VMEM,
         out_shape=jax.ShapeDtypeStruct((grid_cols * orb, grid_rows * orb), jnp.bfloat16),
-        compiler_params=pltpu.CompilerParams(vmem_limit_bytes=dense.size * 6 + SPARE),
+        compiler_params=pltpu.CompilerParams(vmem_limit_bytes=dense.size * 8 + SPARE),
         name="merge_tile",
-    )(sources, targets, dense, *stacks)
+    )(sources, targets, dense, received, *stacks)
 
 
 def apply_tile(tile, pieces, current, previous, center, halfwidth, grid_cols):
@@ -325,19 +331,23 @@
     dense = after(dense, pieces[1:])
     received = lax.all_to_all(dense, "row", 0, 0, tiled=True)
     panel = jnp.concatenate(gather(pieces, same, first=1), axis=0)
-    panels = [panel] + [swap(panel, "col", grid_cols, d) for d in range(1, grid_cols)]
+    turned_panel = turn_panel(early_sources, panel, dense.shape[1])
+    turned_panels = [turned_panel] + [
+        swap(turned_panel, "col", grid_cols, d) for d in range(1, grid_cols)
+    ]
     base, *others = forward_first(
         early_sources, targets, dense, panel, initial, center, halfwidth
     )
     for d, other in enumerate(others, start=1):
         base = base + swap(other, "col", grid_cols, d)
-    turned_panels = turn_panels(early_sources, targets, panels, dense.shape[1])
 
     previous = initial
-    current, panel = backward_first(turned_panels, received, base, halfwidth)
-    stacks = turn_blocks(targets, received, panel, grid_rows)
-    stacks = [stacks[0]] + [swap(stacks[d], "col", grid_cols, d) for d in range(1, grid_cols)]
-    tile = merge_tile(sources, targets, dense, stacks)
+    current, panel = backward_first(targets, turned_panels, received, base, halfwidth)
+    stacks = []
+    if grid_cols > 1:
+        stacks = pick_blocks(targets, received, panel, grid_rows)
+    stacks = [swap(stack, "col", grid_cols, d) for d, stack in enumerate(stacks, start=1)]
+    tile = merge_tile(sources, targets, dense, received, stacks)
     for degree_step in range(1, DEGREE):
         pieces = gather([panel], turned)
         base, *others = apply_tile(tile, pieces, current, previous, center, halfwidth, grid_cols)

time: 76.6 us -> 81.2 us (1.060)
  waiting for transfers between devices: 28.2 us -> 35.3 us
  local copies, waits for them, and re-layouts: 3.01 us -> 0.13 us
    ppermute x18, waiting for transfers between devices: 24.5 us -> 28.4 us  [swap_rows(): return lax.ppermute(x, ('row', 'col'), pairs)]
    all_to_all x1, waiting for transfers between devices: 0.31 us -> 3.51 us  [body(): received = lax.all_to_all(dense, 'row', 0, 0, tiled=True)]
    unnamed x24 -> x16, local copies, waits for them, and re-layouts: 2.98 us -> 0.1 us
    all_to_all x1, starting transfers between devices: 6.48 us -> 5.03 us  [body(): received = lax.all_to_all(dense, 'row', 0, 0, tiled=True)]
    pallas_call x2, Pallas kernels: 0.84 us -> 1.82 us  [apply_tile(): pl.pallas_call(kernel, in_specs=[SMEM] * 2 + [VMEM] * (3 + count), out_sp...]
    ppermute x18, starting transfers between devices: 25.4 us -> 26.4 us  [swap_rows(): return lax.ppermute(x, ('row', 'col'), pairs)]
  transfers between devices with their start and end apart: 24 -> 24, of which waited for: 18 -> 19; matrix products, arithmetic and copies ran while one was open for 0% -> 0% of each run, Pallas kernels for 9% -> 7%
where the time goes in v10:
time: 81.2 us; the launch traced here: 80.8 us
  waiting for transfers between devices  35.3 us (43%)
  starting transfers between devices  32.3 us (40%)
  Pallas kernels  9.35 us (12%)
  between operations  2.2 us (3%)
  other arithmetic  1.54 us (2%)
    ppermute x18, waiting for transfers between devices, swap_rows(): return lax.ppermute(x, ('row', 'col'), pairs)  28.4 us
    ppermute x18, starting transfers between devices, swap_rows(): return lax.ppermute(x, ('row', 'col'), pairs)  26.4 us
    all_to_all x1, starting transfers between devices, body(): received = lax.all_to_all(dense, 'row', 0, 0, tiled=True)  5.03 us
    all_to_all x1, waiting for transfers between devices, body(): received = lax.all_to_all(dense, 'row', 0, 0, tiled=True)  3.51 us
    ppermute x5, waiting for transfers between devices, swap(): lax.ppermute(x, axis, [(source, source ^ offset) for source in range(size)])  3.39 us
    pallas_call x1, Pallas kernels, build_tile(): pl.pallas_call(kernel, in_specs=[HBM, HBM, SMEM, HBM], out_specs=VMEM, sc...  2.78 us
    pallas_call x2, Pallas kernels, apply_tile(): pl.pallas_call(kernel, in_specs=[SMEM] * 2 + [VMEM] * (3 + count), out_sp...  1.82 us
  transfers between devices with their start and end apart: 24, of which 19 were waited for; matrix products, arithmetic and copies ran while one was open for 0% of the time, Pallas kernels for 7%

profile of v10, /device:TPU:0, one launch (start us, length us, event | category | flops | bytes accessed | tf_op | source)
XLA Modules:
  0.0 80.8 jit_solution(2111222816260490843)
XLA Ops:
  0.0 0.8 %constant_dynamic-update-slice_fusion.6 = (bf16[2048,128]{1,0:T(8,128)(2,1)S(1)}, bf16[128,128]{1,0:T(8,128)(2,1)S(1)}) fusion(f32[128,128]{1,0:T(8,128)} %previous_ref.1), kind=kLoop, calls=%fused_computation.8 | loop fusion | flops 16383 | bytes 131072
  0.9 3.1 %collective-permute-start = (bf16[128,128]{1,0:T(8,128)(2,1)S(1)}, bf16[128,128]{1,0:T(8,128)(2,1)S(1)}, u32[]{:S(2)}, u32[]{:S(2)}) collective-permute-start(bf16[128,128]{1,0:T(8,128)(2,1)S(1)} %get-tuple-element.24), channel_id=1, source_target_pairs={{0,8},{1,9},{2,10},{3,11},{4,12},{5,13},{6,14},{7,15},{8,0},{9,1},... | collective-permute-start | bytes 98312 | tf_op jit(solution)/shard_map/ppermute | solution.py:46
  3.9 2.6 %collective-permute-start.1 = (bf16[128,128]{1,0:T(8,128)(2,1)S(1)}, bf16[128,128]{1,0:T(8,128)(2,1)S(1)}, u32[]{:S(2)}, u32[]{:S(2)}) collective-permute-start(bf16[128,128]{1,0:T(8,128)(2,1)S(1)} %get-tuple-element.24), channel_id=1, source_target_pairs={{0,16},{1,17},{2,18},{3,19},{4,20},{5,21},{6,22},{7,23},{8,24},{9,... | collective-permute-start | bytes 98312 | tf_op jit(solution)/shard_map/ppermute | solution.py:46
  7.2 2.8 %build_tile.1.refs_0_ = bf16[32,128,128]{2,1,0:T(8,128)(2,1)} custom-call(s32[1,64]{1,0:T(1,128)} %bitcast.6, s32[1,64]{1,0:T(1,128)} %bitcast.7, s32[1,1]{1,0:T(1,128)S(6)} %copy.21.count_ref, bf16[64,128,128]{2,1,0:T(8,128)(2,1)} %bitcast.5), custom_call_target="tpu_custom_call" | custom-call | tf_op jit(solution)/shard_map/build_tile/pallas_call | solution.py:89
  10.0 2.2 %collective-permute-done.2.refs_3_ = bf16[128,128]{1,0:T(8,128)(2,1)S(1)} collective-permute-done((bf16[128,128]{1,0:T(8,128)(2,1)S(1)}, bf16[128,128]{1,0:T(8,128)(2,1)S(1)}, u32[]{:S(2)}, u32[]{:S(2)}) %collective-permute-start.2) | collective-permute-done | bytes 32800 | tf_op jit(solution)/shard_map/ppermute | solution.py:46
  12.2 5.0 %all-to-all-start = ((bf16[32,128,128]{2,1,0:T(8,128)(2,1)}), bf16[32,128,128]{2,1,0:T(8,128)(2,1)S(1)}, u32[]{:S(2)}, u32[]{:S(2)}) async-start(bf16[32,128,128]{2,1,0:T(8,128)(2,1)} %after.1.dense_ref), calls=%async_computation | async-start | bytes 2097152 | tf_op jit(solution)/shard_map/all_to_all | solution.py:332
  17.3 2.0 %collective-permute-start.3 = (bf16[512,128]{1,0:T(8,128)(2,1)S(1)}, bf16[512,128]{1,0:T(8,128)(2,1)S(1)}, u32[]{:S(2)}, u32[]{:S(2)}) collective-permute-start(bf16[512,128]{1,0:T(8,128)(2,1)S(1)} %pad_maximum_fusion), channel_id=1, source_target_pairs={{0,2},{1,3},{2,0},{3,1},{4,6},{5,7},{6,4},{7,5},{8,10},{9,11},{10,... | collective-permute-start | bytes 393224 | tf_op jit(solution)/shard_map/ppermute | solution.py:46
  19.3 1.5 %collective-permute-start.4 = (bf16[512,128]{1,0:T(8,128)(2,1)S(1)}, bf16[512,128]{1,0:T(8,128)(2,1)S(1)}, u32[]{:S(2)}, u32[]{:S(2)}) collective-permute-start(bf16[512,128]{1,0:T(8,128)(2,1)S(1)} %pad_maximum_fusion), channel_id=1, source_target_pairs={{0,4},{1,5},{2,6},{3,7},{4,0},{5,1},{6,2},{7,3},{8,12},{9,13},{10,... | collective-permute-start | bytes 393224 | tf_op jit(solution)/shard_map/ppermute | solution.py:46
  20.8 0.1 collective-permute-start.5
  20.9 5.2 %collective-permute-done.3 = bf16[512,128]{1,0:T(8,128)(2,1)S(1)} collective-permute-done((bf16[512,128]{1,0:T(8,128)(2,1)S(1)}, bf16[512,128]{1,0:T(8,128)(2,1)S(1)}, u32[]{:S(2)}, u32[]{:S(2)}) %collective-permute-start.3) | collective-permute-done | bytes 131104 | tf_op jit(solution)/shard_map/ppermute | solution.py:46
  26.1 5.6 %collective-permute-done.4 = bf16[512,128]{1,0:T(8,128)(2,1)S(1)} collective-permute-done((bf16[512,128]{1,0:T(8,128)(2,1)S(1)}, bf16[512,128]{1,0:T(8,128)(2,1)S(1)}, u32[]{:S(2)}, u32[]{:S(2)}) %collective-permute-start.4) | collective-permute-done | bytes 131104 | tf_op jit(solution)/shard_map/ppermute | solution.py:46
  31.7 1.1 %collective-permute-done.5 = bf16[512,128]{1,0:T(8,128)(2,1)S(1)} collective-permute-done((bf16[512,128]{1,0:T(8,128)(2,1)S(1)}, bf16[512,128]{1,0:T(8,128)(2,1)S(1)}, u32[]{:S(2)}, u32[]{:S(2)}) %collective-permute-start.5) | collective-permute-done | bytes 131104 | tf_op jit(solution)/shard_map/ppermute | solution.py:46
  32.9 0.7 turn_panel.1.refs_0_
  33.6 0.1 collective-permute-start.7
  35.0 1.0 %forward_first.1 = (f32[128,128]{1,0:T(8,128)S(1)}, f32[128,128]{1,0:T(8,128)S(1)}) custom-call(s32[16]{0:T(128)S(1)} %broadcast_xor_fusion.sources_ref, s32[2]{0:T(128)S(1)} %iota_xor_fusion.targets_ref, f32[1]{0:T(128)S(6)} %copy.22.center_ref, f32[1]{0:T(128)S(6)} %copy.23.halfwidth_ref, bf16[32,128,128]{2,1,0:T(8,128)(2,1)S(1)} %copy-done, ...), custom_call_target="tpu_custom_call" | custom-call | tf_op jit(solution)/shard_map/forward_first/pallas_call | solution.py:160
  36.0 0.6 collective-permute-start.6
  36.6 0.9 %collective-permute-done.6 = f32[128,128]{1,0:T(8,128)S(1)} collective-permute-done((f32[128,128]{1,0:T(8,128)S(1)}, f32[128,128]{1,0:T(8,128)S(1)}, u32[]{:S(2)}, u32[]{:S(2)}) %collective-permute-start.6) | collective-permute-done | bytes 65568 | tf_op jit(solution)/shard_map/ppermute | solution.py:37
  37.5 3.5 %all-to-all-done.received_ref = bf16[32,128,128]{2,1,0:T(8,128)(2,1)S(1)} async-done(((bf16[32,128,128]{2,1,0:T(8,128)(2,1)}), bf16[32,128,128]{2,1,0:T(8,128)(2,1)S(1)}, u32[]{:S(2)}, u32[]{:S(2)}) %all-to-all-start) | async-done | bytes 1048608 | tf_op jit(solution)/shard_map/all_to_all | solution.py:332
  41.0 1.5 %backward_first.1 = (f32[128,128]{1,0:T(8,128)S(1)}, bf16[128,128]{1,0:T(8,128)(2,1)S(1)}) custom-call(s32[2]{0:T(128)S(1)} %iota_xor_fusion.targets_ref, f32[1]{0:T(128)S(6)} %copy.23.halfwidth_ref, bf16[32,128,128]{2,1,0:T(8,128)(2,1)S(1)} %all-to-all-done.received_ref, f32[128,128]{1,0:T(8,128)S(1)} %add.18.base_ref, ...), custom_call_target="tpu_custom_call" | custom-call | tf_op jit(solution)/shard_map/backward_first/pallas_call | solution.py:209
  42.6 3.1 %collective-permute-start.9 = (bf16[128,128]{1,0:T(8,128)(2,1)S(1)}, bf16[128,128]{1,0:T(8,128)(2,1)S(1)}, u32[]{:S(2)}, u32[]{:S(2)}) collective-permute-start(bf16[128,128]{1,0:T(8,128)(2,1)S(1)} %get-tuple-element.15.panel_ref), channel_id=1, source_target_pairs={{0,8},{1,3},{2,10},{3,1},{4,12},{5,7},{6,14},{7,5},{8,0},{9,11},{1... | collective-permute-start | bytes 98312 | tf_op jit(solution)/shard_map/ppermute | solution.py:46
  45.6 0.6 pick_blocks.1
  46.3 0.3 collective-permute-start.10
  46.7 2.1 %collective-permute-start.11 = (bf16[128,128]{1,0:T(8,128)(2,1)S(1)}, bf16[128,128]{1,0:T(8,128)(2,1)S(1)}, u32[]{:S(2)}, u32[]{:S(2)}) collective-permute-start(bf16[128,128]{1,0:T(8,128)(2,1)S(1)} %get-tuple-element.15.panel_ref), channel_id=1, source_target_pairs={{0,24},{1,7},{2,26},{3,5},{4,28},{5,3},{6,30},{7,1},{8,16},{9,15},... | collective-permute-start | bytes 98312 | tf_op jit(solution)/shard_map/ppermute | solution.py:46
  48.8 2.4 %collective-permute-done.10 = bf16[128,128]{1,0:T(8,128)(2,1)S(1)} collective-permute-done((bf16[128,128]{1,0:T(8,128)(2,1)S(1)}, bf16[128,128]{1,0:T(8,128)(2,1)S(1)}, u32[]{:S(2)}, u32[]{:S(2)}) %collective-permute-start.10) | collective-permute-done | bytes 32800 | tf_op jit(solution)/shard_map/ppermute | solution.py:46
  51.2 1.2 %collective-permute-done.11 = bf16[128,128]{1,0:T(8,128)(2,1)S(1)} collective-permute-done((bf16[128,128]{1,0:T(8,128)(2,1)S(1)}, bf16[128,128]{1,0:T(8,128)(2,1)S(1)}, u32[]{:S(2)}, u32[]{:S(2)}) %collective-permute-start.11) | collective-permute-done | bytes 32800 | tf_op jit(solution)/shard_map/ppermute | solution.py:46
  52.4 0.8 %collective-permute-start.12 = (bf16[512,128]{1,0:T(8,128)(2,1)S(1)}, bf16[512,128]{1,0:T(8,128)(2,1)S(1)}, u32[]{:S(2)}, u32[]{:S(2)}) collective-permute-start(bf16[512,128]{1,0:T(8,128)(2,1)S(1)} %constant_dynamic-update-slice_fusion.7.refs_0_), channel_id=1, source_target_pairs={{0,2},{1,9},{2,0},{3,11},{4,6},{5,13},{6,4},{7,15},{8,10},{9,1},{1... | collective-permute-start | bytes 393224 | tf_op jit(solution)/shard_map/ppermute | solution.py:46
  53.2 1.9 %collective-permute-start.13 = (bf16[512,128]{1,0:T(8,128)(2,1)S(1)}, bf16[512,128]{1,0:T(8,128)(2,1)}, u32[]{:S(2)}, u32[]{:S(2)}) collective-permute-start(bf16[512,128]{1,0:T(8,128)(2,1)S(1)} %constant_dynamic-update-slice_fusion.7.refs_0_), channel_id=1, source_target_pairs={{0,4},{1,17},{2,6},{3,19},{4,0},{5,21},{6,2},{7,23},{8,12},{9,25},... | collective-permute-start | bytes 393224 | tf_op jit(solution)/shard_map/ppermute | solution.py:46
  55.1 0.9 %collective-permute-start.14 = (bf16[512,128]{1,0:T(8,128)(2,1)S(1)}, bf16[512,128]{1,0:T(8,128)(2,1)}, u32[]{:S(2)}, u32[]{:S(2)}) collective-permute-start(bf16[512,128]{1,0:T(8,128)(2,1)S(1)} %constant_dynamic-update-slice_fusion.7.refs_0_), channel_id=1, source_target_pairs={{0,6},{1,25},{2,4},{3,27},{4,2},{5,29},{6,0},{7,31},{8,14},{9,17},... | collective-permute-start | bytes 393224 | tf_op jit(solution)/shard_map/ppermute | solution.py:46
  56.0 0.9 %merge_tile.1.tile_ref = bf16[256,2048]{1,0:T(8,128)(2,1)S(1)} custom-call(s32[16]{0:T(128)S(1)} %xor_bitcast_fusion.sources_ref, s32[2]{0:T(128)S(1)} %iota_xor_fusion.targets_ref, bf16[32,128,128]{2,1,0:T(8,128)(2,1)S(1)} %copy-done, bf16[32,128,128]{2,1,0:T(8,128)(2,1)S(1)} %all-to-all-done.received_ref, ...), custom_call_target="tpu_custom_call" | custom-call | tf_op jit(solution)/shard_map/merge_tile/pallas_call | solution.py:257
  56.9 0.4 collective-permute-done.12.refs_1_
  57.4 1.7 %collective-permute-done.13.refs_2_ = bf16[512,128]{1,0:T(8,128)(2,1)} collective-permute-done((bf16[512,128]{1,0:T(8,128)(2,1)S(1)}, bf16[512,128]{1,0:T(8,128)(2,1)}, u32[]{:S(2)}, u32[]{:S(2)}) %collective-permute-start.13) | collective-permute-done | bytes 131104 | tf_op jit(solution)/shard_map/ppermute | solution.py:46
  59.0 2.0 %collective-permute-done.14.refs_3_ = bf16[512,128]{1,0:T(8,128)(2,1)} collective-permute-done((bf16[512,128]{1,0:T(8,128)(2,1)S(1)}, bf16[512,128]{1,0:T(8,128)(2,1)}, u32[]{:S(2)}, u32[]{:S(2)}) %collective-permute-start.14) | collective-permute-done | bytes 131104 | tf_op jit(solution)/shard_map/ppermute | solution.py:46
  61.1 1.4 %apply_tile.2 = (f32[128,128]{1,0:T(8,128)S(1)}, f32[128,128]{1,0:T(8,128)S(1)}) custom-call(f32[1]{0:T(128)S(6)} %copy.22.center_ref, f32[1]{0:T(128)S(6)} %copy.23.halfwidth_ref, bf16[256,2048]{1,0:T(8,128)(2,1)S(1)} %merge_tile.1.tile_ref, f32[128,128]{1,0:T(8,128)S(1)} %get-tuple-element.16.current_ref.previous_ref, f32[128,128]{1,0:T(8,128)S(1)} %copy-done.1, ...), custom_call_target="tpu_custom_call" | custom-call | tf_op jit(solution)/shard_map/apply_tile/pallas_call | solution.py:291
  62.6 1.2 %collective-permute-done.15 = f32[128,128]{1,0:T(8,128)S(1)} collective-permute-done((f32[128,128]{1,0:T(8,128)S(1)}, f32[128,128]{1,0:T(8,128)S(1)}, u32[]{:S(2)}, u32[]{:S(2)}) %collective-permute-start.15) | collective-permute-done | bytes 65568 | tf_op jit(solution)/shard_map/ppermute | solution.py:37
  63.8 1.2 %collective-permute-start.18 = (bf16[128,128]{1,0:T(8,128)(2,1)S(1)}, bf16[128,128]{1,0:T(8,128)(2,1)S(1)}, u32[]{:S(2)}, u32[]{:S(2)}) collective-permute-start(bf16[128,128]{1,0:T(8,128)(2,1)S(1)} %get-tuple-element.21), channel_id=1, source_target_pairs={{0,24},{1,7},{2,26},{3,5},{4,28},{5,3},{6,30},{7,1},{8,16},{9,15},... | collective-permute-start | bytes 98312 | tf_op jit(solution)/shard_map/ppermute | solution.py:46
  65.1 3.2 %collective-permute-start.16 = (bf16[128,128]{1,0:T(8,128)(2,1)S(1)}, bf16[128,128]{1,0:T(8,128)(2,1)S(1)}, u32[]{:S(2)}, u32[]{:S(2)}) collective-permute-start(bf16[128,128]{1,0:T(8,128)(2,1)S(1)} %get-tuple-element.21), channel_id=1, source_target_pairs={{0,8},{1,3},{2,10},{3,1},{4,12},{5,7},{6,14},{7,5},{8,0},{9,11},{1... | collective-permute-start | bytes 98312 | tf_op jit(solution)/shard_map/ppermute | solution.py:46
  68.3 1.3 %collective-permute-done.18 = bf16[128,128]{1,0:T(8,128)(2,1)S(1)} collective-permute-done((bf16[128,128]{1,0:T(8,128)(2,1)S(1)}, bf16[128,128]{1,0:T(8,128)(2,1)S(1)}, u32[]{:S(2)}, u32[]{:S(2)}) %collective-permute-start.18) | collective-permute-done | bytes 32800 | tf_op jit(solution)/shard_map/ppermute | solution.py:46
  69.6 0.8 collective-permute-done.17
  70.4 0.1 collective-permute-done.16
  70.5 1.5 %collective-permute-start.19 = (bf16[512,128]{1,0:T(8,128)(2,1)S(1)}, bf16[512,128]{1,0:T(8,128)(2,1)S(1)}, u32[]{:S(2)}, u32[]{:S(2)}) collective-permute-start(bf16[512,128]{1,0:T(8,128)(2,1)S(1)} %pad_maximum_fusion.1.refs_0_), channel_id=1, source_target_pairs={{0,2},{1,9},{2,0},{3,11},{4,6},{5,13},{6,4},{7,15},{8,10},{9,1},{1... | collective-permute-start | bytes 393224 | tf_op jit(solution)/shard_map/ppermute | solution.py:46
  72.0 0.5 collective-permute-start.20
  72.6 1.5 %collective-permute-start.21 = (bf16[512,128]{1,0:T(8,128)(2,1)S(1)}, bf16[512,128]{1,0:T(8,128)(2,1)S(1)}, u32[]{:S(2)}, u32[]{:S(2)}) collective-permute-start(bf16[512,128]{1,0:T(8,128)(2,1)S(1)} %pad_maximum_fusion.1.refs_0_), channel_id=1, source_target_pairs={{0,6},{1,25},{2,4},{3,27},{4,2},{5,29},{6,0},{7,31},{8,14},{9,17},... | collective-permute-start | bytes 393224 | tf_op jit(solution)/shard_map/ppermute | solution.py:46
  74.1 1.5 %collective-permute-done.19.refs_1_ = bf16[512,128]{1,0:T(8,128)(2,1)S(1)} collective-permute-done((bf16[512,128]{1,0:T(8,128)(2,1)S(1)}, bf16[512,128]{1,0:T(8,128)(2,1)S(1)}, u32[]{:S(2)}, u32[]{:S(2)}) %collective-permute-start.19) | collective-permute-done | bytes 131104 | tf_op jit(solution)/shard_map/ppermute | solution.py:46
  75.5 1.5 %collective-permute-done.20.refs_2_ = bf16[512,128]{1,0:T(8,128)(2,1)S(1)} collective-permute-done((bf16[512,128]{1,0:T(8,128)(2,1)S(1)}, bf16[512,128]{1,0:T(8,128)(2,1)S(1)}, u32[]{:S(2)}, u32[]{:S(2)}) %collective-permute-start.20) | collective-permute-done | bytes 131104 | tf_op jit(solution)/shard_map/ppermute | solution.py:46
  77.0 1.4 %collective-permute-done.21.refs_3_ = bf16[512,128]{1,0:T(8,128)(2,1)S(1)} collective-permute-done((bf16[512,128]{1,0:T(8,128)(2,1)S(1)}, bf16[512,128]{1,0:T(8,128)(2,1)S(1)}, u32[]{:S(2)}, u32[]{:S(2)}) %collective-permute-start.21) | collective-permute-done | bytes 131104 | tf_op jit(solution)/shard_map/ppermute | solution.py:46
  78.4 0.4 apply_tile.3
  78.9 1.2 %collective-permute-done.22 = f32[128,128]{1,0:T(8,128)S(1)} collective-permute-done((f32[128,128]{1,0:T(8,128)S(1)}, f32[128,128]{1,0:T(8,128)S(1)}, u32[]{:S(2)}, u32[]{:S(2)}) %collective-permute-start.22) | collective-permute-done | bytes 65568 | tf_op jit(solution)/shard_map/ppermute | solution.py:37
  80.2 0.6 add.20
  (36 shorter events, 0.5 us)
Async XLA Ops:
  0.9 9.1 %collective-permute-start = (bf16[128,128]{1,0:T(8,128)(2,1)S(1)}, bf16[128,128]{1,0:T(8,128)(2,1)S(1)}, u32[]{:S(2)}, u32[]{:S(2)}) collective-permute-start(bf16[128,128]{1,0:T(8,128)(2,1)S(1)} %get-tuple-element.24), channel_id=1, source_target_pairs={{0,8},{1,9},{2,10},{3,11},{4,12},{5,13},{6,14},{7,15},{8,0},{9,1},... | collective-permute-start | bytes 98312 | tf_op jit(solution)/shard_map/ppermute | solution.py:46
  3.9 6.1 %collective-permute-start.1 = (bf16[128,128]{1,0:T(8,128)(2,1)S(1)}, bf16[128,128]{1,0:T(8,128)(2,1)S(1)}, u32[]{:S(2)}, u32[]{:S(2)}) collective-permute-start(bf16[128,128]{1,0:T(8,128)(2,1)S(1)} %get-tuple-element.24), channel_id=1, source_target_pairs={{0,16},{1,17},{2,18},{3,19},{4,20},{5,21},{6,22},{7,23},{8,24},{9,... | collective-permute-start | bytes 98312 | tf_op jit(solution)/shard_map/ppermute | solution.py:46
  6.5 5.7 %collective-permute-start.2 = (bf16[128,128]{1,0:T(8,128)(2,1)S(1)}, bf16[128,128]{1,0:T(8,128)(2,1)S(1)}, u32[]{:S(2)}, u32[]{:S(2)}) collective-permute-start(bf16[128,128]{1,0:T(8,128)(2,1)S(1)} %get-tuple-element.24), channel_id=1, source_target_pairs={{0,24},{1,25},{2,26},{3,27},{4,28},{5,29},{6,30},{7,31},{8,16},{9,... | collective-permute-start | bytes 98312 | tf_op jit(solution)/shard_map/ppermute | solution.py:46
  10.0 7.3 %copy-start.3 = (s32[16]{0:T(128)S(1)}, s32[16]{0:T(128)}, u32[]{:S(2)}) copy-start(s32[16]{0:T(128)} %constant.26.clone) | copy-start | bytes 196
  12.2 22.8 %copy-start = (bf16[32,128,128]{2,1,0:T(8,128)(2,1)S(1)}, bf16[32,128,128]{2,1,0:T(8,128)(2,1)}, u32[]{:S(2)}) copy-start(bf16[32,128,128]{2,1,0:T(8,128)(2,1)} %after.1.dense_ref) | copy-start | bytes 3145732
  12.2 22.8 %copy-start.1 = (f32[128,128]{1,0:T(8,128)S(1)}, f32[128,128]{1,0:T(8,128)}, u32[]{:S(2)}) copy-start(f32[128,128]{1,0:T(8,128)} %previous_ref.1) | copy-start | bytes 196612
  12.2 28.8 %all-to-all-start = ((bf16[32,128,128]{2,1,0:T(8,128)(2,1)}), bf16[32,128,128]{2,1,0:T(8,128)(2,1)S(1)}, u32[]{:S(2)}, u32[]{:S(2)}) async-start(bf16[32,128,128]{2,1,0:T(8,128)(2,1)} %after.1.dense_ref), calls=%async_computation | async-start | bytes 2097152 | tf_op jit(solution)/shard_map/all_to_all | solution.py:332
  17.3 8.8 %collective-permute-start.3 = (bf16[512,128]{1,0:T(8,128)(2,1)S(1)}, bf16[512,128]{1,0:T(8,128)(2,1)S(1)}, u32[]{:S(2)}, u32[]{:S(2)}) collective-permute-start(bf16[512,128]{1,0:T(8,128)(2,1)S(1)} %pad_maximum_fusion), channel_id=1, source_target_pairs={{0,2},{1,3},{2,0},{3,1},{4,6},{5,7},{6,4},{7,5},{8,10},{9,11},{10,... | collective-permute-start | bytes 393224 | tf_op jit(solution)/shard_map/ppermute | solution.py:46
  19.3 12.4 %collective-permute-start.4 = (bf16[512,128]{1,0:T(8,128)(2,1)S(1)}, bf16[512,128]{1,0:T(8,128)(2,1)S(1)}, u32[]{:S(2)}, u32[]{:S(2)}) collective-permute-start(bf16[512,128]{1,0:T(8,128)(2,1)S(1)} %pad_maximum_fusion), channel_id=1, source_target_pairs={{0,4},{1,5},{2,6},{3,7},{4,0},{5,1},{6,2},{7,3},{8,12},{9,13},{10,... | collective-permute-start | bytes 393224 | tf_op jit(solution)/shard_map/ppermute | solution.py:46
  20.8 12.1 %collective-permute-start.5 = (bf16[512,128]{1,0:T(8,128)(2,1)S(1)}, bf16[512,128]{1,0:T(8,128)(2,1)S(1)}, u32[]{:S(2)}, u32[]{:S(2)}) collective-permute-start(bf16[512,128]{1,0:T(8,128)(2,1)S(1)} %pad_maximum_fusion), channel_id=1, source_target_pairs={{0,6},{1,7},{2,4},{3,5},{4,2},{5,3},{6,0},{7,1},{8,14},{9,15},{10,... | collective-permute-start | bytes 393224 | tf_op jit(solution)/shard_map/ppermute | solution.py:46
  33.6 3.9 %collective-permute-start.7 = (bf16[128,2048]{1,0:T(8,128)(2,1)S(1)}, bf16[128,2048]{1,0:T(8,128)(2,1)}, u32[]{:S(2)}, u32[]{:S(2)}) collective-permute-start(bf16[128,2048]{1,0:T(8,128)(2,1)S(1)} %turn_panel.1.refs_0_), channel_id=1, source_target_pairs={{0,1},{1,0},{2,3},{3,2},{4,5},{5,4},{6,7},{7,6},{8,9},{9,8},{10,11... | collective-permute-start | bytes 1572872 | tf_op jit(solution)/shard_map/ppermute | solution.py:37
  36.0 1.5 %collective-permute-start.6 = (f32[128,128]{1,0:T(8,128)S(1)}, f32[128,128]{1,0:T(8,128)S(1)}, u32[]{:S(2)}, u32[]{:S(2)}) collective-permute-start(f32[128,128]{1,0:T(8,128)S(1)} %get-tuple-element.14), channel_id=1, source_target_pairs={{0,1},{1,0},{2,3},{3,2},{4,5},{5,4},{6,7},{7,6},{8,9},{9,8},{10,11... | collective-permute-start | bytes 196616 | tf_op jit(solution)/shard_map/ppermute | solution.py:37
  37.5 18.5 %copy-start.2 = (s32[2,16]{1,0:T(2,128)S(1)}, s32[2,16]{1,0:T(2,128)}, u32[]{:S(2)}) copy-start(s32[2,16]{1,0:T(2,128)} %constant.27.clone) | copy-start | bytes 388
  42.6 6.2 %collective-permute-start.9 = (bf16[128,128]{1,0:T(8,128)(2,1)S(1)}, bf16[128,128]{1,0:T(8,128)(2,1)S(1)}, u32[]{:S(2)}, u32[]{:S(2)}) collective-permute-start(bf16[128,128]{1,0:T(8,128)(2,1)S(1)} %get-tuple-element.15.panel_ref), channel_id=1, source_target_pairs={{0,8},{1,3},{2,10},{3,1},{4,12},{5,7},{6,14},{7,5},{8,0},{9,11},{1... | collective-permute-start | bytes 98312 | tf_op jit(solution)/shard_map/ppermute | solution.py:46
  46.2 9.8 %collective-permute-start.8 = (bf16[16,128,128]{2,1,0:T(8,128)(2,1)S(1)}, bf16[16,128,128]{2,1,0:T(8,128)(2,1)S(1)}, u32[]{:S(2)}, u32[]{:S(2)}) collective-permute-start(bf16[16,128,128]{2,1,0:T(8,128)(2,1)S(1)} %pick_blocks.1), channel_id=1, source_target_pairs={{0,1},{1,0},{2,3},{3,2},{4,5},{5,4},{6,7},{7,6},{8,9},{9,8},{10,11... | collective-permute-start | bytes 1572872 | tf_op jit(solution)/shard_map/ppermute | solution.py:37
  46.3 4.9 %collective-permute-start.10 = (bf16[128,128]{1,0:T(8,128)(2,1)S(1)}, bf16[128,128]{1,0:T(8,128)(2,1)S(1)}, u32[]{:S(2)}, u32[]{:S(2)}) collective-permute-start(bf16[128,128]{1,0:T(8,128)(2,1)S(1)} %get-tuple-element.15.panel_ref), channel_id=1, source_target_pairs={{0,16},{1,5},{2,18},{3,7},{4,20},{5,1},{6,22},{7,3},{8,24},{9,13},... | collective-permute-start | bytes 98312 | tf_op jit(solution)/shard_map/ppermute | solution.py:46
  46.7 5.7 %collective-permute-start.11 = (bf16[128,128]{1,0:T(8,128)(2,1)S(1)}, bf16[128,128]{1,0:T(8,128)(2,1)S(1)}, u32[]{:S(2)}, u32[]{:S(2)}) collective-permute-start(bf16[128,128]{1,0:T(8,128)(2,1)S(1)} %get-tuple-element.15.panel_ref), channel_id=1, source_target_pairs={{0,24},{1,7},{2,26},{3,5},{4,28},{5,3},{6,30},{7,1},{8,16},{9,15},... | collective-permute-start | bytes 98312 | tf_op jit(solution)/shard_map/ppermute | solution.py:46
  52.4 5.0 %collective-permute-start.12 = (bf16[512,128]{1,0:T(8,128)(2,1)S(1)}, bf16[512,128]{1,0:T(8,128)(2,1)S(1)}, u32[]{:S(2)}, u32[]{:S(2)}) collective-permute-start(bf16[512,128]{1,0:T(8,128)(2,1)S(1)} %constant_dynamic-update-slice_fusion.7.refs_0_), channel_id=1, source_target_pairs={{0,2},{1,9},{2,0},{3,11},{4,6},{5,13},{6,4},{7,15},{8,10},{9,1},{1... | collective-permute-start | bytes 393224 | tf_op jit(solution)/shard_map/ppermute | solution.py:46
  53.2 5.8 %collective-permute-start.13 = (bf16[512,128]{1,0:T(8,128)(2,1)S(1)}, bf16[512,128]{1,0:T(8,128)(2,1)}, u32[]{:S(2)}, u32[]{:S(2)}) collective-permute-start(bf16[512,128]{1,0:T(8,128)(2,1)S(1)} %constant_dynamic-update-slice_fusion.7.refs_0_), channel_id=1, source_target_pairs={{0,4},{1,17},{2,6},{3,19},{4,0},{5,21},{6,2},{7,23},{8,12},{9,25},... | collective-permute-start | bytes 393224 | tf_op jit(solution)/shard_map/ppermute | solution.py:46
  55.1 6.0 %collective-permute-start.14 = (bf16[512,128]{1,0:T(8,128)(2,1)S(1)}, bf16[512,128]{1,0:T(8,128)(2,1)}, u32[]{:S(2)}, u32[]{:S(2)}) collective-permute-start(bf16[512,128]{1,0:T(8,128)(2,1)S(1)} %constant_dynamic-update-slice_fusion.7.refs_0_), channel_id=1, source_target_pairs={{0,6},{1,25},{2,4},{3,27},{4,2},{5,29},{6,0},{7,31},{8,14},{9,17},... | collective-permute-start | bytes 393224 | tf_op jit(solution)/shard_map/ppermute | solution.py:46
  62.5 1.3 %collective-permute-start.15 = (f32[128,128]{1,0:T(8,128)S(1)}, f32[128,128]{1,0:T(8,128)S(1)}, u32[]{:S(2)}, u32[]{:S(2)}) collective-permute-start(f32[128,128]{1,0:T(8,128)S(1)} %get-tuple-element.18), channel_id=1, source_target_pairs={{0,1},{1,0},{2,3},{3,2},{4,5},{5,4},{6,7},{7,6},{8,9},{9,8},{10,11... | collective-permute-start | bytes 196616 | tf_op jit(solution)/shard_map/ppermute | solution.py:37
  63.8 5.8 %collective-permute-start.18 = (bf16[128,128]{1,0:T(8,128)(2,1)S(1)}, bf16[128,128]{1,0:T(8,128)(2,1)S(1)}, u32[]{:S(2)}, u32[]{:S(2)}) collective-permute-start(bf16[128,128]{1,0:T(8,128)(2,1)S(1)} %get-tuple-element.21), channel_id=1, source_target_pairs={{0,24},{1,7},{2,26},{3,5},{4,28},{5,3},{6,30},{7,1},{8,16},{9,15},... | collective-permute-start | bytes 98312 | tf_op jit(solution)/shard_map/ppermute | solution.py:46
  65.0 5.4 %collective-permute-start.17 = (bf16[128,128]{1,0:T(8,128)(2,1)S(1)}, bf16[128,128]{1,0:T(8,128)(2,1)S(1)}, u32[]{:S(2)}, u32[]{:S(2)}) collective-permute-start(bf16[128,128]{1,0:T(8,128)(2,1)S(1)} %get-tuple-element.21), channel_id=1, source_target_pairs={{0,16},{1,5},{2,18},{3,7},{4,20},{5,1},{6,22},{7,3},{8,24},{9,13},... | collective-permute-start | bytes 98312 | tf_op jit(solution)/shard_map/ppermute | solution.py:46
  65.1 5.4 %collective-permute-start.16 = (bf16[128,128]{1,0:T(8,128)(2,1)S(1)}, bf16[128,128]{1,0:T(8,128)(2,1)S(1)}, u32[]{:S(2)}, u32[]{:S(2)}) collective-permute-start(bf16[128,128]{1,0:T(8,128)(2,1)S(1)} %get-tuple-element.21), channel_id=1, source_target_pairs={{0,8},{1,3},{2,10},{3,1},{4,12},{5,7},{6,14},{7,5},{8,0},{9,11},{1... | collective-permute-start | bytes 98312 | tf_op jit(solution)/shard_map/ppermute | solution.py:46
  70.5 5.0 %collective-permute-start.19 = (bf16[512,128]{1,0:T(8,128)(2,1)S(1)}, bf16[512,128]{1,0:T(8,128)(2,1)S(1)}, u32[]{:S(2)}, u32[]{:S(2)}) collective-permute-start(bf16[512,128]{1,0:T(8,128)(2,1)S(1)} %pad_maximum_fusion.1.refs_0_), channel_id=1, source_target_pairs={{0,2},{1,9},{2,0},{3,11},{4,6},{5,13},{6,4},{7,15},{8,10},{9,1},{1... | collective-permute-start | bytes 393224 | tf_op jit(solution)/shard_map/ppermute | solution.py:46
  72.0 5.0 %collective-permute-start.20 = (bf16[512,128]{1,0:T(8,128)(2,1)S(1)}, bf16[512,128]{1,0:T(8,128)(2,1)S(1)}, u32[]{:S(2)}, u32[]{:S(2)}) collective-permute-start(bf16[512,128]{1,0:T(8,128)(2,1)S(1)} %pad_maximum_fusion.1.refs_0_), channel_id=1, source_target_pairs={{0,4},{1,17},{2,6},{3,19},{4,0},{5,21},{6,2},{7,23},{8,12},{9,25},... | collective-permute-start | bytes 393224 | tf_op jit(solution)/shard_map/ppermute | solution.py:46
  72.6 5.9 %collective-permute-start.21 = (bf16[512,128]{1,0:T(8,128)(2,1)S(1)}, bf16[512,128]{1,0:T(8,128)(2,1)S(1)}, u32[]{:S(2)}, u32[]{:S(2)}) collective-permute-start(bf16[512,128]{1,0:T(8,128)(2,1)S(1)} %pad_maximum_fusion.1.refs_0_), channel_id=1, source_target_pairs={{0,6},{1,25},{2,4},{3,27},{4,2},{5,29},{6,0},{7,31},{8,14},{9,17},... | collective-permute-start | bytes 393224 | tf_op jit(solution)/shard_map/ppermute | solution.py:46
  78.9 1.3 %collective-permute-start.22 = (f32[128,128]{1,0:T(8,128)S(1)}, f32[128,128]{1,0:T(8,128)S(1)}, u32[]{:S(2)}, u32[]{:S(2)}) collective-permute-start(f32[128,128]{1,0:T(8,128)S(1)} %get-tuple-element.20), channel_id=1, source_target_pairs={{0,1},{1,0},{2,3},{3,2},{4,5},{5,4},{6,7},{7,6},{8,9},{9,8},{10,11... | collective-permute-start | bytes 196616 | tf_op jit(solution)/shard_map/ppermute | solution.py:37

commit v11 on v10

--- a/solution.py
+++ b/solution.py
@@ -138,9 +138,12 @@
 
     def kernel(
         sources_ref, targets_ref, center_ref, halfwidth_ref,
-        dense_ref, panel_ref, current_ref, *refs,
+        dense_hbm, panel_ref, current_ref, *refs,
     ):
-        *outs, total_ref = refs
+        *outs, total_ref, dense_ref, sem = refs
+        copy = pltpu.make_async_copy(dense_hbm, dense_ref, sem)
+        copy.start()
+        copy.wait()
         total = None
         for k in range(grid_rows):
             blocks = dense_ref[pl.ds(sources_ref[k] * grid_cols, grid_cols)]
@@ -159,13 +162,20 @@
 
     return pl.pallas_call(
         kernel,
-        in_specs=[SMEM] * 4 + [VMEM] * 3,
+        in_specs=[SMEM] * 4 + [HBM] + [VMEM] * 2,
         out_specs=[VMEM] * grid_cols,
         out_shape=[jax.ShapeDtypeStruct((orb, vectors), jnp.float32)] * grid_cols,
-        scratch_shapes=[pltpu.VMEM((grid_cols, orb, vectors), jnp.float32)],
+        scratch_shapes=[
+            pltpu.VMEM((grid_cols, orb, vectors), jnp.float32),
+            pltpu.VMEM(dense.shape, dense.dtype),
+            pltpu.SemaphoreType.DMA,
+        ],
         compiler_params=pltpu.CompilerParams(vmem_limit_bytes=dense.size * 2 + 2 * SPARE),
         name="forward_first",
-    )(sources, targets, center, halfwidth, dense, panel, current)
+    )(
+        sources, targets, center, halfwidth,
+        pltpu.with_memory_space_constraint(dense, pltpu.HBM), panel, current,
+    )
 
 
 def turn_panel(sources, panel, orb):
@@ -187,28 +197,42 @@
     )(sources, panel)
 
 
-def backward_first(targets, turned_panels, received, base, halfwidth):
+def lay_panels(targets, turned_panels, grid_rows):
+    grid_cols = targets.shape[0]
+    vectors, width = turned_panels[0].shape
+    orb = width // grid_rows
+
+    def kernel(targets_ref, *refs):
+        *turned_refs, out_ref = refs
+        for d, turned_ref in enumerate(turned_refs):
+            for c in range(grid_rows):
+                at = pl.multiple_of((c * grid_cols + targets_ref[d]) * orb, orb)
+                out_ref[:, pl.ds(at, orb)] = turned_ref[:, c * orb : (c + 1) * orb]
+
+    return pl.pallas_call(
+        kernel,
+        in_specs=[SMEM] + [VMEM] * grid_cols,
+        out_specs=VMEM,
+        out_shape=jax.ShapeDtypeStruct((vectors, grid_cols * width), jnp.bfloat16),
+        compiler_params=pltpu.CompilerParams(vmem_limit_bytes=vectors * width * 4 * grid_cols + SPARE),
+        name="lay_panels",
+    )(targets, *turned_panels)
+
+
+def backward_first(turned_panels, received, base, halfwidth):
     cells, orb, _ = received.shape
-    grid_cols = targets.shape[0]
     vectors = base.shape[1]
 
-    def kernel(targets_ref, halfwidth_ref, received_ref, base_ref, *refs):
-        turned_refs = refs[:grid_cols]
-        out_ref, panel_ref = refs[grid_cols:]
-        total = None
-        for d, turned_ref in enumerate(turned_refs):
-            blocks = jnp.concatenate(
-                [received_ref[c + targets_ref[d]] for c in range(0, cells, grid_cols)], axis=0
-            )
-            part = jnp.dot(turned_ref[...], blocks, preferred_element_type=jnp.float32)
-            total = part if total is None else total + part
+    def kernel(halfwidth_ref, turned_ref, received_ref, base_ref, out_ref, panel_ref):
+        blocks = received_ref[...].reshape(cells * orb, orb)
+        total = jnp.dot(turned_ref[...], blocks, preferred_element_type=jnp.float32)
         out = base_ref[...] + total.T / jnp.full((1, vectors), halfwidth_ref[0])
         out_ref[...] = out
         panel_ref[...] = out.astype(jnp.bfloat16)
 
     return pl.pallas_call(
         kernel,
-        in_specs=[SMEM] * 2 + [VMEM] * (2 + grid_cols),
+        in_specs=[SMEM] + [VMEM] * 3,
         out_specs=[VMEM] * 2,
         out_shape=[
             jax.ShapeDtypeStruct((orb, vectors), jnp.float32),
@@ -216,7 +240,7 @@
         ],
         compiler_params=pltpu.CompilerParams(vmem_limit_bytes=received.size * 4 + 2 * SPARE),
         name="backward_first",
-    )(targets, halfwidth, received, base, *turned_panels)
+    )(halfwidth, turned_panels, received, base)
 
 
 def pick_blocks(targets, received, panel, grid_rows):
@@ -243,8 +267,11 @@
     grid_rows = sources.shape[0]
     grid_cols = targets.shape[0]
 
-    def kernel(sources_ref, targets_ref, dense_ref, received_ref, *refs):
-        *stack_refs, tile_ref = refs
+    def kernel(sources_ref, targets_ref, dense_hbm, received_ref, *refs):
+        *stack_refs, tile_ref, dense_ref, sem = refs
+        copy = pltpu.make_async_copy(dense_hbm, dense_ref, sem)
+        copy.start()
+        copy.wait()
         for k in range(grid_rows):
             source = sources_ref[k]
             for d in range(grid_cols):
@@ -256,12 +283,15 @@
 
     return pl.pallas_call(
         kernel,
-        in_specs=[SMEM] * 2 + [VMEM] * (1 + grid_cols),
+        in_specs=[SMEM] * 2 + [HBM] + [VMEM] * grid_cols,
         out_specs=VMEM,
         out_shape=jax.ShapeDtypeStruct((grid_cols * orb, grid_rows * orb), jnp.bfloat16),
+        scratch_shapes=[pltpu.VMEM(dense.shape, dense.dtype), pltpu.SemaphoreType.DMA],
         compiler_params=pltpu.CompilerParams(vmem_limit_bytes=dense.size * 8 + SPARE),
         name="merge_tile",
-    )(sources, targets, dense, received, *stacks)
+    )(
+        sources, targets, pltpu.with_memory_space_constraint(dense, pltpu.HBM), received, *stacks
+    )
 
 
 def apply_tile(tile, pieces, current, previous, center, halfwidth, grid_cols):
@@ -342,21 +372,23 @@
         base = base + swap(other, "col", grid_cols, d)
 
     previous = initial
-    current, panel = backward_first(targets, turned_panels, received, base, halfwidth)
+    current, panel = backward_first(lay_panels(targets, turned_panels, grid_rows), received, base, halfwidth)
+    pieces = gather([panel], turned, last=1)
     stacks = []
     if grid_cols > 1:
-        stacks = pick_blocks(targets, received, panel, grid_rows)
+        stacks = pick_blocks(targets, received, pieces[-1], grid_rows)
     stacks = [swap(stack, "col", grid_cols, d) for d, stack in enumerate(stacks, start=1)]
     tile = merge_tile(sources, targets, dense, received, stacks)
     for degree_step in range(1, DEGREE):
-        pieces = gather([panel], turned)
+        if degree_step > 1:
+            pieces = gather([current.astype(jnp.bfloat16)], turned, last=1)
+        pieces = gather(pieces, turned, first=1)
         base, *others = apply_tile(tile, pieces, current, previous, center, halfwidth, grid_cols)
         following = base
         for d, other in enumerate(others, start=1):
             following = following + swap(other, "col", grid_cols, d)
         previous = current
         current = following
-        panel = current.astype(jnp.bfloat16)
     return current
 
 

time: 81.2 us -> 76.7 us (0.945)
  waiting for transfers between devices: 35.3 us -> 29.1 us
  Pallas kernels: 9.35 us -> 10.6 us
    ppermute x18, waiting for transfers between devices: 28.4 us -> 24.3 us  [swap_rows(): return lax.ppermute(x, ('row', 'col'), pairs)]
    pallas_call x3 -> x4, Pallas kernels: 3.42 us -> 5.63 us  [the longest x1 2.21 us: forward_first(): pl.pallas_call(kernel, in_specs=[SMEM] * 4 + [HBM] + [VMEM] * 2, out_spec...]
    all_to_all x1, waiting for transfers between devices: 3.51 us -> 1.41 us  [body(): received = lax.all_to_all(dense, 'row', 0, 0, tiled=True)]
    all_to_all x1, starting transfers between devices: 5.03 us -> 6.48 us  [body(): received = lax.all_to_all(dense, 'row', 0, 0, tiled=True)]
    pallas_call x2, Pallas kernels: 1.82 us -> 0.85 us  [apply_tile(): pl.pallas_call(kernel, in_specs=[SMEM] * 2 + [VMEM] * (3 + count), out_sp...]
    ppermute x18, starting transfers between devices: 26.4 us -> 25.4 us  [swap_rows(): return lax.ppermute(x, ('row', 'col'), pairs)]
  transfers between devices with their start and end apart: 24 -> 24, of which waited for: 19 -> 17; matrix products, arithmetic and copies ran while one was open for 0% -> 0% of each run, Pallas kernels for 7% -> 12%
where the time goes in v11:
time: 76.7 us; the launch traced here: 76.3 us
  starting transfers between devices  32.7 us (43%)
  waiting for transfers between devices  29.1 us (38%)
  Pallas kernels  10.6 us (14%)
  between operations  2.22 us (3%)
  other arithmetic  1.54 us (2%)
    ppermute x18, starting transfers between devices, swap_rows(): return lax.ppermute(x, ('row', 'col'), pairs)  25.4 us
    ppermute x18, waiting for transfers between devices, swap_rows(): return lax.ppermute(x, ('row', 'col'), pairs)  24.3 us
    all_to_all x1, starting transfers between devices, body(): received = lax.all_to_all(dense, 'row', 0, 0, tiled=True)  6.48 us
    ppermute x5, waiting for transfers between devices, swap(): lax.ppermute(x, axis, [(source, source ^ offset) for source in range(size)])  3.39 us
    pallas_call x1, Pallas kernels, build_tile(): pl.pallas_call(kernel, in_specs=[HBM, HBM, SMEM, HBM], out_specs=VMEM, sc...  2.78 us
    pallas_call x1, Pallas kernels, forward_first(): pl.pallas_call(kernel, in_specs=[SMEM] * 4 + [HBM] + [VMEM] * 2, out_spec...  2.21 us
    pallas_call x1, Pallas kernels, merge_tile(): pl.pallas_call(kernel, in_specs=[SMEM] * 2 + [HBM] + [VMEM] * grid_cols,...  2.14 us
  transfers between devices with their start and end apart: 24, of which 17 were waited for; matrix products, arithmetic and copies ran while one was open for 0% of the time, Pallas kernels for 12%

profile of v11, /device:TPU:0, one launch (start us, length us, event | category | flops | bytes accessed | tf_op | source)
XLA Modules:
  0.0 76.3 jit_solution(9598687059371191715)
XLA Ops:
  0.0 0.8 %constant_dynamic-update-slice_fusion.6 = (bf16[2048,128]{1,0:T(8,128)(2,1)S(1)}, bf16[128,128]{1,0:T(8,128)(2,1)S(1)}) fusion(f32[128,128]{1,0:T(8,128)} %previous_ref.1), kind=kLoop, calls=%fused_computation.8 | loop fusion | flops 16383 | bytes 131072
  0.9 5.1 %collective-permute-start.2 = (bf16[128,128]{1,0:T(8,128)(2,1)S(1)}, bf16[128,128]{1,0:T(8,128)(2,1)S(1)}, u32[]{:S(2)}, u32[]{:S(2)}) collective-permute-start(bf16[128,128]{1,0:T(8,128)(2,1)S(1)} %get-tuple-element.24), channel_id=1, source_target_pairs={{0,24},{1,25},{2,26},{3,27},{4,28},{5,29},{6,30},{7,31},{8,16},{9,... | collective-permute-start | bytes 98312 | tf_op jit(solution)/shard_map/ppermute | solution.py:46
  6.0 0.6 collective-permute-start
  7.3 2.8 %build_tile.1.refs_0_ = bf16[32,128,128]{2,1,0:T(8,128)(2,1)} custom-call(s32[1,64]{1,0:T(1,128)} %bitcast.6, s32[1,64]{1,0:T(1,128)} %bitcast.7, s32[1,1]{1,0:T(1,128)S(6)} %copy.21.count_ref, bf16[64,128,128]{2,1,0:T(8,128)(2,1)} %bitcast.5), custom_call_target="tpu_custom_call" | custom-call | tf_op jit(solution)/shard_map/build_tile/pallas_call | solution.py:89
  10.1 0.7 collective-permute-done.1.refs_2_
  10.8 6.5 %all-to-all-start = ((bf16[32,128,128]{2,1,0:T(8,128)(2,1)}), bf16[32,128,128]{2,1,0:T(8,128)(2,1)S(1)}, u32[]{:S(2)}, u32[]{:S(2)}) async-start(bf16[32,128,128]{2,1,0:T(8,128)(2,1)} %after.1.dense_hbm), calls=%async_computation | async-start | bytes 2097152 | tf_op jit(solution)/shard_map/all_to_all | solution.py:362
  17.3 2.9 %collective-permute-start.5 = (bf16[512,128]{1,0:T(8,128)(2,1)S(1)}, bf16[512,128]{1,0:T(8,128)(2,1)S(1)}, u32[]{:S(2)}, u32[]{:S(2)}) collective-permute-start(bf16[512,128]{1,0:T(8,128)(2,1)S(1)} %pad_maximum_fusion), channel_id=1, source_target_pairs={{0,6},{1,7},{2,4},{3,5},{4,2},{5,3},{6,0},{7,1},{8,14},{9,15},{10,... | collective-permute-start | bytes 393224 | tf_op jit(solution)/shard_map/ppermute | solution.py:46
  20.2 0.6 collective-permute-start.4
  20.8 0.1 collective-permute-start.3
  20.9 9.8 %collective-permute-done.3 = bf16[512,128]{1,0:T(8,128)(2,1)S(1)} collective-permute-done((bf16[512,128]{1,0:T(8,128)(2,1)S(1)}, bf16[512,128]{1,0:T(8,128)(2,1)S(1)}, u32[]{:S(2)}, u32[]{:S(2)}) %collective-permute-start.3) | collective-permute-done | bytes 131104 | tf_op jit(solution)/shard_map/ppermute | solution.py:46
  30.7 2.1 %collective-permute-done.4 = bf16[512,128]{1,0:T(8,128)(2,1)S(1)} collective-permute-done((bf16[512,128]{1,0:T(8,128)(2,1)S(1)}, bf16[512,128]{1,0:T(8,128)(2,1)S(1)}, u32[]{:S(2)}, u32[]{:S(2)}) %collective-permute-start.4) | collective-permute-done | bytes 131104 | tf_op jit(solution)/shard_map/ppermute | solution.py:46
  32.9 0.7 turn_panel.1.refs_0_
  33.6 0.1 collective-permute-start.6
  35.0 2.2 %forward_first.1 = (f32[128,128]{1,0:T(8,128)S(1)}, f32[128,128]{1,0:T(8,128)S(1)}) custom-call(s32[16]{0:T(128)S(1)} %broadcast_xor_fusion.sources_ref, s32[2]{0:T(128)S(1)} %iota_xor_fusion.targets_ref, f32[1]{0:T(128)S(6)} %copy.22.center_ref, f32[1]{0:T(128)S(6)} %copy.23.halfwidth_ref, bf16[32,128,128]{2,1,0:T(8,128)(2,1)} %after.1.dense_hbm, ...), custom_call_target="tpu_custom_call" | custom-call | tf_op jit(solution)/shard_map/forward_first/pallas_call | solution.py:163
  37.2 0.6 collective-permute-start.7
  37.8 0.9 %collective-permute-done.7 = f32[128,128]{1,0:T(8,128)S(1)} collective-permute-done((f32[128,128]{1,0:T(8,128)S(1)}, f32[128,128]{1,0:T(8,128)S(1)}, u32[]{:S(2)}, u32[]{:S(2)}) %collective-permute-start.7) | collective-permute-done | bytes 65568 | tf_op jit(solution)/shard_map/ppermute | solution.py:37
  38.7 0.8 %lay_panels.1.turned_ref = bf16[128,4096]{1,0:T(8,128)(2,1)S(1)} custom-call(s32[2]{0:T(128)S(1)} %iota_xor_fusion.targets_ref, bf16[128,2048]{1,0:T(8,128)(2,1)S(1)} %turn_panel.1.refs_0_, bf16[128,2048]{1,0:T(8,128)(2,1)S(1)} %collective-permute-done.6.refs_1_), custom_call_target="tpu_custom_call" | custom-call | tf_op jit(solution)/shard_map/lay_panels/pallas_call | solution.py:212
  39.5 1.4 %all-to-all-done.received_ref = bf16[32,128,128]{2,1,0:T(8,128)(2,1)S(1)} async-done(((bf16[32,128,128]{2,1,0:T(8,128)(2,1)}), bf16[32,128,128]{2,1,0:T(8,128)(2,1)S(1)}, u32[]{:S(2)}, u32[]{:S(2)}) %all-to-all-start) | async-done | bytes 1048608 | tf_op jit(solution)/shard_map/all_to_all | solution.py:362
  40.9 0.5 backward_first.1
  41.4 2.8 %collective-permute-start.8 = (bf16[128,128]{1,0:T(8,128)(2,1)S(1)}, bf16[128,128]{1,0:T(8,128)(2,1)S(1)}, u32[]{:S(2)}, u32[]{:S(2)}) collective-permute-start(bf16[128,128]{1,0:T(8,128)(2,1)S(1)} %get-tuple-element.15), channel_id=1, source_target_pairs={{0,24},{1,7},{2,26},{3,5},{4,28},{5,3},{6,30},{7,1},{8,16},{9,15},... | collective-permute-start | bytes 98312 | tf_op jit(solution)/shard_map/ppermute | solution.py:46
  44.3 1.7 %collective-permute-start.11 = (bf16[128,128]{1,0:T(8,128)(2,1)S(1)}, bf16[128,128]{1,0:T(8,128)(2,1)S(1)}, u32[]{:S(2)}, u32[]{:S(2)}) collective-permute-start(bf16[128,128]{1,0:T(8,128)(2,1)S(1)} %get-tuple-element.15), channel_id=1, source_target_pairs={{0,16},{1,5},{2,18},{3,7},{4,20},{5,1},{6,22},{7,3},{8,24},{9,13},... | collective-permute-start | bytes 98312 | tf_op jit(solution)/shard_map/ppermute | solution.py:46
  46.0 1.2 %collective-permute-done.8.panel_ref = bf16[128,128]{1,0:T(8,128)(2,1)S(1)} collective-permute-done((bf16[128,128]{1,0:T(8,128)(2,1)S(1)}, bf16[128,128]{1,0:T(8,128)(2,1)S(1)}, u32[]{:S(2)}, u32[]{:S(2)}) %collective-permute-start.8) | collective-permute-done | bytes 32800 | tf_op jit(solution)/shard_map/ppermute | solution.py:46
  47.2 0.6 pick_blocks.1
  47.9 2.0 %collective-permute-done.10 = bf16[128,128]{1,0:T(8,128)(2,1)S(1)} collective-permute-done((bf16[128,128]{1,0:T(8,128)(2,1)S(1)}, bf16[128,128]{1,0:T(8,128)(2,1)S(1)}, u32[]{:S(2)}, u32[]{:S(2)}) %collective-permute-start.10) | collective-permute-done | bytes 32800 | tf_op jit(solution)/shard_map/ppermute | solution.py:46
  49.9 1.6 %collective-permute-start.14 = (bf16[512,128]{1,0:T(8,128)(2,1)S(1)}, bf16[512,128]{1,0:T(8,128)(2,1)S(1)}, u32[]{:S(2)}, u32[]{:S(2)}) collective-permute-start(bf16[512,128]{1,0:T(8,128)(2,1)S(1)} %constant_dynamic-update-slice_fusion.7.refs_0_), channel_id=1, source_target_pairs={{0,6},{1,25},{2,4},{3,27},{4,2},{5,29},{6,0},{7,31},{8,14},{9,17},... | collective-permute-start | bytes 393224 | tf_op jit(solution)/shard_map/ppermute | solution.py:46
  51.6 0.6 collective-permute-start.13
  52.2 1.3 %collective-permute-start.12 = (bf16[512,128]{1,0:T(8,128)(2,1)S(1)}, bf16[512,128]{1,0:T(8,128)(2,1)S(1)}, u32[]{:S(2)}, u32[]{:S(2)}) collective-permute-start(bf16[512,128]{1,0:T(8,128)(2,1)S(1)} %constant_dynamic-update-slice_fusion.7.refs_0_), channel_id=1, source_target_pairs={{0,2},{1,9},{2,0},{3,11},{4,6},{5,13},{6,4},{7,15},{8,10},{9,1},{1... | collective-permute-start | bytes 393224 | tf_op jit(solution)/shard_map/ppermute | solution.py:46
  53.5 2.1 %merge_tile.1.tile_ref = bf16[256,2048]{1,0:T(8,128)(2,1)S(1)} custom-call(s32[16]{0:T(128)S(1)} %xor_bitcast_fusion.sources_ref, s32[2]{0:T(128)S(1)} %iota_xor_fusion.targets_ref, bf16[32,128,128]{2,1,0:T(8,128)(2,1)} %after.1.dense_hbm, bf16[32,128,128]{2,1,0:T(8,128)(2,1)S(1)} %all-to-all-done.received_ref, ...), custom_call_target="tpu_custom_call" | custom-call | tf_op jit(solution)/shard_map/merge_tile/pallas_call | solution.py:284
  55.7 0.3 collective-permute-done.14.refs_3_
  55.9 1.3 %collective-permute-done.13.refs_2_ = bf16[512,128]{1,0:T(8,128)(2,1)S(1)} collective-permute-done((bf16[512,128]{1,0:T(8,128)(2,1)S(1)}, bf16[512,128]{1,0:T(8,128)(2,1)S(1)}, u32[]{:S(2)}, u32[]{:S(2)}) %collective-permute-start.13) | collective-permute-done | bytes 131104 | tf_op jit(solution)/shard_map/ppermute | solution.py:46
  57.3 0.2 collective-permute-done.12.refs_1_
  57.5 0.4 apply_tile.2
  58.0 1.2 %collective-permute-done.15 = f32[128,128]{1,0:T(8,128)S(1)} collective-permute-done((f32[128,128]{1,0:T(8,128)S(1)}, f32[128,128]{1,0:T(8,128)S(1)}, u32[]{:S(2)}, u32[]{:S(2)}) %collective-permute-start.15) | collective-permute-done | bytes 65568 | tf_op jit(solution)/shard_map/ppermute | solution.py:37
  59.2 1.8 %collective-permute-start.18 = (bf16[128,128]{1,0:T(8,128)(2,1)S(1)}, bf16[128,128]{1,0:T(8,128)(2,1)S(1)}, u32[]{:S(2)}, u32[]{:S(2)}) collective-permute-start(bf16[128,128]{1,0:T(8,128)(2,1)S(1)} %get-tuple-element.21), channel_id=1, source_target_pairs={{0,24},{1,7},{2,26},{3,5},{4,28},{5,3},{6,30},{7,1},{8,16},{9,15},... | collective-permute-start | bytes 98312 | tf_op jit(solution)/shard_map/ppermute | solution.py:46
  61.1 0.1 collective-permute-start.17
  61.2 2.5 %collective-permute-start.16 = (bf16[128,128]{1,0:T(8,128)(2,1)S(1)}, bf16[128,128]{1,0:T(8,128)(2,1)S(1)}, u32[]{:S(2)}, u32[]{:S(2)}) collective-permute-start(bf16[128,128]{1,0:T(8,128)(2,1)S(1)} %get-tuple-element.21), channel_id=1, source_target_pairs={{0,8},{1,3},{2,10},{3,1},{4,12},{5,7},{6,14},{7,5},{8,0},{9,11},{1... | collective-permute-start | bytes 98312 | tf_op jit(solution)/shard_map/ppermute | solution.py:46
  63.7 1.3 %collective-permute-done.18 = bf16[128,128]{1,0:T(8,128)(2,1)S(1)} collective-permute-done((bf16[128,128]{1,0:T(8,128)(2,1)S(1)}, bf16[128,128]{1,0:T(8,128)(2,1)S(1)}, u32[]{:S(2)}, u32[]{:S(2)}) %collective-permute-start.18) | collective-permute-done | bytes 32800 | tf_op jit(solution)/shard_map/ppermute | solution.py:46
  65.0 1.2 %collective-permute-done.17 = bf16[128,128]{1,0:T(8,128)(2,1)S(1)} collective-permute-done((bf16[128,128]{1,0:T(8,128)(2,1)S(1)}, bf16[128,128]{1,0:T(8,128)(2,1)S(1)}, u32[]{:S(2)}, u32[]{:S(2)}) %collective-permute-start.17) | collective-permute-done | bytes 32800 | tf_op jit(solution)/shard_map/ppermute | solution.py:46
  66.2 2.1 %collective-permute-start.21 = (bf16[512,128]{1,0:T(8,128)(2,1)S(1)}, bf16[512,128]{1,0:T(8,128)(2,1)S(1)}, u32[]{:S(2)}, u32[]{:S(2)}) collective-permute-start(bf16[512,128]{1,0:T(8,128)(2,1)S(1)} %pad_maximum_fusion.1.refs_0_), channel_id=1, source_target_pairs={{0,6},{1,25},{2,4},{3,27},{4,2},{5,29},{6,0},{7,31},{8,14},{9,17},... | collective-permute-start | bytes 393224 | tf_op jit(solution)/shard_map/ppermute | solution.py:46
  68.3 0.1 collective-permute-start.20
  68.5 1.3 %collective-permute-start.19 = (bf16[512,128]{1,0:T(8,128)(2,1)S(1)}, bf16[512,128]{1,0:T(8,128)(2,1)S(1)}, u32[]{:S(2)}, u32[]{:S(2)}) collective-permute-start(bf16[512,128]{1,0:T(8,128)(2,1)S(1)} %pad_maximum_fusion.1.refs_0_), channel_id=1, source_target_pairs={{0,2},{1,9},{2,0},{3,11},{4,6},{5,13},{6,4},{7,15},{8,10},{9,1},{1... | collective-permute-start | bytes 393224 | tf_op jit(solution)/shard_map/ppermute | solution.py:46
  69.8 2.4 %collective-permute-done.21.refs_3_ = bf16[512,128]{1,0:T(8,128)(2,1)S(1)} collective-permute-done((bf16[512,128]{1,0:T(8,128)(2,1)S(1)}, bf16[512,128]{1,0:T(8,128)(2,1)S(1)}, u32[]{:S(2)}, u32[]{:S(2)}) %collective-permute-start.21) | collective-permute-done | bytes 131104 | tf_op jit(solution)/shard_map/ppermute | solution.py:46
  72.2 1.4 %collective-permute-done.20.refs_2_ = bf16[512,128]{1,0:T(8,128)(2,1)S(1)} collective-permute-done((bf16[512,128]{1,0:T(8,128)(2,1)S(1)}, bf16[512,128]{1,0:T(8,128)(2,1)S(1)}, u32[]{:S(2)}, u32[]{:S(2)}) %collective-permute-start.20) | collective-permute-done | bytes 131104 | tf_op jit(solution)/shard_map/ppermute | solution.py:46
  73.6 0.3 collective-permute-done.19.refs_1_
  73.9 0.4 apply_tile.3
  74.3 0.1 collective-permute-start.22
  74.4 1.2 %collective-permute-done.22 = f32[128,128]{1,0:T(8,128)S(1)} collective-permute-done((f32[128,128]{1,0:T(8,128)S(1)}, f32[128,128]{1,0:T(8,128)S(1)}, u32[]{:S(2)}, u32[]{:S(2)}) %collective-permute-start.22) | collective-permute-done | bytes 65568 | tf_op jit(solution)/shard_map/ppermute | solution.py:37
  75.6 0.6 add.20
  (35 shorter events, 0.4 us)
Async XLA Ops:
  0.9 9.2 %collective-permute-start.2 = (bf16[128,128]{1,0:T(8,128)(2,1)S(1)}, bf16[128,128]{1,0:T(8,128)(2,1)S(1)}, u32[]{:S(2)}, u32[]{:S(2)}) collective-permute-start(bf16[128,128]{1,0:T(8,128)(2,1)S(1)} %get-tuple-element.24), channel_id=1, source_target_pairs={{0,24},{1,25},{2,26},{3,27},{4,28},{5,29},{6,30},{7,31},{8,16},{9,... | collective-permute-start | bytes 98312 | tf_op jit(solution)/shard_map/ppermute | solution.py:46
  6.0 4.8 %collective-permute-start.1 = (bf16[128,128]{1,0:T(8,128)(2,1)S(1)}, bf16[128,128]{1,0:T(8,128)(2,1)S(1)}, u32[]{:S(2)}, u32[]{:S(2)}) collective-permute-start(bf16[128,128]{1,0:T(8,128)(2,1)S(1)} %get-tuple-element.24), channel_id=1, source_target_pairs={{0,16},{1,17},{2,18},{3,19},{4,20},{5,21},{6,22},{7,23},{8,24},{9,... | collective-permute-start | bytes 98312 | tf_op jit(solution)/shard_map/ppermute | solution.py:46
  6.0 4.8 %collective-permute-start = (bf16[128,128]{1,0:T(8,128)(2,1)S(1)}, bf16[128,128]{1,0:T(8,128)(2,1)S(1)}, u32[]{:S(2)}, u32[]{:S(2)}) collective-permute-start(bf16[128,128]{1,0:T(8,128)(2,1)S(1)} %get-tuple-element.24), channel_id=1, source_target_pairs={{0,8},{1,9},{2,10},{3,11},{4,12},{5,13},{6,14},{7,15},{8,0},{9,1},... | collective-permute-start | bytes 98312 | tf_op jit(solution)/shard_map/ppermute | solution.py:46
  10.0 7.2 %copy-start.2 = (s32[16]{0:T(128)S(1)}, s32[16]{0:T(128)}, u32[]{:S(2)}) copy-start(s32[16]{0:T(128)} %constant.26.clone) | copy-start | bytes 196
  10.8 24.2 %copy-start = (f32[128,128]{1,0:T(8,128)S(1)}, f32[128,128]{1,0:T(8,128)}, u32[]{:S(2)}) copy-start(f32[128,128]{1,0:T(8,128)} %previous_ref.1) | copy-start | bytes 196612
  10.8 30.1 %all-to-all-start = ((bf16[32,128,128]{2,1,0:T(8,128)(2,1)}), bf16[32,128,128]{2,1,0:T(8,128)(2,1)S(1)}, u32[]{:S(2)}, u32[]{:S(2)}) async-start(bf16[32,128,128]{2,1,0:T(8,128)(2,1)} %after.1.dense_hbm), calls=%async_computation | async-start | bytes 2097152 | tf_op jit(solution)/shard_map/all_to_all | solution.py:362
  17.3 15.5 %collective-permute-start.5 = (bf16[512,128]{1,0:T(8,128)(2,1)S(1)}, bf16[512,128]{1,0:T(8,128)(2,1)S(1)}, u32[]{:S(2)}, u32[]{:S(2)}) collective-permute-start(bf16[512,128]{1,0:T(8,128)(2,1)S(1)} %pad_maximum_fusion), channel_id=1, source_target_pairs={{0,6},{1,7},{2,4},{3,5},{4,2},{5,3},{6,0},{7,1},{8,14},{9,15},{10,... | collective-permute-start | bytes 393224 | tf_op jit(solution)/shard_map/ppermute | solution.py:46
  20.2 12.6 %collective-permute-start.4 = (bf16[512,128]{1,0:T(8,128)(2,1)S(1)}, bf16[512,128]{1,0:T(8,128)(2,1)S(1)}, u32[]{:S(2)}, u32[]{:S(2)}) collective-permute-start(bf16[512,128]{1,0:T(8,128)(2,1)S(1)} %pad_maximum_fusion), channel_id=1, source_target_pairs={{0,4},{1,5},{2,6},{3,7},{4,0},{5,1},{6,2},{7,3},{8,12},{9,13},{10,... | collective-permute-start | bytes 393224 | tf_op jit(solution)/shard_map/ppermute | solution.py:46
  20.8 9.9 %collective-permute-start.3 = (bf16[512,128]{1,0:T(8,128)(2,1)S(1)}, bf16[512,128]{1,0:T(8,128)(2,1)S(1)}, u32[]{:S(2)}, u32[]{:S(2)}) collective-permute-start(bf16[512,128]{1,0:T(8,128)(2,1)S(1)} %pad_maximum_fusion), channel_id=1, source_target_pairs={{0,2},{1,3},{2,0},{3,1},{4,6},{5,7},{6,4},{7,5},{8,10},{9,11},{10,... | collective-permute-start | bytes 393224 | tf_op jit(solution)/shard_map/ppermute | solution.py:46
  33.6 5.1 %collective-permute-start.6 = (bf16[128,2048]{1,0:T(8,128)(2,1)S(1)}, bf16[128,2048]{1,0:T(8,128)(2,1)S(1)}, u32[]{:S(2)}, u32[]{:S(2)}) collective-permute-start(bf16[128,2048]{1,0:T(8,128)(2,1)S(1)} %turn_panel.1.refs_0_), channel_id=1, source_target_pairs={{0,1},{1,0},{2,3},{3,2},{4,5},{5,4},{6,7},{7,6},{8,9},{9,8},{10,11... | collective-permute-start | bytes 1572872 | tf_op jit(solution)/shard_map/ppermute | solution.py:37
  37.2 1.5 %collective-permute-start.7 = (f32[128,128]{1,0:T(8,128)S(1)}, f32[128,128]{1,0:T(8,128)S(1)}, u32[]{:S(2)}, u32[]{:S(2)}) collective-permute-start(f32[128,128]{1,0:T(8,128)S(1)} %get-tuple-element.14), channel_id=1, source_target_pairs={{0,1},{1,0},{2,3},{3,2},{4,5},{5,4},{6,7},{7,6},{8,9},{9,8},{10,11... | collective-permute-start | bytes 196616 | tf_op jit(solution)/shard_map/ppermute | solution.py:37
  39.5 14.0 %copy-start.1 = (s32[2,16]{1,0:T(2,128)S(1)}, s32[2,16]{1,0:T(2,128)}, u32[]{:S(2)}) copy-start(s32[2,16]{1,0:T(2,128)} %constant.27.clone) | copy-start | bytes 388
  41.4 5.8 %collective-permute-start.8 = (bf16[128,128]{1,0:T(8,128)(2,1)S(1)}, bf16[128,128]{1,0:T(8,128)(2,1)S(1)}, u32[]{:S(2)}, u32[]{:S(2)}) collective-permute-start(bf16[128,128]{1,0:T(8,128)(2,1)S(1)} %get-tuple-element.15), channel_id=1, source_target_pairs={{0,24},{1,7},{2,26},{3,5},{4,28},{5,3},{6,30},{7,1},{8,16},{9,15},... | collective-permute-start | bytes 98312 | tf_op jit(solution)/shard_map/ppermute | solution.py:46
  44.3 5.6 %collective-permute-start.11 = (bf16[128,128]{1,0:T(8,128)(2,1)S(1)}, bf16[128,128]{1,0:T(8,128)(2,1)S(1)}, u32[]{:S(2)}, u32[]{:S(2)}) collective-permute-start(bf16[128,128]{1,0:T(8,128)(2,1)S(1)} %get-tuple-element.15), channel_id=1, source_target_pairs={{0,16},{1,5},{2,18},{3,7},{4,20},{5,1},{6,22},{7,3},{8,24},{9,13},... | collective-permute-start | bytes 98312 | tf_op jit(solution)/shard_map/ppermute | solution.py:46
  46.0 3.9 %collective-permute-start.10 = (bf16[128,128]{1,0:T(8,128)(2,1)S(1)}, bf16[128,128]{1,0:T(8,128)(2,1)S(1)}, u32[]{:S(2)}, u32[]{:S(2)}) collective-permute-start(bf16[128,128]{1,0:T(8,128)(2,1)S(1)} %get-tuple-element.15), channel_id=1, source_target_pairs={{0,8},{1,3},{2,10},{3,1},{4,12},{5,7},{6,14},{7,5},{8,0},{9,11},{1... | collective-permute-start | bytes 98312 | tf_op jit(solution)/shard_map/ppermute | solution.py:46
  47.8 5.7 %collective-permute-start.9 = (bf16[16,128,128]{2,1,0:T(8,128)(2,1)S(1)}, bf16[16,128,128]{2,1,0:T(8,128)(2,1)S(1)}, u32[]{:S(2)}, u32[]{:S(2)}) collective-permute-start(bf16[16,128,128]{2,1,0:T(8,128)(2,1)S(1)} %pick_blocks.1), channel_id=1, source_target_pairs={{0,1},{1,0},{2,3},{3,2},{4,5},{5,4},{6,7},{7,6},{8,9},{9,8},{10,11... | collective-permute-start | bytes 1572872 | tf_op jit(solution)/shard_map/ppermute | solution.py:37
  49.9 6.0 %collective-permute-start.14 = (bf16[512,128]{1,0:T(8,128)(2,1)S(1)}, bf16[512,128]{1,0:T(8,128)(2,1)S(1)}, u32[]{:S(2)}, u32[]{:S(2)}) collective-permute-start(bf16[512,128]{1,0:T(8,128)(2,1)S(1)} %constant_dynamic-update-slice_fusion.7.refs_0_), channel_id=1, source_target_pairs={{0,6},{1,25},{2,4},{3,27},{4,2},{5,29},{6,0},{7,31},{8,14},{9,17},... | collective-permute-start | bytes 393224 | tf_op jit(solution)/shard_map/ppermute | solution.py:46
  51.6 5.7 %collective-permute-start.13 = (bf16[512,128]{1,0:T(8,128)(2,1)S(1)}, bf16[512,128]{1,0:T(8,128)(2,1)S(1)}, u32[]{:S(2)}, u32[]{:S(2)}) collective-permute-start(bf16[512,128]{1,0:T(8,128)(2,1)S(1)} %constant_dynamic-update-slice_fusion.7.refs_0_), channel_id=1, source_target_pairs={{0,4},{1,17},{2,6},{3,19},{4,0},{5,21},{6,2},{7,23},{8,12},{9,25},... | collective-permute-start | bytes 393224 | tf_op jit(solution)/shard_map/ppermute | solution.py:46
  52.2 5.3 %collective-permute-start.12 = (bf16[512,128]{1,0:T(8,128)(2,1)S(1)}, bf16[512,128]{1,0:T(8,128)(2,1)S(1)}, u32[]{:S(2)}, u32[]{:S(2)}) collective-permute-start(bf16[512,128]{1,0:T(8,128)(2,1)S(1)} %constant_dynamic-update-slice_fusion.7.refs_0_), channel_id=1, source_target_pairs={{0,2},{1,9},{2,0},{3,11},{4,6},{5,13},{6,4},{7,15},{8,10},{9,1},{1... | collective-permute-start | bytes 393224 | tf_op jit(solution)/shard_map/ppermute | solution.py:46
  57.9 1.3 %collective-permute-start.15 = (f32[128,128]{1,0:T(8,128)S(1)}, f32[128,128]{1,0:T(8,128)S(1)}, u32[]{:S(2)}, u32[]{:S(2)}) collective-permute-start(f32[128,128]{1,0:T(8,128)S(1)} %get-tuple-element.18), channel_id=1, source_target_pairs={{0,1},{1,0},{2,3},{3,2},{4,5},{5,4},{6,7},{7,6},{8,9},{9,8},{10,11... | collective-permute-start | bytes 196616 | tf_op jit(solution)/shard_map/ppermute | solution.py:37
  59.2 5.8 %collective-permute-start.18 = (bf16[128,128]{1,0:T(8,128)(2,1)S(1)}, bf16[128,128]{1,0:T(8,128)(2,1)S(1)}, u32[]{:S(2)}, u32[]{:S(2)}) collective-permute-start(bf16[128,128]{1,0:T(8,128)(2,1)S(1)} %get-tuple-element.21), channel_id=1, source_target_pairs={{0,24},{1,7},{2,26},{3,5},{4,28},{5,3},{6,30},{7,1},{8,16},{9,15},... | collective-permute-start | bytes 98312 | tf_op jit(solution)/shard_map/ppermute | solution.py:46
  61.1 5.2 %collective-permute-start.17 = (bf16[128,128]{1,0:T(8,128)(2,1)S(1)}, bf16[128,128]{1,0:T(8,128)(2,1)S(1)}, u32[]{:S(2)}, u32[]{:S(2)}) collective-permute-start(bf16[128,128]{1,0:T(8,128)(2,1)S(1)} %get-tuple-element.21), channel_id=1, source_target_pairs={{0,16},{1,5},{2,18},{3,7},{4,20},{5,1},{6,22},{7,3},{8,24},{9,13},... | collective-permute-start | bytes 98312 | tf_op jit(solution)/shard_map/ppermute | solution.py:46
  61.2 5.1 %collective-permute-start.16 = (bf16[128,128]{1,0:T(8,128)(2,1)S(1)}, bf16[128,128]{1,0:T(8,128)(2,1)S(1)}, u32[]{:S(2)}, u32[]{:S(2)}) collective-permute-start(bf16[128,128]{1,0:T(8,128)(2,1)S(1)} %get-tuple-element.21), channel_id=1, source_target_pairs={{0,8},{1,3},{2,10},{3,1},{4,12},{5,7},{6,14},{7,5},{8,0},{9,11},{1... | collective-permute-start | bytes 98312 | tf_op jit(solution)/shard_map/ppermute | solution.py:46
  66.2 6.0 %collective-permute-start.21 = (bf16[512,128]{1,0:T(8,128)(2,1)S(1)}, bf16[512,128]{1,0:T(8,128)(2,1)S(1)}, u32[]{:S(2)}, u32[]{:S(2)}) collective-permute-start(bf16[512,128]{1,0:T(8,128)(2,1)S(1)} %pad_maximum_fusion.1.refs_0_), channel_id=1, source_target_pairs={{0,6},{1,25},{2,4},{3,27},{4,2},{5,29},{6,0},{7,31},{8,14},{9,17},... | collective-permute-start | bytes 393224 | tf_op jit(solution)/shard_map/ppermute | solution.py:46
  68.3 5.2 %collective-permute-start.20 = (bf16[512,128]{1,0:T(8,128)(2,1)S(1)}, bf16[512,128]{1,0:T(8,128)(2,1)S(1)}, u32[]{:S(2)}, u32[]{:S(2)}) collective-permute-start(bf16[512,128]{1,0:T(8,128)(2,1)S(1)} %pad_maximum_fusion.1.refs_0_), channel_id=1, source_target_pairs={{0,4},{1,17},{2,6},{3,19},{4,0},{5,21},{6,2},{7,23},{8,12},{9,25},... | collective-permute-start | bytes 393224 | tf_op jit(solution)/shard_map/ppermute | solution.py:46
  68.5 5.4 %collective-permute-start.19 = (bf16[512,128]{1,0:T(8,128)(2,1)S(1)}, bf16[512,128]{1,0:T(8,128)(2,1)S(1)}, u32[]{:S(2)}, u32[]{:S(2)}) collective-permute-start(bf16[512,128]{1,0:T(8,128)(2,1)S(1)} %pad_maximum_fusion.1.refs_0_), channel_id=1, source_target_pairs={{0,2},{1,9},{2,0},{3,11},{4,6},{5,13},{6,4},{7,15},{8,10},{9,1},{1... | collective-permute-start | bytes 393224 | tf_op jit(solution)/shard_map/ppermute | solution.py:46
  74.3 1.3 %collective-permute-start.22 = (f32[128,128]{1,0:T(8,128)S(1)}, f32[128,128]{1,0:T(8,128)S(1)}, u32[]{:S(2)}, u32[]{:S(2)}) collective-permute-start(f32[128,128]{1,0:T(8,128)S(1)} %get-tuple-element.20), channel_id=1, source_target_pairs={{0,1},{1,0},{2,3},{3,2},{4,5},{5,4},{6,7},{7,6},{8,9},{9,8},{10,11... | collective-permute-start | bytes 196616 | tf_op jit(solution)/shard_map/ppermute | solution.py:37

commit v12 on v11

--- a/solution.py
+++ b/solution.py
@@ -9,7 +9,6 @@
 RADIX = 4
 CHUNK = 8
 SPARE = 4 * 2**20
-BUILD_VMEM = 62 * 2**20
 
 VMEM = pl.BlockSpec(memory_space=pltpu.VMEM)
 SMEM = pl.BlockSpec(memory_space=pltpu.SMEM)
@@ -48,13 +47,14 @@
 
 def build_tile(rows, cols, count, stacked, grid_rows, grid_cols):
     slots, orb, _ = stacked.shape
+    cells = grid_rows * grid_cols
+    parts = 4 if cells % 4 == 0 else 1
     chunk = CHUNK if slots % CHUNK == 0 else slots
     chunks = slots // chunk
-    cells = grid_rows * grid_cols
 
     def kernel(
-        rows_hbm, cols_hbm, count_ref, stack_ref, dense_ref,
-        held_ref, acc_ref, rows_ref, cols_ref, sems, index_sems,
+        rows_hbm, cols_hbm, count_ref, stack_hbm, out_hbm,
+        stack_ref, acc_ref, dense_ref, rows_ref, cols_ref, index_sems, stack_sems, sems,
     ):
         indices = [
             pltpu.make_async_copy(source, target, index_sems.at[n])
@@ -62,44 +62,49 @@
         ]
         for copy in indices:
             copy.start()
-        copies = [
-            pltpu.make_async_copy(
-                stack_ref.at[pl.ds(n * chunk, chunk)], held_ref.at[pl.ds(n * chunk, chunk)], sems.at[n]
+        arrivals = []
+        for n in range(chunks):
+            held = pl.ds(n * chunk, chunk)
+            arrivals.append(
+                pltpu.make_async_copy(stack_hbm.at[held], stack_ref.at[held], stack_sems.at[n])
             )
-            for n in range(chunks)
-        ]
-        for copy in copies:
-            copy.start()
+            arrivals[-1].start()
         acc_ref[...] = jnp.zeros_like(acc_ref)
         for copy in indices:
             copy.wait()
         count = count_ref[0, 0]
-        for n, copy in enumerate(copies):
+        for n, copy in enumerate(arrivals):
             copy.wait()
             for s in range(n * chunk, (n + 1) * chunk):
                 cell = jnp.where(s < count, cols_ref[0, s] * grid_cols + rows_ref[0, s], cells)
-                acc_ref[cell] += held_ref[s].astype(jnp.float32)
-
-        def put(cell, carry):
-            dense_ref[cell] = acc_ref[cell].astype(jnp.bfloat16)
-            return carry
-
-        lax.fori_loop(0, cells, put, 0, unroll=4 if cells % 4 == 0 else 1)
+                acc_ref[cell] += stack_ref[s].astype(jnp.float32)
+        copies = []
+        for n in range(parts):
+            held = pl.ds(n * (cells // parts), cells // parts)
+            dense_ref[held] = acc_ref[held].astype(jnp.bfloat16)
+            copies.append(pltpu.make_async_copy(dense_ref.at[held], out_hbm.at[held], sems.at[n]))
+            copies[-1].start()
+        for copy in copies:
+            copy.wait()
 
     return pl.pallas_call(
         kernel,
         in_specs=[HBM, HBM, SMEM, HBM],
-        out_specs=VMEM,
+        out_specs=HBM,
         scratch_shapes=[
             pltpu.VMEM(stacked.shape, jnp.bfloat16),
             pltpu.VMEM((cells + 1, orb, orb), jnp.float32),
+            pltpu.VMEM((cells, orb, orb), jnp.bfloat16),
             pltpu.SMEM(rows.shape, jnp.int32),
             pltpu.SMEM(cols.shape, jnp.int32),
+            pltpu.SemaphoreType.DMA((2,)),
             pltpu.SemaphoreType.DMA((chunks,)),
-            pltpu.SemaphoreType.DMA((2,)),
+            pltpu.SemaphoreType.DMA((parts,)),
         ],
-        out_shape=jax.ShapeDtypeStruct((cells, orb, orb), jnp.bfloat16),
-        compiler_params=pltpu.CompilerParams(vmem_limit_bytes=BUILD_VMEM),
+        out_shape=pltpu.HBM((cells, orb, orb), jnp.bfloat16),
+        compiler_params=pltpu.CompilerParams(
+            vmem_limit_bytes=(cells + 1) * orb * orb * 6 + stacked.size * 2 + SPARE
+        ),
         name="build_tile",
     )(
         pltpu.with_memory_space_constraint(rows, pltpu.HBM),

time: 76.7 us -> 76.6 us (level)
  no operation moved by 1% of the time
where the time goes in v12:
time: 76.6 us; the launch traced here: 76.2 us
  starting transfers between devices  32.7 us (43%)
  waiting for transfers between devices  29.2 us (38%)
  Pallas kernels  10.5 us (14%)
  between operations  2.21 us (3%)
  other arithmetic  1.55 us (2%)
    ppermute x18, starting transfers between devices, swap_rows(): return lax.ppermute(x, ('row', 'col'), pairs)  25.4 us
    ppermute x18, waiting for transfers between devices, swap_rows(): return lax.ppermute(x, ('row', 'col'), pairs)  24.4 us
    all_to_all x1, starting transfers between devices, body(): received = lax.all_to_all(dense, 'row', 0, 0, tiled=True)  6.4 us
    ppermute x5, waiting for transfers between devices, swap(): lax.ppermute(x, axis, [(source, source ^ offset) for source in range(size)])  3.39 us
    pallas_call x1, Pallas kernels, build_tile(): pl.pallas_call(kernel, in_specs=[HBM, HBM, SMEM, HBM], out_specs=HBM, scr...  2.69 us
    pallas_call x1, Pallas kernels, forward_first(): pl.pallas_call(kernel, in_specs=[SMEM] * 4 + [HBM] + [VMEM] * 2, out_spec...  2.21 us
    pallas_call x1, Pallas kernels, merge_tile(): pl.pallas_call(kernel, in_specs=[SMEM] * 2 + [HBM] + [VMEM] * grid_cols,...  2.14 us
  transfers between devices with their start and end apart: 24, of which 17 were waited for; matrix products, arithmetic and copies ran while one was open for 0% of the time, Pallas kernels for 12%

profile of v12, /device:TPU:0, one launch (start us, length us, event | category | flops | bytes accessed | tf_op | source)
XLA Modules:
  0.0 76.2 jit_solution(12763639790202958376)
XLA Ops:
  0.0 0.8 %constant_dynamic-update-slice_fusion.6 = (bf16[2048,128]{1,0:T(8,128)(2,1)S(1)}, bf16[128,128]{1,0:T(8,128)(2,1)S(1)}) fusion(f32[128,128]{1,0:T(8,128)} %previous_ref.1), kind=kLoop, calls=%fused_computation.8 | loop fusion | flops 16383 | bytes 131072
  0.9 5.1 %collective-permute-start.2 = (bf16[128,128]{1,0:T(8,128)(2,1)S(1)}, bf16[128,128]{1,0:T(8,128)(2,1)S(1)}, u32[]{:S(2)}, u32[]{:S(2)}) collective-permute-start(bf16[128,128]{1,0:T(8,128)(2,1)S(1)} %get-tuple-element.24), channel_id=1, source_target_pairs={{0,24},{1,25},{2,26},{3,27},{4,28},{5,29},{6,30},{7,31},{8,16},{9,... | collective-permute-start | bytes 98312 | tf_op jit(solution)/shard_map/ppermute | solution.py:45
  6.0 0.6 collective-permute-start
  7.3 2.7 %build_tile.1.refs_0_ = bf16[32,128,128]{2,1,0:T(8,128)(2,1)} custom-call(s32[1,64]{1,0:T(1,128)} %bitcast.6, s32[1,64]{1,0:T(1,128)} %bitcast.7, s32[1,1]{1,0:T(1,128)S(6)} %copy.21.count_ref, bf16[64,128,128]{2,1,0:T(8,128)(2,1)} %bitcast.5), custom_call_target="tpu_custom_call" | custom-call | tf_op jit(solution)/shard_map/build_tile/pallas_call | solution.py:90
  10.0 0.8 %collective-permute-done.1.refs_2_ = bf16[128,128]{1,0:T(8,128)(2,1)S(1)} collective-permute-done((bf16[128,128]{1,0:T(8,128)(2,1)S(1)}, bf16[128,128]{1,0:T(8,128)(2,1)S(1)}, u32[]{:S(2)}, u32[]{:S(2)}) %collective-permute-start.1) | collective-permute-done | bytes 32800 | tf_op jit(solution)/shard_map/ppermute | solution.py:45
  10.8 6.4 %all-to-all-start = ((bf16[32,128,128]{2,1,0:T(8,128)(2,1)}), bf16[32,128,128]{2,1,0:T(8,128)(2,1)S(1)}, u32[]{:S(2)}, u32[]{:S(2)}) async-start(bf16[32,128,128]{2,1,0:T(8,128)(2,1)} %after.1.dense_hbm), calls=%async_computation | async-start | bytes 2097152 | tf_op jit(solution)/shard_map/all_to_all | solution.py:367
  17.2 2.9 %collective-permute-start.5 = (bf16[512,128]{1,0:T(8,128)(2,1)S(1)}, bf16[512,128]{1,0:T(8,128)(2,1)S(1)}, u32[]{:S(2)}, u32[]{:S(2)}) collective-permute-start(bf16[512,128]{1,0:T(8,128)(2,1)S(1)} %pad_maximum_fusion), channel_id=1, source_target_pairs={{0,6},{1,7},{2,4},{3,5},{4,2},{5,3},{6,0},{7,1},{8,14},{9,15},{10,... | collective-permute-start | bytes 393224 | tf_op jit(solution)/shard_map/ppermute | solution.py:45
  20.1 0.6 collective-permute-start.4
  20.7 0.1 collective-permute-start.3
  20.8 9.8 %collective-permute-done.3 = bf16[512,128]{1,0:T(8,128)(2,1)S(1)} collective-permute-done((bf16[512,128]{1,0:T(8,128)(2,1)S(1)}, bf16[512,128]{1,0:T(8,128)(2,1)S(1)}, u32[]{:S(2)}, u32[]{:S(2)}) %collective-permute-start.3) | collective-permute-done | bytes 131104 | tf_op jit(solution)/shard_map/ppermute | solution.py:45
  30.6 2.1 %collective-permute-done.4 = bf16[512,128]{1,0:T(8,128)(2,1)S(1)} collective-permute-done((bf16[512,128]{1,0:T(8,128)(2,1)S(1)}, bf16[512,128]{1,0:T(8,128)(2,1)S(1)}, u32[]{:S(2)}, u32[]{:S(2)}) %collective-permute-start.4) | collective-permute-done | bytes 131104 | tf_op jit(solution)/shard_map/ppermute | solution.py:45
  32.8 0.7 turn_panel.1.refs_0_
  33.6 0.1 collective-permute-start.6
  35.0 2.2 %forward_first.1 = (f32[128,128]{1,0:T(8,128)S(1)}, f32[128,128]{1,0:T(8,128)S(1)}) custom-call(s32[16]{0:T(128)S(1)} %broadcast_xor_fusion.sources_ref, s32[2]{0:T(128)S(1)} %iota_xor_fusion.targets_ref, f32[1]{0:T(128)S(6)} %copy.22.center_ref, f32[1]{0:T(128)S(6)} %copy.23.halfwidth_ref, bf16[32,128,128]{2,1,0:T(8,128)(2,1)} %after.1.dense_hbm, ...), custom_call_target="tpu_custom_call" | custom-call | tf_op jit(solution)/shard_map/forward_first/pallas_call | solution.py:168
  37.2 0.6 collective-permute-start.7
  37.7 0.9 %collective-permute-done.7 = f32[128,128]{1,0:T(8,128)S(1)} collective-permute-done((f32[128,128]{1,0:T(8,128)S(1)}, f32[128,128]{1,0:T(8,128)S(1)}, u32[]{:S(2)}, u32[]{:S(2)}) %collective-permute-start.7) | collective-permute-done | bytes 65568 | tf_op jit(solution)/shard_map/ppermute | solution.py:36
  38.7 0.8 %lay_panels.1.turned_ref = bf16[128,4096]{1,0:T(8,128)(2,1)S(1)} custom-call(s32[2]{0:T(128)S(1)} %iota_xor_fusion.targets_ref, bf16[128,2048]{1,0:T(8,128)(2,1)S(1)} %turn_panel.1.refs_0_, bf16[128,2048]{1,0:T(8,128)(2,1)S(1)} %collective-permute-done.6.refs_1_), custom_call_target="tpu_custom_call" | custom-call | tf_op jit(solution)/shard_map/lay_panels/pallas_call | solution.py:217
  39.5 1.4 %all-to-all-done.received_ref = bf16[32,128,128]{2,1,0:T(8,128)(2,1)S(1)} async-done(((bf16[32,128,128]{2,1,0:T(8,128)(2,1)}), bf16[32,128,128]{2,1,0:T(8,128)(2,1)S(1)}, u32[]{:S(2)}, u32[]{:S(2)}) %all-to-all-start) | async-done | bytes 1048608 | tf_op jit(solution)/shard_map/all_to_all | solution.py:367
  40.9 0.5 backward_first.1
  41.4 2.8 %collective-permute-start.8 = (bf16[128,128]{1,0:T(8,128)(2,1)S(1)}, bf16[128,128]{1,0:T(8,128)(2,1)S(1)}, u32[]{:S(2)}, u32[]{:S(2)}) collective-permute-start(bf16[128,128]{1,0:T(8,128)(2,1)S(1)} %get-tuple-element.15), channel_id=1, source_target_pairs={{0,24},{1,7},{2,26},{3,5},{4,28},{5,3},{6,30},{7,1},{8,16},{9,15},... | collective-permute-start | bytes 98312 | tf_op jit(solution)/shard_map/ppermute | solution.py:45
  44.2 1.7 %collective-permute-start.11 = (bf16[128,128]{1,0:T(8,128)(2,1)S(1)}, bf16[128,128]{1,0:T(8,128)(2,1)S(1)}, u32[]{:S(2)}, u32[]{:S(2)}) collective-permute-start(bf16[128,128]{1,0:T(8,128)(2,1)S(1)} %get-tuple-element.15), channel_id=1, source_target_pairs={{0,16},{1,5},{2,18},{3,7},{4,20},{5,1},{6,22},{7,3},{8,24},{9,13},... | collective-permute-start | bytes 98312 | tf_op jit(solution)/shard_map/ppermute | solution.py:45
  45.9 1.2 %collective-permute-done.8.panel_ref = bf16[128,128]{1,0:T(8,128)(2,1)S(1)} collective-permute-done((bf16[128,128]{1,0:T(8,128)(2,1)S(1)}, bf16[128,128]{1,0:T(8,128)(2,1)S(1)}, u32[]{:S(2)}, u32[]{:S(2)}) %collective-permute-start.8) | collective-permute-done | bytes 32800 | tf_op jit(solution)/shard_map/ppermute | solution.py:45
  47.1 0.6 pick_blocks.1
  47.7 0.1 collective-permute-start.9
  47.8 2.0 %collective-permute-done.10 = bf16[128,128]{1,0:T(8,128)(2,1)S(1)} collective-permute-done((bf16[128,128]{1,0:T(8,128)(2,1)S(1)}, bf16[128,128]{1,0:T(8,128)(2,1)S(1)}, u32[]{:S(2)}, u32[]{:S(2)}) %collective-permute-start.10) | collective-permute-done | bytes 32800 | tf_op jit(solution)/shard_map/ppermute | solution.py:45
  49.9 1.6 %collective-permute-start.14 = (bf16[512,128]{1,0:T(8,128)(2,1)S(1)}, bf16[512,128]{1,0:T(8,128)(2,1)S(1)}, u32[]{:S(2)}, u32[]{:S(2)}) collective-permute-start(bf16[512,128]{1,0:T(8,128)(2,1)S(1)} %constant_dynamic-update-slice_fusion.7.refs_0_), channel_id=1, source_target_pairs={{0,6},{1,25},{2,4},{3,27},{4,2},{5,29},{6,0},{7,31},{8,14},{9,17},... | collective-permute-start | bytes 393224 | tf_op jit(solution)/shard_map/ppermute | solution.py:45
  51.5 0.6 collective-permute-start.13
  52.1 1.3 %collective-permute-start.12 = (bf16[512,128]{1,0:T(8,128)(2,1)S(1)}, bf16[512,128]{1,0:T(8,128)(2,1)S(1)}, u32[]{:S(2)}, u32[]{:S(2)}) collective-permute-start(bf16[512,128]{1,0:T(8,128)(2,1)S(1)} %constant_dynamic-update-slice_fusion.7.refs_0_), channel_id=1, source_target_pairs={{0,2},{1,9},{2,0},{3,11},{4,6},{5,13},{6,4},{7,15},{8,10},{9,1},{1... | collective-permute-start | bytes 393224 | tf_op jit(solution)/shard_map/ppermute | solution.py:45
  53.4 2.1 %merge_tile.1.tile_ref = bf16[256,2048]{1,0:T(8,128)(2,1)S(1)} custom-call(s32[16]{0:T(128)S(1)} %xor_bitcast_fusion.sources_ref, s32[2]{0:T(128)S(1)} %iota_xor_fusion.targets_ref, bf16[32,128,128]{2,1,0:T(8,128)(2,1)} %after.1.dense_hbm, bf16[32,128,128]{2,1,0:T(8,128)(2,1)S(1)} %all-to-all-done.received_ref, ...), custom_call_target="tpu_custom_call" | custom-call | tf_op jit(solution)/shard_map/merge_tile/pallas_call | solution.py:289
  55.6 0.3 collective-permute-done.14.refs_3_
  55.9 1.3 %collective-permute-done.13.refs_2_ = bf16[512,128]{1,0:T(8,128)(2,1)S(1)} collective-permute-done((bf16[512,128]{1,0:T(8,128)(2,1)S(1)}, bf16[512,128]{1,0:T(8,128)(2,1)S(1)}, u32[]{:S(2)}, u32[]{:S(2)}) %collective-permute-start.13) | collective-permute-done | bytes 131104 | tf_op jit(solution)/shard_map/ppermute | solution.py:45
  57.2 0.2 collective-permute-done.12.refs_1_
  57.4 0.4 apply_tile.2
  57.9 1.2 %collective-permute-done.15 = f32[128,128]{1,0:T(8,128)S(1)} collective-permute-done((f32[128,128]{1,0:T(8,128)S(1)}, f32[128,128]{1,0:T(8,128)S(1)}, u32[]{:S(2)}, u32[]{:S(2)}) %collective-permute-start.15) | collective-permute-done | bytes 65568 | tf_op jit(solution)/shard_map/ppermute | solution.py:36
  59.2 1.8 %collective-permute-start.18 = (bf16[128,128]{1,0:T(8,128)(2,1)S(1)}, bf16[128,128]{1,0:T(8,128)(2,1)S(1)}, u32[]{:S(2)}, u32[]{:S(2)}) collective-permute-start(bf16[128,128]{1,0:T(8,128)(2,1)S(1)} %get-tuple-element.21), channel_id=1, source_target_pairs={{0,24},{1,7},{2,26},{3,5},{4,28},{5,3},{6,30},{7,1},{8,16},{9,15},... | collective-permute-start | bytes 98312 | tf_op jit(solution)/shard_map/ppermute | solution.py:45
  61.0 0.1 collective-permute-start.17
  61.1 2.5 %collective-permute-start.16 = (bf16[128,128]{1,0:T(8,128)(2,1)S(1)}, bf16[128,128]{1,0:T(8,128)(2,1)S(1)}, u32[]{:S(2)}, u32[]{:S(2)}) collective-permute-start(bf16[128,128]{1,0:T(8,128)(2,1)S(1)} %get-tuple-element.21), channel_id=1, source_target_pairs={{0,8},{1,3},{2,10},{3,1},{4,12},{5,7},{6,14},{7,5},{8,0},{9,11},{1... | collective-permute-start | bytes 98312 | tf_op jit(solution)/shard_map/ppermute | solution.py:45
  63.6 1.3 %collective-permute-done.18 = bf16[128,128]{1,0:T(8,128)(2,1)S(1)} collective-permute-done((bf16[128,128]{1,0:T(8,128)(2,1)S(1)}, bf16[128,128]{1,0:T(8,128)(2,1)S(1)}, u32[]{:S(2)}, u32[]{:S(2)}) %collective-permute-start.18) | collective-permute-done | bytes 32800 | tf_op jit(solution)/shard_map/ppermute | solution.py:45
  64.9 1.2 %collective-permute-done.17 = bf16[128,128]{1,0:T(8,128)(2,1)S(1)} collective-permute-done((bf16[128,128]{1,0:T(8,128)(2,1)S(1)}, bf16[128,128]{1,0:T(8,128)(2,1)S(1)}, u32[]{:S(2)}, u32[]{:S(2)}) %collective-permute-start.17) | collective-permute-done | bytes 32800 | tf_op jit(solution)/shard_map/ppermute | solution.py:45
  66.2 2.1 %collective-permute-start.21 = (bf16[512,128]{1,0:T(8,128)(2,1)S(1)}, bf16[512,128]{1,0:T(8,128)(2,1)S(1)}, u32[]{:S(2)}, u32[]{:S(2)}) collective-permute-start(bf16[512,128]{1,0:T(8,128)(2,1)S(1)} %pad_maximum_fusion.1.refs_0_), channel_id=1, source_target_pairs={{0,6},{1,25},{2,4},{3,27},{4,2},{5,29},{6,0},{7,31},{8,14},{9,17},... | collective-permute-start | bytes 393224 | tf_op jit(solution)/shard_map/ppermute | solution.py:45
  68.2 0.1 collective-permute-start.20
  68.4 1.3 %collective-permute-start.19 = (bf16[512,128]{1,0:T(8,128)(2,1)S(1)}, bf16[512,128]{1,0:T(8,128)(2,1)S(1)}, u32[]{:S(2)}, u32[]{:S(2)}) collective-permute-start(bf16[512,128]{1,0:T(8,128)(2,1)S(1)} %pad_maximum_fusion.1.refs_0_), channel_id=1, source_target_pairs={{0,2},{1,9},{2,0},{3,11},{4,6},{5,13},{6,4},{7,15},{8,10},{9,1},{1... | collective-permute-start | bytes 393224 | tf_op jit(solution)/shard_map/ppermute | solution.py:45
  69.7 2.4 %collective-permute-done.21.refs_3_ = bf16[512,128]{1,0:T(8,128)(2,1)S(1)} collective-permute-done((bf16[512,128]{1,0:T(8,128)(2,1)S(1)}, bf16[512,128]{1,0:T(8,128)(2,1)S(1)}, u32[]{:S(2)}, u32[]{:S(2)}) %collective-permute-start.21) | collective-permute-done | bytes 131104 | tf_op jit(solution)/shard_map/ppermute | solution.py:45
  72.1 1.4 %collective-permute-done.20.refs_2_ = bf16[512,128]{1,0:T(8,128)(2,1)S(1)} collective-permute-done((bf16[512,128]{1,0:T(8,128)(2,1)S(1)}, bf16[512,128]{1,0:T(8,128)(2,1)S(1)}, u32[]{:S(2)}, u32[]{:S(2)}) %collective-permute-start.20) | collective-permute-done | bytes 131104 | tf_op jit(solution)/shard_map/ppermute | solution.py:45
  73.5 0.3 collective-permute-done.19.refs_1_
  73.8 0.4 apply_tile.3
  74.3 1.2 %collective-permute-done.22 = f32[128,128]{1,0:T(8,128)S(1)} collective-permute-done((f32[128,128]{1,0:T(8,128)S(1)}, f32[128,128]{1,0:T(8,128)S(1)}, u32[]{:S(2)}, u32[]{:S(2)}) %collective-permute-start.22) | collective-permute-done | bytes 65568 | tf_op jit(solution)/shard_map/ppermute | solution.py:36
  75.5 0.6 add.20
  (35 shorter events, 0.4 us)
Async XLA Ops:
  0.9 9.1 %collective-permute-start.2 = (bf16[128,128]{1,0:T(8,128)(2,1)S(1)}, bf16[128,128]{1,0:T(8,128)(2,1)S(1)}, u32[]{:S(2)}, u32[]{:S(2)}) collective-permute-start(bf16[128,128]{1,0:T(8,128)(2,1)S(1)} %get-tuple-element.24), channel_id=1, source_target_pairs={{0,24},{1,25},{2,26},{3,27},{4,28},{5,29},{6,30},{7,31},{8,16},{9,... | collective-permute-start | bytes 98312 | tf_op jit(solution)/shard_map/ppermute | solution.py:45
  6.0 4.8 %collective-permute-start.1 = (bf16[128,128]{1,0:T(8,128)(2,1)S(1)}, bf16[128,128]{1,0:T(8,128)(2,1)S(1)}, u32[]{:S(2)}, u32[]{:S(2)}) collective-permute-start(bf16[128,128]{1,0:T(8,128)(2,1)S(1)} %get-tuple-element.24), channel_id=1, source_target_pairs={{0,16},{1,17},{2,18},{3,19},{4,20},{5,21},{6,22},{7,23},{8,24},{9,... | collective-permute-start | bytes 98312 | tf_op jit(solution)/shard_map/ppermute | solution.py:45
  6.0 4.8 %collective-permute-start = (bf16[128,128]{1,0:T(8,128)(2,1)S(1)}, bf16[128,128]{1,0:T(8,128)(2,1)S(1)}, u32[]{:S(2)}, u32[]{:S(2)}) collective-permute-start(bf16[128,128]{1,0:T(8,128)(2,1)S(1)} %get-tuple-element.24), channel_id=1, source_target_pairs={{0,8},{1,9},{2,10},{3,11},{4,12},{5,13},{6,14},{7,15},{8,0},{9,1},... | collective-permute-start | bytes 98312 | tf_op jit(solution)/shard_map/ppermute | solution.py:45
  10.0 7.2 %copy-start.2 = (s32[16]{0:T(128)S(1)}, s32[16]{0:T(128)}, u32[]{:S(2)}) copy-start(s32[16]{0:T(128)} %constant.26.clone) | copy-start | bytes 196
  10.8 24.2 %copy-start = (f32[128,128]{1,0:T(8,128)S(1)}, f32[128,128]{1,0:T(8,128)}, u32[]{:S(2)}) copy-start(f32[128,128]{1,0:T(8,128)} %previous_ref.1) | copy-start | bytes 196612
  10.8 30.1 %all-to-all-start = ((bf16[32,128,128]{2,1,0:T(8,128)(2,1)}), bf16[32,128,128]{2,1,0:T(8,128)(2,1)S(1)}, u32[]{:S(2)}, u32[]{:S(2)}) async-start(bf16[32,128,128]{2,1,0:T(8,128)(2,1)} %after.1.dense_hbm), calls=%async_computation | async-start | bytes 2097152 | tf_op jit(solution)/shard_map/all_to_all | solution.py:367
  17.2 15.5 %collective-permute-start.5 = (bf16[512,128]{1,0:T(8,128)(2,1)S(1)}, bf16[512,128]{1,0:T(8,128)(2,1)S(1)}, u32[]{:S(2)}, u32[]{:S(2)}) collective-permute-start(bf16[512,128]{1,0:T(8,128)(2,1)S(1)} %pad_maximum_fusion), channel_id=1, source_target_pairs={{0,6},{1,7},{2,4},{3,5},{4,2},{5,3},{6,0},{7,1},{8,14},{9,15},{10,... | collective-permute-start | bytes 393224 | tf_op jit(solution)/shard_map/ppermute | solution.py:45
  20.1 12.6 %collective-permute-start.4 = (bf16[512,128]{1,0:T(8,128)(2,1)S(1)}, bf16[512,128]{1,0:T(8,128)(2,1)S(1)}, u32[]{:S(2)}, u32[]{:S(2)}) collective-permute-start(bf16[512,128]{1,0:T(8,128)(2,1)S(1)} %pad_maximum_fusion), channel_id=1, source_target_pairs={{0,4},{1,5},{2,6},{3,7},{4,0},{5,1},{6,2},{7,3},{8,12},{9,13},{10,... | collective-permute-start | bytes 393224 | tf_op jit(solution)/shard_map/ppermute | solution.py:45
  20.7 9.9 %collective-permute-start.3 = (bf16[512,128]{1,0:T(8,128)(2,1)S(1)}, bf16[512,128]{1,0:T(8,128)(2,1)S(1)}, u32[]{:S(2)}, u32[]{:S(2)}) collective-permute-start(bf16[512,128]{1,0:T(8,128)(2,1)S(1)} %pad_maximum_fusion), channel_id=1, source_target_pairs={{0,2},{1,3},{2,0},{3,1},{4,6},{5,7},{6,4},{7,5},{8,10},{9,11},{10,... | collective-permute-start | bytes 393224 | tf_op jit(solution)/shard_map/ppermute | solution.py:45
  33.6 5.1 %collective-permute-start.6 = (bf16[128,2048]{1,0:T(8,128)(2,1)S(1)}, bf16[128,2048]{1,0:T(8,128)(2,1)S(1)}, u32[]{:S(2)}, u32[]{:S(2)}) collective-permute-start(bf16[128,2048]{1,0:T(8,128)(2,1)S(1)} %turn_panel.1.refs_0_), channel_id=1, source_target_pairs={{0,1},{1,0},{2,3},{3,2},{4,5},{5,4},{6,7},{7,6},{8,9},{9,8},{10,11... | collective-permute-start | bytes 1572872 | tf_op jit(solution)/shard_map/ppermute | solution.py:36
  37.2 1.5 %collective-permute-start.7 = (f32[128,128]{1,0:T(8,128)S(1)}, f32[128,128]{1,0:T(8,128)S(1)}, u32[]{:S(2)}, u32[]{:S(2)}) collective-permute-start(f32[128,128]{1,0:T(8,128)S(1)} %get-tuple-element.14), channel_id=1, source_target_pairs={{0,1},{1,0},{2,3},{3,2},{4,5},{5,4},{6,7},{7,6},{8,9},{9,8},{10,11... | collective-permute-start | bytes 196616 | tf_op jit(solution)/shard_map/ppermute | solution.py:36
  39.4 14.0 %copy-start.1 = (s32[2,16]{1,0:T(2,128)S(1)}, s32[2,16]{1,0:T(2,128)}, u32[]{:S(2)}) copy-start(s32[2,16]{1,0:T(2,128)} %constant.27.clone) | copy-start | bytes 388
  41.4 5.8 %collective-permute-start.8 = (bf16[128,128]{1,0:T(8,128)(2,1)S(1)}, bf16[128,128]{1,0:T(8,128)(2,1)S(1)}, u32[]{:S(2)}, u32[]{:S(2)}) collective-permute-start(bf16[128,128]{1,0:T(8,128)(2,1)S(1)} %get-tuple-element.15), channel_id=1, source_target_pairs={{0,24},{1,7},{2,26},{3,5},{4,28},{5,3},{6,30},{7,1},{8,16},{9,15},... | collective-permute-start | bytes 98312 | tf_op jit(solution)/shard_map/ppermute | solution.py:45
  44.2 5.6 %collective-permute-start.11 = (bf16[128,128]{1,0:T(8,128)(2,1)S(1)}, bf16[128,128]{1,0:T(8,128)(2,1)S(1)}, u32[]{:S(2)}, u32[]{:S(2)}) collective-permute-start(bf16[128,128]{1,0:T(8,128)(2,1)S(1)} %get-tuple-element.15), channel_id=1, source_target_pairs={{0,16},{1,5},{2,18},{3,7},{4,20},{5,1},{6,22},{7,3},{8,24},{9,13},... | collective-permute-start | bytes 98312 | tf_op jit(solution)/shard_map/ppermute | solution.py:45
  45.9 3.9 %collective-permute-start.10 = (bf16[128,128]{1,0:T(8,128)(2,1)S(1)}, bf16[128,128]{1,0:T(8,128)(2,1)S(1)}, u32[]{:S(2)}, u32[]{:S(2)}) collective-permute-start(bf16[128,128]{1,0:T(8,128)(2,1)S(1)} %get-tuple-element.15), channel_id=1, source_target_pairs={{0,8},{1,3},{2,10},{3,1},{4,12},{5,7},{6,14},{7,5},{8,0},{9,11},{1... | collective-permute-start | bytes 98312 | tf_op jit(solution)/shard_map/ppermute | solution.py:45
  47.7 5.7 %collective-permute-start.9 = (bf16[16,128,128]{2,1,0:T(8,128)(2,1)S(1)}, bf16[16,128,128]{2,1,0:T(8,128)(2,1)S(1)}, u32[]{:S(2)}, u32[]{:S(2)}) collective-permute-start(bf16[16,128,128]{2,1,0:T(8,128)(2,1)S(1)} %pick_blocks.1), channel_id=1, source_target_pairs={{0,1},{1,0},{2,3},{3,2},{4,5},{5,4},{6,7},{7,6},{8,9},{9,8},{10,11... | collective-permute-start | bytes 1572872 | tf_op jit(solution)/shard_map/ppermute | solution.py:36
  49.9 6.0 %collective-permute-start.14 = (bf16[512,128]{1,0:T(8,128)(2,1)S(1)}, bf16[512,128]{1,0:T(8,128)(2,1)S(1)}, u32[]{:S(2)}, u32[]{:S(2)}) collective-permute-start(bf16[512,128]{1,0:T(8,128)(2,1)S(1)} %constant_dynamic-update-slice_fusion.7.refs_0_), channel_id=1, source_target_pairs={{0,6},{1,25},{2,4},{3,27},{4,2},{5,29},{6,0},{7,31},{8,14},{9,17},... | collective-permute-start | bytes 393224 | tf_op jit(solution)/shard_map/ppermute | solution.py:45
  51.5 5.7 %collective-permute-start.13 = (bf16[512,128]{1,0:T(8,128)(2,1)S(1)}, bf16[512,128]{1,0:T(8,128)(2,1)S(1)}, u32[]{:S(2)}, u32[]{:S(2)}) collective-permute-start(bf16[512,128]{1,0:T(8,128)(2,1)S(1)} %constant_dynamic-update-slice_fusion.7.refs_0_), channel_id=1, source_target_pairs={{0,4},{1,17},{2,6},{3,19},{4,0},{5,21},{6,2},{7,23},{8,12},{9,25},... | collective-permute-start | bytes 393224 | tf_op jit(solution)/shard_map/ppermute | solution.py:45
  52.1 5.3 %collective-permute-start.12 = (bf16[512,128]{1,0:T(8,128)(2,1)S(1)}, bf16[512,128]{1,0:T(8,128)(2,1)S(1)}, u32[]{:S(2)}, u32[]{:S(2)}) collective-permute-start(bf16[512,128]{1,0:T(8,128)(2,1)S(1)} %constant_dynamic-update-slice_fusion.7.refs_0_), channel_id=1, source_target_pairs={{0,2},{1,9},{2,0},{3,11},{4,6},{5,13},{6,4},{7,15},{8,10},{9,1},{1... | collective-permute-start | bytes 393224 | tf_op jit(solution)/shard_map/ppermute | solution.py:45
  57.8 1.3 %collective-permute-start.15 = (f32[128,128]{1,0:T(8,128)S(1)}, f32[128,128]{1,0:T(8,128)S(1)}, u32[]{:S(2)}, u32[]{:S(2)}) collective-permute-start(f32[128,128]{1,0:T(8,128)S(1)} %get-tuple-element.18), channel_id=1, source_target_pairs={{0,1},{1,0},{2,3},{3,2},{4,5},{5,4},{6,7},{7,6},{8,9},{9,8},{10,11... | collective-permute-start | bytes 196616 | tf_op jit(solution)/shard_map/ppermute | solution.py:36
  59.2 5.8 %collective-permute-start.18 = (bf16[128,128]{1,0:T(8,128)(2,1)S(1)}, bf16[128,128]{1,0:T(8,128)(2,1)S(1)}, u32[]{:S(2)}, u32[]{:S(2)}) collective-permute-start(bf16[128,128]{1,0:T(8,128)(2,1)S(1)} %get-tuple-element.21), channel_id=1, source_target_pairs={{0,24},{1,7},{2,26},{3,5},{4,28},{5,3},{6,30},{7,1},{8,16},{9,15},... | collective-permute-start | bytes 98312 | tf_op jit(solution)/shard_map/ppermute | solution.py:45
  61.0 5.2 %collective-permute-start.17 = (bf16[128,128]{1,0:T(8,128)(2,1)S(1)}, bf16[128,128]{1,0:T(8,128)(2,1)S(1)}, u32[]{:S(2)}, u32[]{:S(2)}) collective-permute-start(bf16[128,128]{1,0:T(8,128)(2,1)S(1)} %get-tuple-element.21), channel_id=1, source_target_pairs={{0,16},{1,5},{2,18},{3,7},{4,20},{5,1},{6,22},{7,3},{8,24},{9,13},... | collective-permute-start | bytes 98312 | tf_op jit(solution)/shard_map/ppermute | solution.py:45
  61.1 5.1 %collective-permute-start.16 = (bf16[128,128]{1,0:T(8,128)(2,1)S(1)}, bf16[128,128]{1,0:T(8,128)(2,1)S(1)}, u32[]{:S(2)}, u32[]{:S(2)}) collective-permute-start(bf16[128,128]{1,0:T(8,128)(2,1)S(1)} %get-tuple-element.21), channel_id=1, source_target_pairs={{0,8},{1,3},{2,10},{3,1},{4,12},{5,7},{6,14},{7,5},{8,0},{9,11},{1... | collective-permute-start | bytes 98312 | tf_op jit(solution)/shard_map/ppermute | solution.py:45
  66.2 6.0 %collective-permute-start.21 = (bf16[512,128]{1,0:T(8,128)(2,1)S(1)}, bf16[512,128]{1,0:T(8,128)(2,1)S(1)}, u32[]{:S(2)}, u32[]{:S(2)}) collective-permute-start(bf16[512,128]{1,0:T(8,128)(2,1)S(1)} %pad_maximum_fusion.1.refs_0_), channel_id=1, source_target_pairs={{0,6},{1,25},{2,4},{3,27},{4,2},{5,29},{6,0},{7,31},{8,14},{9,17},... | collective-permute-start | bytes 393224 | tf_op jit(solution)/shard_map/ppermute | solution.py:45
  68.2 5.2 %collective-permute-start.20 = (bf16[512,128]{1,0:T(8,128)(2,1)S(1)}, bf16[512,128]{1,0:T(8,128)(2,1)S(1)}, u32[]{:S(2)}, u32[]{:S(2)}) collective-permute-start(bf16[512,128]{1,0:T(8,128)(2,1)S(1)} %pad_maximum_fusion.1.refs_0_), channel_id=1, source_target_pairs={{0,4},{1,17},{2,6},{3,19},{4,0},{5,21},{6,2},{7,23},{8,12},{9,25},... | collective-permute-start | bytes 393224 | tf_op jit(solution)/shard_map/ppermute | solution.py:45
  68.4 5.4 %collective-permute-start.19 = (bf16[512,128]{1,0:T(8,128)(2,1)S(1)}, bf16[512,128]{1,0:T(8,128)(2,1)S(1)}, u32[]{:S(2)}, u32[]{:S(2)}) collective-permute-start(bf16[512,128]{1,0:T(8,128)(2,1)S(1)} %pad_maximum_fusion.1.refs_0_), channel_id=1, source_target_pairs={{0,2},{1,9},{2,0},{3,11},{4,6},{5,13},{6,4},{7,15},{8,10},{9,1},{1... | collective-permute-start | bytes 393224 | tf_op jit(solution)/shard_map/ppermute | solution.py:45
  74.2 1.3 %collective-permute-start.22 = (f32[128,128]{1,0:T(8,128)S(1)}, f32[128,128]{1,0:T(8,128)S(1)}, u32[]{:S(2)}, u32[]{:S(2)}) collective-permute-start(f32[128,128]{1,0:T(8,128)S(1)} %get-tuple-element.20), channel_id=1, source_target_pairs={{0,1},{1,0},{2,3},{3,2},{4,5},{5,4},{6,7},{7,6},{8,9},{9,8},{10,11... | collective-permute-start | bytes 196616 | tf_op jit(solution)/shard_map/ppermute | solution.py:36

commit v13 on v12

--- a/solution.py
+++ b/solution.py
@@ -54,7 +54,7 @@
 
     def kernel(
         rows_hbm, cols_hbm, count_ref, stack_hbm, out_hbm,
-        stack_ref, acc_ref, dense_ref, rows_ref, cols_ref, index_sems, stack_sems, sems,
+        stack_ref, even_ref, odd_ref, dense_ref, rows_ref, cols_ref, index_sems, stack_sems, sems,
     ):
         indices = [
             pltpu.make_async_copy(source, target, index_sems.at[n])
@@ -69,7 +69,8 @@
                 pltpu.make_async_copy(stack_hbm.at[held], stack_ref.at[held], stack_sems.at[n])
             )
             arrivals[-1].start()
-        acc_ref[...] = jnp.zeros_like(acc_ref)
+        even_ref[...] = jnp.zeros_like(even_ref)
+        odd_ref[...] = jnp.zeros_like(odd_ref)
         for copy in indices:
             copy.wait()
         count = count_ref[0, 0]
@@ -77,11 +78,12 @@
             copy.wait()
             for s in range(n * chunk, (n + 1) * chunk):
                 cell = jnp.where(s < count, cols_ref[0, s] * grid_cols + rows_ref[0, s], cells)
+                acc_ref = odd_ref if s % 2 else even_ref
                 acc_ref[cell] += stack_ref[s].astype(jnp.float32)
         copies = []
         for n in range(parts):
             held = pl.ds(n * (cells // parts), cells // parts)
-            dense_ref[held] = acc_ref[held].astype(jnp.bfloat16)
+            dense_ref[held] = (even_ref[held] + odd_ref[held]).astype(jnp.bfloat16)
             copies.append(pltpu.make_async_copy(dense_ref.at[held], out_hbm.at[held], sems.at[n]))
             copies[-1].start()
         for copy in copies:
@@ -93,6 +95,7 @@
         out_specs=HBM,
         scratch_shapes=[
             pltpu.VMEM(stacked.shape, jnp.bfloat16),
+            pltpu.VMEM((cells + 1, orb, orb), jnp.float32),
             pltpu.VMEM((cells + 1, orb, orb), jnp.float32),
             pltpu.VMEM((cells, orb, orb), jnp.bfloat16),
             pltpu.SMEM(rows.shape, jnp.int32),
@@ -103,7 +106,7 @@
         ],
         out_shape=pltpu.HBM((cells, orb, orb), jnp.bfloat16),
         compiler_params=pltpu.CompilerParams(
-            vmem_limit_bytes=(cells + 1) * orb * orb * 6 + stacked.size * 2 + SPARE
+            vmem_limit_bytes=(cells + 1) * orb * orb * 10 + stacked.size * 2 + SPARE
         ),
         name="build_tile",
     )(

time: 76.6 us -> 76.6 us (level)
  no operation moved by 1% of the time
where the time goes in v13:
time: 76.6 us; the launch traced here: 76.2 us
  starting transfers between devices  32.7 us (43%)
  waiting for transfers between devices  29.1 us (38%)
  Pallas kernels  10.5 us (14%)
  between operations  2.21 us (3%)
  other arithmetic  1.55 us (2%)
    ppermute x18, starting transfers between devices, swap_rows(): return lax.ppermute(x, ('row', 'col'), pairs)  25.4 us
    ppermute x18, waiting for transfers between devices, swap_rows(): return lax.ppermute(x, ('row', 'col'), pairs)  24.4 us
    all_to_all x1, starting transfers between devices, body(): received = lax.all_to_all(dense, 'row', 0, 0, tiled=True)  6.4 us
    ppermute x5, waiting for transfers between devices, swap(): lax.ppermute(x, axis, [(source, source ^ offset) for source in range(size)])  3.39 us
    pallas_call x1, Pallas kernels, build_tile(): pl.pallas_call(kernel, in_specs=[HBM, HBM, SMEM, HBM], out_specs=HBM, scr...  2.7 us
    pallas_call x1, Pallas kernels, forward_first(): pl.pallas_call(kernel, in_specs=[SMEM] * 4 + [HBM] + [VMEM] * 2, out_spec...  2.21 us
    pallas_call x1, Pallas kernels, merge_tile(): pl.pallas_call(kernel, in_specs=[SMEM] * 2 + [HBM] + [VMEM] * grid_cols,...  2.14 us
  transfers between devices with their start and end apart: 24, of which 17 were waited for; matrix products, arithmetic and copies ran while one was open for 0% of the time, Pallas kernels for 12%

profile of v13, /device:TPU:0, one launch (start us, length us, event | category | flops | bytes accessed | tf_op | source)
XLA Modules:
  0.0 76.2 jit_solution(8479788480115888311)
XLA Ops:
  0.0 0.8 %constant_dynamic-update-slice_fusion.6 = (bf16[2048,128]{1,0:T(8,128)(2,1)S(1)}, bf16[128,128]{1,0:T(8,128)(2,1)S(1)}) fusion(f32[128,128]{1,0:T(8,128)} %previous_ref.1), kind=kLoop, calls=%fused_computation.8 | loop fusion | flops 16383 | bytes 131072
  0.9 5.1 %collective-permute-start.2 = (bf16[128,128]{1,0:T(8,128)(2,1)S(1)}, bf16[128,128]{1,0:T(8,128)(2,1)S(1)}, u32[]{:S(2)}, u32[]{:S(2)}) collective-permute-start(bf16[128,128]{1,0:T(8,128)(2,1)S(1)} %get-tuple-element.24), channel_id=1, source_target_pairs={{0,24},{1,25},{2,26},{3,27},{4,28},{5,29},{6,30},{7,31},{8,16},{9,... | collective-permute-start | bytes 98312 | tf_op jit(solution)/shard_map/ppermute | solution.py:45
  6.0 0.6 collective-permute-start
  7.3 2.7 %build_tile.1.refs_0_ = bf16[32,128,128]{2,1,0:T(8,128)(2,1)} custom-call(s32[1,64]{1,0:T(1,128)} %bitcast.6, s32[1,64]{1,0:T(1,128)} %bitcast.7, s32[1,1]{1,0:T(1,128)S(6)} %copy.21.count_ref, bf16[64,128,128]{2,1,0:T(8,128)(2,1)} %bitcast.5), custom_call_target="tpu_custom_call" | custom-call | tf_op jit(solution)/shard_map/build_tile/pallas_call | solution.py:92
  10.0 0.8 %collective-permute-done.1.refs_2_ = bf16[128,128]{1,0:T(8,128)(2,1)S(1)} collective-permute-done((bf16[128,128]{1,0:T(8,128)(2,1)S(1)}, bf16[128,128]{1,0:T(8,128)(2,1)S(1)}, u32[]{:S(2)}, u32[]{:S(2)}) %collective-permute-start.1) | collective-permute-done | bytes 32800 | tf_op jit(solution)/shard_map/ppermute | solution.py:45
  10.8 6.4 %all-to-all-start = ((bf16[32,128,128]{2,1,0:T(8,128)(2,1)}), bf16[32,128,128]{2,1,0:T(8,128)(2,1)S(1)}, u32[]{:S(2)}, u32[]{:S(2)}) async-start(bf16[32,128,128]{2,1,0:T(8,128)(2,1)} %after.1.dense_hbm), calls=%async_computation | async-start | bytes 2097152 | tf_op jit(solution)/shard_map/all_to_all | solution.py:370
  17.2 2.9 %collective-permute-start.5 = (bf16[512,128]{1,0:T(8,128)(2,1)S(1)}, bf16[512,128]{1,0:T(8,128)(2,1)S(1)}, u32[]{:S(2)}, u32[]{:S(2)}) collective-permute-start(bf16[512,128]{1,0:T(8,128)(2,1)S(1)} %pad_maximum_fusion), channel_id=1, source_target_pairs={{0,6},{1,7},{2,4},{3,5},{4,2},{5,3},{6,0},{7,1},{8,14},{9,15},{10,... | collective-permute-start | bytes 393224 | tf_op jit(solution)/shard_map/ppermute | solution.py:45
  20.1 0.6 collective-permute-start.4
  20.7 0.1 collective-permute-start.3
  20.8 9.8 %collective-permute-done.3 = bf16[512,128]{1,0:T(8,128)(2,1)S(1)} collective-permute-done((bf16[512,128]{1,0:T(8,128)(2,1)S(1)}, bf16[512,128]{1,0:T(8,128)(2,1)S(1)}, u32[]{:S(2)}, u32[]{:S(2)}) %collective-permute-start.3) | collective-permute-done | bytes 131104 | tf_op jit(solution)/shard_map/ppermute | solution.py:45
  30.6 2.1 %collective-permute-done.4 = bf16[512,128]{1,0:T(8,128)(2,1)S(1)} collective-permute-done((bf16[512,128]{1,0:T(8,128)(2,1)S(1)}, bf16[512,128]{1,0:T(8,128)(2,1)S(1)}, u32[]{:S(2)}, u32[]{:S(2)}) %collective-permute-start.4) | collective-permute-done | bytes 131104 | tf_op jit(solution)/shard_map/ppermute | solution.py:45
  32.8 0.7 turn_panel.1.refs_0_
  35.0 2.2 %forward_first.1 = (f32[128,128]{1,0:T(8,128)S(1)}, f32[128,128]{1,0:T(8,128)S(1)}) custom-call(s32[16]{0:T(128)S(1)} %broadcast_xor_fusion.sources_ref, s32[2]{0:T(128)S(1)} %iota_xor_fusion.targets_ref, f32[1]{0:T(128)S(6)} %copy.22.center_ref, f32[1]{0:T(128)S(6)} %copy.23.halfwidth_ref, bf16[32,128,128]{2,1,0:T(8,128)(2,1)} %after.1.dense_hbm, ...), custom_call_target="tpu_custom_call" | custom-call | tf_op jit(solution)/shard_map/forward_first/pallas_call | solution.py:171
  37.2 0.6 collective-permute-start.7
  37.7 0.9 %collective-permute-done.7 = f32[128,128]{1,0:T(8,128)S(1)} collective-permute-done((f32[128,128]{1,0:T(8,128)S(1)}, f32[128,128]{1,0:T(8,128)S(1)}, u32[]{:S(2)}, u32[]{:S(2)}) %collective-permute-start.7) | collective-permute-done | bytes 65568 | tf_op jit(solution)/shard_map/ppermute | solution.py:36
  38.7 0.8 %lay_panels.1.turned_ref = bf16[128,4096]{1,0:T(8,128)(2,1)S(1)} custom-call(s32[2]{0:T(128)S(1)} %iota_xor_fusion.targets_ref, bf16[128,2048]{1,0:T(8,128)(2,1)S(1)} %turn_panel.1.refs_0_, bf16[128,2048]{1,0:T(8,128)(2,1)S(1)} %collective-permute-done.6.refs_1_), custom_call_target="tpu_custom_call" | custom-call | tf_op jit(solution)/shard_map/lay_panels/pallas_call | solution.py:220
  39.5 1.4 %all-to-all-done.received_ref = bf16[32,128,128]{2,1,0:T(8,128)(2,1)S(1)} async-done(((bf16[32,128,128]{2,1,0:T(8,128)(2,1)}), bf16[32,128,128]{2,1,0:T(8,128)(2,1)S(1)}, u32[]{:S(2)}, u32[]{:S(2)}) %all-to-all-start) | async-done | bytes 1048608 | tf_op jit(solution)/shard_map/all_to_all | solution.py:370
  40.9 0.5 backward_first.1
  41.4 2.8 %collective-permute-start.8 = (bf16[128,128]{1,0:T(8,128)(2,1)S(1)}, bf16[128,128]{1,0:T(8,128)(2,1)S(1)}, u32[]{:S(2)}, u32[]{:S(2)}) collective-permute-start(bf16[128,128]{1,0:T(8,128)(2,1)S(1)} %get-tuple-element.15), channel_id=1, source_target_pairs={{0,24},{1,7},{2,26},{3,5},{4,28},{5,3},{6,30},{7,1},{8,16},{9,15},... | collective-permute-start | bytes 98312 | tf_op jit(solution)/shard_map/ppermute | solution.py:45
  44.2 1.7 %collective-permute-start.11 = (bf16[128,128]{1,0:T(8,128)(2,1)S(1)}, bf16[128,128]{1,0:T(8,128)(2,1)S(1)}, u32[]{:S(2)}, u32[]{:S(2)}) collective-permute-start(bf16[128,128]{1,0:T(8,128)(2,1)S(1)} %get-tuple-element.15), channel_id=1, source_target_pairs={{0,16},{1,5},{2,18},{3,7},{4,20},{5,1},{6,22},{7,3},{8,24},{9,13},... | collective-permute-start | bytes 98312 | tf_op jit(solution)/shard_map/ppermute | solution.py:45
  45.9 1.2 %collective-permute-done.8.panel_ref = bf16[128,128]{1,0:T(8,128)(2,1)S(1)} collective-permute-done((bf16[128,128]{1,0:T(8,128)(2,1)S(1)}, bf16[128,128]{1,0:T(8,128)(2,1)S(1)}, u32[]{:S(2)}, u32[]{:S(2)}) %collective-permute-start.8) | collective-permute-done | bytes 32800 | tf_op jit(solution)/shard_map/ppermute | solution.py:45
  47.1 0.6 pick_blocks.1
  47.7 0.1 collective-permute-start.9
  47.8 2.0 %collective-permute-done.10 = bf16[128,128]{1,0:T(8,128)(2,1)S(1)} collective-permute-done((bf16[128,128]{1,0:T(8,128)(2,1)S(1)}, bf16[128,128]{1,0:T(8,128)(2,1)S(1)}, u32[]{:S(2)}, u32[]{:S(2)}) %collective-permute-start.10) | collective-permute-done | bytes 32800 | tf_op jit(solution)/shard_map/ppermute | solution.py:45
  49.9 1.6 %collective-permute-start.14 = (bf16[512,128]{1,0:T(8,128)(2,1)S(1)}, bf16[512,128]{1,0:T(8,128)(2,1)S(1)}, u32[]{:S(2)}, u32[]{:S(2)}) collective-permute-start(bf16[512,128]{1,0:T(8,128)(2,1)S(1)} %constant_dynamic-update-slice_fusion.7.refs_0_), channel_id=1, source_target_pairs={{0,6},{1,25},{2,4},{3,27},{4,2},{5,29},{6,0},{7,31},{8,14},{9,17},... | collective-permute-start | bytes 393224 | tf_op jit(solution)/shard_map/ppermute | solution.py:45
  51.5 0.6 collective-permute-start.13
  52.1 1.3 %collective-permute-start.12 = (bf16[512,128]{1,0:T(8,128)(2,1)S(1)}, bf16[512,128]{1,0:T(8,128)(2,1)S(1)}, u32[]{:S(2)}, u32[]{:S(2)}) collective-permute-start(bf16[512,128]{1,0:T(8,128)(2,1)S(1)} %constant_dynamic-update-slice_fusion.7.refs_0_), channel_id=1, source_target_pairs={{0,2},{1,9},{2,0},{3,11},{4,6},{5,13},{6,4},{7,15},{8,10},{9,1},{1... | collective-permute-start | bytes 393224 | tf_op jit(solution)/shard_map/ppermute | solution.py:45
  53.4 2.1 %merge_tile.1.tile_ref = bf16[256,2048]{1,0:T(8,128)(2,1)S(1)} custom-call(s32[16]{0:T(128)S(1)} %xor_bitcast_fusion.sources_ref, s32[2]{0:T(128)S(1)} %iota_xor_fusion.targets_ref, bf16[32,128,128]{2,1,0:T(8,128)(2,1)} %after.1.dense_hbm, bf16[32,128,128]{2,1,0:T(8,128)(2,1)S(1)} %all-to-all-done.received_ref, ...), custom_call_target="tpu_custom_call" | custom-call | tf_op jit(solution)/shard_map/merge_tile/pallas_call | solution.py:292
  55.6 0.3 collective-permute-done.14.refs_3_
  55.9 1.3 %collective-permute-done.13.refs_2_ = bf16[512,128]{1,0:T(8,128)(2,1)S(1)} collective-permute-done((bf16[512,128]{1,0:T(8,128)(2,1)S(1)}, bf16[512,128]{1,0:T(8,128)(2,1)S(1)}, u32[]{:S(2)}, u32[]{:S(2)}) %collective-permute-start.13) | collective-permute-done | bytes 131104 | tf_op jit(solution)/shard_map/ppermute | solution.py:45
  57.2 0.2 collective-permute-done.12.refs_1_
  57.4 0.4 apply_tile.2
  57.8 0.1 collective-permute-start.15
  57.9 1.2 %collective-permute-done.15 = f32[128,128]{1,0:T(8,128)S(1)} collective-permute-done((f32[128,128]{1,0:T(8,128)S(1)}, f32[128,128]{1,0:T(8,128)S(1)}, u32[]{:S(2)}, u32[]{:S(2)}) %collective-permute-start.15) | collective-permute-done | bytes 65568 | tf_op jit(solution)/shard_map/ppermute | solution.py:36
  59.2 1.8 %collective-permute-start.18 = (bf16[128,128]{1,0:T(8,128)(2,1)S(1)}, bf16[128,128]{1,0:T(8,128)(2,1)S(1)}, u32[]{:S(2)}, u32[]{:S(2)}) collective-permute-start(bf16[128,128]{1,0:T(8,128)(2,1)S(1)} %get-tuple-element.21), channel_id=1, source_target_pairs={{0,24},{1,7},{2,26},{3,5},{4,28},{5,3},{6,30},{7,1},{8,16},{9,15},... | collective-permute-start | bytes 98312 | tf_op jit(solution)/shard_map/ppermute | solution.py:45
  61.0 0.1 collective-permute-start.17
  61.1 2.5 %collective-permute-start.16 = (bf16[128,128]{1,0:T(8,128)(2,1)S(1)}, bf16[128,128]{1,0:T(8,128)(2,1)S(1)}, u32[]{:S(2)}, u32[]{:S(2)}) collective-permute-start(bf16[128,128]{1,0:T(8,128)(2,1)S(1)} %get-tuple-element.21), channel_id=1, source_target_pairs={{0,8},{1,3},{2,10},{3,1},{4,12},{5,7},{6,14},{7,5},{8,0},{9,11},{1... | collective-permute-start | bytes 98312 | tf_op jit(solution)/shard_map/ppermute | solution.py:45
  63.6 1.3 %collective-permute-done.18 = bf16[128,128]{1,0:T(8,128)(2,1)S(1)} collective-permute-done((bf16[128,128]{1,0:T(8,128)(2,1)S(1)}, bf16[128,128]{1,0:T(8,128)(2,1)S(1)}, u32[]{:S(2)}, u32[]{:S(2)}) %collective-permute-start.18) | collective-permute-done | bytes 32800 | tf_op jit(solution)/shard_map/ppermute | solution.py:45
  64.9 1.2 %collective-permute-done.17 = bf16[128,128]{1,0:T(8,128)(2,1)S(1)} collective-permute-done((bf16[128,128]{1,0:T(8,128)(2,1)S(1)}, bf16[128,128]{1,0:T(8,128)(2,1)S(1)}, u32[]{:S(2)}, u32[]{:S(2)}) %collective-permute-start.17) | collective-permute-done | bytes 32800 | tf_op jit(solution)/shard_map/ppermute | solution.py:45
  66.2 2.1 %collective-permute-start.21 = (bf16[512,128]{1,0:T(8,128)(2,1)S(1)}, bf16[512,128]{1,0:T(8,128)(2,1)S(1)}, u32[]{:S(2)}, u32[]{:S(2)}) collective-permute-start(bf16[512,128]{1,0:T(8,128)(2,1)S(1)} %pad_maximum_fusion.1.refs_0_), channel_id=1, source_target_pairs={{0,6},{1,25},{2,4},{3,27},{4,2},{5,29},{6,0},{7,31},{8,14},{9,17},... | collective-permute-start | bytes 393224 | tf_op jit(solution)/shard_map/ppermute | solution.py:45
  68.2 0.1 collective-permute-start.20
  68.4 1.3 %collective-permute-start.19 = (bf16[512,128]{1,0:T(8,128)(2,1)S(1)}, bf16[512,128]{1,0:T(8,128)(2,1)S(1)}, u32[]{:S(2)}, u32[]{:S(2)}) collective-permute-start(bf16[512,128]{1,0:T(8,128)(2,1)S(1)} %pad_maximum_fusion.1.refs_0_), channel_id=1, source_target_pairs={{0,2},{1,9},{2,0},{3,11},{4,6},{5,13},{6,4},{7,15},{8,10},{9,1},{1... | collective-permute-start | bytes 393224 | tf_op jit(solution)/shard_map/ppermute | solution.py:45
  69.7 2.4 %collective-permute-done.21.refs_3_ = bf16[512,128]{1,0:T(8,128)(2,1)S(1)} collective-permute-done((bf16[512,128]{1,0:T(8,128)(2,1)S(1)}, bf16[512,128]{1,0:T(8,128)(2,1)S(1)}, u32[]{:S(2)}, u32[]{:S(2)}) %collective-permute-start.21) | collective-permute-done | bytes 131104 | tf_op jit(solution)/shard_map/ppermute | solution.py:45
  72.1 1.4 %collective-permute-done.20.refs_2_ = bf16[512,128]{1,0:T(8,128)(2,1)S(1)} collective-permute-done((bf16[512,128]{1,0:T(8,128)(2,1)S(1)}, bf16[512,128]{1,0:T(8,128)(2,1)S(1)}, u32[]{:S(2)}, u32[]{:S(2)}) %collective-permute-start.20) | collective-permute-done | bytes 131104 | tf_op jit(solution)/shard_map/ppermute | solution.py:45
  73.5 0.3 collective-permute-done.19.refs_1_
  73.8 0.4 apply_tile.3
  74.3 1.2 %collective-permute-done.22 = f32[128,128]{1,0:T(8,128)S(1)} collective-permute-done((f32[128,128]{1,0:T(8,128)S(1)}, f32[128,128]{1,0:T(8,128)S(1)}, u32[]{:S(2)}, u32[]{:S(2)}) %collective-permute-start.22) | collective-permute-done | bytes 65568 | tf_op jit(solution)/shard_map/ppermute | solution.py:36
  75.5 0.6 add.20
  (35 shorter events, 0.4 us)
Async XLA Ops:
  0.9 9.1 %collective-permute-start.2 = (bf16[128,128]{1,0:T(8,128)(2,1)S(1)}, bf16[128,128]{1,0:T(8,128)(2,1)S(1)}, u32[]{:S(2)}, u32[]{:S(2)}) collective-permute-start(bf16[128,128]{1,0:T(8,128)(2,1)S(1)} %get-tuple-element.24), channel_id=1, source_target_pairs={{0,24},{1,25},{2,26},{3,27},{4,28},{5,29},{6,30},{7,31},{8,16},{9,... | collective-permute-start | bytes 98312 | tf_op jit(solution)/shard_map/ppermute | solution.py:45
  6.0 4.8 %collective-permute-start.1 = (bf16[128,128]{1,0:T(8,128)(2,1)S(1)}, bf16[128,128]{1,0:T(8,128)(2,1)S(1)}, u32[]{:S(2)}, u32[]{:S(2)}) collective-permute-start(bf16[128,128]{1,0:T(8,128)(2,1)S(1)} %get-tuple-element.24), channel_id=1, source_target_pairs={{0,16},{1,17},{2,18},{3,19},{4,20},{5,21},{6,22},{7,23},{8,24},{9,... | collective-permute-start | bytes 98312 | tf_op jit(solution)/shard_map/ppermute | solution.py:45
  6.0 4.8 %collective-permute-start = (bf16[128,128]{1,0:T(8,128)(2,1)S(1)}, bf16[128,128]{1,0:T(8,128)(2,1)S(1)}, u32[]{:S(2)}, u32[]{:S(2)}) collective-permute-start(bf16[128,128]{1,0:T(8,128)(2,1)S(1)} %get-tuple-element.24), channel_id=1, source_target_pairs={{0,8},{1,9},{2,10},{3,11},{4,12},{5,13},{6,14},{7,15},{8,0},{9,1},... | collective-permute-start | bytes 98312 | tf_op jit(solution)/shard_map/ppermute | solution.py:45
  10.0 7.2 %copy-start.2 = (s32[16]{0:T(128)S(1)}, s32[16]{0:T(128)}, u32[]{:S(2)}) copy-start(s32[16]{0:T(128)} %constant.26.clone) | copy-start | bytes 196
  10.8 24.2 %copy-start = (f32[128,128]{1,0:T(8,128)S(1)}, f32[128,128]{1,0:T(8,128)}, u32[]{:S(2)}) copy-start(f32[128,128]{1,0:T(8,128)} %previous_ref.1) | copy-start | bytes 196612
  10.8 30.1 %all-to-all-start = ((bf16[32,128,128]{2,1,0:T(8,128)(2,1)}), bf16[32,128,128]{2,1,0:T(8,128)(2,1)S(1)}, u32[]{:S(2)}, u32[]{:S(2)}) async-start(bf16[32,128,128]{2,1,0:T(8,128)(2,1)} %after.1.dense_hbm), calls=%async_computation | async-start | bytes 2097152 | tf_op jit(solution)/shard_map/all_to_all | solution.py:370
  17.2 15.5 %collective-permute-start.5 = (bf16[512,128]{1,0:T(8,128)(2,1)S(1)}, bf16[512,128]{1,0:T(8,128)(2,1)S(1)}, u32[]{:S(2)}, u32[]{:S(2)}) collective-permute-start(bf16[512,128]{1,0:T(8,128)(2,1)S(1)} %pad_maximum_fusion), channel_id=1, source_target_pairs={{0,6},{1,7},{2,4},{3,5},{4,2},{5,3},{6,0},{7,1},{8,14},{9,15},{10,... | collective-permute-start | bytes 393224 | tf_op jit(solution)/shard_map/ppermute | solution.py:45
  20.1 12.6 %collective-permute-start.4 = (bf16[512,128]{1,0:T(8,128)(2,1)S(1)}, bf16[512,128]{1,0:T(8,128)(2,1)S(1)}, u32[]{:S(2)}, u32[]{:S(2)}) collective-permute-start(bf16[512,128]{1,0:T(8,128)(2,1)S(1)} %pad_maximum_fusion), channel_id=1, source_target_pairs={{0,4},{1,5},{2,6},{3,7},{4,0},{5,1},{6,2},{7,3},{8,12},{9,13},{10,... | collective-permute-start | bytes 393224 | tf_op jit(solution)/shard_map/ppermute | solution.py:45
  20.7 9.9 %collective-permute-start.3 = (bf16[512,128]{1,0:T(8,128)(2,1)S(1)}, bf16[512,128]{1,0:T(8,128)(2,1)S(1)}, u32[]{:S(2)}, u32[]{:S(2)}) collective-permute-start(bf16[512,128]{1,0:T(8,128)(2,1)S(1)} %pad_maximum_fusion), channel_id=1, source_target_pairs={{0,2},{1,3},{2,0},{3,1},{4,6},{5,7},{6,4},{7,5},{8,10},{9,11},{10,... | collective-permute-start | bytes 393224 | tf_op jit(solution)/shard_map/ppermute | solution.py:45
  33.6 5.1 %collective-permute-start.6 = (bf16[128,2048]{1,0:T(8,128)(2,1)S(1)}, bf16[128,2048]{1,0:T(8,128)(2,1)S(1)}, u32[]{:S(2)}, u32[]{:S(2)}) collective-permute-start(bf16[128,2048]{1,0:T(8,128)(2,1)S(1)} %turn_panel.1.refs_0_), channel_id=1, source_target_pairs={{0,1},{1,0},{2,3},{3,2},{4,5},{5,4},{6,7},{7,6},{8,9},{9,8},{10,11... | collective-permute-start | bytes 1572872 | tf_op jit(solution)/shard_map/ppermute | solution.py:36
  37.2 1.5 %collective-permute-start.7 = (f32[128,128]{1,0:T(8,128)S(1)}, f32[128,128]{1,0:T(8,128)S(1)}, u32[]{:S(2)}, u32[]{:S(2)}) collective-permute-start(f32[128,128]{1,0:T(8,128)S(1)} %get-tuple-element.14), channel_id=1, source_target_pairs={{0,1},{1,0},{2,3},{3,2},{4,5},{5,4},{6,7},{7,6},{8,9},{9,8},{10,11... | collective-permute-start | bytes 196616 | tf_op jit(solution)/shard_map/ppermute | solution.py:36
  39.4 14.0 %copy-start.1 = (s32[2,16]{1,0:T(2,128)S(1)}, s32[2,16]{1,0:T(2,128)}, u32[]{:S(2)}) copy-start(s32[2,16]{1,0:T(2,128)} %constant.27.clone) | copy-start | bytes 388
  41.4 5.8 %collective-permute-start.8 = (bf16[128,128]{1,0:T(8,128)(2,1)S(1)}, bf16[128,128]{1,0:T(8,128)(2,1)S(1)}, u32[]{:S(2)}, u32[]{:S(2)}) collective-permute-start(bf16[128,128]{1,0:T(8,128)(2,1)S(1)} %get-tuple-element.15), channel_id=1, source_target_pairs={{0,24},{1,7},{2,26},{3,5},{4,28},{5,3},{6,30},{7,1},{8,16},{9,15},... | collective-permute-start | bytes 98312 | tf_op jit(solution)/shard_map/ppermute | solution.py:45
  44.2 5.6 %collective-permute-start.11 = (bf16[128,128]{1,0:T(8,128)(2,1)S(1)}, bf16[128,128]{1,0:T(8,128)(2,1)S(1)}, u32[]{:S(2)}, u32[]{:S(2)}) collective-permute-start(bf16[128,128]{1,0:T(8,128)(2,1)S(1)} %get-tuple-element.15), channel_id=1, source_target_pairs={{0,16},{1,5},{2,18},{3,7},{4,20},{5,1},{6,22},{7,3},{8,24},{9,13},... | collective-permute-start | bytes 98312 | tf_op jit(solution)/shard_map/ppermute | solution.py:45
  45.9 3.9 %collective-permute-start.10 = (bf16[128,128]{1,0:T(8,128)(2,1)S(1)}, bf16[128,128]{1,0:T(8,128)(2,1)S(1)}, u32[]{:S(2)}, u32[]{:S(2)}) collective-permute-start(bf16[128,128]{1,0:T(8,128)(2,1)S(1)} %get-tuple-element.15), channel_id=1, source_target_pairs={{0,8},{1,3},{2,10},{3,1},{4,12},{5,7},{6,14},{7,5},{8,0},{9,11},{1... | collective-permute-start | bytes 98312 | tf_op jit(solution)/shard_map/ppermute | solution.py:45
  47.7 5.7 %collective-permute-start.9 = (bf16[16,128,128]{2,1,0:T(8,128)(2,1)S(1)}, bf16[16,128,128]{2,1,0:T(8,128)(2,1)S(1)}, u32[]{:S(2)}, u32[]{:S(2)}) collective-permute-start(bf16[16,128,128]{2,1,0:T(8,128)(2,1)S(1)} %pick_blocks.1), channel_id=1, source_target_pairs={{0,1},{1,0},{2,3},{3,2},{4,5},{5,4},{6,7},{7,6},{8,9},{9,8},{10,11... | collective-permute-start | bytes 1572872 | tf_op jit(solution)/shard_map/ppermute | solution.py:36
  49.9 6.0 %collective-permute-start.14 = (bf16[512,128]{1,0:T(8,128)(2,1)S(1)}, bf16[512,128]{1,0:T(8,128)(2,1)S(1)}, u32[]{:S(2)}, u32[]{:S(2)}) collective-permute-start(bf16[512,128]{1,0:T(8,128)(2,1)S(1)} %constant_dynamic-update-slice_fusion.7.refs_0_), channel_id=1, source_target_pairs={{0,6},{1,25},{2,4},{3,27},{4,2},{5,29},{6,0},{7,31},{8,14},{9,17},... | collective-permute-start | bytes 393224 | tf_op jit(solution)/shard_map/ppermute | solution.py:45
  51.5 5.7 %collective-permute-start.13 = (bf16[512,128]{1,0:T(8,128)(2,1)S(1)}, bf16[512,128]{1,0:T(8,128)(2,1)S(1)}, u32[]{:S(2)}, u32[]{:S(2)}) collective-permute-start(bf16[512,128]{1,0:T(8,128)(2,1)S(1)} %constant_dynamic-update-slice_fusion.7.refs_0_), channel_id=1, source_target_pairs={{0,4},{1,17},{2,6},{3,19},{4,0},{5,21},{6,2},{7,23},{8,12},{9,25},... | collective-permute-start | bytes 393224 | tf_op jit(solution)/shard_map/ppermute | solution.py:45
  52.1 5.3 %collective-permute-start.12 = (bf16[512,128]{1,0:T(8,128)(2,1)S(1)}, bf16[512,128]{1,0:T(8,128)(2,1)S(1)}, u32[]{:S(2)}, u32[]{:S(2)}) collective-permute-start(bf16[512,128]{1,0:T(8,128)(2,1)S(1)} %constant_dynamic-update-slice_fusion.7.refs_0_), channel_id=1, source_target_pairs={{0,2},{1,9},{2,0},{3,11},{4,6},{5,13},{6,4},{7,15},{8,10},{9,1},{1... | collective-permute-start | bytes 393224 | tf_op jit(solution)/shard_map/ppermute | solution.py:45
  57.8 1.3 %collective-permute-start.15 = (f32[128,128]{1,0:T(8,128)S(1)}, f32[128,128]{1,0:T(8,128)S(1)}, u32[]{:S(2)}, u32[]{:S(2)}) collective-permute-start(f32[128,128]{1,0:T(8,128)S(1)} %get-tuple-element.18), channel_id=1, source_target_pairs={{0,1},{1,0},{2,3},{3,2},{4,5},{5,4},{6,7},{7,6},{8,9},{9,8},{10,11... | collective-permute-start | bytes 196616 | tf_op jit(solution)/shard_map/ppermute | solution.py:36
  59.2 5.8 %collective-permute-start.18 = (bf16[128,128]{1,0:T(8,128)(2,1)S(1)}, bf16[128,128]{1,0:T(8,128)(2,1)S(1)}, u32[]{:S(2)}, u32[]{:S(2)}) collective-permute-start(bf16[128,128]{1,0:T(8,128)(2,1)S(1)} %get-tuple-element.21), channel_id=1, source_target_pairs={{0,24},{1,7},{2,26},{3,5},{4,28},{5,3},{6,30},{7,1},{8,16},{9,15},... | collective-permute-start | bytes 98312 | tf_op jit(solution)/shard_map/ppermute | solution.py:45
  61.0 5.2 %collective-permute-start.17 = (bf16[128,128]{1,0:T(8,128)(2,1)S(1)}, bf16[128,128]{1,0:T(8,128)(2,1)S(1)}, u32[]{:S(2)}, u32[]{:S(2)}) collective-permute-start(bf16[128,128]{1,0:T(8,128)(2,1)S(1)} %get-tuple-element.21), channel_id=1, source_target_pairs={{0,16},{1,5},{2,18},{3,7},{4,20},{5,1},{6,22},{7,3},{8,24},{9,13},... | collective-permute-start | bytes 98312 | tf_op jit(solution)/shard_map/ppermute | solution.py:45
  61.1 5.1 %collective-permute-start.16 = (bf16[128,128]{1,0:T(8,128)(2,1)S(1)}, bf16[128,128]{1,0:T(8,128)(2,1)S(1)}, u32[]{:S(2)}, u32[]{:S(2)}) collective-permute-start(bf16[128,128]{1,0:T(8,128)(2,1)S(1)} %get-tuple-element.21), channel_id=1, source_target_pairs={{0,8},{1,3},{2,10},{3,1},{4,12},{5,7},{6,14},{7,5},{8,0},{9,11},{1... | collective-permute-start | bytes 98312 | tf_op jit(solution)/shard_map/ppermute | solution.py:45
  66.2 6.0 %collective-permute-start.21 = (bf16[512,128]{1,0:T(8,128)(2,1)S(1)}, bf16[512,128]{1,0:T(8,128)(2,1)S(1)}, u32[]{:S(2)}, u32[]{:S(2)}) collective-permute-start(bf16[512,128]{1,0:T(8,128)(2,1)S(1)} %pad_maximum_fusion.1.refs_0_), channel_id=1, source_target_pairs={{0,6},{1,25},{2,4},{3,27},{4,2},{5,29},{6,0},{7,31},{8,14},{9,17},... | collective-permute-start | bytes 393224 | tf_op jit(solution)/shard_map/ppermute | solution.py:45
  68.2 5.2 %collective-permute-start.20 = (bf16[512,128]{1,0:T(8,128)(2,1)S(1)}, bf16[512,128]{1,0:T(8,128)(2,1)S(1)}, u32[]{:S(2)}, u32[]{:S(2)}) collective-permute-start(bf16[512,128]{1,0:T(8,128)(2,1)S(1)} %pad_maximum_fusion.1.refs_0_), channel_id=1, source_target_pairs={{0,4},{1,17},{2,6},{3,19},{4,0},{5,21},{6,2},{7,23},{8,12},{9,25},... | collective-permute-start | bytes 393224 | tf_op jit(solution)/shard_map/ppermute | solution.py:45
  68.4 5.4 %collective-permute-start.19 = (bf16[512,128]{1,0:T(8,128)(2,1)S(1)}, bf16[512,128]{1,0:T(8,128)(2,1)S(1)}, u32[]{:S(2)}, u32[]{:S(2)}) collective-permute-start(bf16[512,128]{1,0:T(8,128)(2,1)S(1)} %pad_maximum_fusion.1.refs_0_), channel_id=1, source_target_pairs={{0,2},{1,9},{2,0},{3,11},{4,6},{5,13},{6,4},{7,15},{8,10},{9,1},{1... | collective-permute-start | bytes 393224 | tf_op jit(solution)/shard_map/ppermute | solution.py:45
  74.2 1.3 %collective-permute-start.22 = (f32[128,128]{1,0:T(8,128)S(1)}, f32[128,128]{1,0:T(8,128)S(1)}, u32[]{:S(2)}, u32[]{:S(2)}) collective-permute-start(f32[128,128]{1,0:T(8,128)S(1)} %get-tuple-element.20), channel_id=1, source_target_pairs={{0,1},{1,0},{2,3},{3,2},{4,5},{5,4},{6,7},{7,6},{8,9},{9,8},{10,11... | collective-permute-start | bytes 196616 | tf_op jit(solution)/shard_map/ppermute | solution.py:36

commit v14 on v12

--- a/solution.py
+++ b/solution.py
@@ -224,47 +224,34 @@
     )(targets, *turned_panels)
 
 
-def backward_first(turned_panels, received, base, halfwidth):
+def backward_first(targets, turned_panels, received, base, halfwidth):
     cells, orb, _ = received.shape
+    grid_cols = targets.shape[0]
+    grid_rows = cells // grid_cols
     vectors = base.shape[1]
 
-    def kernel(halfwidth_ref, turned_ref, received_ref, base_ref, out_ref, panel_ref):
+    def kernel(targets_ref, halfwidth_ref, turned_ref, received_ref, base_ref, out_ref, panel_ref, *picked):
         blocks = received_ref[...].reshape(cells * orb, orb)
         total = jnp.dot(turned_ref[...], blocks, preferred_element_type=jnp.float32)
+        for d, picked_ref in enumerate(picked, start=1):
+            for c in range(grid_rows):
+                picked_ref[c] = received_ref[c * grid_cols + targets_ref[d]]
         out = base_ref[...] + total.T / jnp.full((1, vectors), halfwidth_ref[0])
         out_ref[...] = out
         panel_ref[...] = out.astype(jnp.bfloat16)
 
     return pl.pallas_call(
         kernel,
-        in_specs=[SMEM] + [VMEM] * 3,
-        out_specs=[VMEM] * 2,
+        in_specs=[SMEM] * 2 + [VMEM] * 3,
+        out_specs=[VMEM] * (1 + grid_cols),
         out_shape=[
             jax.ShapeDtypeStruct((orb, vectors), jnp.float32),
             jax.ShapeDtypeStruct((orb, vectors), jnp.bfloat16),
-        ],
-        compiler_params=pltpu.CompilerParams(vmem_limit_bytes=received.size * 4 + 2 * SPARE),
+        ]
+        + [jax.ShapeDtypeStruct((grid_rows, orb, orb), jnp.bfloat16)] * (grid_cols - 1),
+        compiler_params=pltpu.CompilerParams(vmem_limit_bytes=received.size * 6 + 2 * SPARE),
         name="backward_first",
-    )(halfwidth, turned_panels, received, base)
-
-
-def pick_blocks(targets, received, panel, grid_rows):
-    _, orb, _ = received.shape
-    grid_cols = targets.shape[0]
-
-    def kernel(targets_ref, received_ref, panel_ref, *outs):
-        for d, out in enumerate(outs, start=1):
-            for c in range(grid_rows):
-                out[c] = received_ref[c * grid_cols + targets_ref[d]]
-
-    return pl.pallas_call(
-        kernel,
-        in_specs=[SMEM, VMEM, VMEM],
-        out_specs=[VMEM] * (grid_cols - 1),
-        out_shape=[jax.ShapeDtypeStruct((grid_rows, orb, orb), jnp.bfloat16)] * (grid_cols - 1),
-        compiler_params=pltpu.CompilerParams(vmem_limit_bytes=received.size * 4 + SPARE),
-        name="pick_blocks",
-    )(targets, received, panel)
+    )(targets, halfwidth, turned_panels, received, base)
 
 
 def merge_tile(sources, targets, dense, received, stacks):
@@ -377,11 +364,10 @@
         base = base + swap(other, "col", grid_cols, d)
 
     previous = initial
-    current, panel = backward_first(lay_panels(targets, turned_panels, grid_rows), received, base, halfwidth)
+    current, panel, *stacks = backward_first(
+        targets, lay_panels(targets, turned_panels, grid_rows), received, base, halfwidth
+    )
     pieces = gather([panel], turned, last=1)
-    stacks = []
-    if grid_cols > 1:
-        stacks = pick_blocks(targets, received, pieces[-1], grid_rows)
     stacks = [swap(stack, "col", grid_cols, d) for d, stack in enumerate(stacks, start=1)]
     tile = merge_tile(sources, targets, dense, received, stacks)
     for degree_step in range(1, DEGREE):

time: 76.6 us -> 76.7 us (level)
  transfers between devices with their start and end apart: 24 -> 24, of which waited for: 17 -> 15; matrix products, arithmetic and copies ran while one was open for 0% -> 0% of each run, Pallas kernels for 12% -> 11%
where the time goes in v14:
time: 76.7 us; the launch traced here: 76.3 us
  starting transfers between devices  32.6 us (43%)
  waiting for transfers between devices  29.4 us (38%)
  Pallas kernels  10.4 us (14%)
  between operations  2.2 us (3%)
  other arithmetic  1.55 us (2%)
    ppermute x18, starting transfers between devices, swap_rows(): return lax.ppermute(x, ('row', 'col'), pairs)  25.4 us
    ppermute x18, waiting for transfers between devices, swap_rows(): return lax.ppermute(x, ('row', 'col'), pairs)  24.6 us
    all_to_all x1, starting transfers between devices, body(): received = lax.all_to_all(dense, 'row', 0, 0, tiled=True)  6.4 us
    ppermute x5, waiting for transfers between devices, swap(): lax.ppermute(x, axis, [(source, source ^ offset) for source in range(size)])  3.39 us
    pallas_call x1, Pallas kernels, build_tile(): pl.pallas_call(kernel, in_specs=[HBM, HBM, SMEM, HBM], out_specs=HBM, scr...  2.69 us
    pallas_call x1, Pallas kernels, forward_first(): pl.pallas_call(kernel, in_specs=[SMEM] * 4 + [HBM] + [VMEM] * 2, out_spec...  2.21 us
    pallas_call x1, Pallas kernels, merge_tile(): pl.pallas_call(kernel, in_specs=[SMEM] * 2 + [HBM] + [VMEM] * grid_cols,...  2.14 us
  transfers between devices with their start and end apart: 24, of which 15 were waited for; matrix products, arithmetic and copies ran while one was open for 0% of the time, Pallas kernels for 11%

profile of v14, /device:TPU:0, one launch (start us, length us, event | category | flops | bytes accessed | tf_op | source)
XLA Modules:
  0.0 76.3 jit_solution(12725679002851307889)
XLA Ops:
  0.0 0.8 %constant_dynamic-update-slice_fusion.6 = (bf16[2048,128]{1,0:T(8,128)(2,1)S(1)}, bf16[128,128]{1,0:T(8,128)(2,1)S(1)}) fusion(f32[128,128]{1,0:T(8,128)} %previous_ref.1), kind=kLoop, calls=%fused_computation.8 | loop fusion | flops 16383 | bytes 131072
  0.9 5.1 %collective-permute-start.2 = (bf16[128,128]{1,0:T(8,128)(2,1)S(1)}, bf16[128,128]{1,0:T(8,128)(2,1)S(1)}, u32[]{:S(2)}, u32[]{:S(2)}) collective-permute-start(bf16[128,128]{1,0:T(8,128)(2,1)S(1)} %get-tuple-element.26), channel_id=1, source_target_pairs={{0,24},{1,25},{2,26},{3,27},{4,28},{5,29},{6,30},{7,31},{8,16},{9,... | collective-permute-start | bytes 98312 | tf_op jit(solution)/shard_map/ppermute | solution.py:45
  6.0 0.6 collective-permute-start
  7.3 2.7 %build_tile.1.refs_0_ = bf16[32,128,128]{2,1,0:T(8,128)(2,1)} custom-call(s32[1,64]{1,0:T(1,128)} %bitcast.6, s32[1,64]{1,0:T(1,128)} %bitcast.7, s32[1,1]{1,0:T(1,128)S(6)} %copy.21.count_ref, bf16[64,128,128]{2,1,0:T(8,128)(2,1)} %bitcast.5), custom_call_target="tpu_custom_call" | custom-call | tf_op jit(solution)/shard_map/build_tile/pallas_call | solution.py:90
  10.0 0.0 copy-start.2
  10.0 0.8 %collective-permute-done.1.refs_2_ = bf16[128,128]{1,0:T(8,128)(2,1)S(1)} collective-permute-done((bf16[128,128]{1,0:T(8,128)(2,1)S(1)}, bf16[128,128]{1,0:T(8,128)(2,1)S(1)}, u32[]{:S(2)}, u32[]{:S(2)}) %collective-permute-start.1) | collective-permute-done | bytes 32800 | tf_op jit(solution)/shard_map/ppermute | solution.py:45
  10.8 6.4 %all-to-all-start = ((bf16[32,128,128]{2,1,0:T(8,128)(2,1)}), bf16[32,128,128]{2,1,0:T(8,128)(2,1)S(1)}, u32[]{:S(2)}, u32[]{:S(2)}) async-start(bf16[32,128,128]{2,1,0:T(8,128)(2,1)} %after.1.dense_hbm), calls=%async_computation | async-start | bytes 2097152 | tf_op jit(solution)/shard_map/all_to_all | solution.py:354
  17.2 2.9 %collective-permute-start.5 = (bf16[512,128]{1,0:T(8,128)(2,1)S(1)}, bf16[512,128]{1,0:T(8,128)(2,1)S(1)}, u32[]{:S(2)}, u32[]{:S(2)}) collective-permute-start(bf16[512,128]{1,0:T(8,128)(2,1)S(1)} %pad_maximum_fusion), channel_id=1, source_target_pairs={{0,6},{1,7},{2,4},{3,5},{4,2},{5,3},{6,0},{7,1},{8,14},{9,15},{10,... | collective-permute-start | bytes 393224 | tf_op jit(solution)/shard_map/ppermute | solution.py:45
  20.1 0.6 collective-permute-start.4
  20.7 0.1 collective-permute-start.3
  20.8 9.7 %collective-permute-done.3 = bf16[512,128]{1,0:T(8,128)(2,1)S(1)} collective-permute-done((bf16[512,128]{1,0:T(8,128)(2,1)S(1)}, bf16[512,128]{1,0:T(8,128)(2,1)S(1)}, u32[]{:S(2)}, u32[]{:S(2)}) %collective-permute-start.3) | collective-permute-done | bytes 131104 | tf_op jit(solution)/shard_map/ppermute | solution.py:45
  30.6 2.1 %collective-permute-done.4 = bf16[512,128]{1,0:T(8,128)(2,1)S(1)} collective-permute-done((bf16[512,128]{1,0:T(8,128)(2,1)S(1)}, bf16[512,128]{1,0:T(8,128)(2,1)S(1)}, u32[]{:S(2)}, u32[]{:S(2)}) %collective-permute-start.4) | collective-permute-done | bytes 131104 | tf_op jit(solution)/shard_map/ppermute | solution.py:45
  32.8 0.7 turn_panel.1.refs_0_
  33.5 0.1 collective-permute-start.6
  34.9 2.2 %forward_first.1 = (f32[128,128]{1,0:T(8,128)S(1)}, f32[128,128]{1,0:T(8,128)S(1)}) custom-call(s32[16]{0:T(128)S(1)} %broadcast_xor_fusion.sources_ref, s32[2]{0:T(128)S(1)} %iota_xor_fusion.targets_ref, f32[1]{0:T(128)S(6)} %copy.22.center_ref, f32[1]{0:T(128)S(6)} %copy.23.halfwidth_ref, bf16[32,128,128]{2,1,0:T(8,128)(2,1)} %after.1.dense_hbm, ...), custom_call_target="tpu_custom_call" | custom-call | tf_op jit(solution)/shard_map/forward_first/pallas_call | solution.py:168
  37.2 0.6 collective-permute-start.7
  37.7 0.9 %collective-permute-done.7 = f32[128,128]{1,0:T(8,128)S(1)} collective-permute-done((f32[128,128]{1,0:T(8,128)S(1)}, f32[128,128]{1,0:T(8,128)S(1)}, u32[]{:S(2)}, u32[]{:S(2)}) %collective-permute-start.7) | collective-permute-done | bytes 65568 | tf_op jit(solution)/shard_map/ppermute | solution.py:36
  38.7 0.8 %lay_panels.1.turned_ref = bf16[128,4096]{1,0:T(8,128)(2,1)S(1)} custom-call(s32[2]{0:T(128)S(1)} %iota_xor_fusion.targets_ref, bf16[128,2048]{1,0:T(8,128)(2,1)S(1)} %turn_panel.1.refs_0_, bf16[128,2048]{1,0:T(8,128)(2,1)S(1)} %collective-permute-done.6.refs_1_), custom_call_target="tpu_custom_call" | custom-call | tf_op jit(solution)/shard_map/lay_panels/pallas_call | solution.py:217
  39.4 1.4 %all-to-all-done.received_ref = bf16[32,128,128]{2,1,0:T(8,128)(2,1)S(1)} async-done(((bf16[32,128,128]{2,1,0:T(8,128)(2,1)}), bf16[32,128,128]{2,1,0:T(8,128)(2,1)S(1)}, u32[]{:S(2)}, u32[]{:S(2)}) %all-to-all-start) | async-done | bytes 1048608 | tf_op jit(solution)/shard_map/all_to_all | solution.py:354
  40.9 1.0 %backward_first.1 = (f32[128,128]{1,0:T(8,128)S(1)}, bf16[128,128]{1,0:T(8,128)(2,1)S(1)}, bf16[16,128,128]{2,1,0:T(8,128)(2,1)S(1)}) custom-call(s32[2]{0:T(128)S(1)} %iota_xor_fusion.targets_ref, f32[1]{0:T(128)S(6)} %copy.23.halfwidth_ref, bf16[128,4096]{1,0:T(8,128)(2,1)S(1)} %lay_panels.1.turned_ref, ...), custom_call_target="tpu_custom_call" | custom-call | tf_op jit(solution)/shard_map/backward_first/pallas_call | solution.py:243
  41.9 2.8 %collective-permute-start.11 = (bf16[128,128]{1,0:T(8,128)(2,1)S(1)}, bf16[128,128]{1,0:T(8,128)(2,1)S(1)}, u32[]{:S(2)}, u32[]{:S(2)}) collective-permute-start(bf16[128,128]{1,0:T(8,128)(2,1)S(1)} %get-tuple-element.18), channel_id=1, source_target_pairs={{0,24},{1,7},{2,26},{3,5},{4,28},{5,3},{6,30},{7,1},{8,16},{9,15},... | collective-permute-start | bytes 98312 | tf_op jit(solution)/shard_map/ppermute | solution.py:45
  44.7 1.7 %collective-permute-start.10 = (bf16[128,128]{1,0:T(8,128)(2,1)S(1)}, bf16[128,128]{1,0:T(8,128)(2,1)S(1)}, u32[]{:S(2)}, u32[]{:S(2)}) collective-permute-start(bf16[128,128]{1,0:T(8,128)(2,1)S(1)} %get-tuple-element.18), channel_id=1, source_target_pairs={{0,16},{1,5},{2,18},{3,7},{4,20},{5,1},{6,22},{7,3},{8,24},{9,13},... | collective-permute-start | bytes 98312 | tf_op jit(solution)/shard_map/ppermute | solution.py:45
  46.4 3.9 %collective-permute-done.9 = bf16[128,128]{1,0:T(8,128)(2,1)S(1)} collective-permute-done((bf16[128,128]{1,0:T(8,128)(2,1)S(1)}, bf16[128,128]{1,0:T(8,128)(2,1)S(1)}, u32[]{:S(2)}, u32[]{:S(2)}) %collective-permute-start.9) | collective-permute-done | bytes 32800 | tf_op jit(solution)/shard_map/ppermute | solution.py:45
  50.4 1.6 %collective-permute-start.14 = (bf16[512,128]{1,0:T(8,128)(2,1)S(1)}, bf16[512,128]{1,0:T(8,128)(2,1)S(1)}, u32[]{:S(2)}, u32[]{:S(2)}) collective-permute-start(bf16[512,128]{1,0:T(8,128)(2,1)S(1)} %constant_dynamic-update-slice_fusion.7.refs_0_), channel_id=1, source_target_pairs={{0,6},{1,25},{2,4},{3,27},{4,2},{5,29},{6,0},{7,31},{8,14},{9,17},... | collective-permute-start | bytes 393224 | tf_op jit(solution)/shard_map/ppermute | solution.py:45
  52.0 0.6 collective-permute-start.13
  52.6 1.3 %collective-permute-start.12 = (bf16[512,128]{1,0:T(8,128)(2,1)S(1)}, bf16[512,128]{1,0:T(8,128)(2,1)S(1)}, u32[]{:S(2)}, u32[]{:S(2)}) collective-permute-start(bf16[512,128]{1,0:T(8,128)(2,1)S(1)} %constant_dynamic-update-slice_fusion.7.refs_0_), channel_id=1, source_target_pairs={{0,2},{1,9},{2,0},{3,11},{4,6},{5,13},{6,4},{7,15},{8,10},{9,1},{1... | collective-permute-start | bytes 393224 | tf_op jit(solution)/shard_map/ppermute | solution.py:45
  54.0 2.1 %merge_tile.1.tile_ref = bf16[256,2048]{1,0:T(8,128)(2,1)S(1)} custom-call(s32[16]{0:T(128)S(1)} %xor_bitcast_fusion.sources_ref, s32[2]{0:T(128)S(1)} %iota_xor_fusion.targets_ref, bf16[32,128,128]{2,1,0:T(8,128)(2,1)} %after.1.dense_hbm, bf16[32,128,128]{2,1,0:T(8,128)(2,1)S(1)} %all-to-all-done.received_ref, ...), custom_call_target="tpu_custom_call" | custom-call | tf_op jit(solution)/shard_map/merge_tile/pallas_call | solution.py:276
  56.1 0.3 collective-permute-done.14.refs_3_
  56.4 1.3 %collective-permute-done.13.refs_2_ = bf16[512,128]{1,0:T(8,128)(2,1)S(1)} collective-permute-done((bf16[512,128]{1,0:T(8,128)(2,1)S(1)}, bf16[512,128]{1,0:T(8,128)(2,1)S(1)}, u32[]{:S(2)}, u32[]{:S(2)}) %collective-permute-start.13) | collective-permute-done | bytes 131104 | tf_op jit(solution)/shard_map/ppermute | solution.py:45
  57.7 0.2 collective-permute-done.12.refs_1_
  57.9 0.4 apply_tile.2
  58.4 0.1 collective-permute-start.15
  58.4 1.2 %collective-permute-done.15 = f32[128,128]{1,0:T(8,128)S(1)} collective-permute-done((f32[128,128]{1,0:T(8,128)S(1)}, f32[128,128]{1,0:T(8,128)S(1)}, u32[]{:S(2)}, u32[]{:S(2)}) %collective-permute-start.15) | collective-permute-done | bytes 65568 | tf_op jit(solution)/shard_map/ppermute | solution.py:36
  59.7 1.6 %collective-permute-start.18 = (bf16[128,128]{1,0:T(8,128)(2,1)S(1)}, bf16[128,128]{1,0:T(8,128)(2,1)S(1)}, u32[]{:S(2)}, u32[]{:S(2)}) collective-permute-start(bf16[128,128]{1,0:T(8,128)(2,1)S(1)} %get-tuple-element.23), channel_id=1, source_target_pairs={{0,24},{1,7},{2,26},{3,5},{4,28},{5,3},{6,30},{7,1},{8,16},{9,15},... | collective-permute-start | bytes 98312 | tf_op jit(solution)/shard_map/ppermute | solution.py:45
  61.4 0.3 collective-permute-start.17
  61.6 2.5 %collective-permute-start.16 = (bf16[128,128]{1,0:T(8,128)(2,1)S(1)}, bf16[128,128]{1,0:T(8,128)(2,1)S(1)}, u32[]{:S(2)}, u32[]{:S(2)}) collective-permute-start(bf16[128,128]{1,0:T(8,128)(2,1)S(1)} %get-tuple-element.23), channel_id=1, source_target_pairs={{0,8},{1,3},{2,10},{3,1},{4,12},{5,7},{6,14},{7,5},{8,0},{9,11},{1... | collective-permute-start | bytes 98312 | tf_op jit(solution)/shard_map/ppermute | solution.py:45
  64.2 1.3 %collective-permute-done.18 = bf16[128,128]{1,0:T(8,128)(2,1)S(1)} collective-permute-done((bf16[128,128]{1,0:T(8,128)(2,1)S(1)}, bf16[128,128]{1,0:T(8,128)(2,1)S(1)}, u32[]{:S(2)}, u32[]{:S(2)}) %collective-permute-start.18) | collective-permute-done | bytes 32800 | tf_op jit(solution)/shard_map/ppermute | solution.py:45
  65.5 1.0 %collective-permute-done.17 = bf16[128,128]{1,0:T(8,128)(2,1)S(1)} collective-permute-done((bf16[128,128]{1,0:T(8,128)(2,1)S(1)}, bf16[128,128]{1,0:T(8,128)(2,1)S(1)}, u32[]{:S(2)}, u32[]{:S(2)}) %collective-permute-start.17) | collective-permute-done | bytes 32800 | tf_op jit(solution)/shard_map/ppermute | solution.py:45
  66.5 1.8 %collective-permute-start.21 = (bf16[512,128]{1,0:T(8,128)(2,1)S(1)}, bf16[512,128]{1,0:T(8,128)(2,1)S(1)}, u32[]{:S(2)}, u32[]{:S(2)}) collective-permute-start(bf16[512,128]{1,0:T(8,128)(2,1)S(1)} %pad_maximum_fusion.1.refs_0_), channel_id=1, source_target_pairs={{0,6},{1,25},{2,4},{3,27},{4,2},{5,29},{6,0},{7,31},{8,14},{9,17},... | collective-permute-start | bytes 393224 | tf_op jit(solution)/shard_map/ppermute | solution.py:45
  68.4 0.6 collective-permute-start.20
  68.9 1.2 %collective-permute-start.19 = (bf16[512,128]{1,0:T(8,128)(2,1)S(1)}, bf16[512,128]{1,0:T(8,128)(2,1)S(1)}, u32[]{:S(2)}, u32[]{:S(2)}) collective-permute-start(bf16[512,128]{1,0:T(8,128)(2,1)S(1)} %pad_maximum_fusion.1.refs_0_), channel_id=1, source_target_pairs={{0,2},{1,9},{2,0},{3,11},{4,6},{5,13},{6,4},{7,15},{8,10},{9,1},{1... | collective-permute-start | bytes 393224 | tf_op jit(solution)/shard_map/ppermute | solution.py:45
  70.1 2.4 %collective-permute-done.21.refs_3_ = bf16[512,128]{1,0:T(8,128)(2,1)S(1)} collective-permute-done((bf16[512,128]{1,0:T(8,128)(2,1)S(1)}, bf16[512,128]{1,0:T(8,128)(2,1)S(1)}, u32[]{:S(2)}, u32[]{:S(2)}) %collective-permute-start.21) | collective-permute-done | bytes 131104 | tf_op jit(solution)/shard_map/ppermute | solution.py:45
  72.5 1.3 %collective-permute-done.20.refs_2_ = bf16[512,128]{1,0:T(8,128)(2,1)S(1)} collective-permute-done((bf16[512,128]{1,0:T(8,128)(2,1)S(1)}, bf16[512,128]{1,0:T(8,128)(2,1)S(1)}, u32[]{:S(2)}, u32[]{:S(2)}) %collective-permute-start.20) | collective-permute-done | bytes 131104 | tf_op jit(solution)/shard_map/ppermute | solution.py:45
  73.9 0.0 collective-permute-done.19.refs_1_
  73.9 0.4 apply_tile.3
  74.3 0.1 collective-permute-start.22
  74.4 1.2 %collective-permute-done.22 = f32[128,128]{1,0:T(8,128)S(1)} collective-permute-done((f32[128,128]{1,0:T(8,128)S(1)}, f32[128,128]{1,0:T(8,128)S(1)}, u32[]{:S(2)}, u32[]{:S(2)}) %collective-permute-start.22) | collective-permute-done | bytes 65568 | tf_op jit(solution)/shard_map/ppermute | solution.py:36
  75.6 0.6 add.20
  (34 shorter events, 0.2 us)
Async XLA Ops:
  0.9 9.1 %collective-permute-start.2 = (bf16[128,128]{1,0:T(8,128)(2,1)S(1)}, bf16[128,128]{1,0:T(8,128)(2,1)S(1)}, u32[]{:S(2)}, u32[]{:S(2)}) collective-permute-start(bf16[128,128]{1,0:T(8,128)(2,1)S(1)} %get-tuple-element.26), channel_id=1, source_target_pairs={{0,24},{1,25},{2,26},{3,27},{4,28},{5,29},{6,30},{7,31},{8,16},{9,... | collective-permute-start | bytes 98312 | tf_op jit(solution)/shard_map/ppermute | solution.py:45
  6.0 4.8 %collective-permute-start.1 = (bf16[128,128]{1,0:T(8,128)(2,1)S(1)}, bf16[128,128]{1,0:T(8,128)(2,1)S(1)}, u32[]{:S(2)}, u32[]{:S(2)}) collective-permute-start(bf16[128,128]{1,0:T(8,128)(2,1)S(1)} %get-tuple-element.26), channel_id=1, source_target_pairs={{0,16},{1,17},{2,18},{3,19},{4,20},{5,21},{6,22},{7,23},{8,24},{9,... | collective-permute-start | bytes 98312 | tf_op jit(solution)/shard_map/ppermute | solution.py:45
  6.0 4.8 %collective-permute-start = (bf16[128,128]{1,0:T(8,128)(2,1)S(1)}, bf16[128,128]{1,0:T(8,128)(2,1)S(1)}, u32[]{:S(2)}, u32[]{:S(2)}) collective-permute-start(bf16[128,128]{1,0:T(8,128)(2,1)S(1)} %get-tuple-element.26), channel_id=1, source_target_pairs={{0,8},{1,9},{2,10},{3,11},{4,12},{5,13},{6,14},{7,15},{8,0},{9,1},... | collective-permute-start | bytes 98312 | tf_op jit(solution)/shard_map/ppermute | solution.py:45
  10.0 7.2 %copy-start.2 = (s32[16]{0:T(128)S(1)}, s32[16]{0:T(128)}, u32[]{:S(2)}) copy-start(s32[16]{0:T(128)} %constant.26.clone) | copy-start | bytes 196
  10.8 24.2 %copy-start = (f32[128,128]{1,0:T(8,128)S(1)}, f32[128,128]{1,0:T(8,128)}, u32[]{:S(2)}) copy-start(f32[128,128]{1,0:T(8,128)} %previous_ref.1) | copy-start | bytes 196612
  10.8 30.1 %all-to-all-start = ((bf16[32,128,128]{2,1,0:T(8,128)(2,1)}), bf16[32,128,128]{2,1,0:T(8,128)(2,1)S(1)}, u32[]{:S(2)}, u32[]{:S(2)}) async-start(bf16[32,128,128]{2,1,0:T(8,128)(2,1)} %after.1.dense_hbm), calls=%async_computation | async-start | bytes 2097152 | tf_op jit(solution)/shard_map/all_to_all | solution.py:354
  17.2 15.5 %collective-permute-start.5 = (bf16[512,128]{1,0:T(8,128)(2,1)S(1)}, bf16[512,128]{1,0:T(8,128)(2,1)S(1)}, u32[]{:S(2)}, u32[]{:S(2)}) collective-permute-start(bf16[512,128]{1,0:T(8,128)(2,1)S(1)} %pad_maximum_fusion), channel_id=1, source_target_pairs={{0,6},{1,7},{2,4},{3,5},{4,2},{5,3},{6,0},{7,1},{8,14},{9,15},{10,... | collective-permute-start | bytes 393224 | tf_op jit(solution)/shard_map/ppermute | solution.py:45
  20.1 12.6 %collective-permute-start.4 = (bf16[512,128]{1,0:T(8,128)(2,1)S(1)}, bf16[512,128]{1,0:T(8,128)(2,1)S(1)}, u32[]{:S(2)}, u32[]{:S(2)}) collective-permute-start(bf16[512,128]{1,0:T(8,128)(2,1)S(1)} %pad_maximum_fusion), channel_id=1, source_target_pairs={{0,4},{1,5},{2,6},{3,7},{4,0},{5,1},{6,2},{7,3},{8,12},{9,13},{10,... | collective-permute-start | bytes 393224 | tf_op jit(solution)/shard_map/ppermute | solution.py:45
  20.7 9.9 %collective-permute-start.3 = (bf16[512,128]{1,0:T(8,128)(2,1)S(1)}, bf16[512,128]{1,0:T(8,128)(2,1)S(1)}, u32[]{:S(2)}, u32[]{:S(2)}) collective-permute-start(bf16[512,128]{1,0:T(8,128)(2,1)S(1)} %pad_maximum_fusion), channel_id=1, source_target_pairs={{0,2},{1,3},{2,0},{3,1},{4,6},{5,7},{6,4},{7,5},{8,10},{9,11},{10,... | collective-permute-start | bytes 393224 | tf_op jit(solution)/shard_map/ppermute | solution.py:45
  33.5 5.1 %collective-permute-start.6 = (bf16[128,2048]{1,0:T(8,128)(2,1)S(1)}, bf16[128,2048]{1,0:T(8,128)(2,1)S(1)}, u32[]{:S(2)}, u32[]{:S(2)}) collective-permute-start(bf16[128,2048]{1,0:T(8,128)(2,1)S(1)} %turn_panel.1.refs_0_), channel_id=1, source_target_pairs={{0,1},{1,0},{2,3},{3,2},{4,5},{5,4},{6,7},{7,6},{8,9},{9,8},{10,11... | collective-permute-start | bytes 1572872 | tf_op jit(solution)/shard_map/ppermute | solution.py:36
  37.2 1.5 %collective-permute-start.7 = (f32[128,128]{1,0:T(8,128)S(1)}, f32[128,128]{1,0:T(8,128)S(1)}, u32[]{:S(2)}, u32[]{:S(2)}) collective-permute-start(f32[128,128]{1,0:T(8,128)S(1)} %get-tuple-element.15), channel_id=1, source_target_pairs={{0,1},{1,0},{2,3},{3,2},{4,5},{5,4},{6,7},{7,6},{8,9},{9,8},{10,11... | collective-permute-start | bytes 196616 | tf_op jit(solution)/shard_map/ppermute | solution.py:36
  38.6 15.3 %copy-start.1 = (s32[2,16]{1,0:T(2,128)S(1)}, s32[2,16]{1,0:T(2,128)}, u32[]{:S(2)}) copy-start(s32[2,16]{1,0:T(2,128)} %constant.27.clone) | copy-start | bytes 388
  41.9 8.5 %collective-permute-start.11 = (bf16[128,128]{1,0:T(8,128)(2,1)S(1)}, bf16[128,128]{1,0:T(8,128)(2,1)S(1)}, u32[]{:S(2)}, u32[]{:S(2)}) collective-permute-start(bf16[128,128]{1,0:T(8,128)(2,1)S(1)} %get-tuple-element.18), channel_id=1, source_target_pairs={{0,24},{1,7},{2,26},{3,5},{4,28},{5,3},{6,30},{7,1},{8,16},{9,15},... | collective-permute-start | bytes 98312 | tf_op jit(solution)/shard_map/ppermute | solution.py:45
  44.7 5.6 %collective-permute-start.10 = (bf16[128,128]{1,0:T(8,128)(2,1)S(1)}, bf16[128,128]{1,0:T(8,128)(2,1)S(1)}, u32[]{:S(2)}, u32[]{:S(2)}) collective-permute-start(bf16[128,128]{1,0:T(8,128)(2,1)S(1)} %get-tuple-element.18), channel_id=1, source_target_pairs={{0,16},{1,5},{2,18},{3,7},{4,20},{5,1},{6,22},{7,3},{8,24},{9,13},... | collective-permute-start | bytes 98312 | tf_op jit(solution)/shard_map/ppermute | solution.py:45
  46.4 3.9 %collective-permute-start.9 = (bf16[128,128]{1,0:T(8,128)(2,1)S(1)}, bf16[128,128]{1,0:T(8,128)(2,1)S(1)}, u32[]{:S(2)}, u32[]{:S(2)}) collective-permute-start(bf16[128,128]{1,0:T(8,128)(2,1)S(1)} %get-tuple-element.18), channel_id=1, source_target_pairs={{0,8},{1,3},{2,10},{3,1},{4,12},{5,7},{6,14},{7,5},{8,0},{9,11},{1... | collective-permute-start | bytes 98312 | tf_op jit(solution)/shard_map/ppermute | solution.py:45
  46.4 7.5 %collective-permute-start.8 = (bf16[16,128,128]{2,1,0:T(8,128)(2,1)S(1)}, bf16[16,128,128]{2,1,0:T(8,128)(2,1)S(1)}, u32[]{:S(2)}, u32[]{:S(2)}) collective-permute-start(bf16[16,128,128]{2,1,0:T(8,128)(2,1)S(1)} %get-tuple-element.16), channel_id=1, source_target_pairs={{0,1},{1,0},{2,3},{3,2},{4,5},{5,4},{6,7},{7,6},{8,9},{9,8},{10,11... | collective-permute-start | bytes 1572872 | tf_op jit(solution)/shard_map/ppermute | solution.py:36
  50.4 6.0 %collective-permute-start.14 = (bf16[512,128]{1,0:T(8,128)(2,1)S(1)}, bf16[512,128]{1,0:T(8,128)(2,1)S(1)}, u32[]{:S(2)}, u32[]{:S(2)}) collective-permute-start(bf16[512,128]{1,0:T(8,128)(2,1)S(1)} %constant_dynamic-update-slice_fusion.7.refs_0_), channel_id=1, source_target_pairs={{0,6},{1,25},{2,4},{3,27},{4,2},{5,29},{6,0},{7,31},{8,14},{9,17},... | collective-permute-start | bytes 393224 | tf_op jit(solution)/shard_map/ppermute | solution.py:45
  52.0 5.7 %collective-permute-start.13 = (bf16[512,128]{1,0:T(8,128)(2,1)S(1)}, bf16[512,128]{1,0:T(8,128)(2,1)S(1)}, u32[]{:S(2)}, u32[]{:S(2)}) collective-permute-start(bf16[512,128]{1,0:T(8,128)(2,1)S(1)} %constant_dynamic-update-slice_fusion.7.refs_0_), channel_id=1, source_target_pairs={{0,4},{1,17},{2,6},{3,19},{4,0},{5,21},{6,2},{7,23},{8,12},{9,25},... | collective-permute-start | bytes 393224 | tf_op jit(solution)/shard_map/ppermute | solution.py:45
  52.6 5.3 %collective-permute-start.12 = (bf16[512,128]{1,0:T(8,128)(2,1)S(1)}, bf16[512,128]{1,0:T(8,128)(2,1)S(1)}, u32[]{:S(2)}, u32[]{:S(2)}) collective-permute-start(bf16[512,128]{1,0:T(8,128)(2,1)S(1)} %constant_dynamic-update-slice_fusion.7.refs_0_), channel_id=1, source_target_pairs={{0,2},{1,9},{2,0},{3,11},{4,6},{5,13},{6,4},{7,15},{8,10},{9,1},{1... | collective-permute-start | bytes 393224 | tf_op jit(solution)/shard_map/ppermute | solution.py:45
  58.4 1.3 %collective-permute-start.15 = (f32[128,128]{1,0:T(8,128)S(1)}, f32[128,128]{1,0:T(8,128)S(1)}, u32[]{:S(2)}, u32[]{:S(2)}) collective-permute-start(f32[128,128]{1,0:T(8,128)S(1)} %get-tuple-element.20), channel_id=1, source_target_pairs={{0,1},{1,0},{2,3},{3,2},{4,5},{5,4},{6,7},{7,6},{8,9},{9,8},{10,11... | collective-permute-start | bytes 196616 | tf_op jit(solution)/shard_map/ppermute | solution.py:36
  59.7 5.8 %collective-permute-start.18 = (bf16[128,128]{1,0:T(8,128)(2,1)S(1)}, bf16[128,128]{1,0:T(8,128)(2,1)S(1)}, u32[]{:S(2)}, u32[]{:S(2)}) collective-permute-start(bf16[128,128]{1,0:T(8,128)(2,1)S(1)} %get-tuple-element.23), channel_id=1, source_target_pairs={{0,24},{1,7},{2,26},{3,5},{4,28},{5,3},{6,30},{7,1},{8,16},{9,15},... | collective-permute-start | bytes 98312 | tf_op jit(solution)/shard_map/ppermute | solution.py:45
  61.4 5.2 %collective-permute-start.17 = (bf16[128,128]{1,0:T(8,128)(2,1)S(1)}, bf16[128,128]{1,0:T(8,128)(2,1)S(1)}, u32[]{:S(2)}, u32[]{:S(2)}) collective-permute-start(bf16[128,128]{1,0:T(8,128)(2,1)S(1)} %get-tuple-element.23), channel_id=1, source_target_pairs={{0,16},{1,5},{2,18},{3,7},{4,20},{5,1},{6,22},{7,3},{8,24},{9,13},... | collective-permute-start | bytes 98312 | tf_op jit(solution)/shard_map/ppermute | solution.py:45
  61.6 4.9 %collective-permute-start.16 = (bf16[128,128]{1,0:T(8,128)(2,1)S(1)}, bf16[128,128]{1,0:T(8,128)(2,1)S(1)}, u32[]{:S(2)}, u32[]{:S(2)}) collective-permute-start(bf16[128,128]{1,0:T(8,128)(2,1)S(1)} %get-tuple-element.23), channel_id=1, source_target_pairs={{0,8},{1,3},{2,10},{3,1},{4,12},{5,7},{6,14},{7,5},{8,0},{9,11},{1... | collective-permute-start | bytes 98312 | tf_op jit(solution)/shard_map/ppermute | solution.py:45
  66.5 6.0 %collective-permute-start.21 = (bf16[512,128]{1,0:T(8,128)(2,1)S(1)}, bf16[512,128]{1,0:T(8,128)(2,1)S(1)}, u32[]{:S(2)}, u32[]{:S(2)}) collective-permute-start(bf16[512,128]{1,0:T(8,128)(2,1)S(1)} %pad_maximum_fusion.1.refs_0_), channel_id=1, source_target_pairs={{0,6},{1,25},{2,4},{3,27},{4,2},{5,29},{6,0},{7,31},{8,14},{9,17},... | collective-permute-start | bytes 393224 | tf_op jit(solution)/shard_map/ppermute | solution.py:45
  68.4 5.5 %collective-permute-start.20 = (bf16[512,128]{1,0:T(8,128)(2,1)S(1)}, bf16[512,128]{1,0:T(8,128)(2,1)S(1)}, u32[]{:S(2)}, u32[]{:S(2)}) collective-permute-start(bf16[512,128]{1,0:T(8,128)(2,1)S(1)} %pad_maximum_fusion.1.refs_0_), channel_id=1, source_target_pairs={{0,4},{1,17},{2,6},{3,19},{4,0},{5,21},{6,2},{7,23},{8,12},{9,25},... | collective-permute-start | bytes 393224 | tf_op jit(solution)/shard_map/ppermute | solution.py:45
  68.9 5.0 %collective-permute-start.19 = (bf16[512,128]{1,0:T(8,128)(2,1)S(1)}, bf16[512,128]{1,0:T(8,128)(2,1)S(1)}, u32[]{:S(2)}, u32[]{:S(2)}) collective-permute-start(bf16[512,128]{1,0:T(8,128)(2,1)S(1)} %pad_maximum_fusion.1.refs_0_), channel_id=1, source_target_pairs={{0,2},{1,9},{2,0},{3,11},{4,6},{5,13},{6,4},{7,15},{8,10},{9,1},{1... | collective-permute-start | bytes 393224 | tf_op jit(solution)/shard_map/ppermute | solution.py:45
  74.3 1.3 %collective-permute-start.22 = (f32[128,128]{1,0:T(8,128)S(1)}, f32[128,128]{1,0:T(8,128)S(1)}, u32[]{:S(2)}, u32[]{:S(2)}) collective-permute-start(f32[128,128]{1,0:T(8,128)S(1)} %get-tuple-element.22), channel_id=1, source_target_pairs={{0,1},{1,0},{2,3},{3,2},{4,5},{5,4},{6,7},{7,6},{8,9},{9,8},{10,11... | collective-permute-start | bytes 196616 | tf_op jit(solution)/shard_map/ppermute | solution.py:36

commit v15 on v14

--- a/solution.py
+++ b/solution.py
@@ -230,20 +230,29 @@
     grid_rows = cells // grid_cols
     vectors = base.shape[1]
 
-    def kernel(targets_ref, halfwidth_ref, turned_ref, received_ref, base_ref, out_ref, panel_ref, *picked):
+    def kernel(
+        targets_ref, halfwidth_ref, turned_ref, received_ref, base_ref, out_ref, panel_ref, *refs
+    ):
+        *picked, sems = refs
+        copies = [
+            pltpu.make_async_copy(received_ref.at[:, targets_ref[d]], picked_ref, sems.at[d - 1])
+            for d, picked_ref in enumerate(picked, start=1)
+        ]
+        for copy in copies:
+            copy.start()
         blocks = received_ref[...].reshape(cells * orb, orb)
         total = jnp.dot(turned_ref[...], blocks, preferred_element_type=jnp.float32)
-        for d, picked_ref in enumerate(picked, start=1):
-            for c in range(grid_rows):
-                picked_ref[c] = received_ref[c * grid_cols + targets_ref[d]]
         out = base_ref[...] + total.T / jnp.full((1, vectors), halfwidth_ref[0])
         out_ref[...] = out
         panel_ref[...] = out.astype(jnp.bfloat16)
+        for copy in copies:
+            copy.wait()
 
     return pl.pallas_call(
         kernel,
         in_specs=[SMEM] * 2 + [VMEM] * 3,
         out_specs=[VMEM] * (1 + grid_cols),
+        scratch_shapes=[pltpu.SemaphoreType.DMA((max(grid_cols - 1, 1),))],
         out_shape=[
             jax.ShapeDtypeStruct((orb, vectors), jnp.float32),
             jax.ShapeDtypeStruct((orb, vectors), jnp.bfloat16),
@@ -251,7 +260,7 @@
         + [jax.ShapeDtypeStruct((grid_rows, orb, orb), jnp.bfloat16)] * (grid_cols - 1),
         compiler_params=pltpu.CompilerParams(vmem_limit_bytes=received.size * 6 + 2 * SPARE),
         name="backward_first",
-    )(targets, halfwidth, turned_panels, received, base)
+    )(targets, halfwidth, turned_panels, received.reshape(grid_rows, grid_cols, orb, orb), base)
 
 
 def merge_tile(sources, targets, dense, received, stacks):

time: 76.7 us -> 76.8 us (level)
  no operation moved by 1% of the time
where the time goes in v15:
time: 76.8 us; the launch traced here: 76.3 us
  starting transfers between devices  32.6 us (42%)
  waiting for transfers between devices  29.4 us (38%)
  Pallas kernels  10.5 us (14%)
  between operations  2.21 us (3%)
  other arithmetic  1.55 us (2%)
    ppermute x18, starting transfers between devices, swap_rows(): return lax.ppermute(x, ('row', 'col'), pairs)  25.4 us
    ppermute x18, waiting for transfers between devices, swap_rows(): return lax.ppermute(x, ('row', 'col'), pairs)  24.6 us
    all_to_all x1, starting transfers between devices, body(): received = lax.all_to_all(dense, 'row', 0, 0, tiled=True)  6.4 us
    ppermute x5, waiting for transfers between devices, swap(): lax.ppermute(x, axis, [(source, source ^ offset) for source in range(size)])  3.39 us
    pallas_call x1, Pallas kernels, build_tile(): pl.pallas_call(kernel, in_specs=[HBM, HBM, SMEM, HBM], out_specs=HBM, scr...  2.7 us
    pallas_call x1, Pallas kernels, forward_first(): pl.pallas_call(kernel, in_specs=[SMEM] * 4 + [HBM] + [VMEM] * 2, out_spec...  2.21 us
    pallas_call x1, Pallas kernels, merge_tile(): pl.pallas_call(kernel, in_specs=[SMEM] * 2 + [HBM] + [VMEM] * grid_cols,...  2.14 us
  transfers between devices with their start and end apart: 24, of which 15 were waited for; matrix products, arithmetic and copies ran while one was open for 0% of the time, Pallas kernels for 11%

profile of v15, /device:TPU:0, one launch (start us, length us, event | category | flops | bytes accessed | tf_op | source)
XLA Modules:
  0.0 76.3 jit_solution(16502763977075566412)
XLA Ops:
  0.0 0.8 %constant_dynamic-update-slice_fusion.6 = (bf16[2048,128]{1,0:T(8,128)(2,1)S(1)}, bf16[128,128]{1,0:T(8,128)(2,1)S(1)}) fusion(f32[128,128]{1,0:T(8,128)} %previous_ref.1), kind=kLoop, calls=%fused_computation.8 | loop fusion | flops 16383 | bytes 131072
  0.9 5.1 %collective-permute-start.2 = (bf16[128,128]{1,0:T(8,128)(2,1)S(1)}, bf16[128,128]{1,0:T(8,128)(2,1)S(1)}, u32[]{:S(2)}, u32[]{:S(2)}) collective-permute-start(bf16[128,128]{1,0:T(8,128)(2,1)S(1)} %get-tuple-element.26), channel_id=1, source_target_pairs={{0,24},{1,25},{2,26},{3,27},{4,28},{5,29},{6,30},{7,31},{8,16},{9,... | collective-permute-start | bytes 98312 | tf_op jit(solution)/shard_map/ppermute | solution.py:45
  6.0 0.6 collective-permute-start
  7.3 2.7 %build_tile.1.refs_0_ = bf16[32,128,128]{2,1,0:T(8,128)(2,1)} custom-call(s32[1,64]{1,0:T(1,128)} %bitcast.8, s32[1,64]{1,0:T(1,128)} %bitcast.9, s32[1,1]{1,0:T(1,128)S(6)} %copy.21.count_ref, bf16[64,128,128]{2,1,0:T(8,128)(2,1)} %bitcast.7), custom_call_target="tpu_custom_call" | custom-call | tf_op jit(solution)/shard_map/build_tile/pallas_call | solution.py:90
  10.0 0.0 copy-start.2
  10.0 0.8 %collective-permute-done.1.refs_2_ = bf16[128,128]{1,0:T(8,128)(2,1)S(1)} collective-permute-done((bf16[128,128]{1,0:T(8,128)(2,1)S(1)}, bf16[128,128]{1,0:T(8,128)(2,1)S(1)}, u32[]{:S(2)}, u32[]{:S(2)}) %collective-permute-start.1) | collective-permute-done | bytes 32800 | tf_op jit(solution)/shard_map/ppermute | solution.py:45
  10.8 6.4 %all-to-all-start = ((bf16[32,128,128]{2,1,0:T(8,128)(2,1)}), bf16[32,128,128]{2,1,0:T(8,128)(2,1)S(1)}, u32[]{:S(2)}, u32[]{:S(2)}) async-start(bf16[32,128,128]{2,1,0:T(8,128)(2,1)} %after.1.dense_hbm), calls=%async_computation | async-start | bytes 2097152 | tf_op jit(solution)/shard_map/all_to_all | solution.py:363
  17.2 2.9 %collective-permute-start.5 = (bf16[512,128]{1,0:T(8,128)(2,1)S(1)}, bf16[512,128]{1,0:T(8,128)(2,1)S(1)}, u32[]{:S(2)}, u32[]{:S(2)}) collective-permute-start(bf16[512,128]{1,0:T(8,128)(2,1)S(1)} %pad_maximum_fusion), channel_id=1, source_target_pairs={{0,6},{1,7},{2,4},{3,5},{4,2},{5,3},{6,0},{7,1},{8,14},{9,15},{10,... | collective-permute-start | bytes 393224 | tf_op jit(solution)/shard_map/ppermute | solution.py:45
  20.1 0.6 collective-permute-start.4
  20.7 0.1 collective-permute-start.3
  20.8 9.8 %collective-permute-done.3 = bf16[512,128]{1,0:T(8,128)(2,1)S(1)} collective-permute-done((bf16[512,128]{1,0:T(8,128)(2,1)S(1)}, bf16[512,128]{1,0:T(8,128)(2,1)S(1)}, u32[]{:S(2)}, u32[]{:S(2)}) %collective-permute-start.3) | collective-permute-done | bytes 131104 | tf_op jit(solution)/shard_map/ppermute | solution.py:45
  30.6 2.1 %collective-permute-done.4 = bf16[512,128]{1,0:T(8,128)(2,1)S(1)} collective-permute-done((bf16[512,128]{1,0:T(8,128)(2,1)S(1)}, bf16[512,128]{1,0:T(8,128)(2,1)S(1)}, u32[]{:S(2)}, u32[]{:S(2)}) %collective-permute-start.4) | collective-permute-done | bytes 131104 | tf_op jit(solution)/shard_map/ppermute | solution.py:45
  32.8 0.7 turn_panel.1.refs_0_
  33.6 0.1 collective-permute-start.6
  35.0 2.2 %forward_first.1 = (f32[128,128]{1,0:T(8,128)S(1)}, f32[128,128]{1,0:T(8,128)S(1)}) custom-call(s32[16]{0:T(128)S(1)} %broadcast_xor_fusion.sources_ref, s32[2]{0:T(128)S(1)} %iota_xor_fusion.targets_ref, f32[1]{0:T(128)S(6)} %copy.22.center_ref, f32[1]{0:T(128)S(6)} %copy.23.halfwidth_ref, bf16[32,128,128]{2,1,0:T(8,128)(2,1)} %after.1.dense_hbm, ...), custom_call_target="tpu_custom_call" | custom-call | tf_op jit(solution)/shard_map/forward_first/pallas_call | solution.py:168
  37.2 0.6 collective-permute-start.7
  37.7 0.9 %collective-permute-done.7 = f32[128,128]{1,0:T(8,128)S(1)} collective-permute-done((f32[128,128]{1,0:T(8,128)S(1)}, f32[128,128]{1,0:T(8,128)S(1)}, u32[]{:S(2)}, u32[]{:S(2)}) %collective-permute-start.7) | collective-permute-done | bytes 65568 | tf_op jit(solution)/shard_map/ppermute | solution.py:36
  38.7 0.8 %lay_panels.1.turned_ref = bf16[128,4096]{1,0:T(8,128)(2,1)S(1)} custom-call(s32[2]{0:T(128)S(1)} %iota_xor_fusion.targets_ref, bf16[128,2048]{1,0:T(8,128)(2,1)S(1)} %turn_panel.1.refs_0_, bf16[128,2048]{1,0:T(8,128)(2,1)S(1)} %collective-permute-done.6.refs_1_), custom_call_target="tpu_custom_call" | custom-call | tf_op jit(solution)/shard_map/lay_panels/pallas_call | solution.py:217
  39.5 1.4 %all-to-all-done.received_ref = bf16[32,128,128]{2,1,0:T(8,128)(2,1)S(1)} async-done(((bf16[32,128,128]{2,1,0:T(8,128)(2,1)}), bf16[32,128,128]{2,1,0:T(8,128)(2,1)S(1)}, u32[]{:S(2)}, u32[]{:S(2)}) %all-to-all-start) | async-done | bytes 1048608 | tf_op jit(solution)/shard_map/all_to_all | solution.py:363
  40.9 1.1 %backward_first.1 = (f32[128,128]{1,0:T(8,128)S(1)}, bf16[128,128]{1,0:T(8,128)(2,1)S(1)}, bf16[16,128,128]{2,1,0:T(8,128)(2,1)S(1)}) custom-call(s32[2]{0:T(128)S(1)} %iota_xor_fusion.targets_ref, f32[1]{0:T(128)S(6)} %copy.23.halfwidth_ref, bf16[128,4096]{1,0:T(8,128)(2,1)S(1)} %lay_panels.1.turned_ref, bf16[16,2,128,128]{3,2,1,0:T(8,128)(2,1)S(1)} %bitcast.6, ...), custom_call_target="tpu_custom_call" | custom-call | tf_op jit(solution)/shard_map/backward_first/pallas_call | solution.py:251
  42.0 2.8 %collective-permute-start.11 = (bf16[128,128]{1,0:T(8,128)(2,1)S(1)}, bf16[128,128]{1,0:T(8,128)(2,1)S(1)}, u32[]{:S(2)}, u32[]{:S(2)}) collective-permute-start(bf16[128,128]{1,0:T(8,128)(2,1)S(1)} %get-tuple-element.18), channel_id=1, source_target_pairs={{0,24},{1,7},{2,26},{3,5},{4,28},{5,3},{6,30},{7,1},{8,16},{9,15},... | collective-permute-start | bytes 98312 | tf_op jit(solution)/shard_map/ppermute | solution.py:45
  44.8 1.7 %collective-permute-start.10 = (bf16[128,128]{1,0:T(8,128)(2,1)S(1)}, bf16[128,128]{1,0:T(8,128)(2,1)S(1)}, u32[]{:S(2)}, u32[]{:S(2)}) collective-permute-start(bf16[128,128]{1,0:T(8,128)(2,1)S(1)} %get-tuple-element.18), channel_id=1, source_target_pairs={{0,16},{1,5},{2,18},{3,7},{4,20},{5,1},{6,22},{7,3},{8,24},{9,13},... | collective-permute-start | bytes 98312 | tf_op jit(solution)/shard_map/ppermute | solution.py:45
  46.5 3.9 %collective-permute-done.9 = bf16[128,128]{1,0:T(8,128)(2,1)S(1)} collective-permute-done((bf16[128,128]{1,0:T(8,128)(2,1)S(1)}, bf16[128,128]{1,0:T(8,128)(2,1)S(1)}, u32[]{:S(2)}, u32[]{:S(2)}) %collective-permute-start.9) | collective-permute-done | bytes 32800 | tf_op jit(solution)/shard_map/ppermute | solution.py:45
  50.5 1.6 %collective-permute-start.14 = (bf16[512,128]{1,0:T(8,128)(2,1)S(1)}, bf16[512,128]{1,0:T(8,128)(2,1)S(1)}, u32[]{:S(2)}, u32[]{:S(2)}) collective-permute-start(bf16[512,128]{1,0:T(8,128)(2,1)S(1)} %constant_dynamic-update-slice_fusion.7.refs_0_), channel_id=1, source_target_pairs={{0,6},{1,25},{2,4},{3,27},{4,2},{5,29},{6,0},{7,31},{8,14},{9,17},... | collective-permute-start | bytes 393224 | tf_op jit(solution)/shard_map/ppermute | solution.py:45
  52.1 0.6 collective-permute-start.13
  52.7 1.3 %collective-permute-start.12 = (bf16[512,128]{1,0:T(8,128)(2,1)S(1)}, bf16[512,128]{1,0:T(8,128)(2,1)S(1)}, u32[]{:S(2)}, u32[]{:S(2)}) collective-permute-start(bf16[512,128]{1,0:T(8,128)(2,1)S(1)} %constant_dynamic-update-slice_fusion.7.refs_0_), channel_id=1, source_target_pairs={{0,2},{1,9},{2,0},{3,11},{4,6},{5,13},{6,4},{7,15},{8,10},{9,1},{1... | collective-permute-start | bytes 393224 | tf_op jit(solution)/shard_map/ppermute | solution.py:45
  54.0 2.1 %merge_tile.1.tile_ref = bf16[256,2048]{1,0:T(8,128)(2,1)S(1)} custom-call(s32[16]{0:T(128)S(1)} %xor_bitcast_fusion.sources_ref, s32[2]{0:T(128)S(1)} %iota_xor_fusion.targets_ref, bf16[32,128,128]{2,1,0:T(8,128)(2,1)} %after.1.dense_hbm, bf16[32,128,128]{2,1,0:T(8,128)(2,1)S(1)} %all-to-all-done.received_ref, ...), custom_call_target="tpu_custom_call" | custom-call | tf_op jit(solution)/shard_map/merge_tile/pallas_call | solution.py:285
  56.2 0.3 collective-permute-done.14.refs_3_
  56.5 1.3 %collective-permute-done.13.refs_2_ = bf16[512,128]{1,0:T(8,128)(2,1)S(1)} collective-permute-done((bf16[512,128]{1,0:T(8,128)(2,1)S(1)}, bf16[512,128]{1,0:T(8,128)(2,1)S(1)}, u32[]{:S(2)}, u32[]{:S(2)}) %collective-permute-start.13) | collective-permute-done | bytes 131104 | tf_op jit(solution)/shard_map/ppermute | solution.py:45
  57.8 0.2 collective-permute-done.12.refs_1_
  58.0 0.4 apply_tile.2
  58.4 0.1 collective-permute-start.15
  58.5 1.2 %collective-permute-done.15 = f32[128,128]{1,0:T(8,128)S(1)} collective-permute-done((f32[128,128]{1,0:T(8,128)S(1)}, f32[128,128]{1,0:T(8,128)S(1)}, u32[]{:S(2)}, u32[]{:S(2)}) %collective-permute-start.15) | collective-permute-done | bytes 65568 | tf_op jit(solution)/shard_map/ppermute | solution.py:36
  59.8 1.6 %collective-permute-start.18 = (bf16[128,128]{1,0:T(8,128)(2,1)S(1)}, bf16[128,128]{1,0:T(8,128)(2,1)S(1)}, u32[]{:S(2)}, u32[]{:S(2)}) collective-permute-start(bf16[128,128]{1,0:T(8,128)(2,1)S(1)} %get-tuple-element.23), channel_id=1, source_target_pairs={{0,24},{1,7},{2,26},{3,5},{4,28},{5,3},{6,30},{7,1},{8,16},{9,15},... | collective-permute-start | bytes 98312 | tf_op jit(solution)/shard_map/ppermute | solution.py:45
  61.4 0.3 collective-permute-start.17
  61.7 2.5 %collective-permute-start.16 = (bf16[128,128]{1,0:T(8,128)(2,1)S(1)}, bf16[128,128]{1,0:T(8,128)(2,1)S(1)}, u32[]{:S(2)}, u32[]{:S(2)}) collective-permute-start(bf16[128,128]{1,0:T(8,128)(2,1)S(1)} %get-tuple-element.23), channel_id=1, source_target_pairs={{0,8},{1,3},{2,10},{3,1},{4,12},{5,7},{6,14},{7,5},{8,0},{9,11},{1... | collective-permute-start | bytes 98312 | tf_op jit(solution)/shard_map/ppermute | solution.py:45
  64.2 1.3 %collective-permute-done.18 = bf16[128,128]{1,0:T(8,128)(2,1)S(1)} collective-permute-done((bf16[128,128]{1,0:T(8,128)(2,1)S(1)}, bf16[128,128]{1,0:T(8,128)(2,1)S(1)}, u32[]{:S(2)}, u32[]{:S(2)}) %collective-permute-start.18) | collective-permute-done | bytes 32800 | tf_op jit(solution)/shard_map/ppermute | solution.py:45
  65.5 1.0 %collective-permute-done.17 = bf16[128,128]{1,0:T(8,128)(2,1)S(1)} collective-permute-done((bf16[128,128]{1,0:T(8,128)(2,1)S(1)}, bf16[128,128]{1,0:T(8,128)(2,1)S(1)}, u32[]{:S(2)}, u32[]{:S(2)}) %collective-permute-start.17) | collective-permute-done | bytes 32800 | tf_op jit(solution)/shard_map/ppermute | solution.py:45
  66.6 1.8 %collective-permute-start.21 = (bf16[512,128]{1,0:T(8,128)(2,1)S(1)}, bf16[512,128]{1,0:T(8,128)(2,1)S(1)}, u32[]{:S(2)}, u32[]{:S(2)}) collective-permute-start(bf16[512,128]{1,0:T(8,128)(2,1)S(1)} %pad_maximum_fusion.1.refs_0_), channel_id=1, source_target_pairs={{0,6},{1,25},{2,4},{3,27},{4,2},{5,29},{6,0},{7,31},{8,14},{9,17},... | collective-permute-start | bytes 393224 | tf_op jit(solution)/shard_map/ppermute | solution.py:45
  68.4 0.6 collective-permute-start.20
  69.0 1.2 %collective-permute-start.19 = (bf16[512,128]{1,0:T(8,128)(2,1)S(1)}, bf16[512,128]{1,0:T(8,128)(2,1)S(1)}, u32[]{:S(2)}, u32[]{:S(2)}) collective-permute-start(bf16[512,128]{1,0:T(8,128)(2,1)S(1)} %pad_maximum_fusion.1.refs_0_), channel_id=1, source_target_pairs={{0,2},{1,9},{2,0},{3,11},{4,6},{5,13},{6,4},{7,15},{8,10},{9,1},{1... | collective-permute-start | bytes 393224 | tf_op jit(solution)/shard_map/ppermute | solution.py:45
  70.1 2.4 %collective-permute-done.21.refs_3_ = bf16[512,128]{1,0:T(8,128)(2,1)S(1)} collective-permute-done((bf16[512,128]{1,0:T(8,128)(2,1)S(1)}, bf16[512,128]{1,0:T(8,128)(2,1)S(1)}, u32[]{:S(2)}, u32[]{:S(2)}) %collective-permute-start.21) | collective-permute-done | bytes 131104 | tf_op jit(solution)/shard_map/ppermute | solution.py:45
  72.6 1.3 %collective-permute-done.20.refs_2_ = bf16[512,128]{1,0:T(8,128)(2,1)S(1)} collective-permute-done((bf16[512,128]{1,0:T(8,128)(2,1)S(1)}, bf16[512,128]{1,0:T(8,128)(2,1)S(1)}, u32[]{:S(2)}, u32[]{:S(2)}) %collective-permute-start.20) | collective-permute-done | bytes 131104 | tf_op jit(solution)/shard_map/ppermute | solution.py:45
  73.9 0.0 collective-permute-done.19.refs_1_
  74.0 0.4 apply_tile.3
  74.4 0.1 collective-permute-start.22
  74.5 1.2 %collective-permute-done.22 = f32[128,128]{1,0:T(8,128)S(1)} collective-permute-done((f32[128,128]{1,0:T(8,128)S(1)}, f32[128,128]{1,0:T(8,128)S(1)}, u32[]{:S(2)}, u32[]{:S(2)}) %collective-permute-start.22) | collective-permute-done | bytes 65568 | tf_op jit(solution)/shard_map/ppermute | solution.py:36
  75.7 0.6 add.20
  (34 shorter events, 0.2 us)
Async XLA Ops:
  0.9 9.1 %collective-permute-start.2 = (bf16[128,128]{1,0:T(8,128)(2,1)S(1)}, bf16[128,128]{1,0:T(8,128)(2,1)S(1)}, u32[]{:S(2)}, u32[]{:S(2)}) collective-permute-start(bf16[128,128]{1,0:T(8,128)(2,1)S(1)} %get-tuple-element.26), channel_id=1, source_target_pairs={{0,24},{1,25},{2,26},{3,27},{4,28},{5,29},{6,30},{7,31},{8,16},{9,... | collective-permute-start | bytes 98312 | tf_op jit(solution)/shard_map/ppermute | solution.py:45
  6.0 4.8 %collective-permute-start.1 = (bf16[128,128]{1,0:T(8,128)(2,1)S(1)}, bf16[128,128]{1,0:T(8,128)(2,1)S(1)}, u32[]{:S(2)}, u32[]{:S(2)}) collective-permute-start(bf16[128,128]{1,0:T(8,128)(2,1)S(1)} %get-tuple-element.26), channel_id=1, source_target_pairs={{0,16},{1,17},{2,18},{3,19},{4,20},{5,21},{6,22},{7,23},{8,24},{9,... | collective-permute-start | bytes 98312 | tf_op jit(solution)/shard_map/ppermute | solution.py:45
  6.0 4.8 %collective-permute-start = (bf16[128,128]{1,0:T(8,128)(2,1)S(1)}, bf16[128,128]{1,0:T(8,128)(2,1)S(1)}, u32[]{:S(2)}, u32[]{:S(2)}) collective-permute-start(bf16[128,128]{1,0:T(8,128)(2,1)S(1)} %get-tuple-element.26), channel_id=1, source_target_pairs={{0,8},{1,9},{2,10},{3,11},{4,12},{5,13},{6,14},{7,15},{8,0},{9,1},... | collective-permute-start | bytes 98312 | tf_op jit(solution)/shard_map/ppermute | solution.py:45
  10.0 7.2 %copy-start.2 = (s32[16]{0:T(128)S(1)}, s32[16]{0:T(128)}, u32[]{:S(2)}) copy-start(s32[16]{0:T(128)} %constant.26.clone) | copy-start | bytes 196
  10.8 24.2 %copy-start = (f32[128,128]{1,0:T(8,128)S(1)}, f32[128,128]{1,0:T(8,128)}, u32[]{:S(2)}) copy-start(f32[128,128]{1,0:T(8,128)} %previous_ref.1) | copy-start | bytes 196612
  10.8 30.1 %all-to-all-start = ((bf16[32,128,128]{2,1,0:T(8,128)(2,1)}), bf16[32,128,128]{2,1,0:T(8,128)(2,1)S(1)}, u32[]{:S(2)}, u32[]{:S(2)}) async-start(bf16[32,128,128]{2,1,0:T(8,128)(2,1)} %after.1.dense_hbm), calls=%async_computation | async-start | bytes 2097152 | tf_op jit(solution)/shard_map/all_to_all | solution.py:363
  17.2 15.5 %collective-permute-start.5 = (bf16[512,128]{1,0:T(8,128)(2,1)S(1)}, bf16[512,128]{1,0:T(8,128)(2,1)S(1)}, u32[]{:S(2)}, u32[]{:S(2)}) collective-permute-start(bf16[512,128]{1,0:T(8,128)(2,1)S(1)} %pad_maximum_fusion), channel_id=1, source_target_pairs={{0,6},{1,7},{2,4},{3,5},{4,2},{5,3},{6,0},{7,1},{8,14},{9,15},{10,... | collective-permute-start | bytes 393224 | tf_op jit(solution)/shard_map/ppermute | solution.py:45
  20.1 12.6 %collective-permute-start.4 = (bf16[512,128]{1,0:T(8,128)(2,1)S(1)}, bf16[512,128]{1,0:T(8,128)(2,1)S(1)}, u32[]{:S(2)}, u32[]{:S(2)}) collective-permute-start(bf16[512,128]{1,0:T(8,128)(2,1)S(1)} %pad_maximum_fusion), channel_id=1, source_target_pairs={{0,4},{1,5},{2,6},{3,7},{4,0},{5,1},{6,2},{7,3},{8,12},{9,13},{10,... | collective-permute-start | bytes 393224 | tf_op jit(solution)/shard_map/ppermute | solution.py:45
  20.7 9.9 %collective-permute-start.3 = (bf16[512,128]{1,0:T(8,128)(2,1)S(1)}, bf16[512,128]{1,0:T(8,128)(2,1)S(1)}, u32[]{:S(2)}, u32[]{:S(2)}) collective-permute-start(bf16[512,128]{1,0:T(8,128)(2,1)S(1)} %pad_maximum_fusion), channel_id=1, source_target_pairs={{0,2},{1,3},{2,0},{3,1},{4,6},{5,7},{6,4},{7,5},{8,10},{9,11},{10,... | collective-permute-start | bytes 393224 | tf_op jit(solution)/shard_map/ppermute | solution.py:45
  33.6 5.1 %collective-permute-start.6 = (bf16[128,2048]{1,0:T(8,128)(2,1)S(1)}, bf16[128,2048]{1,0:T(8,128)(2,1)S(1)}, u32[]{:S(2)}, u32[]{:S(2)}) collective-permute-start(bf16[128,2048]{1,0:T(8,128)(2,1)S(1)} %turn_panel.1.refs_0_), channel_id=1, source_target_pairs={{0,1},{1,0},{2,3},{3,2},{4,5},{5,4},{6,7},{7,6},{8,9},{9,8},{10,11... | collective-permute-start | bytes 1572872 | tf_op jit(solution)/shard_map/ppermute | solution.py:36
  37.2 1.5 %collective-permute-start.7 = (f32[128,128]{1,0:T(8,128)S(1)}, f32[128,128]{1,0:T(8,128)S(1)}, u32[]{:S(2)}, u32[]{:S(2)}) collective-permute-start(f32[128,128]{1,0:T(8,128)S(1)} %get-tuple-element.15), channel_id=1, source_target_pairs={{0,1},{1,0},{2,3},{3,2},{4,5},{5,4},{6,7},{7,6},{8,9},{9,8},{10,11... | collective-permute-start | bytes 196616 | tf_op jit(solution)/shard_map/ppermute | solution.py:36
  38.7 15.4 %copy-start.1 = (s32[2,16]{1,0:T(2,128)S(1)}, s32[2,16]{1,0:T(2,128)}, u32[]{:S(2)}) copy-start(s32[2,16]{1,0:T(2,128)} %constant.27.clone) | copy-start | bytes 388
  42.0 8.5 %collective-permute-start.11 = (bf16[128,128]{1,0:T(8,128)(2,1)S(1)}, bf16[128,128]{1,0:T(8,128)(2,1)S(1)}, u32[]{:S(2)}, u32[]{:S(2)}) collective-permute-start(bf16[128,128]{1,0:T(8,128)(2,1)S(1)} %get-tuple-element.18), channel_id=1, source_target_pairs={{0,24},{1,7},{2,26},{3,5},{4,28},{5,3},{6,30},{7,1},{8,16},{9,15},... | collective-permute-start | bytes 98312 | tf_op jit(solution)/shard_map/ppermute | solution.py:45
  44.8 5.6 %collective-permute-start.10 = (bf16[128,128]{1,0:T(8,128)(2,1)S(1)}, bf16[128,128]{1,0:T(8,128)(2,1)S(1)}, u32[]{:S(2)}, u32[]{:S(2)}) collective-permute-start(bf16[128,128]{1,0:T(8,128)(2,1)S(1)} %get-tuple-element.18), channel_id=1, source_target_pairs={{0,16},{1,5},{2,18},{3,7},{4,20},{5,1},{6,22},{7,3},{8,24},{9,13},... | collective-permute-start | bytes 98312 | tf_op jit(solution)/shard_map/ppermute | solution.py:45
  46.5 3.9 %collective-permute-start.9 = (bf16[128,128]{1,0:T(8,128)(2,1)S(1)}, bf16[128,128]{1,0:T(8,128)(2,1)S(1)}, u32[]{:S(2)}, u32[]{:S(2)}) collective-permute-start(bf16[128,128]{1,0:T(8,128)(2,1)S(1)} %get-tuple-element.18), channel_id=1, source_target_pairs={{0,8},{1,3},{2,10},{3,1},{4,12},{5,7},{6,14},{7,5},{8,0},{9,11},{1... | collective-permute-start | bytes 98312 | tf_op jit(solution)/shard_map/ppermute | solution.py:45
  46.5 7.5 %collective-permute-start.8 = (bf16[16,128,128]{2,1,0:T(8,128)(2,1)S(1)}, bf16[16,128,128]{2,1,0:T(8,128)(2,1)S(1)}, u32[]{:S(2)}, u32[]{:S(2)}) collective-permute-start(bf16[16,128,128]{2,1,0:T(8,128)(2,1)S(1)} %get-tuple-element.16), channel_id=1, source_target_pairs={{0,1},{1,0},{2,3},{3,2},{4,5},{5,4},{6,7},{7,6},{8,9},{9,8},{10,11... | collective-permute-start | bytes 1572872 | tf_op jit(solution)/shard_map/ppermute | solution.py:36
  50.5 6.0 %collective-permute-start.14 = (bf16[512,128]{1,0:T(8,128)(2,1)S(1)}, bf16[512,128]{1,0:T(8,128)(2,1)S(1)}, u32[]{:S(2)}, u32[]{:S(2)}) collective-permute-start(bf16[512,128]{1,0:T(8,128)(2,1)S(1)} %constant_dynamic-update-slice_fusion.7.refs_0_), channel_id=1, source_target_pairs={{0,6},{1,25},{2,4},{3,27},{4,2},{5,29},{6,0},{7,31},{8,14},{9,17},... | collective-permute-start | bytes 393224 | tf_op jit(solution)/shard_map/ppermute | solution.py:45
  52.1 5.7 %collective-permute-start.13 = (bf16[512,128]{1,0:T(8,128)(2,1)S(1)}, bf16[512,128]{1,0:T(8,128)(2,1)S(1)}, u32[]{:S(2)}, u32[]{:S(2)}) collective-permute-start(bf16[512,128]{1,0:T(8,128)(2,1)S(1)} %constant_dynamic-update-slice_fusion.7.refs_0_), channel_id=1, source_target_pairs={{0,4},{1,17},{2,6},{3,19},{4,0},{5,21},{6,2},{7,23},{8,12},{9,25},... | collective-permute-start | bytes 393224 | tf_op jit(solution)/shard_map/ppermute | solution.py:45
  52.7 5.3 %collective-permute-start.12 = (bf16[512,128]{1,0:T(8,128)(2,1)S(1)}, bf16[512,128]{1,0:T(8,128)(2,1)S(1)}, u32[]{:S(2)}, u32[]{:S(2)}) collective-permute-start(bf16[512,128]{1,0:T(8,128)(2,1)S(1)} %constant_dynamic-update-slice_fusion.7.refs_0_), channel_id=1, source_target_pairs={{0,2},{1,9},{2,0},{3,11},{4,6},{5,13},{6,4},{7,15},{8,10},{9,1},{1... | collective-permute-start | bytes 393224 | tf_op jit(solution)/shard_map/ppermute | solution.py:45
  58.4 1.3 %collective-permute-start.15 = (f32[128,128]{1,0:T(8,128)S(1)}, f32[128,128]{1,0:T(8,128)S(1)}, u32[]{:S(2)}, u32[]{:S(2)}) collective-permute-start(f32[128,128]{1,0:T(8,128)S(1)} %get-tuple-element.20), channel_id=1, source_target_pairs={{0,1},{1,0},{2,3},{3,2},{4,5},{5,4},{6,7},{7,6},{8,9},{9,8},{10,11... | collective-permute-start | bytes 196616 | tf_op jit(solution)/shard_map/ppermute | solution.py:36
  59.8 5.8 %collective-permute-start.18 = (bf16[128,128]{1,0:T(8,128)(2,1)S(1)}, bf16[128,128]{1,0:T(8,128)(2,1)S(1)}, u32[]{:S(2)}, u32[]{:S(2)}) collective-permute-start(bf16[128,128]{1,0:T(8,128)(2,1)S(1)} %get-tuple-element.23), channel_id=1, source_target_pairs={{0,24},{1,7},{2,26},{3,5},{4,28},{5,3},{6,30},{7,1},{8,16},{9,15},... | collective-permute-start | bytes 98312 | tf_op jit(solution)/shard_map/ppermute | solution.py:45
  61.4 5.2 %collective-permute-start.17 = (bf16[128,128]{1,0:T(8,128)(2,1)S(1)}, bf16[128,128]{1,0:T(8,128)(2,1)S(1)}, u32[]{:S(2)}, u32[]{:S(2)}) collective-permute-start(bf16[128,128]{1,0:T(8,128)(2,1)S(1)} %get-tuple-element.23), channel_id=1, source_target_pairs={{0,16},{1,5},{2,18},{3,7},{4,20},{5,1},{6,22},{7,3},{8,24},{9,13},... | collective-permute-start | bytes 98312 | tf_op jit(solution)/shard_map/ppermute | solution.py:45
  61.7 4.9 %collective-permute-start.16 = (bf16[128,128]{1,0:T(8,128)(2,1)S(1)}, bf16[128,128]{1,0:T(8,128)(2,1)S(1)}, u32[]{:S(2)}, u32[]{:S(2)}) collective-permute-start(bf16[128,128]{1,0:T(8,128)(2,1)S(1)} %get-tuple-element.23), channel_id=1, source_target_pairs={{0,8},{1,3},{2,10},{3,1},{4,12},{5,7},{6,14},{7,5},{8,0},{9,11},{1... | collective-permute-start | bytes 98312 | tf_op jit(solution)/shard_map/ppermute | solution.py:45
  66.6 6.0 %collective-permute-start.21 = (bf16[512,128]{1,0:T(8,128)(2,1)S(1)}, bf16[512,128]{1,0:T(8,128)(2,1)S(1)}, u32[]{:S(2)}, u32[]{:S(2)}) collective-permute-start(bf16[512,128]{1,0:T(8,128)(2,1)S(1)} %pad_maximum_fusion.1.refs_0_), channel_id=1, source_target_pairs={{0,6},{1,25},{2,4},{3,27},{4,2},{5,29},{6,0},{7,31},{8,14},{9,17},... | collective-permute-start | bytes 393224 | tf_op jit(solution)/shard_map/ppermute | solution.py:45
  68.4 5.5 %collective-permute-start.20 = (bf16[512,128]{1,0:T(8,128)(2,1)S(1)}, bf16[512,128]{1,0:T(8,128)(2,1)S(1)}, u32[]{:S(2)}, u32[]{:S(2)}) collective-permute-start(bf16[512,128]{1,0:T(8,128)(2,1)S(1)} %pad_maximum_fusion.1.refs_0_), channel_id=1, source_target_pairs={{0,4},{1,17},{2,6},{3,19},{4,0},{5,21},{6,2},{7,23},{8,12},{9,25},... | collective-permute-start | bytes 393224 | tf_op jit(solution)/shard_map/ppermute | solution.py:45
  69.0 5.0 %collective-permute-start.19 = (bf16[512,128]{1,0:T(8,128)(2,1)S(1)}, bf16[512,128]{1,0:T(8,128)(2,1)S(1)}, u32[]{:S(2)}, u32[]{:S(2)}) collective-permute-start(bf16[512,128]{1,0:T(8,128)(2,1)S(1)} %pad_maximum_fusion.1.refs_0_), channel_id=1, source_target_pairs={{0,2},{1,9},{2,0},{3,11},{4,6},{5,13},{6,4},{7,15},{8,10},{9,1},{1... | collective-permute-start | bytes 393224 | tf_op jit(solution)/shard_map/ppermute | solution.py:45
  74.4 1.3 %collective-permute-start.22 = (f32[128,128]{1,0:T(8,128)S(1)}, f32[128,128]{1,0:T(8,128)S(1)}, u32[]{:S(2)}, u32[]{:S(2)}) collective-permute-start(f32[128,128]{1,0:T(8,128)S(1)} %get-tuple-element.22), channel_id=1, source_target_pairs={{0,1},{1,0},{2,3},{3,2},{4,5},{5,4},{6,7},{7,6},{8,9},{9,8},{10,11... | collective-permute-start | bytes 196616 | tf_op jit(solution)/shard_map/ppermute | solution.py:36

commit v16 on v12

--- a/solution.py
+++ b/solution.py
@@ -345,10 +345,12 @@
     def gather(parts, orders, first=0, last=None):
         for (stride, radix), (odd_stride, _) in list(zip(*orders))[first:last]:
             panel = jnp.concatenate(parts, axis=0)
-            parts = [panel] + [
-                swap_rows(panel, grid_rows, grid_cols, (k * stride, k * odd_stride))
-                for k in range(1, radix)
-            ]
+            digits = range(radix - 1, 0, -1) if len(parts) > 1 else range(1, radix)
+            found = {
+                k: swap_rows(panel, grid_rows, grid_cols, (k * stride, k * odd_stride))
+                for k in digits
+            }
+            parts = [panel] + [found[k] for k in range(1, radix)]
         return parts
 
     row = lax.axis_index("row")

time: 76.6 us -> 76.6 us (level)
  no operation moved by 1% of the time
where the time goes in v16:
time: 76.6 us; the launch traced here: 76.2 us
  starting transfers between devices  32.7 us (43%)
  waiting for transfers between devices  29.1 us (38%)
  Pallas kernels  10.5 us (14%)
  between operations  2.22 us (3%)
  other arithmetic  1.55 us (2%)
    ppermute x18, starting transfers between devices, swap_rows(): return lax.ppermute(x, ('row', 'col'), pairs)  25.4 us
    ppermute x18, waiting for transfers between devices, swap_rows(): return lax.ppermute(x, ('row', 'col'), pairs)  24.3 us
    all_to_all x1, starting transfers between devices, body(): received = lax.all_to_all(dense, 'row', 0, 0, tiled=True)  6.4 us
    ppermute x5, waiting for transfers between devices, swap(): lax.ppermute(x, axis, [(source, source ^ offset) for source in range(size)])  3.39 us
    pallas_call x1, Pallas kernels, build_tile(): pl.pallas_call(kernel, in_specs=[HBM, HBM, SMEM, HBM], out_specs=HBM, scr...  2.7 us
    pallas_call x1, Pallas kernels, forward_first(): pl.pallas_call(kernel, in_specs=[SMEM] * 4 + [HBM] + [VMEM] * 2, out_spec...  2.21 us
    pallas_call x1, Pallas kernels, merge_tile(): pl.pallas_call(kernel, in_specs=[SMEM] * 2 + [HBM] + [VMEM] * grid_cols,...  2.14 us
  transfers between devices with their start and end apart: 24, of which 17 were waited for; matrix products, arithmetic and copies ran while one was open for 0% of the time, Pallas kernels for 12%

profile of v16, /device:TPU:0, one launch (start us, length us, event | category | flops | bytes accessed | tf_op | source)
XLA Modules:
  0.0 76.2 jit_solution(12763639790202958376)
XLA Ops:
  0.0 0.8 %constant_dynamic-update-slice_fusion.6 = (bf16[2048,128]{1,0:T(8,128)(2,1)S(1)}, bf16[128,128]{1,0:T(8,128)(2,1)S(1)}) fusion(f32[128,128]{1,0:T(8,128)} %previous_ref.1), kind=kLoop, calls=%fused_computation.8 | loop fusion | flops 16383 | bytes 131072
  0.9 5.1 %collective-permute-start.2 = (bf16[128,128]{1,0:T(8,128)(2,1)S(1)}, bf16[128,128]{1,0:T(8,128)(2,1)S(1)}, u32[]{:S(2)}, u32[]{:S(2)}) collective-permute-start(bf16[128,128]{1,0:T(8,128)(2,1)S(1)} %get-tuple-element.24), channel_id=1, source_target_pairs={{0,24},{1,25},{2,26},{3,27},{4,28},{5,29},{6,30},{7,31},{8,16},{9,... | collective-permute-start | bytes 98312 | tf_op jit(solution)/shard_map/ppermute | solution.py:45
  6.0 0.6 collective-permute-start
  7.3 2.7 %build_tile.1.refs_0_ = bf16[32,128,128]{2,1,0:T(8,128)(2,1)} custom-call(s32[1,64]{1,0:T(1,128)} %bitcast.6, s32[1,64]{1,0:T(1,128)} %bitcast.7, s32[1,1]{1,0:T(1,128)S(6)} %copy.21.count_ref, bf16[64,128,128]{2,1,0:T(8,128)(2,1)} %bitcast.5), custom_call_target="tpu_custom_call" | custom-call | tf_op jit(solution)/shard_map/build_tile/pallas_call | solution.py:90
  10.0 0.8 %collective-permute-done.1.refs_2_ = bf16[128,128]{1,0:T(8,128)(2,1)S(1)} collective-permute-done((bf16[128,128]{1,0:T(8,128)(2,1)S(1)}, bf16[128,128]{1,0:T(8,128)(2,1)S(1)}, u32[]{:S(2)}, u32[]{:S(2)}) %collective-permute-start.1) | collective-permute-done | bytes 32800 | tf_op jit(solution)/shard_map/ppermute | solution.py:45
  10.8 6.4 %all-to-all-start = ((bf16[32,128,128]{2,1,0:T(8,128)(2,1)}), bf16[32,128,128]{2,1,0:T(8,128)(2,1)S(1)}, u32[]{:S(2)}, u32[]{:S(2)}) async-start(bf16[32,128,128]{2,1,0:T(8,128)(2,1)} %after.1.dense_hbm), calls=%async_computation | async-start | bytes 2097152 | tf_op jit(solution)/shard_map/all_to_all | solution.py:369
  17.2 2.9 %collective-permute-start.5 = (bf16[512,128]{1,0:T(8,128)(2,1)S(1)}, bf16[512,128]{1,0:T(8,128)(2,1)S(1)}, u32[]{:S(2)}, u32[]{:S(2)}) collective-permute-start(bf16[512,128]{1,0:T(8,128)(2,1)S(1)} %pad_maximum_fusion), channel_id=1, source_target_pairs={{0,6},{1,7},{2,4},{3,5},{4,2},{5,3},{6,0},{7,1},{8,14},{9,15},{10,... | collective-permute-start | bytes 393224 | tf_op jit(solution)/shard_map/ppermute | solution.py:45
  20.1 0.6 collective-permute-start.4
  20.7 0.1 collective-permute-start.3
  20.8 9.8 %collective-permute-done.3 = bf16[512,128]{1,0:T(8,128)(2,1)S(1)} collective-permute-done((bf16[512,128]{1,0:T(8,128)(2,1)S(1)}, bf16[512,128]{1,0:T(8,128)(2,1)S(1)}, u32[]{:S(2)}, u32[]{:S(2)}) %collective-permute-start.3) | collective-permute-done | bytes 131104 | tf_op jit(solution)/shard_map/ppermute | solution.py:45
  30.6 2.1 %collective-permute-done.4 = bf16[512,128]{1,0:T(8,128)(2,1)S(1)} collective-permute-done((bf16[512,128]{1,0:T(8,128)(2,1)S(1)}, bf16[512,128]{1,0:T(8,128)(2,1)S(1)}, u32[]{:S(2)}, u32[]{:S(2)}) %collective-permute-start.4) | collective-permute-done | bytes 131104 | tf_op jit(solution)/shard_map/ppermute | solution.py:45
  32.8 0.7 turn_panel.1.refs_0_
  33.5 0.1 collective-permute-start.6
  34.9 2.2 %forward_first.1 = (f32[128,128]{1,0:T(8,128)S(1)}, f32[128,128]{1,0:T(8,128)S(1)}) custom-call(s32[16]{0:T(128)S(1)} %broadcast_xor_fusion.sources_ref, s32[2]{0:T(128)S(1)} %iota_xor_fusion.targets_ref, f32[1]{0:T(128)S(6)} %copy.22.center_ref, f32[1]{0:T(128)S(6)} %copy.23.halfwidth_ref, bf16[32,128,128]{2,1,0:T(8,128)(2,1)} %after.1.dense_hbm, ...), custom_call_target="tpu_custom_call" | custom-call | tf_op jit(solution)/shard_map/forward_first/pallas_call | solution.py:168
  37.2 0.6 collective-permute-start.7
  37.7 0.9 %collective-permute-done.7 = f32[128,128]{1,0:T(8,128)S(1)} collective-permute-done((f32[128,128]{1,0:T(8,128)S(1)}, f32[128,128]{1,0:T(8,128)S(1)}, u32[]{:S(2)}, u32[]{:S(2)}) %collective-permute-start.7) | collective-permute-done | bytes 65568 | tf_op jit(solution)/shard_map/ppermute | solution.py:36
  38.6 0.8 %lay_panels.1.turned_ref = bf16[128,4096]{1,0:T(8,128)(2,1)S(1)} custom-call(s32[2]{0:T(128)S(1)} %iota_xor_fusion.targets_ref, bf16[128,2048]{1,0:T(8,128)(2,1)S(1)} %turn_panel.1.refs_0_, bf16[128,2048]{1,0:T(8,128)(2,1)S(1)} %collective-permute-done.6.refs_1_), custom_call_target="tpu_custom_call" | custom-call | tf_op jit(solution)/shard_map/lay_panels/pallas_call | solution.py:217
  39.4 1.4 %all-to-all-done.received_ref = bf16[32,128,128]{2,1,0:T(8,128)(2,1)S(1)} async-done(((bf16[32,128,128]{2,1,0:T(8,128)(2,1)}), bf16[32,128,128]{2,1,0:T(8,128)(2,1)S(1)}, u32[]{:S(2)}, u32[]{:S(2)}) %all-to-all-start) | async-done | bytes 1048608 | tf_op jit(solution)/shard_map/all_to_all | solution.py:369
  40.9 0.5 backward_first.1
  41.3 2.8 %collective-permute-start.8 = (bf16[128,128]{1,0:T(8,128)(2,1)S(1)}, bf16[128,128]{1,0:T(8,128)(2,1)S(1)}, u32[]{:S(2)}, u32[]{:S(2)}) collective-permute-start(bf16[128,128]{1,0:T(8,128)(2,1)S(1)} %get-tuple-element.15), channel_id=1, source_target_pairs={{0,24},{1,7},{2,26},{3,5},{4,28},{5,3},{6,30},{7,1},{8,16},{9,15},... | collective-permute-start | bytes 98312 | tf_op jit(solution)/shard_map/ppermute | solution.py:45
  44.2 1.7 %collective-permute-start.11 = (bf16[128,128]{1,0:T(8,128)(2,1)S(1)}, bf16[128,128]{1,0:T(8,128)(2,1)S(1)}, u32[]{:S(2)}, u32[]{:S(2)}) collective-permute-start(bf16[128,128]{1,0:T(8,128)(2,1)S(1)} %get-tuple-element.15), channel_id=1, source_target_pairs={{0,16},{1,5},{2,18},{3,7},{4,20},{5,1},{6,22},{7,3},{8,24},{9,13},... | collective-permute-start | bytes 98312 | tf_op jit(solution)/shard_map/ppermute | solution.py:45
  45.9 1.2 %collective-permute-done.8.panel_ref = bf16[128,128]{1,0:T(8,128)(2,1)S(1)} collective-permute-done((bf16[128,128]{1,0:T(8,128)(2,1)S(1)}, bf16[128,128]{1,0:T(8,128)(2,1)S(1)}, u32[]{:S(2)}, u32[]{:S(2)}) %collective-permute-start.8) | collective-permute-done | bytes 32800 | tf_op jit(solution)/shard_map/ppermute | solution.py:45
  47.1 0.6 pick_blocks.1
  47.7 0.1 collective-permute-start.9
  47.8 2.0 %collective-permute-done.10 = bf16[128,128]{1,0:T(8,128)(2,1)S(1)} collective-permute-done((bf16[128,128]{1,0:T(8,128)(2,1)S(1)}, bf16[128,128]{1,0:T(8,128)(2,1)S(1)}, u32[]{:S(2)}, u32[]{:S(2)}) %collective-permute-start.10) | collective-permute-done | bytes 32800 | tf_op jit(solution)/shard_map/ppermute | solution.py:45
  49.8 1.6 %collective-permute-start.14 = (bf16[512,128]{1,0:T(8,128)(2,1)S(1)}, bf16[512,128]{1,0:T(8,128)(2,1)S(1)}, u32[]{:S(2)}, u32[]{:S(2)}) collective-permute-start(bf16[512,128]{1,0:T(8,128)(2,1)S(1)} %constant_dynamic-update-slice_fusion.7.refs_0_), channel_id=1, source_target_pairs={{0,6},{1,25},{2,4},{3,27},{4,2},{5,29},{6,0},{7,31},{8,14},{9,17},... | collective-permute-start | bytes 393224 | tf_op jit(solution)/shard_map/ppermute | solution.py:45
  51.5 0.6 collective-permute-start.13
  52.1 1.3 %collective-permute-start.12 = (bf16[512,128]{1,0:T(8,128)(2,1)S(1)}, bf16[512,128]{1,0:T(8,128)(2,1)S(1)}, u32[]{:S(2)}, u32[]{:S(2)}) collective-permute-start(bf16[512,128]{1,0:T(8,128)(2,1)S(1)} %constant_dynamic-update-slice_fusion.7.refs_0_), channel_id=1, source_target_pairs={{0,2},{1,9},{2,0},{3,11},{4,6},{5,13},{6,4},{7,15},{8,10},{9,1},{1... | collective-permute-start | bytes 393224 | tf_op jit(solution)/shard_map/ppermute | solution.py:45
  53.4 2.1 %merge_tile.1.tile_ref = bf16[256,2048]{1,0:T(8,128)(2,1)S(1)} custom-call(s32[16]{0:T(128)S(1)} %xor_bitcast_fusion.sources_ref, s32[2]{0:T(128)S(1)} %iota_xor_fusion.targets_ref, bf16[32,128,128]{2,1,0:T(8,128)(2,1)} %after.1.dense_hbm, bf16[32,128,128]{2,1,0:T(8,128)(2,1)S(1)} %all-to-all-done.received_ref, ...), custom_call_target="tpu_custom_call" | custom-call | tf_op jit(solution)/shard_map/merge_tile/pallas_call | solution.py:289
  55.6 0.3 collective-permute-done.14.refs_3_
  55.9 1.3 %collective-permute-done.13.refs_2_ = bf16[512,128]{1,0:T(8,128)(2,1)S(1)} collective-permute-done((bf16[512,128]{1,0:T(8,128)(2,1)S(1)}, bf16[512,128]{1,0:T(8,128)(2,1)S(1)}, u32[]{:S(2)}, u32[]{:S(2)}) %collective-permute-start.13) | collective-permute-done | bytes 131104 | tf_op jit(solution)/shard_map/ppermute | solution.py:45
  57.2 0.2 collective-permute-done.12.refs_1_
  57.4 0.4 apply_tile.2
  57.9 1.2 %collective-permute-done.15 = f32[128,128]{1,0:T(8,128)S(1)} collective-permute-done((f32[128,128]{1,0:T(8,128)S(1)}, f32[128,128]{1,0:T(8,128)S(1)}, u32[]{:S(2)}, u32[]{:S(2)}) %collective-permute-start.15) | collective-permute-done | bytes 65568 | tf_op jit(solution)/shard_map/ppermute | solution.py:36
  59.1 1.8 %collective-permute-start.18 = (bf16[128,128]{1,0:T(8,128)(2,1)S(1)}, bf16[128,128]{1,0:T(8,128)(2,1)S(1)}, u32[]{:S(2)}, u32[]{:S(2)}) collective-permute-start(bf16[128,128]{1,0:T(8,128)(2,1)S(1)} %get-tuple-element.21), channel_id=1, source_target_pairs={{0,24},{1,7},{2,26},{3,5},{4,28},{5,3},{6,30},{7,1},{8,16},{9,15},... | collective-permute-start | bytes 98312 | tf_op jit(solution)/shard_map/ppermute | solution.py:45
  61.0 0.1 collective-permute-start.17
  61.1 2.5 %collective-permute-start.16 = (bf16[128,128]{1,0:T(8,128)(2,1)S(1)}, bf16[128,128]{1,0:T(8,128)(2,1)S(1)}, u32[]{:S(2)}, u32[]{:S(2)}) collective-permute-start(bf16[128,128]{1,0:T(8,128)(2,1)S(1)} %get-tuple-element.21), channel_id=1, source_target_pairs={{0,8},{1,3},{2,10},{3,1},{4,12},{5,7},{6,14},{7,5},{8,0},{9,11},{1... | collective-permute-start | bytes 98312 | tf_op jit(solution)/shard_map/ppermute | solution.py:45
  63.6 1.3 %collective-permute-done.18 = bf16[128,128]{1,0:T(8,128)(2,1)S(1)} collective-permute-done((bf16[128,128]{1,0:T(8,128)(2,1)S(1)}, bf16[128,128]{1,0:T(8,128)(2,1)S(1)}, u32[]{:S(2)}, u32[]{:S(2)}) %collective-permute-start.18) | collective-permute-done | bytes 32800 | tf_op jit(solution)/shard_map/ppermute | solution.py:45
  64.9 1.2 %collective-permute-done.17 = bf16[128,128]{1,0:T(8,128)(2,1)S(1)} collective-permute-done((bf16[128,128]{1,0:T(8,128)(2,1)S(1)}, bf16[128,128]{1,0:T(8,128)(2,1)S(1)}, u32[]{:S(2)}, u32[]{:S(2)}) %collective-permute-start.17) | collective-permute-done | bytes 32800 | tf_op jit(solution)/shard_map/ppermute | solution.py:45
  66.1 2.1 %collective-permute-start.21 = (bf16[512,128]{1,0:T(8,128)(2,1)S(1)}, bf16[512,128]{1,0:T(8,128)(2,1)S(1)}, u32[]{:S(2)}, u32[]{:S(2)}) collective-permute-start(bf16[512,128]{1,0:T(8,128)(2,1)S(1)} %pad_maximum_fusion.1.refs_0_), channel_id=1, source_target_pairs={{0,6},{1,25},{2,4},{3,27},{4,2},{5,29},{6,0},{7,31},{8,14},{9,17},... | collective-permute-start | bytes 393224 | tf_op jit(solution)/shard_map/ppermute | solution.py:45
  68.2 0.1 collective-permute-start.20
  68.4 1.3 %collective-permute-start.19 = (bf16[512,128]{1,0:T(8,128)(2,1)S(1)}, bf16[512,128]{1,0:T(8,128)(2,1)S(1)}, u32[]{:S(2)}, u32[]{:S(2)}) collective-permute-start(bf16[512,128]{1,0:T(8,128)(2,1)S(1)} %pad_maximum_fusion.1.refs_0_), channel_id=1, source_target_pairs={{0,2},{1,9},{2,0},{3,11},{4,6},{5,13},{6,4},{7,15},{8,10},{9,1},{1... | collective-permute-start | bytes 393224 | tf_op jit(solution)/shard_map/ppermute | solution.py:45
  69.7 2.4 %collective-permute-done.21.refs_3_ = bf16[512,128]{1,0:T(8,128)(2,1)S(1)} collective-permute-done((bf16[512,128]{1,0:T(8,128)(2,1)S(1)}, bf16[512,128]{1,0:T(8,128)(2,1)S(1)}, u32[]{:S(2)}, u32[]{:S(2)}) %collective-permute-start.21) | collective-permute-done | bytes 131104 | tf_op jit(solution)/shard_map/ppermute | solution.py:45
  72.1 1.4 %collective-permute-done.20.refs_2_ = bf16[512,128]{1,0:T(8,128)(2,1)S(1)} collective-permute-done((bf16[512,128]{1,0:T(8,128)(2,1)S(1)}, bf16[512,128]{1,0:T(8,128)(2,1)S(1)}, u32[]{:S(2)}, u32[]{:S(2)}) %collective-permute-start.20) | collective-permute-done | bytes 131104 | tf_op jit(solution)/shard_map/ppermute | solution.py:45
  73.5 0.3 collective-permute-done.19.refs_1_
  73.8 0.4 apply_tile.3
  74.3 1.2 %collective-permute-done.22 = f32[128,128]{1,0:T(8,128)S(1)} collective-permute-done((f32[128,128]{1,0:T(8,128)S(1)}, f32[128,128]{1,0:T(8,128)S(1)}, u32[]{:S(2)}, u32[]{:S(2)}) %collective-permute-start.22) | collective-permute-done | bytes 65568 | tf_op jit(solution)/shard_map/ppermute | solution.py:36
  75.5 0.6 add.20
  (35 shorter events, 0.4 us)
Async XLA Ops:
  0.9 9.1 %collective-permute-start.2 = (bf16[128,128]{1,0:T(8,128)(2,1)S(1)}, bf16[128,128]{1,0:T(8,128)(2,1)S(1)}, u32[]{:S(2)}, u32[]{:S(2)}) collective-permute-start(bf16[128,128]{1,0:T(8,128)(2,1)S(1)} %get-tuple-element.24), channel_id=1, source_target_pairs={{0,24},{1,25},{2,26},{3,27},{4,28},{5,29},{6,30},{7,31},{8,16},{9,... | collective-permute-start | bytes 98312 | tf_op jit(solution)/shard_map/ppermute | solution.py:45
  6.0 4.8 %collective-permute-start.1 = (bf16[128,128]{1,0:T(8,128)(2,1)S(1)}, bf16[128,128]{1,0:T(8,128)(2,1)S(1)}, u32[]{:S(2)}, u32[]{:S(2)}) collective-permute-start(bf16[128,128]{1,0:T(8,128)(2,1)S(1)} %get-tuple-element.24), channel_id=1, source_target_pairs={{0,16},{1,17},{2,18},{3,19},{4,20},{5,21},{6,22},{7,23},{8,24},{9,... | collective-permute-start | bytes 98312 | tf_op jit(solution)/shard_map/ppermute | solution.py:45
  6.0 4.8 %collective-permute-start = (bf16[128,128]{1,0:T(8,128)(2,1)S(1)}, bf16[128,128]{1,0:T(8,128)(2,1)S(1)}, u32[]{:S(2)}, u32[]{:S(2)}) collective-permute-start(bf16[128,128]{1,0:T(8,128)(2,1)S(1)} %get-tuple-element.24), channel_id=1, source_target_pairs={{0,8},{1,9},{2,10},{3,11},{4,12},{5,13},{6,14},{7,15},{8,0},{9,1},... | collective-permute-start | bytes 98312 | tf_op jit(solution)/shard_map/ppermute | solution.py:45
  10.0 7.2 %copy-start.2 = (s32[16]{0:T(128)S(1)}, s32[16]{0:T(128)}, u32[]{:S(2)}) copy-start(s32[16]{0:T(128)} %constant.26.clone) | copy-start | bytes 196
  10.8 24.1 %copy-start = (f32[128,128]{1,0:T(8,128)S(1)}, f32[128,128]{1,0:T(8,128)}, u32[]{:S(2)}) copy-start(f32[128,128]{1,0:T(8,128)} %previous_ref.1) | copy-start | bytes 196612
  10.8 30.1 %all-to-all-start = ((bf16[32,128,128]{2,1,0:T(8,128)(2,1)}), bf16[32,128,128]{2,1,0:T(8,128)(2,1)S(1)}, u32[]{:S(2)}, u32[]{:S(2)}) async-start(bf16[32,128,128]{2,1,0:T(8,128)(2,1)} %after.1.dense_hbm), calls=%async_computation | async-start | bytes 2097152 | tf_op jit(solution)/shard_map/all_to_all | solution.py:369
  17.2 15.5 %collective-permute-start.5 = (bf16[512,128]{1,0:T(8,128)(2,1)S(1)}, bf16[512,128]{1,0:T(8,128)(2,1)S(1)}, u32[]{:S(2)}, u32[]{:S(2)}) collective-permute-start(bf16[512,128]{1,0:T(8,128)(2,1)S(1)} %pad_maximum_fusion), channel_id=1, source_target_pairs={{0,6},{1,7},{2,4},{3,5},{4,2},{5,3},{6,0},{7,1},{8,14},{9,15},{10,... | collective-permute-start | bytes 393224 | tf_op jit(solution)/shard_map/ppermute | solution.py:45
  20.1 12.6 %collective-permute-start.4 = (bf16[512,128]{1,0:T(8,128)(2,1)S(1)}, bf16[512,128]{1,0:T(8,128)(2,1)S(1)}, u32[]{:S(2)}, u32[]{:S(2)}) collective-permute-start(bf16[512,128]{1,0:T(8,128)(2,1)S(1)} %pad_maximum_fusion), channel_id=1, source_target_pairs={{0,4},{1,5},{2,6},{3,7},{4,0},{5,1},{6,2},{7,3},{8,12},{9,13},{10,... | collective-permute-start | bytes 393224 | tf_op jit(solution)/shard_map/ppermute | solution.py:45
  20.7 9.9 %collective-permute-start.3 = (bf16[512,128]{1,0:T(8,128)(2,1)S(1)}, bf16[512,128]{1,0:T(8,128)(2,1)S(1)}, u32[]{:S(2)}, u32[]{:S(2)}) collective-permute-start(bf16[512,128]{1,0:T(8,128)(2,1)S(1)} %pad_maximum_fusion), channel_id=1, source_target_pairs={{0,2},{1,3},{2,0},{3,1},{4,6},{5,7},{6,4},{7,5},{8,10},{9,11},{10,... | collective-permute-start | bytes 393224 | tf_op jit(solution)/shard_map/ppermute | solution.py:45
  33.5 5.1 %collective-permute-start.6 = (bf16[128,2048]{1,0:T(8,128)(2,1)S(1)}, bf16[128,2048]{1,0:T(8,128)(2,1)S(1)}, u32[]{:S(2)}, u32[]{:S(2)}) collective-permute-start(bf16[128,2048]{1,0:T(8,128)(2,1)S(1)} %turn_panel.1.refs_0_), channel_id=1, source_target_pairs={{0,1},{1,0},{2,3},{3,2},{4,5},{5,4},{6,7},{7,6},{8,9},{9,8},{10,11... | collective-permute-start | bytes 1572872 | tf_op jit(solution)/shard_map/ppermute | solution.py:36
  37.2 1.5 %collective-permute-start.7 = (f32[128,128]{1,0:T(8,128)S(1)}, f32[128,128]{1,0:T(8,128)S(1)}, u32[]{:S(2)}, u32[]{:S(2)}) collective-permute-start(f32[128,128]{1,0:T(8,128)S(1)} %get-tuple-element.14), channel_id=1, source_target_pairs={{0,1},{1,0},{2,3},{3,2},{4,5},{5,4},{6,7},{7,6},{8,9},{9,8},{10,11... | collective-permute-start | bytes 196616 | tf_op jit(solution)/shard_map/ppermute | solution.py:36
  39.4 14.0 %copy-start.1 = (s32[2,16]{1,0:T(2,128)S(1)}, s32[2,16]{1,0:T(2,128)}, u32[]{:S(2)}) copy-start(s32[2,16]{1,0:T(2,128)} %constant.27.clone) | copy-start | bytes 388
  41.3 5.8 %collective-permute-start.8 = (bf16[128,128]{1,0:T(8,128)(2,1)S(1)}, bf16[128,128]{1,0:T(8,128)(2,1)S(1)}, u32[]{:S(2)}, u32[]{:S(2)}) collective-permute-start(bf16[128,128]{1,0:T(8,128)(2,1)S(1)} %get-tuple-element.15), channel_id=1, source_target_pairs={{0,24},{1,7},{2,26},{3,5},{4,28},{5,3},{6,30},{7,1},{8,16},{9,15},... | collective-permute-start | bytes 98312 | tf_op jit(solution)/shard_map/ppermute | solution.py:45
  44.2 5.6 %collective-permute-start.11 = (bf16[128,128]{1,0:T(8,128)(2,1)S(1)}, bf16[128,128]{1,0:T(8,128)(2,1)S(1)}, u32[]{:S(2)}, u32[]{:S(2)}) collective-permute-start(bf16[128,128]{1,0:T(8,128)(2,1)S(1)} %get-tuple-element.15), channel_id=1, source_target_pairs={{0,16},{1,5},{2,18},{3,7},{4,20},{5,1},{6,22},{7,3},{8,24},{9,13},... | collective-permute-start | bytes 98312 | tf_op jit(solution)/shard_map/ppermute | solution.py:45
  45.9 3.9 %collective-permute-start.10 = (bf16[128,128]{1,0:T(8,128)(2,1)S(1)}, bf16[128,128]{1,0:T(8,128)(2,1)S(1)}, u32[]{:S(2)}, u32[]{:S(2)}) collective-permute-start(bf16[128,128]{1,0:T(8,128)(2,1)S(1)} %get-tuple-element.15), channel_id=1, source_target_pairs={{0,8},{1,3},{2,10},{3,1},{4,12},{5,7},{6,14},{7,5},{8,0},{9,11},{1... | collective-permute-start | bytes 98312 | tf_op jit(solution)/shard_map/ppermute | solution.py:45
  47.7 5.7 %collective-permute-start.9 = (bf16[16,128,128]{2,1,0:T(8,128)(2,1)S(1)}, bf16[16,128,128]{2,1,0:T(8,128)(2,1)S(1)}, u32[]{:S(2)}, u32[]{:S(2)}) collective-permute-start(bf16[16,128,128]{2,1,0:T(8,128)(2,1)S(1)} %pick_blocks.1), channel_id=1, source_target_pairs={{0,1},{1,0},{2,3},{3,2},{4,5},{5,4},{6,7},{7,6},{8,9},{9,8},{10,11... | collective-permute-start | bytes 1572872 | tf_op jit(solution)/shard_map/ppermute | solution.py:36
  49.8 6.0 %collective-permute-start.14 = (bf16[512,128]{1,0:T(8,128)(2,1)S(1)}, bf16[512,128]{1,0:T(8,128)(2,1)S(1)}, u32[]{:S(2)}, u32[]{:S(2)}) collective-permute-start(bf16[512,128]{1,0:T(8,128)(2,1)S(1)} %constant_dynamic-update-slice_fusion.7.refs_0_), channel_id=1, source_target_pairs={{0,6},{1,25},{2,4},{3,27},{4,2},{5,29},{6,0},{7,31},{8,14},{9,17},... | collective-permute-start | bytes 393224 | tf_op jit(solution)/shard_map/ppermute | solution.py:45
  51.5 5.7 %collective-permute-start.13 = (bf16[512,128]{1,0:T(8,128)(2,1)S(1)}, bf16[512,128]{1,0:T(8,128)(2,1)S(1)}, u32[]{:S(2)}, u32[]{:S(2)}) collective-permute-start(bf16[512,128]{1,0:T(8,128)(2,1)S(1)} %constant_dynamic-update-slice_fusion.7.refs_0_), channel_id=1, source_target_pairs={{0,4},{1,17},{2,6},{3,19},{4,0},{5,21},{6,2},{7,23},{8,12},{9,25},... | collective-permute-start | bytes 393224 | tf_op jit(solution)/shard_map/ppermute | solution.py:45
  52.1 5.3 %collective-permute-start.12 = (bf16[512,128]{1,0:T(8,128)(2,1)S(1)}, bf16[512,128]{1,0:T(8,128)(2,1)S(1)}, u32[]{:S(2)}, u32[]{:S(2)}) collective-permute-start(bf16[512,128]{1,0:T(8,128)(2,1)S(1)} %constant_dynamic-update-slice_fusion.7.refs_0_), channel_id=1, source_target_pairs={{0,2},{1,9},{2,0},{3,11},{4,6},{5,13},{6,4},{7,15},{8,10},{9,1},{1... | collective-permute-start | bytes 393224 | tf_op jit(solution)/shard_map/ppermute | solution.py:45
  57.8 1.3 %collective-permute-start.15 = (f32[128,128]{1,0:T(8,128)S(1)}, f32[128,128]{1,0:T(8,128)S(1)}, u32[]{:S(2)}, u32[]{:S(2)}) collective-permute-start(f32[128,128]{1,0:T(8,128)S(1)} %get-tuple-element.18), channel_id=1, source_target_pairs={{0,1},{1,0},{2,3},{3,2},{4,5},{5,4},{6,7},{7,6},{8,9},{9,8},{10,11... | collective-permute-start | bytes 196616 | tf_op jit(solution)/shard_map/ppermute | solution.py:36
  59.1 5.8 %collective-permute-start.18 = (bf16[128,128]{1,0:T(8,128)(2,1)S(1)}, bf16[128,128]{1,0:T(8,128)(2,1)S(1)}, u32[]{:S(2)}, u32[]{:S(2)}) collective-permute-start(bf16[128,128]{1,0:T(8,128)(2,1)S(1)} %get-tuple-element.21), channel_id=1, source_target_pairs={{0,24},{1,7},{2,26},{3,5},{4,28},{5,3},{6,30},{7,1},{8,16},{9,15},... | collective-permute-start | bytes 98312 | tf_op jit(solution)/shard_map/ppermute | solution.py:45
  61.0 5.2 %collective-permute-start.17 = (bf16[128,128]{1,0:T(8,128)(2,1)S(1)}, bf16[128,128]{1,0:T(8,128)(2,1)S(1)}, u32[]{:S(2)}, u32[]{:S(2)}) collective-permute-start(bf16[128,128]{1,0:T(8,128)(2,1)S(1)} %get-tuple-element.21), channel_id=1, source_target_pairs={{0,16},{1,5},{2,18},{3,7},{4,20},{5,1},{6,22},{7,3},{8,24},{9,13},... | collective-permute-start | bytes 98312 | tf_op jit(solution)/shard_map/ppermute | solution.py:45
  61.1 5.1 %collective-permute-start.16 = (bf16[128,128]{1,0:T(8,128)(2,1)S(1)}, bf16[128,128]{1,0:T(8,128)(2,1)S(1)}, u32[]{:S(2)}, u32[]{:S(2)}) collective-permute-start(bf16[128,128]{1,0:T(8,128)(2,1)S(1)} %get-tuple-element.21), channel_id=1, source_target_pairs={{0,8},{1,3},{2,10},{3,1},{4,12},{5,7},{6,14},{7,5},{8,0},{9,11},{1... | collective-permute-start | bytes 98312 | tf_op jit(solution)/shard_map/ppermute | solution.py:45
  66.1 6.0 %collective-permute-start.21 = (bf16[512,128]{1,0:T(8,128)(2,1)S(1)}, bf16[512,128]{1,0:T(8,128)(2,1)S(1)}, u32[]{:S(2)}, u32[]{:S(2)}) collective-permute-start(bf16[512,128]{1,0:T(8,128)(2,1)S(1)} %pad_maximum_fusion.1.refs_0_), channel_id=1, source_target_pairs={{0,6},{1,25},{2,4},{3,27},{4,2},{5,29},{6,0},{7,31},{8,14},{9,17},... | collective-permute-start | bytes 393224 | tf_op jit(solution)/shard_map/ppermute | solution.py:45
  68.2 5.2 %collective-permute-start.20 = (bf16[512,128]{1,0:T(8,128)(2,1)S(1)}, bf16[512,128]{1,0:T(8,128)(2,1)S(1)}, u32[]{:S(2)}, u32[]{:S(2)}) collective-permute-start(bf16[512,128]{1,0:T(8,128)(2,1)S(1)} %pad_maximum_fusion.1.refs_0_), channel_id=1, source_target_pairs={{0,4},{1,17},{2,6},{3,19},{4,0},{5,21},{6,2},{7,23},{8,12},{9,25},... | collective-permute-start | bytes 393224 | tf_op jit(solution)/shard_map/ppermute | solution.py:45
  68.4 5.4 %collective-permute-start.19 = (bf16[512,128]{1,0:T(8,128)(2,1)S(1)}, bf16[512,128]{1,0:T(8,128)(2,1)S(1)}, u32[]{:S(2)}, u32[]{:S(2)}) collective-permute-start(bf16[512,128]{1,0:T(8,128)(2,1)S(1)} %pad_maximum_fusion.1.refs_0_), channel_id=1, source_target_pairs={{0,2},{1,9},{2,0},{3,11},{4,6},{5,13},{6,4},{7,15},{8,10},{9,1},{1... | collective-permute-start | bytes 393224 | tf_op jit(solution)/shard_map/ppermute | solution.py:45
  74.2 1.3 %collective-permute-start.22 = (f32[128,128]{1,0:T(8,128)S(1)}, f32[128,128]{1,0:T(8,128)S(1)}, u32[]{:S(2)}, u32[]{:S(2)}) collective-permute-start(f32[128,128]{1,0:T(8,128)S(1)} %get-tuple-element.20), channel_id=1, source_target_pairs={{0,1},{1,0},{2,3},{3,2},{4,5},{5,4},{6,7},{7,6},{8,9},{9,8},{10,11... | collective-permute-start | bytes 196616 | tf_op jit(solution)/shard_map/ppermute | solution.py:36

commit v17 on v12

--- a/solution.py
+++ b/solution.py
@@ -7,7 +7,7 @@
 
 DEGREE = 3
 RADIX = 4
-CHUNK = 8
+CHUNK = 16
 SPARE = 4 * 2**20
 
 VMEM = pl.BlockSpec(memory_space=pltpu.VMEM)

time: 76.6 us -> 76.6 us (level)
  no operation moved by 1% of the time
where the time goes in v17:
time: 76.6 us; the launch traced here: 76.2 us
  starting transfers between devices  32.7 us (43%)
  waiting for transfers between devices  29.1 us (38%)
  Pallas kernels  10.5 us (14%)
  between operations  2.21 us (3%)
  other arithmetic  1.55 us (2%)
    ppermute x18, starting transfers between devices, swap_rows(): return lax.ppermute(x, ('row', 'col'), pairs)  25.4 us
    ppermute x18, waiting for transfers between devices, swap_rows(): return lax.ppermute(x, ('row', 'col'), pairs)  24.3 us
    all_to_all x1, starting transfers between devices, body(): received = lax.all_to_all(dense, 'row', 0, 0, tiled=True)  6.45 us
    ppermute x5, waiting for transfers between devices, swap(): lax.ppermute(x, axis, [(source, source ^ offset) for source in range(size)])  3.39 us
    pallas_call x1, Pallas kernels, build_tile(): pl.pallas_call(kernel, in_specs=[HBM, HBM, SMEM, HBM], out_specs=HBM, scr...  2.75 us
    pallas_call x1, Pallas kernels, forward_first(): pl.pallas_call(kernel, in_specs=[SMEM] * 4 + [HBM] + [VMEM] * 2, out_spec...  2.21 us
    pallas_call x1, Pallas kernels, merge_tile(): pl.pallas_call(kernel, in_specs=[SMEM] * 2 + [HBM] + [VMEM] * grid_cols,...  2.14 us
  transfers between devices with their start and end apart: 24, of which 17 were waited for; matrix products, arithmetic and copies ran while one was open for 0% of the time, Pallas kernels for 12%

profile of v17, /device:TPU:0, one launch (start us, length us, event | category | flops | bytes accessed | tf_op | source)
XLA Modules:
  0.0 76.2 jit_solution(15713651244889730569)
XLA Ops:
  0.0 0.8 %constant_dynamic-update-slice_fusion.6 = (bf16[2048,128]{1,0:T(8,128)(2,1)S(1)}, bf16[128,128]{1,0:T(8,128)(2,1)S(1)}) fusion(f32[128,128]{1,0:T(8,128)} %previous_ref.1), kind=kLoop, calls=%fused_computation.8 | loop fusion | flops 16383 | bytes 131072
  0.9 5.1 %collective-permute-start.2 = (bf16[128,128]{1,0:T(8,128)(2,1)S(1)}, bf16[128,128]{1,0:T(8,128)(2,1)S(1)}, u32[]{:S(2)}, u32[]{:S(2)}) collective-permute-start(bf16[128,128]{1,0:T(8,128)(2,1)S(1)} %get-tuple-element.24), channel_id=1, source_target_pairs={{0,24},{1,25},{2,26},{3,27},{4,28},{5,29},{6,30},{7,31},{8,16},{9,... | collective-permute-start | bytes 98312 | tf_op jit(solution)/shard_map/ppermute | solution.py:45
  6.0 0.6 collective-permute-start
  7.3 2.8 %build_tile.1.refs_0_ = bf16[32,128,128]{2,1,0:T(8,128)(2,1)} custom-call(s32[1,64]{1,0:T(1,128)} %bitcast.6, s32[1,64]{1,0:T(1,128)} %bitcast.7, s32[1,1]{1,0:T(1,128)S(6)} %copy.21.count_ref, bf16[64,128,128]{2,1,0:T(8,128)(2,1)} %bitcast.5), custom_call_target="tpu_custom_call" | custom-call | tf_op jit(solution)/shard_map/build_tile/pallas_call | solution.py:90
  10.0 0.7 collective-permute-done.1.refs_2_
  10.8 6.5 %all-to-all-start = ((bf16[32,128,128]{2,1,0:T(8,128)(2,1)}), bf16[32,128,128]{2,1,0:T(8,128)(2,1)S(1)}, u32[]{:S(2)}, u32[]{:S(2)}) async-start(bf16[32,128,128]{2,1,0:T(8,128)(2,1)} %after.1.dense_hbm), calls=%async_computation | async-start | bytes 2097152 | tf_op jit(solution)/shard_map/all_to_all | solution.py:367
  17.3 2.9 %collective-permute-start.5 = (bf16[512,128]{1,0:T(8,128)(2,1)S(1)}, bf16[512,128]{1,0:T(8,128)(2,1)S(1)}, u32[]{:S(2)}, u32[]{:S(2)}) collective-permute-start(bf16[512,128]{1,0:T(8,128)(2,1)S(1)} %pad_maximum_fusion), channel_id=1, source_target_pairs={{0,6},{1,7},{2,4},{3,5},{4,2},{5,3},{6,0},{7,1},{8,14},{9,15},{10,... | collective-permute-start | bytes 393224 | tf_op jit(solution)/shard_map/ppermute | solution.py:45
  20.2 0.6 collective-permute-start.4
  20.7 0.1 collective-permute-start.3
  20.9 9.8 %collective-permute-done.3 = bf16[512,128]{1,0:T(8,128)(2,1)S(1)} collective-permute-done((bf16[512,128]{1,0:T(8,128)(2,1)S(1)}, bf16[512,128]{1,0:T(8,128)(2,1)S(1)}, u32[]{:S(2)}, u32[]{:S(2)}) %collective-permute-start.3) | collective-permute-done | bytes 131104 | tf_op jit(solution)/shard_map/ppermute | solution.py:45
  30.7 2.1 %collective-permute-done.4 = bf16[512,128]{1,0:T(8,128)(2,1)S(1)} collective-permute-done((bf16[512,128]{1,0:T(8,128)(2,1)S(1)}, bf16[512,128]{1,0:T(8,128)(2,1)S(1)}, u32[]{:S(2)}, u32[]{:S(2)}) %collective-permute-start.4) | collective-permute-done | bytes 131104 | tf_op jit(solution)/shard_map/ppermute | solution.py:45
  32.9 0.7 turn_panel.1.refs_0_
  33.6 0.1 collective-permute-start.6
  35.0 2.2 %forward_first.1 = (f32[128,128]{1,0:T(8,128)S(1)}, f32[128,128]{1,0:T(8,128)S(1)}) custom-call(s32[16]{0:T(128)S(1)} %broadcast_xor_fusion.sources_ref, s32[2]{0:T(128)S(1)} %iota_xor_fusion.targets_ref, f32[1]{0:T(128)S(6)} %copy.22.center_ref, f32[1]{0:T(128)S(6)} %copy.23.halfwidth_ref, bf16[32,128,128]{2,1,0:T(8,128)(2,1)} %after.1.dense_hbm, ...), custom_call_target="tpu_custom_call" | custom-call | tf_op jit(solution)/shard_map/forward_first/pallas_call | solution.py:168
  37.2 0.6 collective-permute-start.7
  37.8 0.9 %collective-permute-done.7 = f32[128,128]{1,0:T(8,128)S(1)} collective-permute-done((f32[128,128]{1,0:T(8,128)S(1)}, f32[128,128]{1,0:T(8,128)S(1)}, u32[]{:S(2)}, u32[]{:S(2)}) %collective-permute-start.7) | collective-permute-done | bytes 65568 | tf_op jit(solution)/shard_map/ppermute | solution.py:36
  38.7 0.8 %lay_panels.1.turned_ref = bf16[128,4096]{1,0:T(8,128)(2,1)S(1)} custom-call(s32[2]{0:T(128)S(1)} %iota_xor_fusion.targets_ref, bf16[128,2048]{1,0:T(8,128)(2,1)S(1)} %turn_panel.1.refs_0_, bf16[128,2048]{1,0:T(8,128)(2,1)S(1)} %collective-permute-done.6.refs_1_), custom_call_target="tpu_custom_call" | custom-call | tf_op jit(solution)/shard_map/lay_panels/pallas_call | solution.py:217
  39.5 1.4 %all-to-all-done.received_ref = bf16[32,128,128]{2,1,0:T(8,128)(2,1)S(1)} async-done(((bf16[32,128,128]{2,1,0:T(8,128)(2,1)}), bf16[32,128,128]{2,1,0:T(8,128)(2,1)S(1)}, u32[]{:S(2)}, u32[]{:S(2)}) %all-to-all-start) | async-done | bytes 1048608 | tf_op jit(solution)/shard_map/all_to_all | solution.py:367
  40.9 0.5 backward_first.1
  41.4 2.8 %collective-permute-start.8 = (bf16[128,128]{1,0:T(8,128)(2,1)S(1)}, bf16[128,128]{1,0:T(8,128)(2,1)S(1)}, u32[]{:S(2)}, u32[]{:S(2)}) collective-permute-start(bf16[128,128]{1,0:T(8,128)(2,1)S(1)} %get-tuple-element.15), channel_id=1, source_target_pairs={{0,24},{1,7},{2,26},{3,5},{4,28},{5,3},{6,30},{7,1},{8,16},{9,15},... | collective-permute-start | bytes 98312 | tf_op jit(solution)/shard_map/ppermute | solution.py:45
  44.3 1.7 %collective-permute-start.11 = (bf16[128,128]{1,0:T(8,128)(2,1)S(1)}, bf16[128,128]{1,0:T(8,128)(2,1)S(1)}, u32[]{:S(2)}, u32[]{:S(2)}) collective-permute-start(bf16[128,128]{1,0:T(8,128)(2,1)S(1)} %get-tuple-element.15), channel_id=1, source_target_pairs={{0,16},{1,5},{2,18},{3,7},{4,20},{5,1},{6,22},{7,3},{8,24},{9,13},... | collective-permute-start | bytes 98312 | tf_op jit(solution)/shard_map/ppermute | solution.py:45
  45.9 1.2 %collective-permute-done.8.panel_ref = bf16[128,128]{1,0:T(8,128)(2,1)S(1)} collective-permute-done((bf16[128,128]{1,0:T(8,128)(2,1)S(1)}, bf16[128,128]{1,0:T(8,128)(2,1)S(1)}, u32[]{:S(2)}, u32[]{:S(2)}) %collective-permute-start.8) | collective-permute-done | bytes 32800 | tf_op jit(solution)/shard_map/ppermute | solution.py:45
  47.2 0.6 pick_blocks.1
  47.9 2.0 %collective-permute-done.10 = bf16[128,128]{1,0:T(8,128)(2,1)S(1)} collective-permute-done((bf16[128,128]{1,0:T(8,128)(2,1)S(1)}, bf16[128,128]{1,0:T(8,128)(2,1)S(1)}, u32[]{:S(2)}, u32[]{:S(2)}) %collective-permute-start.10) | collective-permute-done | bytes 32800 | tf_op jit(solution)/shard_map/ppermute | solution.py:45
  49.9 1.6 %collective-permute-start.14 = (bf16[512,128]{1,0:T(8,128)(2,1)S(1)}, bf16[512,128]{1,0:T(8,128)(2,1)S(1)}, u32[]{:S(2)}, u32[]{:S(2)}) collective-permute-start(bf16[512,128]{1,0:T(8,128)(2,1)S(1)} %constant_dynamic-update-slice_fusion.7.refs_0_), channel_id=1, source_target_pairs={{0,6},{1,25},{2,4},{3,27},{4,2},{5,29},{6,0},{7,31},{8,14},{9,17},... | collective-permute-start | bytes 393224 | tf_op jit(solution)/shard_map/ppermute | solution.py:45
  51.5 0.6 collective-permute-start.13
  52.1 1.3 %collective-permute-start.12 = (bf16[512,128]{1,0:T(8,128)(2,1)S(1)}, bf16[512,128]{1,0:T(8,128)(2,1)S(1)}, u32[]{:S(2)}, u32[]{:S(2)}) collective-permute-start(bf16[512,128]{1,0:T(8,128)(2,1)S(1)} %constant_dynamic-update-slice_fusion.7.refs_0_), channel_id=1, source_target_pairs={{0,2},{1,9},{2,0},{3,11},{4,6},{5,13},{6,4},{7,15},{8,10},{9,1},{1... | collective-permute-start | bytes 393224 | tf_op jit(solution)/shard_map/ppermute | solution.py:45
  53.5 2.1 %merge_tile.1.tile_ref = bf16[256,2048]{1,0:T(8,128)(2,1)S(1)} custom-call(s32[16]{0:T(128)S(1)} %xor_bitcast_fusion.sources_ref, s32[2]{0:T(128)S(1)} %iota_xor_fusion.targets_ref, bf16[32,128,128]{2,1,0:T(8,128)(2,1)} %after.1.dense_hbm, bf16[32,128,128]{2,1,0:T(8,128)(2,1)S(1)} %all-to-all-done.received_ref, ...), custom_call_target="tpu_custom_call" | custom-call | tf_op jit(solution)/shard_map/merge_tile/pallas_call | solution.py:289
  55.6 0.3 collective-permute-done.14.refs_3_
  55.9 1.3 %collective-permute-done.13.refs_2_ = bf16[512,128]{1,0:T(8,128)(2,1)S(1)} collective-permute-done((bf16[512,128]{1,0:T(8,128)(2,1)S(1)}, bf16[512,128]{1,0:T(8,128)(2,1)S(1)}, u32[]{:S(2)}, u32[]{:S(2)}) %collective-permute-start.13) | collective-permute-done | bytes 131104 | tf_op jit(solution)/shard_map/ppermute | solution.py:45
  57.2 0.2 collective-permute-done.12.refs_1_
  57.4 0.4 apply_tile.2
  57.9 1.2 %collective-permute-done.15 = f32[128,128]{1,0:T(8,128)S(1)} collective-permute-done((f32[128,128]{1,0:T(8,128)S(1)}, f32[128,128]{1,0:T(8,128)S(1)}, u32[]{:S(2)}, u32[]{:S(2)}) %collective-permute-start.15) | collective-permute-done | bytes 65568 | tf_op jit(solution)/shard_map/ppermute | solution.py:36
  59.2 1.8 %collective-permute-start.18 = (bf16[128,128]{1,0:T(8,128)(2,1)S(1)}, bf16[128,128]{1,0:T(8,128)(2,1)S(1)}, u32[]{:S(2)}, u32[]{:S(2)}) collective-permute-start(bf16[128,128]{1,0:T(8,128)(2,1)S(1)} %get-tuple-element.21), channel_id=1, source_target_pairs={{0,24},{1,7},{2,26},{3,5},{4,28},{5,3},{6,30},{7,1},{8,16},{9,15},... | collective-permute-start | bytes 98312 | tf_op jit(solution)/shard_map/ppermute | solution.py:45
  61.0 0.1 collective-permute-start.17
  61.1 2.5 %collective-permute-start.16 = (bf16[128,128]{1,0:T(8,128)(2,1)S(1)}, bf16[128,128]{1,0:T(8,128)(2,1)S(1)}, u32[]{:S(2)}, u32[]{:S(2)}) collective-permute-start(bf16[128,128]{1,0:T(8,128)(2,1)S(1)} %get-tuple-element.21), channel_id=1, source_target_pairs={{0,8},{1,3},{2,10},{3,1},{4,12},{5,7},{6,14},{7,5},{8,0},{9,11},{1... | collective-permute-start | bytes 98312 | tf_op jit(solution)/shard_map/ppermute | solution.py:45
  63.7 1.3 %collective-permute-done.18 = bf16[128,128]{1,0:T(8,128)(2,1)S(1)} collective-permute-done((bf16[128,128]{1,0:T(8,128)(2,1)S(1)}, bf16[128,128]{1,0:T(8,128)(2,1)S(1)}, u32[]{:S(2)}, u32[]{:S(2)}) %collective-permute-start.18) | collective-permute-done | bytes 32800 | tf_op jit(solution)/shard_map/ppermute | solution.py:45
  65.0 1.2 %collective-permute-done.17 = bf16[128,128]{1,0:T(8,128)(2,1)S(1)} collective-permute-done((bf16[128,128]{1,0:T(8,128)(2,1)S(1)}, bf16[128,128]{1,0:T(8,128)(2,1)S(1)}, u32[]{:S(2)}, u32[]{:S(2)}) %collective-permute-start.17) | collective-permute-done | bytes 32800 | tf_op jit(solution)/shard_map/ppermute | solution.py:45
  66.2 2.1 %collective-permute-start.21 = (bf16[512,128]{1,0:T(8,128)(2,1)S(1)}, bf16[512,128]{1,0:T(8,128)(2,1)S(1)}, u32[]{:S(2)}, u32[]{:S(2)}) collective-permute-start(bf16[512,128]{1,0:T(8,128)(2,1)S(1)} %pad_maximum_fusion.1.refs_0_), channel_id=1, source_target_pairs={{0,6},{1,25},{2,4},{3,27},{4,2},{5,29},{6,0},{7,31},{8,14},{9,17},... | collective-permute-start | bytes 393224 | tf_op jit(solution)/shard_map/ppermute | solution.py:45
  68.3 0.1 collective-permute-start.20
  68.4 1.3 %collective-permute-start.19 = (bf16[512,128]{1,0:T(8,128)(2,1)S(1)}, bf16[512,128]{1,0:T(8,128)(2,1)S(1)}, u32[]{:S(2)}, u32[]{:S(2)}) collective-permute-start(bf16[512,128]{1,0:T(8,128)(2,1)S(1)} %pad_maximum_fusion.1.refs_0_), channel_id=1, source_target_pairs={{0,2},{1,9},{2,0},{3,11},{4,6},{5,13},{6,4},{7,15},{8,10},{9,1},{1... | collective-permute-start | bytes 393224 | tf_op jit(solution)/shard_map/ppermute | solution.py:45
  69.8 2.4 %collective-permute-done.21.refs_3_ = bf16[512,128]{1,0:T(8,128)(2,1)S(1)} collective-permute-done((bf16[512,128]{1,0:T(8,128)(2,1)S(1)}, bf16[512,128]{1,0:T(8,128)(2,1)S(1)}, u32[]{:S(2)}, u32[]{:S(2)}) %collective-permute-start.21) | collective-permute-done | bytes 131104 | tf_op jit(solution)/shard_map/ppermute | solution.py:45
  72.2 1.4 %collective-permute-done.20.refs_2_ = bf16[512,128]{1,0:T(8,128)(2,1)S(1)} collective-permute-done((bf16[512,128]{1,0:T(8,128)(2,1)S(1)}, bf16[512,128]{1,0:T(8,128)(2,1)S(1)}, u32[]{:S(2)}, u32[]{:S(2)}) %collective-permute-start.20) | collective-permute-done | bytes 131104 | tf_op jit(solution)/shard_map/ppermute | solution.py:45
  73.5 0.3 collective-permute-done.19.refs_1_
  73.8 0.4 apply_tile.3
  74.3 0.1 collective-permute-start.22
  74.3 1.2 %collective-permute-done.22 = f32[128,128]{1,0:T(8,128)S(1)} collective-permute-done((f32[128,128]{1,0:T(8,128)S(1)}, f32[128,128]{1,0:T(8,128)S(1)}, u32[]{:S(2)}, u32[]{:S(2)}) %collective-permute-start.22) | collective-permute-done | bytes 65568 | tf_op jit(solution)/shard_map/ppermute | solution.py:36
  75.6 0.6 add.20
  (35 shorter events, 0.4 us)
Async XLA Ops:
  0.9 9.2 %collective-permute-start.2 = (bf16[128,128]{1,0:T(8,128)(2,1)S(1)}, bf16[128,128]{1,0:T(8,128)(2,1)S(1)}, u32[]{:S(2)}, u32[]{:S(2)}) collective-permute-start(bf16[128,128]{1,0:T(8,128)(2,1)S(1)} %get-tuple-element.24), channel_id=1, source_target_pairs={{0,24},{1,25},{2,26},{3,27},{4,28},{5,29},{6,30},{7,31},{8,16},{9,... | collective-permute-start | bytes 98312 | tf_op jit(solution)/shard_map/ppermute | solution.py:45
  6.0 4.8 %collective-permute-start.1 = (bf16[128,128]{1,0:T(8,128)(2,1)S(1)}, bf16[128,128]{1,0:T(8,128)(2,1)S(1)}, u32[]{:S(2)}, u32[]{:S(2)}) collective-permute-start(bf16[128,128]{1,0:T(8,128)(2,1)S(1)} %get-tuple-element.24), channel_id=1, source_target_pairs={{0,16},{1,17},{2,18},{3,19},{4,20},{5,21},{6,22},{7,23},{8,24},{9,... | collective-permute-start | bytes 98312 | tf_op jit(solution)/shard_map/ppermute | solution.py:45
  6.0 4.8 %collective-permute-start = (bf16[128,128]{1,0:T(8,128)(2,1)S(1)}, bf16[128,128]{1,0:T(8,128)(2,1)S(1)}, u32[]{:S(2)}, u32[]{:S(2)}) collective-permute-start(bf16[128,128]{1,0:T(8,128)(2,1)S(1)} %get-tuple-element.24), channel_id=1, source_target_pairs={{0,8},{1,9},{2,10},{3,11},{4,12},{5,13},{6,14},{7,15},{8,0},{9,1},... | collective-permute-start | bytes 98312 | tf_op jit(solution)/shard_map/ppermute | solution.py:45
  10.0 7.2 %copy-start.2 = (s32[16]{0:T(128)S(1)}, s32[16]{0:T(128)}, u32[]{:S(2)}) copy-start(s32[16]{0:T(128)} %constant.26.clone) | copy-start | bytes 196
  10.8 24.2 %copy-start = (f32[128,128]{1,0:T(8,128)S(1)}, f32[128,128]{1,0:T(8,128)}, u32[]{:S(2)}) copy-start(f32[128,128]{1,0:T(8,128)} %previous_ref.1) | copy-start | bytes 196612
  10.8 30.1 %all-to-all-start = ((bf16[32,128,128]{2,1,0:T(8,128)(2,1)}), bf16[32,128,128]{2,1,0:T(8,128)(2,1)S(1)}, u32[]{:S(2)}, u32[]{:S(2)}) async-start(bf16[32,128,128]{2,1,0:T(8,128)(2,1)} %after.1.dense_hbm), calls=%async_computation | async-start | bytes 2097152 | tf_op jit(solution)/shard_map/all_to_all | solution.py:367
  17.3 15.5 %collective-permute-start.5 = (bf16[512,128]{1,0:T(8,128)(2,1)S(1)}, bf16[512,128]{1,0:T(8,128)(2,1)S(1)}, u32[]{:S(2)}, u32[]{:S(2)}) collective-permute-start(bf16[512,128]{1,0:T(8,128)(2,1)S(1)} %pad_maximum_fusion), channel_id=1, source_target_pairs={{0,6},{1,7},{2,4},{3,5},{4,2},{5,3},{6,0},{7,1},{8,14},{9,15},{10,... | collective-permute-start | bytes 393224 | tf_op jit(solution)/shard_map/ppermute | solution.py:45
  20.2 12.6 %collective-permute-start.4 = (bf16[512,128]{1,0:T(8,128)(2,1)S(1)}, bf16[512,128]{1,0:T(8,128)(2,1)S(1)}, u32[]{:S(2)}, u32[]{:S(2)}) collective-permute-start(bf16[512,128]{1,0:T(8,128)(2,1)S(1)} %pad_maximum_fusion), channel_id=1, source_target_pairs={{0,4},{1,5},{2,6},{3,7},{4,0},{5,1},{6,2},{7,3},{8,12},{9,13},{10,... | collective-permute-start | bytes 393224 | tf_op jit(solution)/shard_map/ppermute | solution.py:45
  20.7 9.9 %collective-permute-start.3 = (bf16[512,128]{1,0:T(8,128)(2,1)S(1)}, bf16[512,128]{1,0:T(8,128)(2,1)S(1)}, u32[]{:S(2)}, u32[]{:S(2)}) collective-permute-start(bf16[512,128]{1,0:T(8,128)(2,1)S(1)} %pad_maximum_fusion), channel_id=1, source_target_pairs={{0,2},{1,3},{2,0},{3,1},{4,6},{5,7},{6,4},{7,5},{8,10},{9,11},{10,... | collective-permute-start | bytes 393224 | tf_op jit(solution)/shard_map/ppermute | solution.py:45
  33.6 5.1 %collective-permute-start.6 = (bf16[128,2048]{1,0:T(8,128)(2,1)S(1)}, bf16[128,2048]{1,0:T(8,128)(2,1)S(1)}, u32[]{:S(2)}, u32[]{:S(2)}) collective-permute-start(bf16[128,2048]{1,0:T(8,128)(2,1)S(1)} %turn_panel.1.refs_0_), channel_id=1, source_target_pairs={{0,1},{1,0},{2,3},{3,2},{4,5},{5,4},{6,7},{7,6},{8,9},{9,8},{10,11... | collective-permute-start | bytes 1572872 | tf_op jit(solution)/shard_map/ppermute | solution.py:36
  37.2 1.5 %collective-permute-start.7 = (f32[128,128]{1,0:T(8,128)S(1)}, f32[128,128]{1,0:T(8,128)S(1)}, u32[]{:S(2)}, u32[]{:S(2)}) collective-permute-start(f32[128,128]{1,0:T(8,128)S(1)} %get-tuple-element.14), channel_id=1, source_target_pairs={{0,1},{1,0},{2,3},{3,2},{4,5},{5,4},{6,7},{7,6},{8,9},{9,8},{10,11... | collective-permute-start | bytes 196616 | tf_op jit(solution)/shard_map/ppermute | solution.py:36
  39.5 14.0 %copy-start.1 = (s32[2,16]{1,0:T(2,128)S(1)}, s32[2,16]{1,0:T(2,128)}, u32[]{:S(2)}) copy-start(s32[2,16]{1,0:T(2,128)} %constant.27.clone) | copy-start | bytes 388
  41.4 5.8 %collective-permute-start.8 = (bf16[128,128]{1,0:T(8,128)(2,1)S(1)}, bf16[128,128]{1,0:T(8,128)(2,1)S(1)}, u32[]{:S(2)}, u32[]{:S(2)}) collective-permute-start(bf16[128,128]{1,0:T(8,128)(2,1)S(1)} %get-tuple-element.15), channel_id=1, source_target_pairs={{0,24},{1,7},{2,26},{3,5},{4,28},{5,3},{6,30},{7,1},{8,16},{9,15},... | collective-permute-start | bytes 98312 | tf_op jit(solution)/shard_map/ppermute | solution.py:45
  44.3 5.6 %collective-permute-start.11 = (bf16[128,128]{1,0:T(8,128)(2,1)S(1)}, bf16[128,128]{1,0:T(8,128)(2,1)S(1)}, u32[]{:S(2)}, u32[]{:S(2)}) collective-permute-start(bf16[128,128]{1,0:T(8,128)(2,1)S(1)} %get-tuple-element.15), channel_id=1, source_target_pairs={{0,16},{1,5},{2,18},{3,7},{4,20},{5,1},{6,22},{7,3},{8,24},{9,13},... | collective-permute-start | bytes 98312 | tf_op jit(solution)/shard_map/ppermute | solution.py:45
  45.9 3.9 %collective-permute-start.10 = (bf16[128,128]{1,0:T(8,128)(2,1)S(1)}, bf16[128,128]{1,0:T(8,128)(2,1)S(1)}, u32[]{:S(2)}, u32[]{:S(2)}) collective-permute-start(bf16[128,128]{1,0:T(8,128)(2,1)S(1)} %get-tuple-element.15), channel_id=1, source_target_pairs={{0,8},{1,3},{2,10},{3,1},{4,12},{5,7},{6,14},{7,5},{8,0},{9,11},{1... | collective-permute-start | bytes 98312 | tf_op jit(solution)/shard_map/ppermute | solution.py:45
  47.8 5.7 %collective-permute-start.9 = (bf16[16,128,128]{2,1,0:T(8,128)(2,1)S(1)}, bf16[16,128,128]{2,1,0:T(8,128)(2,1)S(1)}, u32[]{:S(2)}, u32[]{:S(2)}) collective-permute-start(bf16[16,128,128]{2,1,0:T(8,128)(2,1)S(1)} %pick_blocks.1), channel_id=1, source_target_pairs={{0,1},{1,0},{2,3},{3,2},{4,5},{5,4},{6,7},{7,6},{8,9},{9,8},{10,11... | collective-permute-start | bytes 1572872 | tf_op jit(solution)/shard_map/ppermute | solution.py:36
  49.9 6.0 %collective-permute-start.14 = (bf16[512,128]{1,0:T(8,128)(2,1)S(1)}, bf16[512,128]{1,0:T(8,128)(2,1)S(1)}, u32[]{:S(2)}, u32[]{:S(2)}) collective-permute-start(bf16[512,128]{1,0:T(8,128)(2,1)S(1)} %constant_dynamic-update-slice_fusion.7.refs_0_), channel_id=1, source_target_pairs={{0,6},{1,25},{2,4},{3,27},{4,2},{5,29},{6,0},{7,31},{8,14},{9,17},... | collective-permute-start | bytes 393224 | tf_op jit(solution)/shard_map/ppermute | solution.py:45
  51.5 5.7 %collective-permute-start.13 = (bf16[512,128]{1,0:T(8,128)(2,1)S(1)}, bf16[512,128]{1,0:T(8,128)(2,1)S(1)}, u32[]{:S(2)}, u32[]{:S(2)}) collective-permute-start(bf16[512,128]{1,0:T(8,128)(2,1)S(1)} %constant_dynamic-update-slice_fusion.7.refs_0_), channel_id=1, source_target_pairs={{0,4},{1,17},{2,6},{3,19},{4,0},{5,21},{6,2},{7,23},{8,12},{9,25},... | collective-permute-start | bytes 393224 | tf_op jit(solution)/shard_map/ppermute | solution.py:45
  52.1 5.3 %collective-permute-start.12 = (bf16[512,128]{1,0:T(8,128)(2,1)S(1)}, bf16[512,128]{1,0:T(8,128)(2,1)S(1)}, u32[]{:S(2)}, u32[]{:S(2)}) collective-permute-start(bf16[512,128]{1,0:T(8,128)(2,1)S(1)} %constant_dynamic-update-slice_fusion.7.refs_0_), channel_id=1, source_target_pairs={{0,2},{1,9},{2,0},{3,11},{4,6},{5,13},{6,4},{7,15},{8,10},{9,1},{1... | collective-permute-start | bytes 393224 | tf_op jit(solution)/shard_map/ppermute | solution.py:45
  57.9 1.3 %collective-permute-start.15 = (f32[128,128]{1,0:T(8,128)S(1)}, f32[128,128]{1,0:T(8,128)S(1)}, u32[]{:S(2)}, u32[]{:S(2)}) collective-permute-start(f32[128,128]{1,0:T(8,128)S(1)} %get-tuple-element.18), channel_id=1, source_target_pairs={{0,1},{1,0},{2,3},{3,2},{4,5},{5,4},{6,7},{7,6},{8,9},{9,8},{10,11... | collective-permute-start | bytes 196616 | tf_op jit(solution)/shard_map/ppermute | solution.py:36
  59.2 5.8 %collective-permute-start.18 = (bf16[128,128]{1,0:T(8,128)(2,1)S(1)}, bf16[128,128]{1,0:T(8,128)(2,1)S(1)}, u32[]{:S(2)}, u32[]{:S(2)}) collective-permute-start(bf16[128,128]{1,0:T(8,128)(2,1)S(1)} %get-tuple-element.21), channel_id=1, source_target_pairs={{0,24},{1,7},{2,26},{3,5},{4,28},{5,3},{6,30},{7,1},{8,16},{9,15},... | collective-permute-start | bytes 98312 | tf_op jit(solution)/shard_map/ppermute | solution.py:45
  61.0 5.2 %collective-permute-start.17 = (bf16[128,128]{1,0:T(8,128)(2,1)S(1)}, bf16[128,128]{1,0:T(8,128)(2,1)S(1)}, u32[]{:S(2)}, u32[]{:S(2)}) collective-permute-start(bf16[128,128]{1,0:T(8,128)(2,1)S(1)} %get-tuple-element.21), channel_id=1, source_target_pairs={{0,16},{1,5},{2,18},{3,7},{4,20},{5,1},{6,22},{7,3},{8,24},{9,13},... | collective-permute-start | bytes 98312 | tf_op jit(solution)/shard_map/ppermute | solution.py:45
  61.1 5.1 %collective-permute-start.16 = (bf16[128,128]{1,0:T(8,128)(2,1)S(1)}, bf16[128,128]{1,0:T(8,128)(2,1)S(1)}, u32[]{:S(2)}, u32[]{:S(2)}) collective-permute-start(bf16[128,128]{1,0:T(8,128)(2,1)S(1)} %get-tuple-element.21), channel_id=1, source_target_pairs={{0,8},{1,3},{2,10},{3,1},{4,12},{5,7},{6,14},{7,5},{8,0},{9,11},{1... | collective-permute-start | bytes 98312 | tf_op jit(solution)/shard_map/ppermute | solution.py:45
  66.2 6.0 %collective-permute-start.21 = (bf16[512,128]{1,0:T(8,128)(2,1)S(1)}, bf16[512,128]{1,0:T(8,128)(2,1)S(1)}, u32[]{:S(2)}, u32[]{:S(2)}) collective-permute-start(bf16[512,128]{1,0:T(8,128)(2,1)S(1)} %pad_maximum_fusion.1.refs_0_), channel_id=1, source_target_pairs={{0,6},{1,25},{2,4},{3,27},{4,2},{5,29},{6,0},{7,31},{8,14},{9,17},... | collective-permute-start | bytes 393224 | tf_op jit(solution)/shard_map/ppermute | solution.py:45
  68.3 5.2 %collective-permute-start.20 = (bf16[512,128]{1,0:T(8,128)(2,1)S(1)}, bf16[512,128]{1,0:T(8,128)(2,1)S(1)}, u32[]{:S(2)}, u32[]{:S(2)}) collective-permute-start(bf16[512,128]{1,0:T(8,128)(2,1)S(1)} %pad_maximum_fusion.1.refs_0_), channel_id=1, source_target_pairs={{0,4},{1,17},{2,6},{3,19},{4,0},{5,21},{6,2},{7,23},{8,12},{9,25},... | collective-permute-start | bytes 393224 | tf_op jit(solution)/shard_map/ppermute | solution.py:45
  68.4 5.4 %collective-permute-start.19 = (bf16[512,128]{1,0:T(8,128)(2,1)S(1)}, bf16[512,128]{1,0:T(8,128)(2,1)S(1)}, u32[]{:S(2)}, u32[]{:S(2)}) collective-permute-start(bf16[512,128]{1,0:T(8,128)(2,1)S(1)} %pad_maximum_fusion.1.refs_0_), channel_id=1, source_target_pairs={{0,2},{1,9},{2,0},{3,11},{4,6},{5,13},{6,4},{7,15},{8,10},{9,1},{1... | collective-permute-start | bytes 393224 | tf_op jit(solution)/shard_map/ppermute | solution.py:45
  74.3 1.3 %collective-permute-start.22 = (f32[128,128]{1,0:T(8,128)S(1)}, f32[128,128]{1,0:T(8,128)S(1)}, u32[]{:S(2)}, u32[]{:S(2)}) collective-permute-start(f32[128,128]{1,0:T(8,128)S(1)} %get-tuple-element.20), channel_id=1, source_target_pairs={{0,1},{1,0},{2,3},{3,2},{4,5},{5,4},{6,7},{7,6},{8,9},{9,8},{10,11... | collective-permute-start | bytes 196616 | tf_op jit(solution)/shard_map/ppermute | solution.py:36
